TPU v7x, 32 devices: a whole 2x2x4 slice. The times are simulated.
32 devices in a mesh: blk: 16 (over z, y, x), beamk: 2 (over core).
Axes of the slice: x: 2, y: 2, z: 4, core: 2. Of those that a mesh axis runs over, the one named last changes fastest.
Arguments:
- sky: bfloat16 [32, 3072, 384], P('blk', 'beamk'), may hold values from -6 to 6
- beam: float32 [40, 2, 3072], P('beamk'), may hold values from -6 to 6
- wigner: bfloat16 [32, 40, 16, 3072], P('blk', 'beamk'), may hold values from -0.109375 to 0.109375
- m_list: int32 [32], P('blk'), may hold values from 0 to 3071, as said below
Outputs:
- cycle_coeffs: bfloat16 [16, 32, 40, 384], P('blk', None, 'beamk')
Inputs may be any that keep to these rules, and one draw needn't show every extreme that they name: `m_list`: entries 2i and 2i+1 hold m and 3071-m for some m below 1536; all entries are distinct, and some slot holds 0.
All inputs are finite; a program needn't handle non-finite values.
Results may differ from a plain program's by a relative error of at most 0.0049.
Values may be sent and summed in bfloat16 or wider, within the bound.
No kernel may reach another device: no remote copies, remote signals or barrier semaphores. Data moves between devices by JAX's collectives and lax.ppermute only.
A program may use at most 64 MiB of HBM per device.

v0:
```python
import functools

import jax
import jax.numpy as jnp
from jax import lax
from jax.experimental import pallas as pl
from jax.experimental.pallas import tpu as pltpu
from jax.sharding import PartitionSpec as P

KB = 40
LANES = 128
VMEM_LIMIT = 24 * 1024 * 1024


def tile_of(rows):
    return max(t for t in range(LANES, min(rows, 512) + 1, LANES) if rows % t == 0)


def whole(memory):
    return pl.BlockSpec(memory_space=memory)


def combine(acc):
    rows = acc.shape[0] // 2
    half = acc.shape[1] // 2
    swapped = pltpu.roll(acc[rows:], half, 1)
    column = lax.broadcasted_iota(jnp.int32, swapped.shape, 1)
    return acc[:rows] + jnp.where(column < half, -swapped, swapped)


def owner_of(distance, ways):
    return lax.rem(lax.axis_index("beamk") - distance + ways, ways)


def first_tile(m_value, owner, piece_rows, tile):
    return jnp.minimum(jnp.maximum(m_value - owner * piece_rows, 0) // tile, piece_rows // tile)


def first_kernel(ways, tile, m_ref, sky, wigner, beam, part, factors, sky_in, wigner_in, beam_in, own, acc, sky_sem, wigner_sem, beam_sem):
    slots, piece_rows, _ = sky.shape
    k_local, cycles = wigner.shape[1], wigner.shape[2]
    rows = k_local * cycles
    tiles = piece_rows // tile
    first_k = lax.axis_index("beamk") * k_local - KB // 2

    def beam_copy():
        return pltpu.make_async_copy(beam, beam_in, beam_sem)

    def sky_copy(slot, step):
        span = pl.ds(pl.multiple_of(step * tile, tile), tile)
        return pltpu.make_async_copy(sky.at[slot, span], sky_in.at[slot, step], sky_sem.at[slot, step])

    def wigner_copy(distance, slot, step):
        start = pl.multiple_of(owner_of(distance, ways) * piece_rows + step * tile, tile)
        return pltpu.make_async_copy(
            wigner.at[slot, :, :, pl.ds(start, tile)],
            wigner_in.at[distance, slot, step],
            wigner_sem.at[distance, slot, step],
        )

    def begin(distance, slot):
        return first_tile(m_ref[slot], owner_of(distance, ways), piece_rows, tile)

    def fill(target, distance, slot, step):
        start = pl.multiple_of(owner_of(distance, ways) * piece_rows + step * tile, tile)
        degrees = start + lax.broadcasted_iota(jnp.int32, (1, tile), 1)
        for k in range(k_local):
            lowest = jnp.maximum(m_ref[slot], jnp.abs(first_k + k))
            inside = degrees >= lowest
            values = wigner_in[distance, slot, step, k].astype(jnp.float32)
            beam_re = jnp.where(inside, beam_in[k, 0:1, pl.ds(start, tile)], 0.0)
            beam_im = jnp.where(inside, beam_in[k, 1:2, pl.ds(start, tile)], 0.0)
            target[k * cycles : (k + 1) * cycles, :] = (values * beam_re).astype(jnp.bfloat16)
            target[rows + k * cycles : rows + (k + 1) * cycles, :] = (values * beam_im).astype(jnp.bfloat16)

    beam_copy().start()
    for slot in range(slots):

        @pl.loop(begin(0, slot), tiles)
        def _(step):
            wigner_copy(0, slot, step).start()
            sky_copy(slot, step).start()

    for distance in range(1, ways):
        for slot in range(slots):

            @pl.loop(begin(distance, slot), tiles)
            def _(step):
                wigner_copy(distance, slot, step).start()

    beam_copy().wait()
    for slot in range(slots):
        acc[...] = jnp.zeros_like(acc)

        @pl.loop(begin(0, slot), tiles)
        def _(step):
            wigner_copy(0, slot, step).wait()
            fill(own, 0, slot, step)
            sky_copy(slot, step).wait()
            acc[...] += jnp.dot(own[...], sky_in[slot, step], preferred_element_type=jnp.float32)

        part[slot] = combine(acc[...])
    for distance in range(1, ways):
        for slot in range(slots):

            @pl.loop(begin(distance, slot), tiles)
            def _(step):
                wigner_copy(distance, slot, step).wait()
                fill(factors.at[distance - 1, slot, step], distance, slot, step)


def second_kernel(ways, tile, m_ref, part, factors, *refs):
    pieces, (out, acc, turned) = refs[: ways - 1], refs[ways - 1 :]
    slots, rows, columns = part.shape
    piece_rows = pieces[0].shape[1]
    tiles = piece_rows // tile
    cycles, width, _ = out.shape
    k_local = width // slots
    for slot in range(slots):
        acc[...] = jnp.zeros_like(acc)
        for distance in range(1, ways):
            begin = first_tile(m_ref[slot], owner_of(distance, ways), piece_rows, tile)

            @pl.loop(begin, tiles)
            def _(step):
                span = pl.ds(pl.multiple_of(step * tile, tile), tile)
                acc[...] += jnp.dot(
                    factors[distance - 1, slot, step], pieces[distance - 1][slot, span], preferred_element_type=jnp.float32
                )

        total = part[slot] + combine(acc[...])
        for lane in range(columns // LANES):
            for k in range(k_local):
                turned[lane, pl.ds(slot * k_local + k, cycles, stride=width), :] = total[
                    k * cycles : (k + 1) * cycles, lane * LANES : (lane + 1) * LANES
                ]
    for cycle in range(cycles):
        for lane in range(columns // LANES):
            out[cycle, :, lane * LANES : (lane + 1) * LANES] = turned[lane, cycle * width : (cycle + 1) * width].astype(out.dtype)


def local(sky, beam, wigner, m_list, *, ways):
    slots, piece_rows, columns = sky.shape
    _, k_local, cycles, degrees = wigner.shape
    rows = k_local * cycles
    tile = tile_of(piece_rows)
    tiles = piece_rows // tile
    lane_tiles = columns // LANES
    width = slots * k_local
    params = pltpu.CompilerParams(vmem_limit_bytes=VMEM_LIMIT)

    pieces = []
    for shift in range(1, ways):
        perm = [(c, (c + shift) % ways) for c in range(ways)]
        pieces.append(pltpu.with_memory_space_constraint(lax.ppermute(sky, "beamk", perm), pltpu.VMEM))
    sky, beam, wigner, m_list = (pltpu.with_memory_space_constraint(x, pltpu.HBM) for x in (sky, beam, wigner, m_list))

    part, factors = pl.pallas_call(
        functools.partial(first_kernel, ways, tile),
        out_shape=(
            pltpu.VMEM((slots, rows, columns), jnp.float32),
            pltpu.VMEM((ways - 1, slots, tiles, 2 * rows, tile), jnp.bfloat16),
        ),
        in_specs=[whole(pltpu.SMEM), whole(pltpu.HBM), whole(pltpu.HBM), whole(pltpu.HBM)],
        out_specs=(whole(pltpu.VMEM), whole(pltpu.VMEM)),
        scratch_shapes=[
            pltpu.VMEM((slots, tiles, tile, columns), jnp.bfloat16),
            pltpu.VMEM((ways, slots, tiles, k_local, cycles, tile), jnp.bfloat16),
            pltpu.VMEM(beam.shape, jnp.float32),
            pltpu.VMEM((2 * rows, tile), jnp.bfloat16),
            pltpu.VMEM((2 * rows, columns), jnp.float32),
            pltpu.SemaphoreType.DMA((slots, tiles)),
            pltpu.SemaphoreType.DMA((ways, slots, tiles)),
            pltpu.SemaphoreType.DMA,
        ],
        compiler_params=params,
        cost_estimate=pl.CostEstimate(
            flops=4 * slots * rows * piece_rows * columns, bytes_accessed=8 * 1024 * 1024, transcendentals=0
        ),
        name="own_half",
    )(m_list, sky, wigner, beam)

    blocks = pl.pallas_call(
        functools.partial(second_kernel, ways, tile),
        out_shape=pltpu.VMEM((cycles, width, columns), jnp.bfloat16),
        in_specs=[whole(pltpu.SMEM)] + [whole(pltpu.VMEM)] * (ways + 1),
        out_specs=whole(pltpu.VMEM),
        scratch_shapes=[
            pltpu.VMEM((2 * rows, columns), jnp.float32),
            pltpu.VMEM((lane_tiles, cycles * width, LANES), jnp.float32),
        ],
        compiler_params=params,
        cost_estimate=pl.CostEstimate(
            flops=4 * slots * rows * piece_rows * columns, bytes_accessed=8 * 1024 * 1024, transcendentals=0
        ),
        name="other_half",
    )(m_list, part, factors, *pieces)
    received = lax.all_to_all(blocks, "blk", split_axis=0, concat_axis=0, tiled=True)
    return received.reshape(1, -1, k_local, columns)


def solution(mesh):
    in_specs = (
        P("blk", "beamk", None),
        P("beamk", None, None),
        P("blk", "beamk", None, None),
        P("blk"),
    )
    out_specs = P("blk", None, "beamk", None)
    body = functools.partial(local, ways=mesh.shape["beamk"])
    return jax.shard_map(body, mesh=mesh, in_specs=in_specs, out_specs=out_specs, check_vma=False)
```

profile of v0, /device:TPU:0, one launch (start us, length us, event | category | flops | bytes accessed | tf_op | source)
XLA Modules:
  0.0 32.2 jit_solution(3592805034005914361)
XLA Ops:
  0.0 0.5 %collective-permute-start = (bf16[2,1536,384]{2,1,0:T(8,128)(2,1)}, bf16[2,1536,384]{2,1,0:T(8,128)(2,1)S(1)}, u32[]{:S(2)}, u32[]{:S(2)}) collective-permute-start(bf16[2,1536,384]{2,1,0:T(8,128)(2,1)} %sky.1), channel_id=1, source_target_pairs={{0,1},{1,0},{2,3},{3,2},{4,5},{5,4},{6,7},{7,6},{8,9},{9,8},{10,11... | collective-permute-start | bytes 7077896 | tf_op jit(solution)/shard_map/ppermute | solution.py:155
  0.5 3.9 %own_half.1 = (f32[2,320,384]{2,1,0:T(8,128)S(1)}, bf16[1,2,3,640,512]{4,3,2,1,0:T(8,128)(2,1)S(1)}) custom-call(s32[2]{0:T(128)} %m_ref.3, bf16[2,1536,384]{2,1,0:T(8,128)(2,1)} %sky.1, bf16[2,20,16,3072]{3,2,1,0:T(8,128)(2,1)} %wigner.1, f32[20,2,3072]{2,1,0:T(2,128)} %beam.1), custom_call_target="tpu_custom_call" | custom-call | flops 1509949440 | bytes 8388608 | tf_op jit(solution)/shard_map/own_half/pallas_call | solution.py:158
  4.4 0.4 %collective-permute-done.refs_0_ = bf16[2,1536,384]{2,1,0:T(8,128)(2,1)S(1)} collective-permute-done((bf16[2,1536,384]{2,1,0:T(8,128)(2,1)}, bf16[2,1536,384]{2,1,0:T(8,128)(2,1)S(1)}, u32[]{:S(2)}, u32[]{:S(2)}) %collective-permute-start) | collective-permute-done | bytes 2359328 | tf_op jit(solution)/shard_map/ppermute | solution.py:155
  4.8 4.3 %other_half.1 = bf16[16,40,384]{2,1,0:T(8,128)(2,1)S(1)} custom-call(s32[2]{0:T(128)} %m_ref.3, f32[2,320,384]{2,1,0:T(8,128)S(1)} %get-tuple-element.7.part, bf16[1,2,3,640,512]{4,3,2,1,0:T(8,128)(2,1)S(1)} %get-tuple-element.8.factors, bf16[2,1536,384]{2,1,0:T(8,128)(2,1)S(1)} %collective-permute-done.refs_0_), custom_call_target="tpu_custom_call" | custom-call | flops 1509949440 | bytes 8388608 | tf_op jit(solution)/shard_map/other_half/pallas_call | solution.py:183
  9.1 22.1 %all_to_all.5 = bf16[16,40,384]{2,1,0:T(8,128)(2,1)S(1)} all-to-all(bf16[16,40,384]{2,1,0:T(8,128)(2,1)S(1)} %other_half.1), channel_id=1, replica_groups=mesh['blk'=16,'beamk'=2] {'blk'}, dimensions={0} | all-to-all | bytes 983040 | tf_op jit(solution)/shard_map/all_to_all | solution.py:198
  31.3 0.1 reshape.3
  31.4 0.8 %copy.6 = bf16[1,32,20,384]{3,1,2,0:T(8,128)(2,1)} copy(bf16[1,32,20,384]{3,2,1,0:T(8,128)(2,1)S(1)} %reshape.3) | data formatting | bytes 983040 | tf_op jit(solution)/shard_map/reshape | solution.py:199
Async XLA Ops:
  0.0 4.8 %collective-permute-start = (bf16[2,1536,384]{2,1,0:T(8,128)(2,1)}, bf16[2,1536,384]{2,1,0:T(8,128)(2,1)S(1)}, u32[]{:S(2)}, u32[]{:S(2)}) collective-permute-start(bf16[2,1536,384]{2,1,0:T(8,128)(2,1)} %sky.1), channel_id=1, source_target_pairs={{0,1},{1,0},{2,3},{3,2},{4,5},{5,4},{6,7},{7,6},{8,9},{9,8},{10,11... | collective-permute-start | bytes 7077896 | tf_op jit(solution)/shard_map/ppermute | solution.py:155
where the time goes:
time: 32.5 us; the launch traced here: 32.2 us
  blocking collectives  22.1 us (68%)
  Pallas kernels  8.24 us (25%)
  local copies, waits for them, and re-layouts  0.94 us (3%)
  starting transfers between devices  0.45 us (1%)
  waiting for transfers between devices  0.43 us (1%)
    all_to_all x1, blocking collectives, local(): lax.all_to_all(blocks, 'blk', split_axis=0, concat_axis=0, tiled=True)  22.1 us
    pallas_call x1, Pallas kernels, local(): pl.pallas_call(functools.partial(second_kernel, ways, tile), out_shape=pl...  4.31 us
    pallas_call x1, Pallas kernels, local(): pl.pallas_call(functools.partial(first_kernel, ways, tile), out_shape=(pl...  3.93 us
    reshape x2, local copies, waits for them, and re-layouts, local(): return received.reshape(1, -1, k_local, columns)  0.94 us
  transfers between devices with their start and end apart: 1, of which 1 were waited for; matrix products, arithmetic and copies ran while one was open for 0% of the time, Pallas kernels for 12%

commit v1 on v0

--- a/solution.py
+++ b/solution.py
@@ -20,12 +20,11 @@
     return pl.BlockSpec(memory_space=memory)
 
 
-def combine(acc):
-    rows = acc.shape[0] // 2
-    half = acc.shape[1] // 2
-    swapped = pltpu.roll(acc[rows:], half, 1)
+def turn_by_i(rows):
+    half = rows.shape[1] // 2
+    swapped = pltpu.roll(rows, half, 1)
     column = lax.broadcasted_iota(jnp.int32, swapped.shape, 1)
-    return acc[:rows] + jnp.where(column < half, -swapped, swapped)
+    return jnp.where(column < half, -swapped, swapped)
 
 
 def owner_of(distance, ways):
@@ -36,15 +35,17 @@
     return jnp.minimum(jnp.maximum(m_value - owner * piece_rows, 0) // tile, piece_rows // tile)
 
 
-def first_kernel(ways, tile, m_ref, sky, wigner, beam, part, factors, sky_in, wigner_in, beam_in, own, acc, sky_sem, wigner_sem, beam_sem):
-    slots, piece_rows, _ = sky.shape
+def first_kernel(ways, tile, m_ref, sky, wigner, beam, part, factors, sky_in, wigner_in, beam_in, even, odd, acc, sky_sem, wigner_sem, beam_sem):
+    slots, piece_rows, columns = sky.shape
     k_local, cycles = wigner.shape[1], wigner.shape[2]
     rows = k_local * cycles
     tiles = piece_rows // tile
+    all_tiles = ways * tiles
     first_k = lax.axis_index("beamk") * k_local - KB // 2
 
-    def beam_copy():
-        return pltpu.make_async_copy(beam, beam_in, beam_sem)
+    def beam_copy(index):
+        span = pl.ds(pl.multiple_of(index * tile, tile), tile)
+        return pltpu.make_async_copy(beam.at[:, :, span], beam_in.at[index], beam_sem.at[index])
 
     def sky_copy(slot, step):
         span = pl.ds(pl.multiple_of(step * tile, tile), tile)
@@ -62,18 +63,15 @@
         return first_tile(m_ref[slot], owner_of(distance, ways), piece_rows, tile)
 
     def fill(target, distance, slot, step):
-        start = pl.multiple_of(owner_of(distance, ways) * piece_rows + step * tile, tile)
-        degrees = start + lax.broadcasted_iota(jnp.int32, (1, tile), 1)
-        for k in range(k_local):
-            lowest = jnp.maximum(m_ref[slot], jnp.abs(first_k + k))
-            inside = degrees >= lowest
+        index = owner_of(distance, ways) * tiles + step
+        index = jnp.where(index == m_ref[slot] // tile, all_tiles + slot, index)
+        for k in range(k_local):
             values = wigner_in[distance, slot, step, k].astype(jnp.float32)
-            beam_re = jnp.where(inside, beam_in[k, 0:1, pl.ds(start, tile)], 0.0)
-            beam_im = jnp.where(inside, beam_in[k, 1:2, pl.ds(start, tile)], 0.0)
-            target[k * cycles : (k + 1) * cycles, :] = (values * beam_re).astype(jnp.bfloat16)
-            target[rows + k * cycles : rows + (k + 1) * cycles, :] = (values * beam_im).astype(jnp.bfloat16)
-
-    beam_copy().start()
+            target[k * cycles : (k + 1) * cycles, :] = (values * beam_in[index, k, 0:1, :]).astype(jnp.bfloat16)
+            target[rows + k * cycles : rows + (k + 1) * cycles, :] = (values * beam_in[index, k, 1:2, :]).astype(jnp.bfloat16)
+
+    for index in range(all_tiles):
+        beam_copy(index).start()
     for slot in range(slots):
 
         @pl.loop(begin(0, slot), tiles)
@@ -88,25 +86,72 @@
             def _(step):
                 wigner_copy(distance, slot, step).start()
 
-    beam_copy().wait()
+    acc[...] = jnp.zeros_like(acc)
+    for index in range(all_tiles):
+        beam_copy(index).wait()
     for slot in range(slots):
-        acc[...] = jnp.zeros_like(acc)
-
-        @pl.loop(begin(0, slot), tiles)
-        def _(step):
+        index = m_ref[slot] // tile
+        degrees = index * tile + lax.broadcasted_iota(jnp.int32, (2, tile), 1)
+        for k in range(k_local):
+            lowest = jnp.maximum(m_ref[slot], jnp.abs(first_k + k))
+            beam_in[all_tiles + slot, k] = jnp.where(degrees >= lowest, beam_in[index, k], 0.0)
+
+    starts = [begin(0, slot) for slot in range(slots)]
+    ends = []
+    for slot in range(slots):
+        ends.append((ends[-1] if ends else 0) + tiles - starts[slot])
+    count = ends[-1]
+
+    def place(item):
+        item = jnp.minimum(item, count - 1)
+        slot = jnp.int32(0)
+        step = item + starts[0]
+        for later in range(1, slots):
+            beyond = item >= ends[later - 1]
+            slot = jnp.where(beyond, later, slot)
+            step = jnp.where(beyond, item - ends[later - 1] + starts[later], step)
+        return slot, step
+
+    def arrive(item):
+        @pl.when(item < count)
+        def _():
+            slot, step = place(item)
             wigner_copy(0, slot, step).wait()
-            fill(own, 0, slot, step)
             sky_copy(slot, step).wait()
-            acc[...] += jnp.dot(own[...], sky_in[slot, step], preferred_element_type=jnp.float32)
-
-        part[slot] = combine(acc[...])
+
+    def work(item, present, other):
+        arrive(item + 1)
+        slot, step = place(item)
+        fill(other, 0, *place(item + 1))
+        acc[slot] += jnp.dot(present[...], sky_in[slot, step], preferred_element_type=jnp.float32)
+
+    @pl.when(count > 0)
+    def _():
+        arrive(jnp.int32(0))
+        fill(even, 0, *place(jnp.int32(0)))
+
+        @pl.loop(0, (count + 1) // 2)
+        def _(pair):
+            work(2 * pair, even, odd)
+
+            @pl.when(2 * pair + 1 < count)
+            def _():
+                work(2 * pair + 1, odd, even)
+
     for distance in range(1, ways):
         for slot in range(slots):
 
             @pl.loop(begin(distance, slot), tiles)
             def _(step):
                 wigner_copy(distance, slot, step).wait()
-                fill(factors.at[distance - 1, slot, step], distance, slot, step)
+                span = pl.ds(pl.multiple_of(step * tile, tile), tile)
+                fill(factors.at[distance - 1, slot, :, span], distance, slot, step)
+
+    @pl.loop(0, slots)
+    def _(slot):
+        for k in range(k_local):
+            span = slice(k * cycles, (k + 1) * cycles)
+            part[slot, span] = acc[slot, span] + turn_by_i(acc[slot, rows + k * cycles : rows + (k + 1) * cycles])
 
 
 def second_kernel(ways, tile, m_ref, part, factors, *refs):
@@ -116,24 +161,35 @@
     tiles = piece_rows // tile
     cycles, width, _ = out.shape
     k_local = width // slots
-    for slot in range(slots):
-        acc[...] = jnp.zeros_like(acc)
+
+    @pl.loop(0, slots)
+    def _(slot):
         for distance in range(1, ways):
-            begin = first_tile(m_ref[slot], owner_of(distance, ways), piece_rows, tile)
-
-            @pl.loop(begin, tiles)
-            def _(step):
-                span = pl.ds(pl.multiple_of(step * tile, tile), tile)
-                acc[...] += jnp.dot(
-                    factors[distance - 1, slot, step], pieces[distance - 1][slot, span], preferred_element_type=jnp.float32
-                )
-
-        total = part[slot] + combine(acc[...])
-        for lane in range(columns // LANES):
-            for k in range(k_local):
-                turned[lane, pl.ds(slot * k_local + k, cycles, stride=width), :] = total[
-                    k * cycles : (k + 1) * cycles, lane * LANES : (lane + 1) * LANES
-                ]
+            missing = first_tile(m_ref[slot], owner_of(distance, ways), piece_rows, tile)
+            for skipped in range(tiles):
+
+                @pl.when(missing == skipped)
+                def _():
+                    span = slice(skipped * tile, piece_rows)
+                    term = jnp.dot(
+                        factors[distance - 1, slot, :, span],
+                        pieces[distance - 1][slot, span],
+                        preferred_element_type=jnp.float32,
+                    )
+                    acc[...] = term if distance == 1 else acc[...] + term
+
+            if distance == 1:
+
+                @pl.when(missing == tiles)
+                def _():
+                    acc[...] = jnp.zeros_like(acc)
+
+        for k in range(k_local):
+            span = slice(k * cycles, (k + 1) * cycles)
+            total = part[slot, span] + acc[span] + turn_by_i(acc[rows + k * cycles : rows + (k + 1) * cycles])
+            for lane in range(columns // LANES):
+                turned[lane, pl.ds(slot * k_local + k, cycles, stride=width), :] = total[:, lane * LANES : (lane + 1) * LANES]
+
     for cycle in range(cycles):
         for lane in range(columns // LANES):
             out[cycle, :, lane * LANES : (lane + 1) * LANES] = turned[lane, cycle * width : (cycle + 1) * width].astype(out.dtype)
@@ -159,19 +215,20 @@
         functools.partial(first_kernel, ways, tile),
         out_shape=(
             pltpu.VMEM((slots, rows, columns), jnp.float32),
-            pltpu.VMEM((ways - 1, slots, tiles, 2 * rows, tile), jnp.bfloat16),
+            pltpu.VMEM((ways - 1, slots, 2 * rows, piece_rows), jnp.bfloat16),
         ),
         in_specs=[whole(pltpu.SMEM), whole(pltpu.HBM), whole(pltpu.HBM), whole(pltpu.HBM)],
         out_specs=(whole(pltpu.VMEM), whole(pltpu.VMEM)),
         scratch_shapes=[
             pltpu.VMEM((slots, tiles, tile, columns), jnp.bfloat16),
             pltpu.VMEM((ways, slots, tiles, k_local, cycles, tile), jnp.bfloat16),
-            pltpu.VMEM(beam.shape, jnp.float32),
+            pltpu.VMEM((ways * tiles + slots, k_local, 2, tile), jnp.float32),
             pltpu.VMEM((2 * rows, tile), jnp.bfloat16),
-            pltpu.VMEM((2 * rows, columns), jnp.float32),
+            pltpu.VMEM((2 * rows, tile), jnp.bfloat16),
+            pltpu.VMEM((slots, 2 * rows, columns), jnp.float32),
             pltpu.SemaphoreType.DMA((slots, tiles)),
             pltpu.SemaphoreType.DMA((ways, slots, tiles)),
-            pltpu.SemaphoreType.DMA,
+            pltpu.SemaphoreType.DMA((ways * tiles,)),
         ],
         compiler_params=params,
         cost_estimate=pl.CostEstimate(

time: 32.5 us -> 32.1 us (0.988)
  Pallas kernels: 8.24 us -> 7.54 us
  blocking collectives: 22.1 us -> 22.6 us
    pallas_call x1, Pallas kernels: 4.31 us -> 3.57 us  [local(): pl.pallas_call(functools.partial(second_kernel, ways, tile), out_shape=pl...]
    all_to_all x1, blocking collectives: 22.1 us -> 22.6 us  [local(): lax.all_to_all(blocks, 'blk', split_axis=0, concat_axis=0, tiled=True)]
where the time goes in v1:
time: 32.1 us; the launch traced here: 31.9 us
  blocking collectives  22.6 us (70%)
  Pallas kernels  7.54 us (23%)
  local copies, waits for them, and re-layouts  0.94 us (3%)
  starting transfers between devices  0.45 us (1%)
  waiting for transfers between devices  0.39 us (1%)
    all_to_all x1, blocking collectives, local(): lax.all_to_all(blocks, 'blk', split_axis=0, concat_axis=0, tiled=True)  22.6 us
    pallas_call x1, Pallas kernels, local(): pl.pallas_call(functools.partial(first_kernel, ways, tile), out_shape=(pl...  3.98 us
    pallas_call x1, Pallas kernels, local(): pl.pallas_call(functools.partial(second_kernel, ways, tile), out_shape=pl...  3.57 us
    reshape x2, local copies, waits for them, and re-layouts, local(): return received.reshape(1, -1, k_local, columns)  0.94 us
  transfers between devices with their start and end apart: 1, of which 1 were waited for; matrix products, arithmetic and copies ran while one was open for 0% of the time, Pallas kernels for 12%

profile of v1, /device:TPU:0, one launch (start us, length us, event | category | flops | bytes accessed | tf_op | source)
XLA Modules:
  0.0 31.9 jit_solution(6427858930506471347)
XLA Ops:
  0.0 0.5 %collective-permute-start = (bf16[2,1536,384]{2,1,0:T(8,128)(2,1)}, bf16[2,1536,384]{2,1,0:T(8,128)(2,1)S(1)}, u32[]{:S(2)}, u32[]{:S(2)}) collective-permute-start(bf16[2,1536,384]{2,1,0:T(8,128)(2,1)} %sky.1), channel_id=1, source_target_pairs={{0,1},{1,0},{2,3},{3,2},{4,5},{5,4},{6,7},{7,6},{8,9},{9,8},{10,11... | collective-permute-start | bytes 7077896 | tf_op jit(solution)/shard_map/ppermute | solution.py:211
  0.5 4.0 %own_half.1 = (f32[2,320,384]{2,1,0:T(8,128)S(1)}, bf16[1,2,640,1536]{3,2,1,0:T(8,128)(2,1)S(1)}) custom-call(s32[2]{0:T(128)} %m_ref.3, bf16[2,1536,384]{2,1,0:T(8,128)(2,1)} %sky.1, bf16[2,20,16,3072]{3,2,1,0:T(8,128)(2,1)} %wigner.1, f32[20,2,3072]{2,1,0:T(2,128)} %beam.1), custom_call_target="tpu_custom_call" | custom-call | flops 1509949440 | bytes 8388608 | tf_op jit(solution)/shard_map/own_half/pallas_call | solution.py:214
  4.4 0.4 %collective-permute-done.refs_0_ = bf16[2,1536,384]{2,1,0:T(8,128)(2,1)S(1)} collective-permute-done((bf16[2,1536,384]{2,1,0:T(8,128)(2,1)}, bf16[2,1536,384]{2,1,0:T(8,128)(2,1)S(1)}, u32[]{:S(2)}, u32[]{:S(2)}) %collective-permute-start) | collective-permute-done | bytes 2359328 | tf_op jit(solution)/shard_map/ppermute | solution.py:211
  4.8 3.6 %other_half.1 = bf16[16,40,384]{2,1,0:T(8,128)(2,1)S(1)} custom-call(s32[2]{0:T(128)} %m_ref.3, f32[2,320,384]{2,1,0:T(8,128)S(1)} %get-tuple-element.7.part, bf16[1,2,640,1536]{3,2,1,0:T(8,128)(2,1)S(1)} %get-tuple-element.8.factors, bf16[2,1536,384]{2,1,0:T(8,128)(2,1)S(1)} %collective-permute-done.refs_0_), custom_call_target="tpu_custom_call" | custom-call | flops 1509949440 | bytes 8388608 | tf_op jit(solution)/shard_map/other_half/pallas_call | solution.py:240
  8.4 22.6 %all_to_all.5 = bf16[16,40,384]{2,1,0:T(8,128)(2,1)S(1)} all-to-all(bf16[16,40,384]{2,1,0:T(8,128)(2,1)S(1)} %other_half.1), channel_id=1, replica_groups=mesh['blk'=16,'beamk'=2] {'blk'}, dimensions={0} | all-to-all | bytes 983040 | tf_op jit(solution)/shard_map/all_to_all | solution.py:255
  31.0 0.1 reshape.3
  31.1 0.8 %copy.6 = bf16[1,32,20,384]{3,1,2,0:T(8,128)(2,1)} copy(bf16[1,32,20,384]{3,2,1,0:T(8,128)(2,1)S(1)} %reshape.3) | data formatting | bytes 983040 | tf_op jit(solution)/shard_map/reshape | solution.py:256
Async XLA Ops:
  0.0 4.8 %collective-permute-start = (bf16[2,1536,384]{2,1,0:T(8,128)(2,1)}, bf16[2,1536,384]{2,1,0:T(8,128)(2,1)S(1)}, u32[]{:S(2)}, u32[]{:S(2)}) collective-permute-start(bf16[2,1536,384]{2,1,0:T(8,128)(2,1)} %sky.1), channel_id=1, source_target_pairs={{0,1},{1,0},{2,3},{3,2},{4,5},{5,4},{6,7},{7,6},{8,9},{9,8},{10,11... | collective-permute-start | bytes 7077896 | tf_op jit(solution)/shard_map/ppermute | solution.py:211

commit v2 on v1

--- a/solution.py
+++ b/solution.py
@@ -35,13 +35,19 @@
     return jnp.minimum(jnp.maximum(m_value - owner * piece_rows, 0) // tile, piece_rows // tile)
 
 
-def first_kernel(ways, tile, m_ref, sky, wigner, beam, part, factors, sky_in, wigner_in, beam_in, even, odd, acc, sky_sem, wigner_sem, beam_sem):
+def first_kernel(
+    ways, tile, m_list, sky, wigner, beam, part, factors, info, m_ref, sky_in, wigner_in, beam_in, own, acc, m_sem, sky_sem, wigner_sem, beam_sem
+):
     slots, piece_rows, columns = sky.shape
     k_local, cycles = wigner.shape[1], wigner.shape[2]
     rows = k_local * cycles
     tiles = piece_rows // tile
     all_tiles = ways * tiles
     first_k = lax.axis_index("beamk") * k_local - KB // 2
+    last = tiles - 1
+
+    def m_copy():
+        return pltpu.make_async_copy(m_list, m_ref, m_sem)
 
     def beam_copy(index):
         span = pl.ds(pl.multiple_of(index * tile, tile), tile)
@@ -49,7 +55,7 @@
 
     def sky_copy(slot, step):
         span = pl.ds(pl.multiple_of(step * tile, tile), tile)
-        return pltpu.make_async_copy(sky.at[slot, span], sky_in.at[slot, step], sky_sem.at[slot, step])
+        return pltpu.make_async_copy(sky.at[slot, span], sky_in.at[slot, span], sky_sem.at[slot, step])
 
     def wigner_copy(distance, slot, step):
         start = pl.multiple_of(owner_of(distance, ways) * piece_rows + step * tile, tile)
@@ -70,12 +76,30 @@
             target[k * cycles : (k + 1) * cycles, :] = (values * beam_in[index, k, 0:1, :]).astype(jnp.bfloat16)
             target[rows + k * cycles : rows + (k + 1) * cycles, :] = (values * beam_in[index, k, 1:2, :]).astype(jnp.bfloat16)
 
+    upper = 2 * (owner_of(0, ways) + 1) > ways
+    early = [jnp.bool_(True) if slot % 2 == 0 else upper for slot in range(slots)]
+    m_copy().start()
+    for slot in range(slots):
+
+        @pl.when(early[slot])
+        def _():
+            wigner_copy(0, slot, last).start()
+            sky_copy(slot, last).start()
+
     for index in range(all_tiles):
         beam_copy(index).start()
-    for slot in range(slots):
-
-        @pl.loop(begin(0, slot), tiles)
-        def _(step):
+    m_copy().wait()
+    for slot in range(slots):
+        begins = begin(0, slot)
+
+        @pl.when(jnp.logical_and(begins < tiles, jnp.logical_not(early[slot])))
+        def _():
+            wigner_copy(0, slot, last).start()
+            sky_copy(slot, last).start()
+
+        @pl.loop(begins + 1, tiles)
+        def _(later):
+            step = tiles - 1 - later + begins
             wigner_copy(0, slot, step).start()
             sky_copy(slot, step).start()
 
@@ -86,7 +110,8 @@
             def _(step):
                 wigner_copy(distance, slot, step).start()
 
-    acc[...] = jnp.zeros_like(acc)
+    for slot in range(slots):
+        info[slot : slot + 1, :] = jnp.full((1, LANES), m_ref[slot].astype(jnp.float32))
     for index in range(all_tiles):
         beam_copy(index).wait()
     for slot in range(slots):
@@ -96,76 +121,65 @@
             lowest = jnp.maximum(m_ref[slot], jnp.abs(first_k + k))
             beam_in[all_tiles + slot, k] = jnp.where(degrees >= lowest, beam_in[index, k], 0.0)
 
-    starts = [begin(0, slot) for slot in range(slots)]
-    ends = []
-    for slot in range(slots):
-        ends.append((ends[-1] if ends else 0) + tiles - starts[slot])
-    count = ends[-1]
-
-    def place(item):
-        item = jnp.minimum(item, count - 1)
-        slot = jnp.int32(0)
-        step = item + starts[0]
-        for later in range(1, slots):
-            beyond = item >= ends[later - 1]
-            slot = jnp.where(beyond, later, slot)
-            step = jnp.where(beyond, item - ends[later - 1] + starts[later], step)
-        return slot, step
-
-    def arrive(item):
-        @pl.when(item < count)
-        def _():
-            slot, step = place(item)
+    @pl.loop(0, slots)
+    def _(slot):
+        begins = begin(0, slot)
+
+        @pl.loop(begins, tiles)
+        def _(later):
+            step = tiles - 1 - later + begins
             wigner_copy(0, slot, step).wait()
+            span = pl.ds(pl.multiple_of(step * tile, tile), tile)
+            fill(own.at[:, span], 0, slot, step)
             sky_copy(slot, step).wait()
 
-    def work(item, present, other):
-        arrive(item + 1)
-        slot, step = place(item)
-        fill(other, 0, *place(item + 1))
-        acc[slot] += jnp.dot(present[...], sky_in[slot, step], preferred_element_type=jnp.float32)
-
-    @pl.when(count > 0)
-    def _():
-        arrive(jnp.int32(0))
-        fill(even, 0, *place(jnp.int32(0)))
-
-        @pl.loop(0, (count + 1) // 2)
-        def _(pair):
-            work(2 * pair, even, odd)
-
-            @pl.when(2 * pair + 1 < count)
+        for skipped in range(tiles):
+
+            @pl.when(begins == skipped)
             def _():
-                work(2 * pair + 1, odd, even)
+                span = slice(skipped * tile, piece_rows)
+                acc[...] = jnp.dot(own[:, span], sky_in[slot, span], preferred_element_type=jnp.float32)
+
+        @pl.when(begins == tiles)
+        def _():
+            acc[...] = jnp.zeros_like(acc)
+
+        for k in range(k_local):
+            span = slice(k * cycles, (k + 1) * cycles)
+            part[slot, span] = acc[span] + turn_by_i(acc[rows + k * cycles : rows + (k + 1) * cycles])
 
     for distance in range(1, ways):
-        for slot in range(slots):
-
+
+        @pl.loop(0, slots)
+        def _(slot):
             @pl.loop(begin(distance, slot), tiles)
             def _(step):
                 wigner_copy(distance, slot, step).wait()
                 span = pl.ds(pl.multiple_of(step * tile, tile), tile)
                 fill(factors.at[distance - 1, slot, :, span], distance, slot, step)
 
-    @pl.loop(0, slots)
-    def _(slot):
-        for k in range(k_local):
-            span = slice(k * cycles, (k + 1) * cycles)
-            part[slot, span] = acc[slot, span] + turn_by_i(acc[slot, rows + k * cycles : rows + (k + 1) * cycles])
-
-
-def second_kernel(ways, tile, m_ref, part, factors, *refs):
+    for slot in range(slots):
+
+        @pl.when(jnp.logical_and(begin(0, slot) == tiles, early[slot]))
+        def _():
+            wigner_copy(0, slot, last).wait()
+            sky_copy(slot, last).wait()
+
+
+def second_kernel(ways, tile, info, part, factors, *refs):
     pieces, (out, acc, turned) = refs[: ways - 1], refs[ways - 1 :]
     slots, rows, columns = part.shape
     piece_rows = pieces[0].shape[1]
     tiles = piece_rows // tile
     cycles, width, _ = out.shape
     k_local = width // slots
+    pitch = turned.shape[1] // cycles
 
     @pl.loop(0, slots)
     def _(slot):
+        m_value = jnp.max(info[pl.ds(slot, 1), :]).astype(jnp.int32)
         for distance in range(1, ways):
-            missing = first_tile(m_ref[slot], owner_of(distance, ways), piece_rows, tile)
+            missing = first_tile(m_value, owner_of(distance, ways), piece_rows, tile)
             for skipped in range(tiles):
 
                 @pl.when(missing == skipped)
@@ -188,11 +202,11 @@
             span = slice(k * cycles, (k + 1) * cycles)
             total = part[slot, span] + acc[span] + turn_by_i(acc[rows + k * cycles : rows + (k + 1) * cycles])
             for lane in range(columns // LANES):
-                turned[lane, pl.ds(slot * k_local + k, cycles, stride=width), :] = total[:, lane * LANES : (lane + 1) * LANES]
+                turned[lane, pl.ds(slot * k_local + k, cycles, stride=pitch), :] = total[:, lane * LANES : (lane + 1) * LANES]
 
     for cycle in range(cycles):
         for lane in range(columns // LANES):
-            out[cycle, :, lane * LANES : (lane + 1) * LANES] = turned[lane, cycle * width : (cycle + 1) * width].astype(out.dtype)
+            out[cycle, :, lane * LANES : (lane + 1) * LANES] = turned[lane, cycle * pitch : cycle * pitch + width].astype(out.dtype)
 
 
 def local(sky, beam, wigner, m_list, *, ways):
@@ -211,21 +225,23 @@
         pieces.append(pltpu.with_memory_space_constraint(lax.ppermute(sky, "beamk", perm), pltpu.VMEM))
     sky, beam, wigner, m_list = (pltpu.with_memory_space_constraint(x, pltpu.HBM) for x in (sky, beam, wigner, m_list))
 
-    part, factors = pl.pallas_call(
+    part, factors, info = pl.pallas_call(
         functools.partial(first_kernel, ways, tile),
         out_shape=(
             pltpu.VMEM((slots, rows, columns), jnp.float32),
             pltpu.VMEM((ways - 1, slots, 2 * rows, piece_rows), jnp.bfloat16),
+            pltpu.VMEM((8, LANES), jnp.float32),
         ),
-        in_specs=[whole(pltpu.SMEM), whole(pltpu.HBM), whole(pltpu.HBM), whole(pltpu.HBM)],
-        out_specs=(whole(pltpu.VMEM), whole(pltpu.VMEM)),
+        in_specs=[whole(pltpu.HBM)] * 4,
+        out_specs=(whole(pltpu.VMEM),) * 3,
         scratch_shapes=[
-            pltpu.VMEM((slots, tiles, tile, columns), jnp.bfloat16),
+            pltpu.SMEM(m_list.shape, jnp.int32),
+            pltpu.VMEM((slots, piece_rows, columns), jnp.bfloat16),
             pltpu.VMEM((ways, slots, tiles, k_local, cycles, tile), jnp.bfloat16),
             pltpu.VMEM((ways * tiles + slots, k_local, 2, tile), jnp.float32),
-            pltpu.VMEM((2 * rows, tile), jnp.bfloat16),
-            pltpu.VMEM((2 * rows, tile), jnp.bfloat16),
-            pltpu.VMEM((slots, 2 * rows, columns), jnp.float32),
+            pltpu.VMEM((2 * rows, piece_rows), jnp.bfloat16),
+            pltpu.VMEM((2 * rows, columns), jnp.float32),
+            pltpu.SemaphoreType.DMA,
             pltpu.SemaphoreType.DMA((slots, tiles)),
             pltpu.SemaphoreType.DMA((ways, slots, tiles)),
             pltpu.SemaphoreType.DMA((ways * tiles,)),
@@ -240,18 +256,18 @@
     blocks = pl.pallas_call(
         functools.partial(second_kernel, ways, tile),
         out_shape=pltpu.VMEM((cycles, width, columns), jnp.bfloat16),
-        in_specs=[whole(pltpu.SMEM)] + [whole(pltpu.VMEM)] * (ways + 1),
+        in_specs=[whole(pltpu.VMEM)] * (ways + 2),
         out_specs=whole(pltpu.VMEM),
         scratch_shapes=[
             pltpu.VMEM((2 * rows, columns), jnp.float32),
-            pltpu.VMEM((lane_tiles, cycles * width, LANES), jnp.float32),
+            pltpu.VMEM((lane_tiles, cycles * (width + 1 - width % 2), LANES), jnp.float32),
         ],
         compiler_params=params,
         cost_estimate=pl.CostEstimate(
             flops=4 * slots * rows * piece_rows * columns, bytes_accessed=8 * 1024 * 1024, transcendentals=0
         ),
         name="other_half",
-    )(m_list, part, factors, *pieces)
+    )(info, part, factors, *pieces)
     received = lax.all_to_all(blocks, "blk", split_axis=0, concat_axis=0, tiled=True)
     return received.reshape(1, -1, k_local, columns)
 

time: 32.1 us -> 31.5 us (0.981)
  Pallas kernels: 7.54 us -> 6.71 us
  waiting for transfers between devices: 0.39 us -> 0.76 us
    pallas_call x1, Pallas kernels: 3.57 us -> 3.1 us  [local(): pl.pallas_call(functools.partial(second_kernel, ways, tile), out_shape=pl...]
    ppermute x1, waiting for transfers between devices: 0.39 us -> 0.76 us  [local(): lax.ppermute(sky, 'beamk', perm)]
    pallas_call x1, Pallas kernels: 3.98 us -> 3.61 us  [local(): pl.pallas_call(functools.partial(first_kernel, ways, tile), out_shape=(pl...]
where the time goes in v2:
time: 31.5 us; the launch traced here: 31.3 us
  blocking collectives  22.4 us (71%)
  Pallas kernels  6.71 us (21%)
  local copies, waits for them, and re-layouts  0.94 us (3%)
  waiting for transfers between devices  0.76 us (2%)
  starting transfers between devices  0.45 us (1%)
    all_to_all x1, blocking collectives, local(): lax.all_to_all(blocks, 'blk', split_axis=0, concat_axis=0, tiled=True)  22.4 us
    pallas_call x1, Pallas kernels, local(): pl.pallas_call(functools.partial(first_kernel, ways, tile), out_shape=(pl...  3.61 us
    pallas_call x1, Pallas kernels, local(): pl.pallas_call(functools.partial(second_kernel, ways, tile), out_shape=pl...  3.1 us
    reshape x2, local copies, waits for them, and re-layouts, local(): return received.reshape(1, -1, k_local, columns)  0.94 us
    ppermute x1, waiting for transfers between devices, local(): lax.ppermute(sky, 'beamk', perm)  0.76 us
  transfers between devices with their start and end apart: 1, of which 1 were waited for; matrix products, arithmetic and copies ran while one was open for 0% of the time, Pallas kernels for 12%

profile of v2, /device:TPU:0, one launch (start us, length us, event | category | flops | bytes accessed | tf_op | source)
XLA Modules:
  0.0 31.3 jit_solution(1046812342587692618)
XLA Ops:
  0.0 0.5 %collective-permute-start = (bf16[2,1536,384]{2,1,0:T(8,128)(2,1)}, bf16[2,1536,384]{2,1,0:T(8,128)(2,1)S(1)}, u32[]{:S(2)}, u32[]{:S(2)}) collective-permute-start(bf16[2,1536,384]{2,1,0:T(8,128)(2,1)} %sky.1), channel_id=1, source_target_pairs={{0,1},{1,0},{2,3},{3,2},{4,5},{5,4},{6,7},{7,6},{8,9},{9,8},{10,11... | collective-permute-start | bytes 7077896 | tf_op jit(solution)/shard_map/ppermute | solution.py:225
  0.5 3.6 %own_half.1 = (f32[2,320,384]{2,1,0:T(8,128)S(1)}, bf16[1,2,640,1536]{3,2,1,0:T(8,128)(2,1)S(1)}, f32[8,128]{1,0:T(8,128)S(1)}) custom-call(s32[2]{0:T(128)} %m_list.1, bf16[2,1536,384]{2,1,0:T(8,128)(2,1)} %sky.1, bf16[2,20,16,3072]{3,2,1,0:T(8,128)(2,1)} %wigner.1, f32[20,2,3072]{2,1,0:T(2,128)} %beam.1), custom_call_target="tpu_custom_call" | custom-call | flops 1509949440 | bytes 8388608 | tf_op jit(solution)/shard_map/own_half/pallas_call | solution.py:228
  4.1 0.8 %collective-permute-done.refs_0_ = bf16[2,1536,384]{2,1,0:T(8,128)(2,1)S(1)} collective-permute-done((bf16[2,1536,384]{2,1,0:T(8,128)(2,1)}, bf16[2,1536,384]{2,1,0:T(8,128)(2,1)S(1)}, u32[]{:S(2)}, u32[]{:S(2)}) %collective-permute-start) | collective-permute-done | bytes 2359328 | tf_op jit(solution)/shard_map/ppermute | solution.py:225
  4.8 3.1 %other_half.1 = bf16[16,40,384]{2,1,0:T(8,128)(2,1)S(1)} custom-call(f32[8,128]{1,0:T(8,128)S(1)} %get-tuple-element.8.info, f32[2,320,384]{2,1,0:T(8,128)S(1)} %get-tuple-element.9.part, bf16[1,2,640,1536]{3,2,1,0:T(8,128)(2,1)S(1)} %get-tuple-element.10.factors, bf16[2,1536,384]{2,1,0:T(8,128)(2,1)S(1)} %collective-permute-done.refs_0_), custom_call_target="tpu_custom_call" | custom-call | flops 1509949440 | bytes 8388608 | tf_op jit(solution)/shard_map/other_half/pallas_call | solution.py:256
  7.9 22.4 %all_to_all.5 = bf16[16,40,384]{2,1,0:T(8,128)(2,1)S(1)} all-to-all(bf16[16,40,384]{2,1,0:T(8,128)(2,1)S(1)} %other_half.1), channel_id=1, replica_groups=mesh['blk'=16,'beamk'=2] {'blk'}, dimensions={0} | all-to-all | bytes 983040 | tf_op jit(solution)/shard_map/all_to_all | solution.py:271
  30.4 0.1 reshape.3
  30.5 0.8 %copy.6 = bf16[1,32,20,384]{3,1,2,0:T(8,128)(2,1)} copy(bf16[1,32,20,384]{3,2,1,0:T(8,128)(2,1)S(1)} %reshape.3) | data formatting | bytes 983040 | tf_op jit(solution)/shard_map/reshape | solution.py:272
Async XLA Ops:
  0.0 4.8 %collective-permute-start = (bf16[2,1536,384]{2,1,0:T(8,128)(2,1)}, bf16[2,1536,384]{2,1,0:T(8,128)(2,1)S(1)}, u32[]{:S(2)}, u32[]{:S(2)}) collective-permute-start(bf16[2,1536,384]{2,1,0:T(8,128)(2,1)} %sky.1), channel_id=1, source_target_pairs={{0,1},{1,0},{2,3},{3,2},{4,5},{5,4},{6,7},{7,6},{8,9},{9,8},{10,11... | collective-permute-start | bytes 7077896 | tf_op jit(solution)/shard_map/ppermute | solution.py:225

commit v3 on v2

--- a/solution.py
+++ b/solution.py
@@ -49,9 +49,9 @@
     def m_copy():
         return pltpu.make_async_copy(m_list, m_ref, m_sem)
 
-    def beam_copy(index):
+    def beam_copy(index, half):
         span = pl.ds(pl.multiple_of(index * tile, tile), tile)
-        return pltpu.make_async_copy(beam.at[:, :, span], beam_in.at[index], beam_sem.at[index])
+        return pltpu.make_async_copy(beam.at[:, half, span], beam_in.at[index, half], beam_sem.at[index, half])
 
     def sky_copy(slot, step):
         span = pl.ds(pl.multiple_of(step * tile, tile), tile)
@@ -73,8 +73,8 @@
         index = jnp.where(index == m_ref[slot] // tile, all_tiles + slot, index)
         for k in range(k_local):
             values = wigner_in[distance, slot, step, k].astype(jnp.float32)
-            target[k * cycles : (k + 1) * cycles, :] = (values * beam_in[index, k, 0:1, :]).astype(jnp.bfloat16)
-            target[rows + k * cycles : rows + (k + 1) * cycles, :] = (values * beam_in[index, k, 1:2, :]).astype(jnp.bfloat16)
+            target[k * cycles : (k + 1) * cycles, :] = (values * beam_in[index, 0, k : k + 1, :]).astype(jnp.bfloat16)
+            target[rows + k * cycles : rows + (k + 1) * cycles, :] = (values * beam_in[index, 1, k : k + 1, :]).astype(jnp.bfloat16)
 
     upper = 2 * (owner_of(0, ways) + 1) > ways
     early = [jnp.bool_(True) if slot % 2 == 0 else upper for slot in range(slots)]
@@ -87,7 +87,8 @@
             sky_copy(slot, last).start()
 
     for index in range(all_tiles):
-        beam_copy(index).start()
+        for half in range(2):
+            beam_copy(index, half).start()
     m_copy().wait()
     for slot in range(slots):
         begins = begin(0, slot)
@@ -113,13 +114,15 @@
     for slot in range(slots):
         info[slot : slot + 1, :] = jnp.full((1, LANES), m_ref[slot].astype(jnp.float32))
     for index in range(all_tiles):
-        beam_copy(index).wait()
+        for half in range(2):
+            beam_copy(index, half).wait()
     for slot in range(slots):
         index = m_ref[slot] // tile
-        degrees = index * tile + lax.broadcasted_iota(jnp.int32, (2, tile), 1)
-        for k in range(k_local):
-            lowest = jnp.maximum(m_ref[slot], jnp.abs(first_k + k))
-            beam_in[all_tiles + slot, k] = jnp.where(degrees >= lowest, beam_in[index, k], 0.0)
+        degrees = index * tile + lax.broadcasted_iota(jnp.int32, (k_local, tile), 1)
+        k_values = first_k + lax.broadcasted_iota(jnp.int32, (k_local, tile), 0)
+        inside = degrees >= jnp.maximum(m_ref[slot], jnp.abs(k_values))
+        for half in range(2):
+            beam_in[all_tiles + slot, half] = jnp.where(inside, beam_in[index, half], 0.0)
 
     @pl.loop(0, slots)
     def _(slot):
@@ -238,13 +241,13 @@
             pltpu.SMEM(m_list.shape, jnp.int32),
             pltpu.VMEM((slots, piece_rows, columns), jnp.bfloat16),
             pltpu.VMEM((ways, slots, tiles, k_local, cycles, tile), jnp.bfloat16),
-            pltpu.VMEM((ways * tiles + slots, k_local, 2, tile), jnp.float32),
+            pltpu.VMEM((ways * tiles + slots, 2, k_local, tile), jnp.float32),
             pltpu.VMEM((2 * rows, piece_rows), jnp.bfloat16),
             pltpu.VMEM((2 * rows, columns), jnp.float32),
             pltpu.SemaphoreType.DMA,
             pltpu.SemaphoreType.DMA((slots, tiles)),
             pltpu.SemaphoreType.DMA((ways, slots, tiles)),
-            pltpu.SemaphoreType.DMA((ways * tiles,)),
+            pltpu.SemaphoreType.DMA((ways * tiles, 2)),
         ],
         compiler_params=params,
         cost_estimate=pl.CostEstimate(

time: 31.5 us -> 31.4 us (level)
  transfers between devices with their start and end apart: 1 -> 1, of which waited for: 1 -> 1; matrix products, arithmetic and copies ran while one was open for 0% -> 0% of each run, Pallas kernels for 12% -> 11%
where the time goes in v3:
time: 31.4 us
  blocking collectives  22.5 us (72%)
  Pallas kernels  6.4 us (20%)
  waiting for transfers between devices  1.06 us (3%)
  local copies, waits for them, and re-layouts  0.94 us (3%)
  starting transfers between devices  0.45 us (1%)
    all_to_all x1, blocking collectives, local(): lax.all_to_all(blocks, 'blk', split_axis=0, concat_axis=0, tiled=True)  22.5 us
    pallas_call x1, Pallas kernels, local(): pl.pallas_call(functools.partial(first_kernel, ways, tile), out_shape=(pl...  3.3 us
    pallas_call x1, Pallas kernels, local(): pl.pallas_call(functools.partial(second_kernel, ways, tile), out_shape=pl...  3.1 us
    ppermute x1, waiting for transfers between devices, local(): lax.ppermute(sky, 'beamk', perm)  1.06 us
    reshape x2, local copies, waits for them, and re-layouts, local(): return received.reshape(1, -1, k_local, columns)  0.94 us
  transfers between devices with their start and end apart: 1, of which 1 were waited for; matrix products, arithmetic and copies ran while one was open for 0% of the time, Pallas kernels for 11%

profile of v3, /device:TPU:0, one launch (start us, length us, event | category | flops | bytes accessed | tf_op | source)
XLA Modules:
  0.0 31.4 jit_solution(879067513759263902)
XLA Ops:
  0.0 0.5 %collective-permute-start = (bf16[2,1536,384]{2,1,0:T(8,128)(2,1)}, bf16[2,1536,384]{2,1,0:T(8,128)(2,1)S(1)}, u32[]{:S(2)}, u32[]{:S(2)}) collective-permute-start(bf16[2,1536,384]{2,1,0:T(8,128)(2,1)} %sky.1), channel_id=1, source_target_pairs={{0,1},{1,0},{2,3},{3,2},{4,5},{5,4},{6,7},{7,6},{8,9},{9,8},{10,11... | collective-permute-start | bytes 7077896 | tf_op jit(solution)/shard_map/ppermute | solution.py:228
  0.5 3.3 %own_half.1 = (f32[2,320,384]{2,1,0:T(8,128)S(1)}, bf16[1,2,640,1536]{3,2,1,0:T(8,128)(2,1)S(1)}, f32[8,128]{1,0:T(8,128)S(1)}) custom-call(s32[2]{0:T(128)} %m_list.1, bf16[2,1536,384]{2,1,0:T(8,128)(2,1)} %sky.1, bf16[2,20,16,3072]{3,2,1,0:T(8,128)(2,1)} %wigner.1, f32[20,2,3072]{2,1,0:T(2,128)} %beam.1), custom_call_target="tpu_custom_call" | custom-call | flops 1509949440 | bytes 8388608 | tf_op jit(solution)/shard_map/own_half/pallas_call | solution.py:231
  3.8 1.1 %collective-permute-done.refs_0_ = bf16[2,1536,384]{2,1,0:T(8,128)(2,1)S(1)} collective-permute-done((bf16[2,1536,384]{2,1,0:T(8,128)(2,1)}, bf16[2,1536,384]{2,1,0:T(8,128)(2,1)S(1)}, u32[]{:S(2)}, u32[]{:S(2)}) %collective-permute-start) | collective-permute-done | bytes 2359328 | tf_op jit(solution)/shard_map/ppermute | solution.py:228
  4.8 3.1 %other_half.1 = bf16[16,40,384]{2,1,0:T(8,128)(2,1)S(1)} custom-call(f32[8,128]{1,0:T(8,128)S(1)} %get-tuple-element.8.info, f32[2,320,384]{2,1,0:T(8,128)S(1)} %get-tuple-element.9.part, bf16[1,2,640,1536]{3,2,1,0:T(8,128)(2,1)S(1)} %get-tuple-element.10.factors, bf16[2,1536,384]{2,1,0:T(8,128)(2,1)S(1)} %collective-permute-done.refs_0_), custom_call_target="tpu_custom_call" | custom-call | flops 1509949440 | bytes 8388608 | tf_op jit(solution)/shard_map/other_half/pallas_call | solution.py:259
  7.9 22.5 %all_to_all.5 = bf16[16,40,384]{2,1,0:T(8,128)(2,1)S(1)} all-to-all(bf16[16,40,384]{2,1,0:T(8,128)(2,1)S(1)} %other_half.1), channel_id=1, replica_groups=mesh['blk'=16,'beamk'=2] {'blk'}, dimensions={0} | all-to-all | bytes 983040 | tf_op jit(solution)/shard_map/all_to_all | solution.py:274
  30.4 0.1 reshape.3
  30.5 0.8 %copy.6 = bf16[1,32,20,384]{3,1,2,0:T(8,128)(2,1)} copy(bf16[1,32,20,384]{3,2,1,0:T(8,128)(2,1)S(1)} %reshape.3) | data formatting | bytes 983040 | tf_op jit(solution)/shard_map/reshape | solution.py:275
Async XLA Ops:
  0.0 4.8 %collective-permute-start = (bf16[2,1536,384]{2,1,0:T(8,128)(2,1)}, bf16[2,1536,384]{2,1,0:T(8,128)(2,1)S(1)}, u32[]{:S(2)}, u32[]{:S(2)}) collective-permute-start(bf16[2,1536,384]{2,1,0:T(8,128)(2,1)} %sky.1), channel_id=1, source_target_pairs={{0,1},{1,0},{2,3},{3,2},{4,5},{5,4},{6,7},{7,6},{8,9},{9,8},{10,11... | collective-permute-start | bytes 7077896 | tf_op jit(solution)/shard_map/ppermute | solution.py:228

commit v4 on v2

--- a/solution.py
+++ b/solution.py
@@ -36,7 +36,7 @@
 
 
 def first_kernel(
-    ways, tile, m_list, sky, wigner, beam, part, factors, info, m_ref, sky_in, wigner_in, beam_in, own, acc, m_sem, sky_sem, wigner_sem, beam_sem
+    ways, tile, m_list, sky, wigner, beam, part, factors, info, m_ref, sky_in, wigner_in, beam_in, own, m_sem, sky_sem, wigner_sem, beam_sem
 ):
     slots, piece_rows, columns = sky.shape
     k_local, cycles = wigner.shape[1], wigner.shape[2]
@@ -49,9 +49,9 @@
     def m_copy():
         return pltpu.make_async_copy(m_list, m_ref, m_sem)
 
-    def beam_copy(index):
-        span = pl.ds(pl.multiple_of(index * tile, tile), tile)
-        return pltpu.make_async_copy(beam.at[:, :, span], beam_in.at[index], beam_sem.at[index])
+    def beam_copy(distance, half):
+        span = pl.ds(pl.multiple_of(owner_of(distance, ways) * piece_rows, tile), piece_rows)
+        return pltpu.make_async_copy(beam.at[:, half, span], beam_in.at[half, :, span], beam_sem.at[distance, half])
 
     def sky_copy(slot, step):
         span = pl.ds(pl.multiple_of(step * tile, tile), tile)
@@ -71,10 +71,24 @@
     def fill(target, distance, slot, step):
         index = owner_of(distance, ways) * tiles + step
         index = jnp.where(index == m_ref[slot] // tile, all_tiles + slot, index)
+        span = pl.ds(pl.multiple_of(index * tile, tile), tile)
         for k in range(k_local):
-            values = wigner_in[distance, slot, step, k].astype(jnp.float32)
-            target[k * cycles : (k + 1) * cycles, :] = (values * beam_in[index, k, 0:1, :]).astype(jnp.bfloat16)
-            target[rows + k * cycles : rows + (k + 1) * cycles, :] = (values * beam_in[index, k, 1:2, :]).astype(jnp.bfloat16)
+            values = wigner_in[distance, slot, step, k]
+            for half in range(2):
+                factor = jnp.broadcast_to(beam_in[half, k : k + 1, span], (cycles, tile)).astype(jnp.bfloat16)
+                target[half * rows + k * cycles : half * rows + (k + 1) * cycles, :] = values * factor
+
+    def cut(slot):
+        index = m_ref[slot] // tile
+        degrees = index * tile + lax.broadcasted_iota(jnp.int32, (k_local, tile), 1)
+        k_values = first_k + lax.broadcasted_iota(jnp.int32, (k_local, tile), 0)
+        inside = degrees >= jnp.maximum(m_ref[slot], jnp.abs(k_values))
+        span = pl.ds(pl.multiple_of(index * tile, tile), tile)
+        for half in range(2):
+            beam_in[half, :, (all_tiles + slot) * tile : (all_tiles + slot + 1) * tile] = jnp.where(inside, beam_in[half, :, span], 0.0)
+
+    def cut_in(distance, slot):
+        return m_ref[slot] // piece_rows == owner_of(distance, ways)
 
     upper = 2 * (owner_of(0, ways) + 1) > ways
     early = [jnp.bool_(True) if slot % 2 == 0 else upper for slot in range(slots)]
@@ -86,8 +100,10 @@
             wigner_copy(0, slot, last).start()
             sky_copy(slot, last).start()
 
-    for index in range(all_tiles):
-        beam_copy(index).start()
+        if slot == 0:
+            for half in range(2):
+                beam_copy(0, half).start()
+
     m_copy().wait()
     for slot in range(slots):
         begins = begin(0, slot)
@@ -104,6 +120,8 @@
             sky_copy(slot, step).start()
 
     for distance in range(1, ways):
+        for half in range(2):
+            beam_copy(distance, half).start()
         for slot in range(slots):
 
             @pl.loop(begin(distance, slot), tiles)
@@ -112,14 +130,13 @@
 
     for slot in range(slots):
         info[slot : slot + 1, :] = jnp.full((1, LANES), m_ref[slot].astype(jnp.float32))
-    for index in range(all_tiles):
-        beam_copy(index).wait()
-    for slot in range(slots):
-        index = m_ref[slot] // tile
-        degrees = index * tile + lax.broadcasted_iota(jnp.int32, (2, tile), 1)
-        for k in range(k_local):
-            lowest = jnp.maximum(m_ref[slot], jnp.abs(first_k + k))
-            beam_in[all_tiles + slot, k] = jnp.where(degrees >= lowest, beam_in[index, k], 0.0)
+    def beam_arrives(distance):
+        for half in range(2):
+            beam_copy(distance, half).wait()
+        for slot in range(slots):
+            pl.when(cut_in(distance, slot))(functools.partial(cut, slot))
+
+    beam_arrives(0)
 
     @pl.loop(0, slots)
     def _(slot):
@@ -138,17 +155,14 @@
             @pl.when(begins == skipped)
             def _():
                 span = slice(skipped * tile, piece_rows)
-                acc[...] = jnp.dot(own[:, span], sky_in[slot, span], preferred_element_type=jnp.float32)
+                part[slot] = jnp.dot(own[:, span], sky_in[slot, span], preferred_element_type=jnp.float32)
 
         @pl.when(begins == tiles)
         def _():
-            acc[...] = jnp.zeros_like(acc)
-
-        for k in range(k_local):
-            span = slice(k * cycles, (k + 1) * cycles)
-            part[slot, span] = acc[span] + turn_by_i(acc[rows + k * cycles : rows + (k + 1) * cycles])
+            part[slot] = jnp.zeros(part.shape[1:], part.dtype)
 
     for distance in range(1, ways):
+        beam_arrives(distance)
 
         @pl.loop(0, slots)
         def _(slot):
@@ -166,9 +180,10 @@
             sky_copy(slot, last).wait()
 
 
-def second_kernel(ways, tile, info, part, factors, *refs):
+def second_kernel(ways, tile, info, _, factors, *refs):
     pieces, (out, acc, turned) = refs[: ways - 1], refs[ways - 1 :]
-    slots, rows, columns = part.shape
+    slots, rows, columns = acc.shape
+    rows = rows // 2
     piece_rows = pieces[0].shape[1]
     tiles = piece_rows // tile
     cycles, width, _ = out.shape
@@ -185,22 +200,15 @@
                 @pl.when(missing == skipped)
                 def _():
                     span = slice(skipped * tile, piece_rows)
-                    term = jnp.dot(
+                    acc[slot] += jnp.dot(
                         factors[distance - 1, slot, :, span],
                         pieces[distance - 1][slot, span],
                         preferred_element_type=jnp.float32,
                     )
-                    acc[...] = term if distance == 1 else acc[...] + term
-
-            if distance == 1:
-
-                @pl.when(missing == tiles)
-                def _():
-                    acc[...] = jnp.zeros_like(acc)
 
         for k in range(k_local):
             span = slice(k * cycles, (k + 1) * cycles)
-            total = part[slot, span] + acc[span] + turn_by_i(acc[rows + k * cycles : rows + (k + 1) * cycles])
+            total = acc[slot, span] + turn_by_i(acc[slot, rows + k * cycles : rows + (k + 1) * cycles])
             for lane in range(columns // LANES):
                 turned[lane, pl.ds(slot * k_local + k, cycles, stride=pitch), :] = total[:, lane * LANES : (lane + 1) * LANES]
 
@@ -228,7 +236,7 @@
     part, factors, info = pl.pallas_call(
         functools.partial(first_kernel, ways, tile),
         out_shape=(
-            pltpu.VMEM((slots, rows, columns), jnp.float32),
+            pltpu.VMEM((slots, 2 * rows, columns), jnp.float32),
             pltpu.VMEM((ways - 1, slots, 2 * rows, piece_rows), jnp.bfloat16),
             pltpu.VMEM((8, LANES), jnp.float32),
         ),
@@ -238,13 +246,12 @@
             pltpu.SMEM(m_list.shape, jnp.int32),
             pltpu.VMEM((slots, piece_rows, columns), jnp.bfloat16),
             pltpu.VMEM((ways, slots, tiles, k_local, cycles, tile), jnp.bfloat16),
-            pltpu.VMEM((ways * tiles + slots, k_local, 2, tile), jnp.float32),
+            pltpu.VMEM((2, k_local, degrees + slots * tile), jnp.float32),
             pltpu.VMEM((2 * rows, piece_rows), jnp.bfloat16),
-            pltpu.VMEM((2 * rows, columns), jnp.float32),
             pltpu.SemaphoreType.DMA,
             pltpu.SemaphoreType.DMA((slots, tiles)),
             pltpu.SemaphoreType.DMA((ways, slots, tiles)),
-            pltpu.SemaphoreType.DMA((ways * tiles,)),
+            pltpu.SemaphoreType.DMA((ways, 2)),
         ],
         compiler_params=params,
         cost_estimate=pl.CostEstimate(
@@ -253,13 +260,13 @@
         name="own_half",
     )(m_list, sky, wigner, beam)
 
-    blocks = pl.pallas_call(
+    blocks, _ = pl.pallas_call(
         functools.partial(second_kernel, ways, tile),
-        out_shape=pltpu.VMEM((cycles, width, columns), jnp.bfloat16),
+        out_shape=(pltpu.VMEM((cycles, width, columns), jnp.bfloat16), pltpu.VMEM(part.shape, part.dtype)),
         in_specs=[whole(pltpu.VMEM)] * (ways + 2),
-        out_specs=whole(pltpu.VMEM),
+        out_specs=(whole(pltpu.VMEM),) * 2,
+        input_output_aliases={1: 1},
         scratch_shapes=[
-            pltpu.VMEM((2 * rows, columns), jnp.float32),
             pltpu.VMEM((lane_tiles, cycles * (width + 1 - width % 2), LANES), jnp.float32),
         ],
         compiler_params=params,

time: 31.5 us -> 30.9 us (0.981)
  waiting for transfers between devices: 0.76 us -> 1.68 us
  Pallas kernels: 6.71 us -> 5.8 us
  blocking collectives: 22.4 us -> 21.8 us
    pallas_call x1, Pallas kernels: 3.61 us -> 2.68 us  [local(): pl.pallas_call(functools.partial(first_kernel, ways, tile), out_shape=(pl...]
    ppermute x1, waiting for transfers between devices: 0.76 us -> 1.68 us  [local(): lax.ppermute(sky, 'beamk', perm)]
    all_to_all x1, blocking collectives: 22.4 us -> 21.8 us  [local(): lax.all_to_all(blocks, 'blk', split_axis=0, concat_axis=0, tiled=True)]
  transfers between devices with their start and end apart: 1 -> 1, of which waited for: 1 -> 1; matrix products, arithmetic and copies ran while one was open for 0% -> 0% of each run, Pallas kernels for 12% -> 9%
where the time goes in v4:
time: 30.9 us; the launch traced here: 30.7 us
  blocking collectives  21.8 us (71%)
  Pallas kernels  5.8 us (19%)
  waiting for transfers between devices  1.68 us (5%)
  local copies, waits for them, and re-layouts  0.94 us (3%)
  starting transfers between devices  0.45 us (1%)
    all_to_all x1, blocking collectives, local(): lax.all_to_all(blocks, 'blk', split_axis=0, concat_axis=0, tiled=True)  21.8 us
    pallas_call x1, Pallas kernels, local(): pl.pallas_call(functools.partial(second_kernel, ways, tile), out_shape=(p...  3.12 us
    pallas_call x1, Pallas kernels, local(): pl.pallas_call(functools.partial(first_kernel, ways, tile), out_shape=(pl...  2.68 us
    ppermute x1, waiting for transfers between devices, local(): lax.ppermute(sky, 'beamk', perm)  1.68 us
    reshape x2, local copies, waits for them, and re-layouts, local(): return received.reshape(1, -1, k_local, columns)  0.94 us
  transfers between devices with their start and end apart: 1, of which 1 were waited for; matrix products, arithmetic and copies ran while one was open for 0% of the time, Pallas kernels for 9%

profile of v4, /device:TPU:0, one launch (start us, length us, event | category | flops | bytes accessed | tf_op | source)
XLA Modules:
  0.0 30.7 jit_solution(9172115419650988944)
XLA Ops:
  0.0 0.5 %collective-permute-start = (bf16[2,1536,384]{2,1,0:T(8,128)(2,1)}, bf16[2,1536,384]{2,1,0:T(8,128)(2,1)S(1)}, u32[]{:S(2)}, u32[]{:S(2)}) collective-permute-start(bf16[2,1536,384]{2,1,0:T(8,128)(2,1)} %sky.1), channel_id=1, source_target_pairs={{0,1},{1,0},{2,3},{3,2},{4,5},{5,4},{6,7},{7,6},{8,9},{9,8},{10,11... | collective-permute-start | bytes 7077896 | tf_op jit(solution)/shard_map/ppermute | solution.py:233
  0.5 2.7 %own_half.1 = (f32[2,640,384]{2,1,0:T(8,128)S(1)}, bf16[1,2,640,1536]{3,2,1,0:T(8,128)(2,1)S(1)}, f32[8,128]{1,0:T(8,128)S(1)}) custom-call(s32[2]{0:T(128)} %m_list.1, bf16[2,1536,384]{2,1,0:T(8,128)(2,1)} %sky.1, bf16[2,20,16,3072]{3,2,1,0:T(8,128)(2,1)} %wigner.1, f32[20,2,3072]{2,1,0:T(2,128)} %beam.1), custom_call_target="tpu_custom_call" | custom-call | flops 1509949440 | bytes 8388608 | tf_op jit(solution)/shard_map/own_half/pallas_call | solution.py:236
  3.1 1.7 %collective-permute-done.refs_0_ = bf16[2,1536,384]{2,1,0:T(8,128)(2,1)S(1)} collective-permute-done((bf16[2,1536,384]{2,1,0:T(8,128)(2,1)}, bf16[2,1536,384]{2,1,0:T(8,128)(2,1)S(1)}, u32[]{:S(2)}, u32[]{:S(2)}) %collective-permute-start) | collective-permute-done | bytes 2359328 | tf_op jit(solution)/shard_map/ppermute | solution.py:233
  4.8 3.1 %other_half.1 = (bf16[16,40,384]{2,1,0:T(8,128)(2,1)S(1)}, f32[2,640,384]{2,1,0:T(8,128)S(1)}) custom-call(f32[8,128]{1,0:T(8,128)S(1)} %get-tuple-element.9.info, f32[2,640,384]{2,1,0:T(8,128)S(1)} %get-tuple-element.10._, bf16[1,2,640,1536]{3,2,1,0:T(8,128)(2,1)S(1)} %get-tuple-element.11.factors, ...), custom_call_target="tpu_custom_call", output_to_operand_aliasing={{1}: (1, {})} | custom-call | flops 1509949440 | bytes 8388608 | tf_op jit(solution)/shard_map/other_half/pallas_call | solution.py:263
  8.0 21.8 %all_to_all.5 = bf16[16,40,384]{2,1,0:T(8,128)(2,1)S(1)} all-to-all(bf16[16,40,384]{2,1,0:T(8,128)(2,1)S(1)} %get-tuple-element.12), channel_id=1, replica_groups=mesh['blk'=16,'beamk'=2] {'blk'}, dimensions={0} | all-to-all | bytes 983040 | tf_op jit(solution)/shard_map/all_to_all | solution.py:278
  29.7 0.1 reshape.3
  29.9 0.8 %copy.7 = bf16[1,32,20,384]{3,1,2,0:T(8,128)(2,1)} copy(bf16[1,32,20,384]{3,2,1,0:T(8,128)(2,1)S(1)} %reshape.3) | data formatting | bytes 983040 | tf_op jit(solution)/shard_map/reshape | solution.py:279
Async XLA Ops:
  0.0 4.8 %collective-permute-start = (bf16[2,1536,384]{2,1,0:T(8,128)(2,1)}, bf16[2,1536,384]{2,1,0:T(8,128)(2,1)S(1)}, u32[]{:S(2)}, u32[]{:S(2)}) collective-permute-start(bf16[2,1536,384]{2,1,0:T(8,128)(2,1)} %sky.1), channel_id=1, source_target_pairs={{0,1},{1,0},{2,3},{3,2},{4,5},{5,4},{6,7},{7,6},{8,9},{9,8},{10,11... | collective-permute-start | bytes 7077896 | tf_op jit(solution)/shard_map/ppermute | solution.py:233

commit v5 on v4

--- a/solution.py
+++ b/solution.py
@@ -36,7 +36,7 @@
 
 
 def first_kernel(
-    ways, tile, m_list, sky, wigner, beam, part, factors, info, m_ref, sky_in, wigner_in, beam_in, own, m_sem, sky_sem, wigner_sem, beam_sem
+    ways, tile, m_list, sky, wigner, beam, part, factors, info, m_ref, sky_in, wigner_in, beam_in, own, m_sem, sky_sem, wigner_sem, distant_sem, beam_sem
 ):
     slots, piece_rows, columns = sky.shape
     k_local, cycles = wigner.shape[1], wigner.shape[2]
@@ -57,23 +57,25 @@
         span = pl.ds(pl.multiple_of(step * tile, tile), tile)
         return pltpu.make_async_copy(sky.at[slot, span], sky_in.at[slot, span], sky_sem.at[slot, step])
 
-    def wigner_copy(distance, slot, step):
-        start = pl.multiple_of(owner_of(distance, ways) * piece_rows + step * tile, tile)
-        return pltpu.make_async_copy(
-            wigner.at[slot, :, :, pl.ds(start, tile)],
-            wigner_in.at[distance, slot, step],
-            wigner_sem.at[distance, slot, step],
-        )
+    def wigner_copy(slot, step):
+        start = pl.multiple_of(owner_of(0, ways) * piece_rows + step * tile, tile)
+        span = pl.ds(start, tile)
+        return pltpu.make_async_copy(wigner.at[slot, :, :, span], wigner_in.at[slot, :, :, span], wigner_sem.at[slot, step])
+
+    def distant_copy(distance, slot):
+        span = pl.ds(pl.multiple_of(owner_of(distance, ways) * piece_rows, tile), piece_rows)
+        return pltpu.make_async_copy(wigner.at[slot, :, :, span], wigner_in.at[slot, :, :, span], distant_sem.at[distance - 1, slot])
 
     def begin(distance, slot):
         return first_tile(m_ref[slot], owner_of(distance, ways), piece_rows, tile)
 
     def fill(target, distance, slot, step):
         index = owner_of(distance, ways) * tiles + step
+        rows_of = pl.ds(pl.multiple_of(index * tile, tile), tile)
         index = jnp.where(index == m_ref[slot] // tile, all_tiles + slot, index)
         span = pl.ds(pl.multiple_of(index * tile, tile), tile)
         for k in range(k_local):
-            values = wigner_in[distance, slot, step, k]
+            values = wigner_in[slot, k, :, rows_of]
             for half in range(2):
                 factor = jnp.broadcast_to(beam_in[half, k : k + 1, span], (cycles, tile)).astype(jnp.bfloat16)
                 target[half * rows + k * cycles : half * rows + (k + 1) * cycles, :] = values * factor
@@ -90,44 +92,33 @@
     def cut_in(distance, slot):
         return m_ref[slot] // piece_rows == owner_of(distance, ways)
 
-    upper = 2 * (owner_of(0, ways) + 1) > ways
-    early = [jnp.bool_(True) if slot % 2 == 0 else upper for slot in range(slots)]
+    def upper(distance):
+        return 2 * (owner_of(distance, ways) + 1) > ways
+
+    def where_needed(distance, slot, do):
+        if slot % 2 == 0:
+            do()
+        else:
+            pl.when(upper(distance))(do)
+
     m_copy().start()
     for slot in range(slots):
 
-        @pl.when(early[slot])
-        def _():
-            wigner_copy(0, slot, last).start()
-            sky_copy(slot, last).start()
-
-        if slot == 0:
-            for half in range(2):
-                beam_copy(0, half).start()
-
-    m_copy().wait()
-    for slot in range(slots):
-        begins = begin(0, slot)
-
-        @pl.when(jnp.logical_and(begins < tiles, jnp.logical_not(early[slot])))
-        def _():
-            wigner_copy(0, slot, last).start()
-            sky_copy(slot, last).start()
-
-        @pl.loop(begins + 1, tiles)
-        def _(later):
-            step = tiles - 1 - later + begins
-            wigner_copy(0, slot, step).start()
-            sky_copy(slot, step).start()
-
+        def fetch(slot=slot):
+            for step in reversed(range(tiles)):
+                wigner_copy(slot, step).start()
+                if slot == 0 and step == last:
+                    for half in range(2):
+                        beam_copy(0, half).start()
+                sky_copy(slot, step).start()
+
+        where_needed(0, slot, fetch)
     for distance in range(1, ways):
         for half in range(2):
             beam_copy(distance, half).start()
         for slot in range(slots):
-
-            @pl.loop(begin(distance, slot), tiles)
-            def _(step):
-                wigner_copy(distance, slot, step).start()
-
+            where_needed(distance, slot, lambda distance=distance, slot=slot: distant_copy(distance, slot).start())
+    m_copy().wait()
     for slot in range(slots):
         info[slot : slot + 1, :] = jnp.full((1, LANES), m_ref[slot].astype(jnp.float32))
     def beam_arrives(distance):
@@ -145,7 +136,7 @@
         @pl.loop(begins, tiles)
         def _(later):
             step = tiles - 1 - later + begins
-            wigner_copy(0, slot, step).wait()
+            wigner_copy(slot, step).wait()
             span = pl.ds(pl.multiple_of(step * tile, tile), tile)
             fill(own.at[:, span], 0, slot, step)
             sky_copy(slot, step).wait()
@@ -163,21 +154,25 @@
 
     for distance in range(1, ways):
         beam_arrives(distance)
+        for slot in range(slots):
+            where_needed(distance, slot, lambda distance=distance, slot=slot: distant_copy(distance, slot).wait())
 
         @pl.loop(0, slots)
         def _(slot):
             @pl.loop(begin(distance, slot), tiles)
             def _(step):
-                wigner_copy(distance, slot, step).wait()
                 span = pl.ds(pl.multiple_of(step * tile, tile), tile)
                 fill(factors.at[distance - 1, slot, :, span], distance, slot, step)
 
     for slot in range(slots):
 
-        @pl.when(jnp.logical_and(begin(0, slot) == tiles, early[slot]))
-        def _():
-            wigner_copy(0, slot, last).wait()
-            sky_copy(slot, last).wait()
+        def drop(slot=slot):
+            @pl.loop(0, begin(0, slot))
+            def _(step):
+                wigner_copy(slot, step).wait()
+                sky_copy(slot, step).wait()
+
+        where_needed(0, slot, drop)
 
 
 def second_kernel(ways, tile, info, _, factors, *refs):
@@ -245,12 +240,13 @@
         scratch_shapes=[
             pltpu.SMEM(m_list.shape, jnp.int32),
             pltpu.VMEM((slots, piece_rows, columns), jnp.bfloat16),
-            pltpu.VMEM((ways, slots, tiles, k_local, cycles, tile), jnp.bfloat16),
+            pltpu.VMEM(wigner.shape, jnp.bfloat16),
             pltpu.VMEM((2, k_local, degrees + slots * tile), jnp.float32),
             pltpu.VMEM((2 * rows, piece_rows), jnp.bfloat16),
             pltpu.SemaphoreType.DMA,
             pltpu.SemaphoreType.DMA((slots, tiles)),
-            pltpu.SemaphoreType.DMA((ways, slots, tiles)),
+            pltpu.SemaphoreType.DMA((slots, tiles)),
+            pltpu.SemaphoreType.DMA((ways - 1, slots)),
             pltpu.SemaphoreType.DMA((ways, 2)),
         ],
         compiler_params=params,

time: 30.9 us -> 30.6 us (level)
  blocking collectives: 21.8 us -> 21.4 us
  Pallas kernels: 5.8 us -> 6.19 us
  waiting for transfers between devices: 1.68 us -> 1.29 us
    all_to_all x1, blocking collectives: 21.8 us -> 21.4 us  [local(): lax.all_to_all(blocks, 'blk', split_axis=0, concat_axis=0, tiled=True)]
    ppermute x1, waiting for transfers between devices: 1.68 us -> 1.29 us  [local(): lax.ppermute(sky, 'beamk', perm)]
    pallas_call x1, Pallas kernels: 2.68 us -> 3.07 us  [local(): pl.pallas_call(functools.partial(first_kernel, ways, tile), out_shape=(pl...]
  transfers between devices with their start and end apart: 1 -> 1, of which waited for: 1 -> 1; matrix products, arithmetic and copies ran while one was open for 0% -> 0% of each run, Pallas kernels for 9% -> 10%
where the time goes in v5:
time: 30.6 us; the launch traced here: 30.2 us
  blocking collectives  21.4 us (70%)
  Pallas kernels  6.19 us (20%)
  waiting for transfers between devices  1.29 us (4%)
  local copies, waits for them, and re-layouts  0.94 us (3%)
  starting transfers between devices  0.45 us (1%)
    all_to_all x1, blocking collectives, local(): lax.all_to_all(blocks, 'blk', split_axis=0, concat_axis=0, tiled=True)  21.4 us
    pallas_call x1, Pallas kernels, local(): pl.pallas_call(functools.partial(second_kernel, ways, tile), out_shape=(p...  3.12 us
    pallas_call x1, Pallas kernels, local(): pl.pallas_call(functools.partial(first_kernel, ways, tile), out_shape=(pl...  3.07 us
    ppermute x1, waiting for transfers between devices, local(): lax.ppermute(sky, 'beamk', perm)  1.29 us
    reshape x2, local copies, waits for them, and re-layouts, local(): return received.reshape(1, -1, k_local, columns)  0.94 us
  transfers between devices with their start and end apart: 1, of which 1 were waited for; matrix products, arithmetic and copies ran while one was open for 0% of the time, Pallas kernels for 10%

profile of v5, /device:TPU:0, one launch (start us, length us, event | category | flops | bytes accessed | tf_op | source)
XLA Modules:
  0.0 30.2 jit_solution(5303941338697653873)
XLA Ops:
  0.0 0.5 %collective-permute-start = (bf16[2,1536,384]{2,1,0:T(8,128)(2,1)}, bf16[2,1536,384]{2,1,0:T(8,128)(2,1)S(1)}, u32[]{:S(2)}, u32[]{:S(2)}) collective-permute-start(bf16[2,1536,384]{2,1,0:T(8,128)(2,1)} %sky.1), channel_id=1, source_target_pairs={{0,1},{1,0},{2,3},{3,2},{4,5},{5,4},{6,7},{7,6},{8,9},{9,8},{10,11... | collective-permute-start | bytes 7077896 | tf_op jit(solution)/shard_map/ppermute | solution.py:228
  0.5 3.1 %own_half.1 = (f32[2,640,384]{2,1,0:T(8,128)S(1)}, bf16[1,2,640,1536]{3,2,1,0:T(8,128)(2,1)S(1)}, f32[8,128]{1,0:T(8,128)S(1)}) custom-call(s32[2]{0:T(128)} %m_list.1, bf16[2,1536,384]{2,1,0:T(8,128)(2,1)} %sky.1, bf16[2,20,16,3072]{3,2,1,0:T(8,128)(2,1)} %wigner.1, f32[20,2,3072]{2,1,0:T(2,128)} %beam.1), custom_call_target="tpu_custom_call" | custom-call | flops 1509949440 | bytes 8388608 | tf_op jit(solution)/shard_map/own_half/pallas_call | solution.py:231
  3.5 1.3 %collective-permute-done.refs_0_ = bf16[2,1536,384]{2,1,0:T(8,128)(2,1)S(1)} collective-permute-done((bf16[2,1536,384]{2,1,0:T(8,128)(2,1)}, bf16[2,1536,384]{2,1,0:T(8,128)(2,1)S(1)}, u32[]{:S(2)}, u32[]{:S(2)}) %collective-permute-start) | collective-permute-done | bytes 2359328 | tf_op jit(solution)/shard_map/ppermute | solution.py:228
  4.8 3.1 %other_half.1 = (bf16[16,40,384]{2,1,0:T(8,128)(2,1)S(1)}, f32[2,640,384]{2,1,0:T(8,128)S(1)}) custom-call(f32[8,128]{1,0:T(8,128)S(1)} %get-tuple-element.9.info, f32[2,640,384]{2,1,0:T(8,128)S(1)} %get-tuple-element.10._, bf16[1,2,640,1536]{3,2,1,0:T(8,128)(2,1)S(1)} %get-tuple-element.11.factors, ...), custom_call_target="tpu_custom_call", output_to_operand_aliasing={{1}: (1, {})} | custom-call | flops 1509949440 | bytes 8388608 | tf_op jit(solution)/shard_map/other_half/pallas_call | solution.py:259
  8.0 21.4 %all_to_all.5 = bf16[16,40,384]{2,1,0:T(8,128)(2,1)S(1)} all-to-all(bf16[16,40,384]{2,1,0:T(8,128)(2,1)S(1)} %get-tuple-element.12), channel_id=1, replica_groups=mesh['blk'=16,'beamk'=2] {'blk'}, dimensions={0} | all-to-all | bytes 983040 | tf_op jit(solution)/shard_map/all_to_all | solution.py:274
  29.3 0.1 reshape.3
  29.4 0.8 %copy.7 = bf16[1,32,20,384]{3,1,2,0:T(8,128)(2,1)} copy(bf16[1,32,20,384]{3,2,1,0:T(8,128)(2,1)S(1)} %reshape.3) | data formatting | bytes 983040 | tf_op jit(solution)/shard_map/reshape | solution.py:275
Async XLA Ops:
  0.0 4.8 %collective-permute-start = (bf16[2,1536,384]{2,1,0:T(8,128)(2,1)}, bf16[2,1536,384]{2,1,0:T(8,128)(2,1)S(1)}, u32[]{:S(2)}, u32[]{:S(2)}) collective-permute-start(bf16[2,1536,384]{2,1,0:T(8,128)(2,1)} %sky.1), channel_id=1, source_target_pairs={{0,1},{1,0},{2,3},{3,2},{4,5},{5,4},{6,7},{7,6},{8,9},{9,8},{10,11... | collective-permute-start | bytes 7077896 | tf_op jit(solution)/shard_map/ppermute | solution.py:228

commit v6 on v5

--- a/solution.py
+++ b/solution.py
@@ -16,6 +16,11 @@
     return max(t for t in range(LANES, min(rows, 512) + 1, LANES) if rows % t == 0)
 
 
+def groups_of(k_local):
+    cut = 4 * (3 * k_local // 20)
+    return [(0, cut), (cut, k_local)] if cut else [(0, k_local)]
+
+
 def whole(memory):
     return pl.BlockSpec(memory_space=memory)
 
@@ -35,10 +40,10 @@
     return jnp.minimum(jnp.maximum(m_value - owner * piece_rows, 0) // tile, piece_rows // tile)
 
 
-def first_kernel(
-    ways, tile, m_list, sky, wigner, beam, part, factors, info, m_ref, sky_in, wigner_in, beam_in, own, m_sem, sky_sem, wigner_sem, distant_sem, beam_sem
-):
+def first_kernel(ways, tile, groups, m_list, sky, wigner, beam, *refs):
     slots, piece_rows, columns = sky.shape
+    parts, refs = refs[: len(groups)], refs[len(groups) :]
+    factors, info, m_ref, sky_in, wigner_in, beam_in, own, m_sem, sky_sem, wigner_sem, distant_sem, beam_sem = refs
     k_local, cycles = wigner.shape[1], wigner.shape[2]
     rows = k_local * cycles
     tiles = piece_rows // tile
@@ -74,11 +79,13 @@
         rows_of = pl.ds(pl.multiple_of(index * tile, tile), tile)
         index = jnp.where(index == m_ref[slot] // tile, all_tiles + slot, index)
         span = pl.ds(pl.multiple_of(index * tile, tile), tile)
-        for k in range(k_local):
-            values = wigner_in[slot, k, :, rows_of]
-            for half in range(2):
-                factor = jnp.broadcast_to(beam_in[half, k : k + 1, span], (cycles, tile)).astype(jnp.bfloat16)
-                target[half * rows + k * cycles : half * rows + (k + 1) * cycles, :] = values * factor
+        for first, end in groups:
+            for k in range(first, end):
+                values = wigner_in[slot, k, :, rows_of]
+                for half in range(2):
+                    factor = jnp.broadcast_to(beam_in[half, k : k + 1, span], (cycles, tile)).astype(jnp.bfloat16)
+                    row = (first + half * (end - first) + k) * cycles
+                    target[row : row + cycles, :] = values * factor
 
     def cut(slot):
         index = m_ref[slot] // tile
@@ -146,11 +153,14 @@
             @pl.when(begins == skipped)
             def _():
                 span = slice(skipped * tile, piece_rows)
-                part[slot] = jnp.dot(own[:, span], sky_in[slot, span], preferred_element_type=jnp.float32)
+                sums = jnp.dot(own[:, span], sky_in[slot, span], preferred_element_type=jnp.float32)
+                for part, (first, end) in zip(parts, groups):
+                    part[slot] = sums[2 * first * cycles : 2 * end * cycles]
 
         @pl.when(begins == tiles)
         def _():
-            part[slot] = jnp.zeros(part.shape[1:], part.dtype)
+            for part in parts:
+                part[slot] = jnp.zeros(part.shape[1:], part.dtype)
 
     for distance in range(1, ways):
         beam_arrives(distance)
@@ -175,7 +185,7 @@
         where_needed(0, slot, drop)
 
 
-def second_kernel(ways, tile, info, _, factors, *refs):
+def second_kernel(ways, tile, first_row, info, _, factors, *refs):
     pieces, (out, acc, turned) = refs[: ways - 1], refs[ways - 1 :]
     slots, rows, columns = acc.shape
     rows = rows // 2
@@ -196,7 +206,7 @@
                 def _():
                     span = slice(skipped * tile, piece_rows)
                     acc[slot] += jnp.dot(
-                        factors[distance - 1, slot, :, span],
+                        factors[distance - 1, slot, first_row : first_row + 2 * rows, span],
                         pieces[distance - 1][slot, span],
                         preferred_element_type=jnp.float32,
                     )
@@ -219,7 +229,6 @@
     tile = tile_of(piece_rows)
     tiles = piece_rows // tile
     lane_tiles = columns // LANES
-    width = slots * k_local
     params = pltpu.CompilerParams(vmem_limit_bytes=VMEM_LIMIT)
 
     pieces = []
@@ -228,15 +237,17 @@
         pieces.append(pltpu.with_memory_space_constraint(lax.ppermute(sky, "beamk", perm), pltpu.VMEM))
     sky, beam, wigner, m_list = (pltpu.with_memory_space_constraint(x, pltpu.HBM) for x in (sky, beam, wigner, m_list))
 
-    part, factors, info = pl.pallas_call(
-        functools.partial(first_kernel, ways, tile),
+    groups = groups_of(k_local)
+    sums = [pltpu.VMEM((slots, 2 * (end - first) * cycles, columns), jnp.float32) for first, end in groups]
+    *parts, factors, info = pl.pallas_call(
+        functools.partial(first_kernel, ways, tile, groups),
         out_shape=(
-            pltpu.VMEM((slots, 2 * rows, columns), jnp.float32),
+            *sums,
             pltpu.VMEM((ways - 1, slots, 2 * rows, piece_rows), jnp.bfloat16),
             pltpu.VMEM((8, LANES), jnp.float32),
         ),
         in_specs=[whole(pltpu.HBM)] * 4,
-        out_specs=(whole(pltpu.VMEM),) * 3,
+        out_specs=(whole(pltpu.VMEM),) * (len(groups) + 2),
         scratch_shapes=[
             pltpu.SMEM(m_list.shape, jnp.int32),
             pltpu.VMEM((slots, piece_rows, columns), jnp.bfloat16),
@@ -256,23 +267,27 @@
         name="own_half",
     )(m_list, sky, wigner, beam)
 
-    blocks, _ = pl.pallas_call(
-        functools.partial(second_kernel, ways, tile),
-        out_shape=(pltpu.VMEM((cycles, width, columns), jnp.bfloat16), pltpu.VMEM(part.shape, part.dtype)),
-        in_specs=[whole(pltpu.VMEM)] * (ways + 2),
-        out_specs=(whole(pltpu.VMEM),) * 2,
-        input_output_aliases={1: 1},
-        scratch_shapes=[
-            pltpu.VMEM((lane_tiles, cycles * (width + 1 - width % 2), LANES), jnp.float32),
-        ],
-        compiler_params=params,
-        cost_estimate=pl.CostEstimate(
-            flops=4 * slots * rows * piece_rows * columns, bytes_accessed=8 * 1024 * 1024, transcendentals=0
-        ),
-        name="other_half",
-    )(info, part, factors, *pieces)
-    received = lax.all_to_all(blocks, "blk", split_axis=0, concat_axis=0, tiled=True)
-    return received.reshape(1, -1, k_local, columns)
+    received = []
+    for part, shape, (first, end) in zip(parts, sums, groups):
+        width = slots * (end - first)
+        blocks, _ = pl.pallas_call(
+            functools.partial(second_kernel, ways, tile, 2 * first * cycles),
+            out_shape=(pltpu.VMEM((cycles, width, columns), jnp.bfloat16), shape),
+            in_specs=[whole(pltpu.VMEM)] * (ways + 2),
+            out_specs=(whole(pltpu.VMEM),) * 2,
+            input_output_aliases={1: 1},
+            scratch_shapes=[
+                pltpu.VMEM((lane_tiles, cycles * (width + 1 - width % 2), LANES), jnp.float32),
+            ],
+            compiler_params=params,
+            cost_estimate=pl.CostEstimate(
+                flops=4 * slots * (end - first) * cycles * piece_rows * columns, bytes_accessed=4 * 1024 * 1024, transcendentals=0
+            ),
+            name="other_half",
+        )(info, part, factors, *pieces)
+        blocks = lax.all_to_all(blocks, "blk", split_axis=0, concat_axis=0, tiled=True)
+        received.append(blocks.reshape(1, -1, end - first, columns))
+    return jnp.concatenate(received, axis=2)
 
 
 def solution(mesh):

time: 30.6 us -> 39 us (1.27)
  blocking collectives: 21.4 us -> 0 us
  waiting for transfers between devices: 1.29 us -> 15.2 us
  starting transfers between devices: 0.45 us -> 12.2 us
  local copies, waits for them, and re-layouts: 0.94 us -> 3.02 us
  Pallas kernels: 6.19 us -> 8.14 us
    all_to_all x1 -> x0, blocking collectives: 21.4 us -> none  [local(): lax.all_to_all(blocks, 'blk', split_axis=0, concat_axis=0, tiled=True)]
    all_to_all x0 -> x2, waiting for transfers between devices: none -> 14.4 us  [local(): lax.all_to_all(blocks, 'blk', split_axis=0, concat_axis=0, tiled=True)]
    all_to_all x0 -> x2, starting transfers between devices: none -> 11.8 us  [local(): lax.all_to_all(blocks, 'blk', split_axis=0, concat_axis=0, tiled=True)]
    unnamed x0 -> x4, local copies, waits for them, and re-layouts: none -> 2.11 us
    pallas_call x2 -> x3, Pallas kernels: 6.19 us -> 8.14 us  [the longest x2 4.58 us: local(): pl.pallas_call(functools.partial(second_kernel, ways, tile, 2 * first * c...]
    reshape x2 -> x1, local copies, waits for them, and re-layouts: 0.94 us -> 0.07 us  [local(): received.append(blocks.reshape(1, -1, end - first, columns))]
    concatenate x0 -> x1, local copies, waits for them, and re-layouts: none -> 0.84 us  [local(): return jnp.concatenate(received, axis=2)]
    ppermute x1, waiting for transfers between devices: 1.29 us -> 0.79 us  [local(): lax.ppermute(sky, 'beamk', perm)]
  transfers between devices with their start and end apart: 1 -> 3, of which waited for: 1 -> 3; matrix products, arithmetic and copies ran while one was open for 0% -> 0% of each run, Pallas kernels for 10% -> 15%
where the time goes in v6:
time: 39 us; the launch traced here: 38.7 us
  waiting for transfers between devices  15.2 us (39%)
  starting transfers between devices  12.2 us (31%)
  Pallas kernels  8.14 us (21%)
  local copies, waits for them, and re-layouts  3.02 us (8%)
    all_to_all x2, waiting for transfers between devices, local(): lax.all_to_all(blocks, 'blk', split_axis=0, concat_axis=0, tiled=True)  14.4 us
    all_to_all x2, starting transfers between devices, local(): lax.all_to_all(blocks, 'blk', split_axis=0, concat_axis=0, tiled=True)  11.8 us
    pallas_call x2, Pallas kernels, local(): pl.pallas_call(functools.partial(second_kernel, ways, tile, 2 * first * c...  4.58 us
    pallas_call x1, Pallas kernels, local(): pl.pallas_call(functools.partial(first_kernel, ways, tile, groups), out_s...  3.56 us
    unnamed x4, local copies, waits for them, and re-layouts  2.11 us
    concatenate x1, local copies, waits for them, and re-layouts, local(): return jnp.concatenate(received, axis=2)  0.84 us
    ppermute x1, waiting for transfers between devices, local(): lax.ppermute(sky, 'beamk', perm)  0.79 us
  transfers between devices with their start and end apart: 3, of which 3 were waited for; matrix products, arithmetic and copies ran while one was open for 0% of the time, Pallas kernels for 15%

profile of v6, /device:TPU:0, one launch (start us, length us, event | category | flops | bytes accessed | tf_op | source)
XLA Modules:
  0.0 38.7 jit_solution(13663438967282407909)
XLA Ops:
  0.0 0.5 %collective-permute-start = (bf16[2,1536,384]{2,1,0:T(8,128)(2,1)}, bf16[2,1536,384]{2,1,0:T(8,128)(2,1)S(1)}, u32[]{:S(2)}, u32[]{:S(2)}) collective-permute-start(bf16[2,1536,384]{2,1,0:T(8,128)(2,1)} %sky.1), channel_id=1, source_target_pairs={{0,1},{1,0},{2,3},{3,2},{4,5},{5,4},{6,7},{7,6},{8,9},{9,8},{10,11... | collective-permute-start | bytes 7077896 | tf_op jit(solution)/shard_map/ppermute | solution.py:237
  0.5 3.6 %own_half.1 = (f32[2,384,384]{2,1,0:T(8,128)S(1)}, f32[2,256,384]{2,1,0:T(8,128)S(1)}, bf16[1,2,640,1536]{3,2,1,0:T(8,128)(2,1)S(1)}, f32[8,128]{1,0:T(8,128)S(1)}) custom-call(s32[2]{0:T(128)} %m_list.1, bf16[2,1536,384]{2,1,0:T(8,128)(2,1)} %sky.1, bf16[2,20,16,3072]{3,2,1,0:T(8,128)(2,1)} %wigner.1, f32[20,2,3072]{2,1,0:T(2,128)} %beam.1), custom_call_target="tpu_custom_call" | custom-call | flops 1509949440 | bytes 8388608 | tf_op jit(solution)/shard_map/own_half/pallas_call | solution.py:242
  4.0 0.0 copy-start
  4.0 0.8 %collective-permute-done.refs_0_ = bf16[2,1536,384]{2,1,0:T(8,128)(2,1)S(1)} collective-permute-done((bf16[2,1536,384]{2,1,0:T(8,128)(2,1)}, bf16[2,1536,384]{2,1,0:T(8,128)(2,1)S(1)}, u32[]{:S(2)}, u32[]{:S(2)}) %collective-permute-start) | collective-permute-done | bytes 2359328 | tf_op jit(solution)/shard_map/ppermute | solution.py:237
  4.8 2.5 %other_half.2 = (bf16[16,24,384]{2,1,0:T(8,128)(2,1)}, f32[2,384,384]{2,1,0:T(8,128)S(1)}) custom-call(f32[8,128]{1,0:T(8,128)S(1)} %get-tuple-element.11.info, f32[2,384,384]{2,1,0:T(8,128)S(1)} %get-tuple-element.12._, bf16[1,2,640,1536]{3,2,1,0:T(8,128)(2,1)S(1)} %get-tuple-element.13.factors, ...), custom_call_target="tpu_custom_call", output_to_operand_aliasing={{1}: (1, {})} | custom-call | flops 905969664 | bytes 4194304 | tf_op jit(solution)/shard_map/other_half/pallas_call | solution.py:273
  7.3 0.0 copy-done
  7.3 8.2 %all-to-all-start = ((bf16[16,24,384]{2,1,0:T(8,128)(2,1)}), bf16[16,24,384]{2,1,0:T(8,128)(2,1)S(1)}, u32[]{:S(2)}, u32[]{:S(2)}) async-start(bf16[16,24,384]{2,1,0:T(8,128)(2,1)} %get-tuple-element.14), calls=%async_computation | async-start | bytes 589824 | tf_op jit(solution)/shard_map/all_to_all | solution.py:288
  15.6 0.0 copy-start.1
  15.6 2.1 %copy-done.1 = bf16[1,2,640,1536]{3,2,1,0:T(8,128)(2,1)S(1)} copy-done((bf16[1,2,640,1536]{3,2,1,0:T(8,128)(2,1)S(1)}, bf16[1,2,640,1536]{3,2,1,0:T(8,128)(2,1)}, u32[]{:S(2)}) %copy-start.1) | copy-done | bytes 3932184
  17.7 2.1 %other_half.3 = (bf16[16,16,384]{2,1,0:T(8,128)(2,1)}, f32[2,256,384]{2,1,0:T(8,128)S(1)}) custom-call(f32[8,128]{1,0:T(8,128)S(1)} %get-tuple-element.11.info, f32[2,256,384]{2,1,0:T(8,128)S(1)} %get-tuple-element.15._, bf16[1,2,640,1536]{3,2,1,0:T(8,128)(2,1)S(1)} %copy-done.1, ...), custom_call_target="tpu_custom_call", output_to_operand_aliasing={{1}: (1, {})} | custom-call | flops 603979776 | bytes 4194304 | tf_op jit(solution)/shard_map/other_half/pallas_call | solution.py:273
  19.8 6.4 %all-to-all-done = bf16[16,24,384]{2,1,0:T(8,128)(2,1)S(1)} async-done(((bf16[16,24,384]{2,1,0:T(8,128)(2,1)}), bf16[16,24,384]{2,1,0:T(8,128)(2,1)S(1)}, u32[]{:S(2)}, u32[]{:S(2)}) %all-to-all-start) | async-done | bytes 294944 | tf_op jit(solution)/shard_map/all_to_all | solution.py:288
  26.2 3.5 %all-to-all-start.1 = ((bf16[16,16,384]{2,1,0:T(8,128)(2,1)}), bf16[16,16,384]{2,1,0:T(8,128)(2,1)S(1)}, u32[]{:S(2)}, u32[]{:S(2)}) async-start(bf16[16,16,384]{2,1,0:T(8,128)(2,1)} %get-tuple-element.16), calls=%async_computation.1 | async-start | bytes 393216 | tf_op jit(solution)/shard_map/all_to_all | solution.py:288
  29.7 0.1 reshape.6
  29.8 8.0 %all-to-all-done.1 = bf16[16,16,384]{2,1,0:T(8,128)(2,1)S(1)} async-done(((bf16[16,16,384]{2,1,0:T(8,128)(2,1)}), bf16[16,16,384]{2,1,0:T(8,128)(2,1)S(1)}, u32[]{:S(2)}, u32[]{:S(2)}) %all-to-all-start.1) | async-done | bytes 196640 | tf_op jit(solution)/shard_map/all_to_all | solution.py:288
  37.7 0.1 pad_maximum_fusion
  37.9 0.8 %copy.9 = bf16[1,32,20,384]{3,1,2,0:T(8,128)(2,1)} copy(bf16[1,32,20,384]{3,2,1,0:T(8,128)(2,1)S(1)} %pad_maximum_fusion) | data formatting | bytes 983040 | tf_op jit(solution)/shard_map/concatenate | solution.py:290
Async XLA Ops:
  0.0 4.8 %collective-permute-start = (bf16[2,1536,384]{2,1,0:T(8,128)(2,1)}, bf16[2,1536,384]{2,1,0:T(8,128)(2,1)S(1)}, u32[]{:S(2)}, u32[]{:S(2)}) collective-permute-start(bf16[2,1536,384]{2,1,0:T(8,128)(2,1)} %sky.1), channel_id=1, source_target_pairs={{0,1},{1,0},{2,3},{3,2},{4,5},{5,4},{6,7},{7,6},{8,9},{9,8},{10,11... | collective-permute-start | bytes 7077896 | tf_op jit(solution)/shard_map/ppermute | solution.py:237
  4.0 3.3 %copy-start = (bf16[1,2,640,1536]{3,2,1,0:T(8,128)(2,1)}, bf16[1,2,640,1536]{3,2,1,0:T(8,128)(2,1)S(1)}, u32[]{:S(2)}) copy-start(bf16[1,2,640,1536]{3,2,1,0:T(8,128)(2,1)S(1)} %get-tuple-element.13.factors) | copy-start | bytes 11796484
  7.3 18.9 %all-to-all-start = ((bf16[16,24,384]{2,1,0:T(8,128)(2,1)}), bf16[16,24,384]{2,1,0:T(8,128)(2,1)S(1)}, u32[]{:S(2)}, u32[]{:S(2)}) async-start(bf16[16,24,384]{2,1,0:T(8,128)(2,1)} %get-tuple-element.14), calls=%async_computation | async-start | bytes 589824 | tf_op jit(solution)/shard_map/all_to_all | solution.py:288
  15.6 2.1 %copy-start.1 = (bf16[1,2,640,1536]{3,2,1,0:T(8,128)(2,1)S(1)}, bf16[1,2,640,1536]{3,2,1,0:T(8,128)(2,1)}, u32[]{:S(2)}) copy-start(bf16[1,2,640,1536]{3,2,1,0:T(8,128)(2,1)} %copy-done) | copy-start | bytes 11796484
  26.2 11.6 %all-to-all-start.1 = ((bf16[16,16,384]{2,1,0:T(8,128)(2,1)}), bf16[16,16,384]{2,1,0:T(8,128)(2,1)S(1)}, u32[]{:S(2)}, u32[]{:S(2)}) async-start(bf16[16,16,384]{2,1,0:T(8,128)(2,1)} %get-tuple-element.16), calls=%async_computation.1 | async-start | bytes 393216 | tf_op jit(solution)/shard_map/all_to_all | solution.py:288

commit v7 on v5

--- a/solution.py
+++ b/solution.py
@@ -9,6 +9,7 @@
 
 KB = 40
 LANES = 128
+INNER = 4
 VMEM_LIMIT = 24 * 1024 * 1024
 
 
@@ -175,13 +176,15 @@
         where_needed(0, slot, drop)
 
 
-def second_kernel(ways, tile, info, _, factors, *refs):
-    pieces, (out, acc, turned) = refs[: ways - 1], refs[ways - 1 :]
+def second_kernel(ways, outer, tile, info, _, factors, *refs):
+    pieces, refs = refs[: ways - 1], refs[ways - 1 :]
+    outs, (acc, turned) = refs[:outer], refs[outer:]
     slots, rows, columns = acc.shape
     rows = rows // 2
     piece_rows = pieces[0].shape[1]
     tiles = piece_rows // tile
-    cycles, width, _ = out.shape
+    width = outs[0].shape[1]
+    cycles = outer * INNER
     k_local = width // slots
     pitch = turned.shape[1] // cycles
 
@@ -207,12 +210,48 @@
             for lane in range(columns // LANES):
                 turned[lane, pl.ds(slot * k_local + k, cycles, stride=pitch), :] = total[:, lane * LANES : (lane + 1) * LANES]
 
-    for cycle in range(cycles):
+    me = lax.axis_index("blk")
+    for distance in range(cycles):
+        start = (me ^ distance) * pitch
         for lane in range(columns // LANES):
-            out[cycle, :, lane * LANES : (lane + 1) * LANES] = turned[lane, cycle * pitch : cycle * pitch + width].astype(out.dtype)
-
-
-def local(sky, beam, wigner, m_list, *, ways):
+            block = turned[lane, pl.ds(start, width), :].astype(jnp.bfloat16)
+            outs[distance // INNER][distance % INNER, :, lane * LANES : (lane + 1) * LANES] = block
+
+
+def regroup_kernel(*refs):
+    count = len(refs) - INNER + 1
+    for inner in range(1, INNER):
+        for index in range(count):
+            refs[count + inner - 1][index] = refs[index][inner]
+
+
+def place_kernel(half, count, *refs):
+    direct, moved, refs = refs[:count], refs[count : count + INNER - 1], refs[count + INNER - 1 :]
+    out, turned, staged, sem = refs[-4:]
+    k_local, slot_count, columns = staged.shape
+    width = direct[0].shape[1]
+    slots = width // k_local
+    pitch = turned.shape[1] // k_local
+    me = lax.axis_index("blk")
+    for lane in range(columns // LANES):
+        span = slice(lane * LANES, (lane + 1) * LANES)
+        for index in range(count):
+            for inner in range(INNER):
+                block = direct[index][0, :, span] if inner == 0 else moved[inner - 1][index, :, span]
+                block = block.astype(jnp.float32)
+                source = (me ^ (index * INNER + inner)) % (count * INNER)
+                for slot in range(slots):
+                    turned[lane, pl.ds(slots * source + slot, k_local, stride=pitch), :] = block[slot * k_local : (slot + 1) * k_local]
+        for k in range(k_local):
+            staged[k, :, span] = turned[lane, k * pitch : k * pitch + slot_count].astype(staged.dtype)
+    here = me // (count * INNER)
+    start = pl.multiple_of((here if half == 0 else 1 - here) * slot_count, slot_count)
+    copy = pltpu.make_async_copy(staged, out.at[:, pl.ds(start, slot_count), :], sem)
+    copy.start()
+    copy.wait()
+
+
+def local(sky, beam, wigner, m_list, *, ways, peers):
     slots, piece_rows, columns = sky.shape
     _, k_local, cycles, degrees = wigner.shape
     rows = k_local * cycles
@@ -256,12 +295,14 @@
         name="own_half",
     )(m_list, sky, wigner, beam)
 
-    blocks, _ = pl.pallas_call(
-        functools.partial(second_kernel, ways, tile),
-        out_shape=(pltpu.VMEM((cycles, width, columns), jnp.bfloat16), pltpu.VMEM(part.shape, part.dtype)),
+    outer = peers // INNER
+    block = (width, columns)
+    *sends, _ = pl.pallas_call(
+        functools.partial(second_kernel, ways, outer, tile),
+        out_shape=[pltpu.VMEM((INNER, *block), jnp.bfloat16)] * outer + [pltpu.VMEM(part.shape, part.dtype)],
         in_specs=[whole(pltpu.VMEM)] * (ways + 2),
-        out_specs=(whole(pltpu.VMEM),) * 2,
-        input_output_aliases={1: 1},
+        out_specs=[whole(pltpu.VMEM)] * (outer + 1),
+        input_output_aliases={1: outer},
         scratch_shapes=[
             pltpu.VMEM((lane_tiles, cycles * (width + 1 - width % 2), LANES), jnp.float32),
         ],
@@ -271,8 +312,50 @@
         ),
         name="other_half",
     )(info, part, factors, *pieces)
-    received = lax.all_to_all(blocks, "blk", split_axis=0, concat_axis=0, tiled=True)
-    return received.reshape(1, -1, k_local, columns)
+
+    def send(array, distance):
+        perm = [(b, b ^ distance) for b in range(peers)]
+        return pltpu.with_memory_space_constraint(lax.ppermute(array, "blk", perm), pltpu.VMEM)
+
+    count = outer // 2
+    arrived = [sends[0]] + [None] * (outer - 1)
+    for distance in [*range(count, outer), *range(1, count)]:
+        arrived[distance] = send(sends[distance], distance * INNER)
+    out = None
+    for half in range(2):
+        direct = arrived[half * count : (half + 1) * count]
+        grouped = pl.pallas_call(
+            regroup_kernel,
+            out_shape=[pltpu.VMEM((count, *block), jnp.bfloat16)] * (INNER - 1),
+            in_specs=[whole(pltpu.VMEM)] * count,
+            out_specs=[whole(pltpu.VMEM)] * (INNER - 1),
+            compiler_params=params,
+            name="regroup",
+        )(*direct)
+        moved = [None] * (INNER - 1)
+        for inner in reversed(range(1, INNER)):
+            moved[inner - 1] = send(grouped[inner - 1], inner)
+        slot_count = slots * count * INNER
+        operands = [*direct, *moved]
+        in_specs = [whole(pltpu.VMEM)] * len(operands)
+        if half:
+            operands.append(out)
+            in_specs.append(whole(pltpu.HBM))
+        out = pl.pallas_call(
+            functools.partial(place_kernel, half, count),
+            out_shape=pltpu.HBM((k_local, slots * peers, columns), jnp.bfloat16),
+            in_specs=in_specs,
+            out_specs=whole(pltpu.HBM),
+            input_output_aliases={len(operands) - 1: 0} if half else {},
+            scratch_shapes=[
+                pltpu.VMEM((lane_tiles, k_local * (slot_count + 1), LANES), jnp.float32),
+                pltpu.VMEM((k_local, slot_count, columns), jnp.bfloat16),
+                pltpu.SemaphoreType.DMA,
+            ],
+            compiler_params=params,
+            name="place",
+        )(*operands)
+    return out.transpose(1, 0, 2)[None]
 
 
 def solution(mesh):
@@ -283,5 +366,5 @@
         P("blk"),
     )
     out_specs = P("blk", None, "beamk", None)
-    body = functools.partial(local, ways=mesh.shape["beamk"])
+    body = functools.partial(local, ways=mesh.shape["beamk"], peers=mesh.shape["blk"])
     return jax.shard_map(body, mesh=mesh, in_specs=in_specs, out_specs=out_specs, check_vma=False)

time: 30.6 us -> 31.3 us (1.023)
  blocking collectives: 21.4 us -> 0 us
  starting transfers between devices: 0.45 us -> 13.2 us
  waiting for transfers between devices: 1.29 us -> 10 us
  Pallas kernels: 6.19 us -> 7.87 us
  local copies, waits for them, and re-layouts: 0.94 us -> 0 us
    all_to_all x1 -> x0, blocking collectives: 21.4 us -> none  [local(): lax.all_to_all(blocks, 'blk', split_axis=0, concat_axis=0, tiled=True)]
    ppermute x0 -> x9, starting transfers between devices: none -> 12.7 us  [send(): lax.ppermute(array, 'blk', perm)]
    ppermute x0 -> x9, waiting for transfers between devices: none -> 8.72 us  [send(): lax.ppermute(array, 'blk', perm)]
    pallas_call x1 -> x5, Pallas kernels: 3.12 us -> 4.8 us  [the longest x1 3.13 us: local(): pl.pallas_call(functools.partial(second_kernel, ways, outer, tile), out_s...]
    reshape x2 -> x0, local copies, waits for them, and re-layouts: 0.94 us -> none  [local(): return received.reshape(1, -1, k_local, columns)]
  transfers between devices with their start and end apart: 1 -> 10, of which waited for: 1 -> 5; matrix products, arithmetic and copies ran while one was open for 0% -> 0% of each run, Pallas kernels for 10% -> 13%
where the time goes in v7:
time: 31.3 us; the launch traced here: 31.1 us
  starting transfers between devices  13.2 us (42%)
  waiting for transfers between devices  10 us (32%)
  Pallas kernels  7.87 us (25%)
    ppermute x9, starting transfers between devices, send(): lax.ppermute(array, 'blk', perm)  12.7 us
    ppermute x9, waiting for transfers between devices, send(): lax.ppermute(array, 'blk', perm)  8.72 us
    pallas_call x1, Pallas kernels, local(): pl.pallas_call(functools.partial(second_kernel, ways, outer, tile), out_s...  3.13 us
    pallas_call x1, Pallas kernels, local(): pl.pallas_call(functools.partial(first_kernel, ways, tile), out_shape=(pl...  3.07 us
    pallas_call x2, Pallas kernels, local(): pl.pallas_call(functools.partial(place_kernel, half, count), out_shape=pl...  1.64 us
    ppermute x1, waiting for transfers between devices, local(): lax.ppermute(sky, 'beamk', perm)  1.29 us
  transfers between devices with their start and end apart: 10, of which 5 were waited for; matrix products, arithmetic and copies ran while one was open for 0% of the time, Pallas kernels for 13%

profile of v7, /device:TPU:0, one launch (start us, length us, event | category | flops | bytes accessed | tf_op | source)
XLA Modules:
  0.0 31.1 jit_solution(11828263587535440487)
XLA Ops:
  0.0 0.5 %collective-permute-start = (bf16[2,1536,384]{2,1,0:T(8,128)(2,1)}, bf16[2,1536,384]{2,1,0:T(8,128)(2,1)S(1)}, u32[]{:S(2)}, u32[]{:S(2)}) collective-permute-start(bf16[2,1536,384]{2,1,0:T(8,128)(2,1)} %sky.1), channel_id=1, source_target_pairs={{0,1},{1,0},{2,3},{3,2},{4,5},{5,4},{6,7},{7,6},{8,9},{9,8},{10,11... | collective-permute-start | bytes 7077896 | tf_op jit(solution)/shard_map/ppermute | solution.py:267
  0.5 3.1 %own_half.1 = (f32[2,640,384]{2,1,0:T(8,128)S(1)}, bf16[1,2,640,1536]{3,2,1,0:T(8,128)(2,1)S(1)}, f32[8,128]{1,0:T(8,128)S(1)}) custom-call(s32[2]{0:T(128)} %m_list.1, bf16[2,1536,384]{2,1,0:T(8,128)(2,1)} %sky.1, bf16[2,20,16,3072]{3,2,1,0:T(8,128)(2,1)} %wigner.1, f32[20,2,3072]{2,1,0:T(2,128)} %beam.1), custom_call_target="tpu_custom_call" | custom-call | flops 1509949440 | bytes 8388608 | tf_op jit(solution)/shard_map/own_half/pallas_call | solution.py:270
  3.5 1.3 %collective-permute-done.refs_0_ = bf16[2,1536,384]{2,1,0:T(8,128)(2,1)S(1)} collective-permute-done((bf16[2,1536,384]{2,1,0:T(8,128)(2,1)}, bf16[2,1536,384]{2,1,0:T(8,128)(2,1)S(1)}, u32[]{:S(2)}, u32[]{:S(2)}) %collective-permute-start) | collective-permute-done | bytes 2359328 | tf_op jit(solution)/shard_map/ppermute | solution.py:267
  4.8 3.1 %other_half.1 = (bf16[4,40,384]{2,1,0:T(8,128)(2,1)S(1)}, bf16[4,40,384]{2,1,0:T(8,128)(2,1)S(1)}, bf16[4,40,384]{2,1,0:T(8,128)(2,1)S(1)}, bf16[4,40,384]{2,1,0:T(8,128)(2,1)S(1)}, f32[2,640,384]{2,1,0:T(8,128)S(1)}) custom-call(f32[8,128]{1,0:T(8,128)S(1)} %get-tuple-element.18.info, ...), custom_call_target="tpu_custom_call", output_to_operand_aliasing={{4}: (1, {})} | custom-call | flops 1509949440 | bytes 8388608 | tf_op jit(solution)/shard_map/other_half/pallas_call | solution.py:300
  8.0 3.0 %collective-permute-start.6 = (bf16[4,40,384]{2,1,0:T(8,128)(2,1)S(1)}, bf16[4,40,384]{2,1,0:T(8,128)(2,1)S(1)}, u32[]{:S(2)}, u32[]{:S(2)}) collective-permute-start(bf16[4,40,384]{2,1,0:T(8,128)(2,1)S(1)} %get-tuple-element.27), channel_id=1, source_target_pairs={{0,8},{2,10},{4,12},{6,14},{8,0},{10,2},{12,4},{14,6},{16,24},{18,... | collective-permute-start | bytes 368648 | tf_op jit(solution)/shard_map/ppermute | solution.py:318
  11.0 2.6 %collective-permute-start.1 = (bf16[4,40,384]{2,1,0:T(8,128)(2,1)S(1)}, bf16[4,40,384]{2,1,0:T(8,128)(2,1)S(1)}, u32[]{:S(2)}, u32[]{:S(2)}) collective-permute-start(bf16[4,40,384]{2,1,0:T(8,128)(2,1)S(1)} %get-tuple-element.21), channel_id=1, source_target_pairs={{0,16},{2,18},{4,20},{6,22},{8,24},{10,26},{12,28},{14,30},{16,0},... | collective-permute-start | bytes 368648 | tf_op jit(solution)/shard_map/ppermute | solution.py:318
  13.6 0.0 collective-permute-start.2
  13.6 1.6 %collective-permute-done.6.refs_1_ = bf16[4,40,384]{2,1,0:T(8,128)(2,1)S(1)} collective-permute-done((bf16[4,40,384]{2,1,0:T(8,128)(2,1)S(1)}, bf16[4,40,384]{2,1,0:T(8,128)(2,1)S(1)}, u32[]{:S(2)}, u32[]{:S(2)}) %collective-permute-start.6) | collective-permute-done | bytes 122912 | tf_op jit(solution)/shard_map/ppermute | solution.py:318
  15.2 1.4 %collective-permute-start.7 = (bf16[2,40,384]{2,1,0:T(8,128)(2,1)S(1)}, bf16[2,40,384]{2,1,0:T(8,128)(2,1)S(1)}, u32[]{:S(2)}, u32[]{:S(2)}) collective-permute-start(bf16[2,40,384]{2,1,0:T(8,128)(2,1)S(1)} %get-tuple-element.28), channel_id=1, source_target_pairs={{0,2},{2,0},{4,6},{6,4},{8,10},{10,8},{12,14},{14,12},{16,18},{18,... | collective-permute-start | bytes 184328 | tf_op jit(solution)/shard_map/ppermute | solution.py:318
  16.6 1.6 %collective-permute-start.8 = (bf16[2,40,384]{2,1,0:T(8,128)(2,1)S(1)}, bf16[2,40,384]{2,1,0:T(8,128)(2,1)S(1)}, u32[]{:S(2)}, u32[]{:S(2)}) collective-permute-start(bf16[2,40,384]{2,1,0:T(8,128)(2,1)S(1)} %get-tuple-element.29), channel_id=1, source_target_pairs={{0,4},{2,6},{4,0},{6,2},{8,12},{10,14},{12,8},{14,10},{16,20},{18,... | collective-permute-start | bytes 184328 | tf_op jit(solution)/shard_map/ppermute | solution.py:318
  18.1 0.6 %collective-permute-start.9 = (bf16[2,40,384]{2,1,0:T(8,128)(2,1)S(1)}, bf16[2,40,384]{2,1,0:T(8,128)(2,1)S(1)}, u32[]{:S(2)}, u32[]{:S(2)}) collective-permute-start(bf16[2,40,384]{2,1,0:T(8,128)(2,1)S(1)} %get-tuple-element.30), channel_id=1, source_target_pairs={{0,6},{2,4},{4,2},{6,0},{8,14},{10,12},{12,10},{14,8},{16,22},{18,... | collective-permute-start | bytes 184328 | tf_op jit(solution)/shard_map/ppermute | solution.py:318
  18.7 3.5 %collective-permute-done.1.refs_0_ = bf16[4,40,384]{2,1,0:T(8,128)(2,1)S(1)} collective-permute-done((bf16[4,40,384]{2,1,0:T(8,128)(2,1)S(1)}, bf16[4,40,384]{2,1,0:T(8,128)(2,1)S(1)}, u32[]{:S(2)}, u32[]{:S(2)}) %collective-permute-start.1) | collective-permute-done | bytes 122912 | tf_op jit(solution)/shard_map/ppermute | solution.py:318
  22.2 0.0 collective-permute-done.2.refs_1_
  22.2 1.6 %collective-permute-start.3 = (bf16[2,40,384]{2,1,0:T(8,128)(2,1)S(1)}, bf16[2,40,384]{2,1,0:T(8,128)(2,1)S(1)}, u32[]{:S(2)}, u32[]{:S(2)}) collective-permute-start(bf16[2,40,384]{2,1,0:T(8,128)(2,1)S(1)} %get-tuple-element.23), channel_id=1, source_target_pairs={{0,2},{2,0},{4,6},{6,4},{8,10},{10,8},{12,14},{14,12},{16,18},{18,... | collective-permute-start | bytes 184328 | tf_op jit(solution)/shard_map/ppermute | solution.py:318
  23.8 1.4 %collective-permute-start.4 = (bf16[2,40,384]{2,1,0:T(8,128)(2,1)S(1)}, bf16[2,40,384]{2,1,0:T(8,128)(2,1)S(1)}, u32[]{:S(2)}, u32[]{:S(2)}) collective-permute-start(bf16[2,40,384]{2,1,0:T(8,128)(2,1)S(1)} %get-tuple-element.24), channel_id=1, source_target_pairs={{0,4},{2,6},{4,0},{6,2},{8,12},{10,14},{12,8},{14,10},{16,20},{18,... | collective-permute-start | bytes 184328 | tf_op jit(solution)/shard_map/ppermute | solution.py:318
  25.2 0.0 collective-permute-done.7.refs_2_
  25.2 0.6 %collective-permute-start.5 = (bf16[2,40,384]{2,1,0:T(8,128)(2,1)S(1)}, bf16[2,40,384]{2,1,0:T(8,128)(2,1)S(1)}, u32[]{:S(2)}, u32[]{:S(2)}) collective-permute-start(bf16[2,40,384]{2,1,0:T(8,128)(2,1)S(1)} %get-tuple-element.25), channel_id=1, source_target_pairs={{0,6},{2,4},{4,2},{6,0},{8,14},{10,12},{12,10},{14,8},{16,22},{18,... | collective-permute-start | bytes 184328 | tf_op jit(solution)/shard_map/ppermute | solution.py:318
  25.8 0.0 collective-permute-done.8.refs_3_
  25.8 0.0 collective-permute-done.9.refs_4_
  25.8 0.8 %place.2.refs_5_ = bf16[20,32,384]{2,1,0:T(8,128)(2,1)} custom-call(bf16[4,40,384]{2,1,0:T(8,128)(2,1)S(1)} %get-tuple-element.26.refs_0_, bf16[4,40,384]{2,1,0:T(8,128)(2,1)S(1)} %collective-permute-done.6.refs_1_, bf16[2,40,384]{2,1,0:T(8,128)(2,1)S(1)} %collective-permute-done.7.refs_2_, bf16[2,40,384]{2,1,0:T(8,128)(2,1)S(1)} %collective-permute-done.8.refs_3_, ...), custom_call_target="tpu_custom_call" | custom-call | tf_op jit(solution)/shard_map/place/pallas_call | solution.py:344
  26.6 0.0 collective-permute-done.3.refs_2_
  26.6 1.4 %collective-permute-done.4.refs_3_ = bf16[2,40,384]{2,1,0:T(8,128)(2,1)S(1)} collective-permute-done((bf16[2,40,384]{2,1,0:T(8,128)(2,1)S(1)}, bf16[2,40,384]{2,1,0:T(8,128)(2,1)S(1)}, u32[]{:S(2)}, u32[]{:S(2)}) %collective-permute-start.4) | collective-permute-done | bytes 61472 | tf_op jit(solution)/shard_map/ppermute | solution.py:318
  28.0 2.3 %collective-permute-done.5.refs_4_ = bf16[2,40,384]{2,1,0:T(8,128)(2,1)S(1)} collective-permute-done((bf16[2,40,384]{2,1,0:T(8,128)(2,1)S(1)}, bf16[2,40,384]{2,1,0:T(8,128)(2,1)S(1)}, u32[]{:S(2)}, u32[]{:S(2)}) %collective-permute-start.5) | collective-permute-done | bytes 61472 | tf_op jit(solution)/shard_map/ppermute | solution.py:318
  30.3 0.8 %place.3 = bf16[20,32,384]{2,1,0:T(8,128)(2,1)} custom-call(bf16[4,40,384]{2,1,0:T(8,128)(2,1)S(1)} %collective-permute-done.1.refs_0_, bf16[4,40,384]{2,1,0:T(8,128)(2,1)S(1)} %collective-permute-done.2.refs_1_, bf16[2,40,384]{2,1,0:T(8,128)(2,1)S(1)} %collective-permute-done.3.refs_2_, ...), custom_call_target="tpu_custom_call", output_to_operand_aliasing={{}: (5, {})} | custom-call | tf_op jit(solution)/shard_map/place/pallas_call | solution.py:344
  (2 shorter events, 0.0 us)
Async XLA Ops:
  0.0 4.8 %collective-permute-start = (bf16[2,1536,384]{2,1,0:T(8,128)(2,1)}, bf16[2,1536,384]{2,1,0:T(8,128)(2,1)S(1)}, u32[]{:S(2)}, u32[]{:S(2)}) collective-permute-start(bf16[2,1536,384]{2,1,0:T(8,128)(2,1)} %sky.1), channel_id=1, source_target_pairs={{0,1},{1,0},{2,3},{3,2},{4,5},{5,4},{6,7},{7,6},{8,9},{9,8},{10,11... | collective-permute-start | bytes 7077896 | tf_op jit(solution)/shard_map/ppermute | solution.py:267
  8.0 7.2 %collective-permute-start.6 = (bf16[4,40,384]{2,1,0:T(8,128)(2,1)S(1)}, bf16[4,40,384]{2,1,0:T(8,128)(2,1)S(1)}, u32[]{:S(2)}, u32[]{:S(2)}) collective-permute-start(bf16[4,40,384]{2,1,0:T(8,128)(2,1)S(1)} %get-tuple-element.27), channel_id=1, source_target_pairs={{0,8},{2,10},{4,12},{6,14},{8,0},{10,2},{12,4},{14,6},{16,24},{18,... | collective-permute-start | bytes 368648 | tf_op jit(solution)/shard_map/ppermute | solution.py:318
  11.0 11.2 %collective-permute-start.1 = (bf16[4,40,384]{2,1,0:T(8,128)(2,1)S(1)}, bf16[4,40,384]{2,1,0:T(8,128)(2,1)S(1)}, u32[]{:S(2)}, u32[]{:S(2)}) collective-permute-start(bf16[4,40,384]{2,1,0:T(8,128)(2,1)S(1)} %get-tuple-element.21), channel_id=1, source_target_pairs={{0,16},{2,18},{4,20},{6,22},{8,24},{10,26},{12,28},{14,30},{16,0},... | collective-permute-start | bytes 368648 | tf_op jit(solution)/shard_map/ppermute | solution.py:318
  13.6 8.6 %collective-permute-start.2 = (bf16[4,40,384]{2,1,0:T(8,128)(2,1)S(1)}, bf16[4,40,384]{2,1,0:T(8,128)(2,1)S(1)}, u32[]{:S(2)}, u32[]{:S(2)}) collective-permute-start(bf16[4,40,384]{2,1,0:T(8,128)(2,1)S(1)} %get-tuple-element.22), channel_id=1, source_target_pairs={{0,24},{2,26},{4,28},{6,30},{8,16},{10,18},{12,20},{14,22},{16,8},... | collective-permute-start | bytes 368648 | tf_op jit(solution)/shard_map/ppermute | solution.py:318
  15.2 10.0 %collective-permute-start.7 = (bf16[2,40,384]{2,1,0:T(8,128)(2,1)S(1)}, bf16[2,40,384]{2,1,0:T(8,128)(2,1)S(1)}, u32[]{:S(2)}, u32[]{:S(2)}) collective-permute-start(bf16[2,40,384]{2,1,0:T(8,128)(2,1)S(1)} %get-tuple-element.28), channel_id=1, source_target_pairs={{0,2},{2,0},{4,6},{6,4},{8,10},{10,8},{12,14},{14,12},{16,18},{18,... | collective-permute-start | bytes 184328 | tf_op jit(solution)/shard_map/ppermute | solution.py:318
  16.6 9.2 %collective-permute-start.8 = (bf16[2,40,384]{2,1,0:T(8,128)(2,1)S(1)}, bf16[2,40,384]{2,1,0:T(8,128)(2,1)S(1)}, u32[]{:S(2)}, u32[]{:S(2)}) collective-permute-start(bf16[2,40,384]{2,1,0:T(8,128)(2,1)S(1)} %get-tuple-element.29), channel_id=1, source_target_pairs={{0,4},{2,6},{4,0},{6,2},{8,12},{10,14},{12,8},{14,10},{16,20},{18,... | collective-permute-start | bytes 184328 | tf_op jit(solution)/shard_map/ppermute | solution.py:318
  18.1 7.6 %collective-permute-start.9 = (bf16[2,40,384]{2,1,0:T(8,128)(2,1)S(1)}, bf16[2,40,384]{2,1,0:T(8,128)(2,1)S(1)}, u32[]{:S(2)}, u32[]{:S(2)}) collective-permute-start(bf16[2,40,384]{2,1,0:T(8,128)(2,1)S(1)} %get-tuple-element.30), channel_id=1, source_target_pairs={{0,6},{2,4},{4,2},{6,0},{8,14},{10,12},{12,10},{14,8},{16,22},{18,... | collective-permute-start | bytes 184328 | tf_op jit(solution)/shard_map/ppermute | solution.py:318
  22.2 4.4 %collective-permute-start.3 = (bf16[2,40,384]{2,1,0:T(8,128)(2,1)S(1)}, bf16[2,40,384]{2,1,0:T(8,128)(2,1)S(1)}, u32[]{:S(2)}, u32[]{:S(2)}) collective-permute-start(bf16[2,40,384]{2,1,0:T(8,128)(2,1)S(1)} %get-tuple-element.23), channel_id=1, source_target_pairs={{0,2},{2,0},{4,6},{6,4},{8,10},{10,8},{12,14},{14,12},{16,18},{18,... | collective-permute-start | bytes 184328 | tf_op jit(solution)/shard_map/ppermute | solution.py:318
  23.8 4.2 %collective-permute-start.4 = (bf16[2,40,384]{2,1,0:T(8,128)(2,1)S(1)}, bf16[2,40,384]{2,1,0:T(8,128)(2,1)S(1)}, u32[]{:S(2)}, u32[]{:S(2)}) collective-permute-start(bf16[2,40,384]{2,1,0:T(8,128)(2,1)S(1)} %get-tuple-element.24), channel_id=1, source_target_pairs={{0,4},{2,6},{4,0},{6,2},{8,12},{10,14},{12,8},{14,10},{16,20},{18,... | collective-permute-start | bytes 184328 | tf_op jit(solution)/shard_map/ppermute | solution.py:318
  25.2 5.1 %collective-permute-start.5 = (bf16[2,40,384]{2,1,0:T(8,128)(2,1)S(1)}, bf16[2,40,384]{2,1,0:T(8,128)(2,1)S(1)}, u32[]{:S(2)}, u32[]{:S(2)}) collective-permute-start(bf16[2,40,384]{2,1,0:T(8,128)(2,1)S(1)} %get-tuple-element.25), channel_id=1, source_target_pairs={{0,6},{2,4},{4,2},{6,0},{8,14},{10,12},{12,10},{14,8},{16,22},{18,... | collective-permute-start | bytes 184328 | tf_op jit(solution)/shard_map/ppermute | solution.py:318

commit v8 on v7

--- a/solution.py
+++ b/solution.py
@@ -178,12 +178,13 @@
 
 def second_kernel(ways, outer, tile, info, _, factors, *refs):
     pieces, refs = refs[: ways - 1], refs[ways - 1 :]
-    outs, (acc, turned) = refs[:outer], refs[outer:]
+    count = outer // 2
+    near, far, (acc, turned) = refs[:count], refs[count : count + INNER], refs[count + INNER :]
     slots, rows, columns = acc.shape
     rows = rows // 2
     piece_rows = pieces[0].shape[1]
     tiles = piece_rows // tile
-    width = outs[0].shape[1]
+    width = far[0].shape[1]
     cycles = outer * INNER
     k_local = width // slots
     pitch = turned.shape[1] // cycles
@@ -215,21 +216,27 @@
         start = (me ^ distance) * pitch
         for lane in range(columns // LANES):
             block = turned[lane, pl.ds(start, width), :].astype(jnp.bfloat16)
-            outs[distance // INNER][distance % INNER, :, lane * LANES : (lane + 1) * LANES] = block
-
-
-def regroup_kernel(*refs):
-    count = len(refs) - INNER + 1
-    for inner in range(1, INNER):
-        for index in range(count):
-            refs[count + inner - 1][index] = refs[index][inner]
+            away, inner = divmod(distance, INNER)
+            span = slice(lane * LANES, (lane + 1) * LANES)
+            if away < count:
+                near[away][inner, :, span] = block
+            else:
+                far[inner][away - count, :, span] = block
+
+
+def regroup_kernel(count, *refs):
+    near, far, refs = refs[:count], refs[count : count + INNER], refs[count + INNER :]
+    for index in range(count):
+        for inner in range(INNER):
+            refs[index][inner] = far[inner][index]
+            if inner:
+                refs[count + inner - 1][index] = near[index][inner]
 
 
 def place_kernel(half, count, *refs):
-    direct, moved, refs = refs[:count], refs[count : count + INNER - 1], refs[count + INNER - 1 :]
     out, turned, staged, sem = refs[-4:]
     k_local, slot_count, columns = staged.shape
-    width = direct[0].shape[1]
+    width = refs[0].shape[1]
     slots = width // k_local
     pitch = turned.shape[1] // k_local
     me = lax.axis_index("blk")
@@ -237,7 +244,10 @@
         span = slice(lane * LANES, (lane + 1) * LANES)
         for index in range(count):
             for inner in range(INNER):
-                block = direct[index][0, :, span] if inner == 0 else moved[inner - 1][index, :, span]
+                if half:
+                    block = refs[index][inner, :, span]
+                else:
+                    block = refs[count + inner - 1][index, :, span] if inner else refs[index][0, :, span]
                 block = block.astype(jnp.float32)
                 source = (me ^ (index * INNER + inner)) % (count * INNER)
                 for slot in range(slots):
@@ -296,13 +306,17 @@
     )(m_list, sky, wigner, beam)
 
     outer = peers // INNER
-    block = (width, columns)
+    count = outer // 2
+
+    def blocks(number):
+        return pltpu.VMEM((number, width, columns), jnp.bfloat16)
+
     *sends, _ = pl.pallas_call(
         functools.partial(second_kernel, ways, outer, tile),
-        out_shape=[pltpu.VMEM((INNER, *block), jnp.bfloat16)] * outer + [pltpu.VMEM(part.shape, part.dtype)],
+        out_shape=[blocks(INNER)] * count + [blocks(count)] * INNER + [pltpu.VMEM(part.shape, part.dtype)],
         in_specs=[whole(pltpu.VMEM)] * (ways + 2),
-        out_specs=[whole(pltpu.VMEM)] * (outer + 1),
-        input_output_aliases={1: outer},
+        out_specs=[whole(pltpu.VMEM)] * (count + INNER + 1),
+        input_output_aliases={1: count + INNER},
         scratch_shapes=[
             pltpu.VMEM((lane_tiles, cycles * (width + 1 - width % 2), LANES), jnp.float32),
         ],
@@ -317,26 +331,28 @@
         perm = [(b, b ^ distance) for b in range(peers)]
         return pltpu.with_memory_space_constraint(lax.ppermute(array, "blk", perm), pltpu.VMEM)
 
-    count = outer // 2
-    arrived = [sends[0]] + [None] * (outer - 1)
-    for distance in [*range(count, outer), *range(1, count)]:
-        arrived[distance] = send(sends[distance], distance * INNER)
+    near, far = list(sends[:count]), list(sends[count:])
+    for inner in reversed(range(1, INNER)):
+        far[inner] = send(far[inner], inner)
+    for index in range(1, count):
+        near[index] = send(near[index], index * INNER)
+    shapes = [blocks(INNER)] * count + [blocks(count)] * (INNER - 1)
+    regrouped = pl.pallas_call(
+        functools.partial(regroup_kernel, count),
+        out_shape=shapes,
+        in_specs=[whole(pltpu.VMEM)] * (count + INNER),
+        out_specs=[whole(pltpu.VMEM)] * len(shapes),
+        compiler_params=params,
+        name="regroup",
+    )(*near, *far)
+    far = [send(array, (count + index) * INNER) for index, array in enumerate(regrouped[:count])]
+    moved = list(regrouped[count:])
+    for inner in reversed(range(1, INNER)):
+        moved[inner - 1] = send(moved[inner - 1], inner)
+    near += moved
     out = None
-    for half in range(2):
-        direct = arrived[half * count : (half + 1) * count]
-        grouped = pl.pallas_call(
-            regroup_kernel,
-            out_shape=[pltpu.VMEM((count, *block), jnp.bfloat16)] * (INNER - 1),
-            in_specs=[whole(pltpu.VMEM)] * count,
-            out_specs=[whole(pltpu.VMEM)] * (INNER - 1),
-            compiler_params=params,
-            name="regroup",
-        )(*direct)
-        moved = [None] * (INNER - 1)
-        for inner in reversed(range(1, INNER)):
-            moved[inner - 1] = send(grouped[inner - 1], inner)
+    for half, operands in enumerate((near, far)):
         slot_count = slots * count * INNER
-        operands = [*direct, *moved]
         in_specs = [whole(pltpu.VMEM)] * len(operands)
         if half:
             operands.append(out)

time: 31.3 us -> 30.1 us (0.962)
  waiting for transfers between devices: 10 us -> 8.7 us
  starting transfers between devices: 13.2 us -> 13.7 us
  Pallas kernels: 7.87 us -> 7.53 us
    ppermute x9, waiting for transfers between devices: 8.72 us -> 7.4 us  [send(): lax.ppermute(array, 'blk', perm)]
    ppermute x9, starting transfers between devices: 12.7 us -> 13.2 us  [send(): lax.ppermute(array, 'blk', perm)]
    pallas_call x1, Pallas kernels: 3.13 us -> 2.78 us  [local(): pl.pallas_call(functools.partial(second_kernel, ways, outer, tile), out_s...]
  transfers between devices with their start and end apart: 10 -> 10, of which waited for: 5 -> 8; matrix products, arithmetic and copies ran while one was open for 0% -> 0% of each run, Pallas kernels for 13% -> 13%
where the time goes in v8:
time: 30.1 us; the launch traced here: 29.9 us
  starting transfers between devices  13.7 us (46%)
  waiting for transfers between devices  8.7 us (29%)
  Pallas kernels  7.53 us (25%)
    ppermute x9, starting transfers between devices, send(): lax.ppermute(array, 'blk', perm)  13.2 us
    ppermute x9, waiting for transfers between devices, send(): lax.ppermute(array, 'blk', perm)  7.4 us
    pallas_call x1, Pallas kernels, local(): pl.pallas_call(functools.partial(first_kernel, ways, tile), out_shape=(pl...  3.07 us
    pallas_call x1, Pallas kernels, local(): pl.pallas_call(functools.partial(second_kernel, ways, outer, tile), out_s...  2.78 us
    pallas_call x2, Pallas kernels, local(): pl.pallas_call(functools.partial(place_kernel, half, count), out_shape=pl...  1.63 us
    ppermute x1, waiting for transfers between devices, local(): lax.ppermute(sky, 'beamk', perm)  1.29 us
  transfers between devices with their start and end apart: 10, of which 8 were waited for; matrix products, arithmetic and copies ran while one was open for 0% of the time, Pallas kernels for 13%

profile of v8, /device:TPU:0, one launch (start us, length us, event | category | flops | bytes accessed | tf_op | source)
XLA Modules:
  0.0 29.9 jit_solution(248872260625132919)
XLA Ops:
  0.0 0.5 %collective-permute-start = (bf16[2,1536,384]{2,1,0:T(8,128)(2,1)}, bf16[2,1536,384]{2,1,0:T(8,128)(2,1)S(1)}, u32[]{:S(2)}, u32[]{:S(2)}) collective-permute-start(bf16[2,1536,384]{2,1,0:T(8,128)(2,1)} %sky.1), channel_id=1, source_target_pairs={{0,1},{1,0},{2,3},{3,2},{4,5},{5,4},{6,7},{7,6},{8,9},{9,8},{10,11... | collective-permute-start | bytes 7077896 | tf_op jit(solution)/shard_map/ppermute | solution.py:277
  0.5 3.1 %own_half.1 = (f32[2,640,384]{2,1,0:T(8,128)S(1)}, bf16[1,2,640,1536]{3,2,1,0:T(8,128)(2,1)S(1)}, f32[8,128]{1,0:T(8,128)S(1)}) custom-call(s32[2]{0:T(128)} %m_list.1, bf16[2,1536,384]{2,1,0:T(8,128)(2,1)} %sky.1, bf16[2,20,16,3072]{3,2,1,0:T(8,128)(2,1)} %wigner.1, f32[20,2,3072]{2,1,0:T(2,128)} %beam.1), custom_call_target="tpu_custom_call" | custom-call | flops 1509949440 | bytes 8388608 | tf_op jit(solution)/shard_map/own_half/pallas_call | solution.py:280
  3.5 1.3 %collective-permute-done.refs_0_ = bf16[2,1536,384]{2,1,0:T(8,128)(2,1)S(1)} collective-permute-done((bf16[2,1536,384]{2,1,0:T(8,128)(2,1)}, bf16[2,1536,384]{2,1,0:T(8,128)(2,1)S(1)}, u32[]{:S(2)}, u32[]{:S(2)}) %collective-permute-start) | collective-permute-done | bytes 2359328 | tf_op jit(solution)/shard_map/ppermute | solution.py:277
  4.8 2.8 %other_half.1 = (bf16[4,40,384]{2,1,0:T(8,128)(2,1)S(1)}, bf16[4,40,384]{2,1,0:T(8,128)(2,1)S(1)}, bf16[2,40,384]{2,1,0:T(8,128)(2,1)S(1)}, bf16[2,40,384]{2,1,0...) custom-call(f32[8,128]{1,0:T(8,128)S(1)} %get-tuple-element.19.info,, ...), custom_call_target="tpu_custom_call", output_to_operand_aliasing={{6}: (1, {})} | custom-call | flops 1509949440 | bytes 8388608 | tf_op jit(solution)/shard_map/other_half/pallas_call | solution.py:314
  7.6 3.4 %collective-permute-start.1 = (bf16[4,40,384]{2,1,0:T(8,128)(2,1)S(1)}, bf16[4,40,384]{2,1,0:T(8,128)(2,1)S(1)}, u32[]{:S(2)}, u32[]{:S(2)}) collective-permute-start(bf16[4,40,384]{2,1,0:T(8,128)(2,1)S(1)} %get-tuple-element.23), channel_id=1, source_target_pairs={{0,8},{2,10},{4,12},{6,14},{8,0},{10,2},{12,4},{14,6},{16,24},{18,... | collective-permute-start | bytes 368648 | tf_op jit(solution)/shard_map/ppermute | solution.py:332
  11.0 1.2 %collective-permute-start.2 = (bf16[2,40,384]{2,1,0:T(8,128)(2,1)S(1)}, bf16[2,40,384]{2,1,0:T(8,128)(2,1)S(1)}, u32[]{:S(2)}, u32[]{:S(2)}) collective-permute-start(bf16[2,40,384]{2,1,0:T(8,128)(2,1)S(1)} %get-tuple-element.25), channel_id=1, source_target_pairs={{0,2},{2,0},{4,6},{6,4},{8,10},{10,8},{12,14},{14,12},{16,18},{18,... | collective-permute-start | bytes 184328 | tf_op jit(solution)/shard_map/ppermute | solution.py:332
  12.1 1.9 %collective-permute-start.3 = (bf16[2,40,384]{2,1,0:T(8,128)(2,1)S(1)}, bf16[2,40,384]{2,1,0:T(8,128)(2,1)S(1)}, u32[]{:S(2)}, u32[]{:S(2)}) collective-permute-start(bf16[2,40,384]{2,1,0:T(8,128)(2,1)S(1)} %get-tuple-element.26), channel_id=1, source_target_pairs={{0,4},{2,6},{4,0},{6,2},{8,12},{10,14},{12,8},{14,10},{16,20},{18,... | collective-permute-start | bytes 184328 | tf_op jit(solution)/shard_map/ppermute | solution.py:332
  14.0 0.5 %collective-permute-start.4 = (bf16[2,40,384]{2,1,0:T(8,128)(2,1)S(1)}, bf16[2,40,384]{2,1,0:T(8,128)(2,1)S(1)}, u32[]{:S(2)}, u32[]{:S(2)}) collective-permute-start(bf16[2,40,384]{2,1,0:T(8,128)(2,1)S(1)} %get-tuple-element.27), channel_id=1, source_target_pairs={{0,6},{2,4},{4,2},{6,0},{8,14},{10,12},{12,10},{14,8},{16,22},{18,... | collective-permute-start | bytes 184328 | tf_op jit(solution)/shard_map/ppermute | solution.py:332
  14.5 1.1 %collective-permute-done.2.refs_3_ = bf16[2,40,384]{2,1,0:T(8,128)(2,1)S(1)} collective-permute-done((bf16[2,40,384]{2,1,0:T(8,128)(2,1)S(1)}, bf16[2,40,384]{2,1,0:T(8,128)(2,1)S(1)}, u32[]{:S(2)}, u32[]{:S(2)}) %collective-permute-start.2) | collective-permute-done | bytes 61472 | tf_op jit(solution)/shard_map/ppermute | solution.py:332
  15.6 1.2 %collective-permute-done.3.refs_4_ = bf16[2,40,384]{2,1,0:T(8,128)(2,1)S(1)} collective-permute-done((bf16[2,40,384]{2,1,0:T(8,128)(2,1)S(1)}, bf16[2,40,384]{2,1,0:T(8,128)(2,1)S(1)}, u32[]{:S(2)}, u32[]{:S(2)}) %collective-permute-start.3) | collective-permute-done | bytes 61472 | tf_op jit(solution)/shard_map/ppermute | solution.py:332
  16.8 2.3 %collective-permute-done.4.refs_5_ = bf16[2,40,384]{2,1,0:T(8,128)(2,1)S(1)} collective-permute-done((bf16[2,40,384]{2,1,0:T(8,128)(2,1)S(1)}, bf16[2,40,384]{2,1,0:T(8,128)(2,1)S(1)}, u32[]{:S(2)}, u32[]{:S(2)}) %collective-permute-start.4) | collective-permute-done | bytes 61472 | tf_op jit(solution)/shard_map/ppermute | solution.py:332
  19.1 0.0 collective-permute-done.1.refs_1_
  19.1 2.3 %collective-permute-start.5 = (bf16[4,40,384]{2,1,0:T(8,128)(2,1)S(1)}, bf16[4,40,384]{2,1,0:T(8,128)(2,1)S(1)}, u32[]{:S(2)}, u32[]{:S(2)}) collective-permute-start(bf16[4,40,384]{2,1,0:T(8,128)(2,1)S(1)} %get-tuple-element.28), channel_id=1, source_target_pairs={{0,16},{2,18},{4,20},{6,22},{8,24},{10,26},{12,28},{14,30},{16,0},... | collective-permute-start | bytes 368648 | tf_op jit(solution)/shard_map/ppermute | solution.py:332
  21.5 0.6 %collective-permute-start.6 = (bf16[4,40,384]{2,1,0:T(8,128)(2,1)S(1)}, bf16[4,40,384]{2,1,0:T(8,128)(2,1)S(1)}, u32[]{:S(2)}, u32[]{:S(2)}) collective-permute-start(bf16[4,40,384]{2,1,0:T(8,128)(2,1)S(1)} %get-tuple-element.29), channel_id=1, source_target_pairs={{0,24},{2,26},{4,28},{6,30},{8,16},{10,18},{12,20},{14,22},{16,8},... | collective-permute-start | bytes 368648 | tf_op jit(solution)/shard_map/ppermute | solution.py:332
  22.0 0.2 collective-permute-start.7
  22.2 0.5 %collective-permute-start.8 = (bf16[2,40,384]{2,1,0:T(8,128)(2,1)S(1)}, bf16[2,40,384]{2,1,0:T(8,128)(2,1)S(1)}, u32[]{:S(2)}, u32[]{:S(2)}) collective-permute-start(bf16[2,40,384]{2,1,0:T(8,128)(2,1)S(1)} %get-tuple-element.31), channel_id=1, source_target_pairs={{0,4},{2,6},{4,0},{6,2},{8,12},{10,14},{12,8},{14,10},{16,20},{18,... | collective-permute-start | bytes 184328 | tf_op jit(solution)/shard_map/ppermute | solution.py:332
  22.7 2.8 %collective-permute-start.9 = (bf16[2,40,384]{2,1,0:T(8,128)(2,1)S(1)}, bf16[2,40,384]{2,1,0:T(8,128)(2,1)S(1)}, u32[]{:S(2)}, u32[]{:S(2)}) collective-permute-start(bf16[2,40,384]{2,1,0:T(8,128)(2,1)S(1)} %get-tuple-element.32), channel_id=1, source_target_pairs={{0,6},{2,4},{4,2},{6,0},{8,14},{10,12},{12,10},{14,8},{16,22},{18,... | collective-permute-start | bytes 184328 | tf_op jit(solution)/shard_map/ppermute | solution.py:332
  25.5 0.7 %collective-permute-done.7.refs_2_ = bf16[2,40,384]{2,1,0:T(8,128)(2,1)S(1)} collective-permute-done((bf16[2,40,384]{2,1,0:T(8,128)(2,1)S(1)}, bf16[2,40,384]{2,1,0:T(8,128)(2,1)S(1)}, u32[]{:S(2)}, u32[]{:S(2)}) %collective-permute-start.7) | collective-permute-done | bytes 61472 | tf_op jit(solution)/shard_map/ppermute | solution.py:332
  26.2 0.2 collective-permute-done.8.refs_3_
  26.4 1.4 %collective-permute-done.9.refs_4_ = bf16[2,40,384]{2,1,0:T(8,128)(2,1)S(1)} collective-permute-done((bf16[2,40,384]{2,1,0:T(8,128)(2,1)S(1)}, bf16[2,40,384]{2,1,0:T(8,128)(2,1)S(1)}, u32[]{:S(2)}, u32[]{:S(2)}) %collective-permute-start.9) | collective-permute-done | bytes 61472 | tf_op jit(solution)/shard_map/ppermute | solution.py:332
  27.8 0.8 %place.2.refs_2_ = bf16[20,32,384]{2,1,0:T(8,128)(2,1)} custom-call(bf16[4,40,384]{2,1,0:T(8,128)(2,1)S(1)} %get-tuple-element.22.refs_0_, bf16[4,40,384]{2,1,0:T(8,128)(2,1)S(1)} %collective-permute-done.1.refs_1_, bf16[2,40,384]{2,1,0:T(8,128)(2,1)S(1)} %collective-permute-done.7.refs_2_, bf16[2,40,384]{2,1,0:T(8,128)(2,1)S(1)} %collective-permute-done.8.refs_3_, ...), custom_call_target="tpu_custom_call" | custom-call | tf_op jit(solution)/shard_map/place/pallas_call | solution.py:360
  28.6 0.5 %collective-permute-done.5.refs_0_ = bf16[4,40,384]{2,1,0:T(8,128)(2,1)S(1)} collective-permute-done((bf16[4,40,384]{2,1,0:T(8,128)(2,1)S(1)}, bf16[4,40,384]{2,1,0:T(8,128)(2,1)S(1)}, u32[]{:S(2)}, u32[]{:S(2)}) %collective-permute-start.5) | collective-permute-done | bytes 122912 | tf_op jit(solution)/shard_map/ppermute | solution.py:332
  29.1 0.0 collective-permute-done.6.refs_1_
  29.1 0.8 %place.3 = bf16[20,32,384]{2,1,0:T(8,128)(2,1)} custom-call(bf16[4,40,384]{2,1,0:T(8,128)(2,1)S(1)} %collective-permute-done.5.refs_0_, bf16[4,40,384]{2,1,0:T(8,128)(2,1)S(1)} %collective-permute-done.6.refs_1_, bf16[20,32,384]{2,1,0:T(8,128)(2,1)} %place.2.refs_2_), custom_call_target="tpu_custom_call", output_to_operand_aliasing={{}: (2, {})} | custom-call | tf_op jit(solution)/shard_map/place/pallas_call | solution.py:360
  (1 shorter events, 0.0 us)
Async XLA Ops:
  0.0 4.8 %collective-permute-start = (bf16[2,1536,384]{2,1,0:T(8,128)(2,1)}, bf16[2,1536,384]{2,1,0:T(8,128)(2,1)S(1)}, u32[]{:S(2)}, u32[]{:S(2)}) collective-permute-start(bf16[2,1536,384]{2,1,0:T(8,128)(2,1)} %sky.1), channel_id=1, source_target_pairs={{0,1},{1,0},{2,3},{3,2},{4,5},{5,4},{6,7},{7,6},{8,9},{9,8},{10,11... | collective-permute-start | bytes 7077896 | tf_op jit(solution)/shard_map/ppermute | solution.py:277
  7.6 11.5 %collective-permute-start.1 = (bf16[4,40,384]{2,1,0:T(8,128)(2,1)S(1)}, bf16[4,40,384]{2,1,0:T(8,128)(2,1)S(1)}, u32[]{:S(2)}, u32[]{:S(2)}) collective-permute-start(bf16[4,40,384]{2,1,0:T(8,128)(2,1)S(1)} %get-tuple-element.23), channel_id=1, source_target_pairs={{0,8},{2,10},{4,12},{6,14},{8,0},{10,2},{12,4},{14,6},{16,24},{18,... | collective-permute-start | bytes 368648 | tf_op jit(solution)/shard_map/ppermute | solution.py:332
  11.0 4.6 %collective-permute-start.2 = (bf16[2,40,384]{2,1,0:T(8,128)(2,1)S(1)}, bf16[2,40,384]{2,1,0:T(8,128)(2,1)S(1)}, u32[]{:S(2)}, u32[]{:S(2)}) collective-permute-start(bf16[2,40,384]{2,1,0:T(8,128)(2,1)S(1)} %get-tuple-element.25), channel_id=1, source_target_pairs={{0,2},{2,0},{4,6},{6,4},{8,10},{10,8},{12,14},{14,12},{16,18},{18,... | collective-permute-start | bytes 184328 | tf_op jit(solution)/shard_map/ppermute | solution.py:332
  12.1 4.7 %collective-permute-start.3 = (bf16[2,40,384]{2,1,0:T(8,128)(2,1)S(1)}, bf16[2,40,384]{2,1,0:T(8,128)(2,1)S(1)}, u32[]{:S(2)}, u32[]{:S(2)}) collective-permute-start(bf16[2,40,384]{2,1,0:T(8,128)(2,1)S(1)} %get-tuple-element.26), channel_id=1, source_target_pairs={{0,4},{2,6},{4,0},{6,2},{8,12},{10,14},{12,8},{14,10},{16,20},{18,... | collective-permute-start | bytes 184328 | tf_op jit(solution)/shard_map/ppermute | solution.py:332
  14.0 5.1 %collective-permute-start.4 = (bf16[2,40,384]{2,1,0:T(8,128)(2,1)S(1)}, bf16[2,40,384]{2,1,0:T(8,128)(2,1)S(1)}, u32[]{:S(2)}, u32[]{:S(2)}) collective-permute-start(bf16[2,40,384]{2,1,0:T(8,128)(2,1)S(1)} %get-tuple-element.27), channel_id=1, source_target_pairs={{0,6},{2,4},{4,2},{6,0},{8,14},{10,12},{12,10},{14,8},{16,22},{18,... | collective-permute-start | bytes 184328 | tf_op jit(solution)/shard_map/ppermute | solution.py:332
  19.1 9.9 %collective-permute-start.5 = (bf16[4,40,384]{2,1,0:T(8,128)(2,1)S(1)}, bf16[4,40,384]{2,1,0:T(8,128)(2,1)S(1)}, u32[]{:S(2)}, u32[]{:S(2)}) collective-permute-start(bf16[4,40,384]{2,1,0:T(8,128)(2,1)S(1)} %get-tuple-element.28), channel_id=1, source_target_pairs={{0,16},{2,18},{4,20},{6,22},{8,24},{10,26},{12,28},{14,30},{16,0},... | collective-permute-start | bytes 368648 | tf_op jit(solution)/shard_map/ppermute | solution.py:332
  21.5 7.6 %collective-permute-start.6 = (bf16[4,40,384]{2,1,0:T(8,128)(2,1)S(1)}, bf16[4,40,384]{2,1,0:T(8,128)(2,1)S(1)}, u32[]{:S(2)}, u32[]{:S(2)}) collective-permute-start(bf16[4,40,384]{2,1,0:T(8,128)(2,1)S(1)} %get-tuple-element.29), channel_id=1, source_target_pairs={{0,24},{2,26},{4,28},{6,30},{8,16},{10,18},{12,20},{14,22},{16,8},... | collective-permute-start | bytes 368648 | tf_op jit(solution)/shard_map/ppermute | solution.py:332
  22.0 4.2 %collective-permute-start.7 = (bf16[2,40,384]{2,1,0:T(8,128)(2,1)S(1)}, bf16[2,40,384]{2,1,0:T(8,128)(2,1)S(1)}, u32[]{:S(2)}, u32[]{:S(2)}) collective-permute-start(bf16[2,40,384]{2,1,0:T(8,128)(2,1)S(1)} %get-tuple-element.30), channel_id=1, source_target_pairs={{0,2},{2,0},{4,6},{6,4},{8,10},{10,8},{12,14},{14,12},{16,18},{18,... | collective-permute-start | bytes 184328 | tf_op jit(solution)/shard_map/ppermute | solution.py:332
  22.2 4.2 %collective-permute-start.8 = (bf16[2,40,384]{2,1,0:T(8,128)(2,1)S(1)}, bf16[2,40,384]{2,1,0:T(8,128)(2,1)S(1)}, u32[]{:S(2)}, u32[]{:S(2)}) collective-permute-start(bf16[2,40,384]{2,1,0:T(8,128)(2,1)S(1)} %get-tuple-element.31), channel_id=1, source_target_pairs={{0,4},{2,6},{4,0},{6,2},{8,12},{10,14},{12,8},{14,10},{16,20},{18,... | collective-permute-start | bytes 184328 | tf_op jit(solution)/shard_map/ppermute | solution.py:332
  22.7 5.1 %collective-permute-start.9 = (bf16[2,40,384]{2,1,0:T(8,128)(2,1)S(1)}, bf16[2,40,384]{2,1,0:T(8,128)(2,1)S(1)}, u32[]{:S(2)}, u32[]{:S(2)}) collective-permute-start(bf16[2,40,384]{2,1,0:T(8,128)(2,1)S(1)} %get-tuple-element.32), channel_id=1, source_target_pairs={{0,6},{2,4},{4,2},{6,0},{8,14},{10,12},{12,10},{14,8},{16,22},{18,... | collective-permute-start | bytes 184328 | tf_op jit(solution)/shard_map/ppermute | solution.py:332

commit v9 on v5

--- a/solution.py
+++ b/solution.py
@@ -9,6 +9,7 @@
 
 KB = 40
 LANES = 128
+INNER = 4
 VMEM_LIMIT = 24 * 1024 * 1024
 
 
@@ -175,13 +176,24 @@
         where_needed(0, slot, drop)
 
 
-def second_kernel(ways, tile, info, _, factors, *refs):
-    pieces, (out, acc, turned) = refs[: ways - 1], refs[ways - 1 :]
+def crossed(core, outer):
+    return (core % 2) * (outer == INNER)
+
+
+def distance_of(first, second, outer):
+    straight = second * INNER + first
+    return jnp.where(crossed(lax.axis_index("beamk"), outer) == 1, first * INNER + second, straight)
+
+
+def second_kernel(ways, outer, tile, info, _, factors, *refs):
+    pieces, refs = refs[: ways - 1], refs[ways - 1 :]
+    outs, (acc, turned) = refs[:INNER], refs[INNER:]
     slots, rows, columns = acc.shape
     rows = rows // 2
     piece_rows = pieces[0].shape[1]
     tiles = piece_rows // tile
-    cycles, width, _ = out.shape
+    width = outs[0].shape[1]
+    cycles = outer * INNER
     k_local = width // slots
     pitch = turned.shape[1] // cycles
 
@@ -207,12 +219,51 @@
             for lane in range(columns // LANES):
                 turned[lane, pl.ds(slot * k_local + k, cycles, stride=pitch), :] = total[:, lane * LANES : (lane + 1) * LANES]
 
-    for cycle in range(cycles):
-        for lane in range(columns // LANES):
-            out[cycle, :, lane * LANES : (lane + 1) * LANES] = turned[lane, cycle * pitch : cycle * pitch + width].astype(out.dtype)
-
-
-def local(sky, beam, wigner, m_list, *, ways):
+    me = lax.axis_index("blk")
+    for first in range(INNER):
+        for second in range(outer):
+            start = (me ^ distance_of(first, second, outer)) * pitch
+            for lane in range(columns // LANES):
+                block = turned[lane, pl.ds(start, width), :].astype(jnp.bfloat16)
+                outs[first][second, :, lane * LANES : (lane + 1) * LANES] = block
+
+
+def regroup_kernel(outer, *refs):
+    for second in range(outer):
+        for first in range(INNER):
+            refs[INNER + second][first] = refs[first][second]
+
+
+def place_kernel(outer, *refs):
+    out, turned, staged, sem = refs[outer:]
+    k_local, slot_count, columns = staged.shape
+    width = refs[0].shape[1]
+    slots = width // k_local
+    pitch = turned.shape[1] // k_local
+    me = lax.axis_index("blk")
+    for lane in range(columns // LANES):
+        span = slice(lane * LANES, (lane + 1) * LANES)
+        for second in range(outer):
+            for first in range(INNER):
+                block = refs[second][first, :, span].astype(jnp.float32)
+                source = me ^ distance_of(first, second, outer)
+                for slot in range(slots):
+                    turned[lane, pl.ds(slots * source + slot, k_local, stride=pitch), :] = block[slot * k_local : (slot + 1) * k_local]
+    copies = []
+    step = -(-k_local // 4)
+    for number, start in enumerate(range(0, k_local, step)):
+        end = min(start + step, k_local)
+        for k in range(start, end):
+            for lane in range(columns // LANES):
+                values = turned[lane, k * pitch : k * pitch + slot_count]
+                staged[k, :, lane * LANES : (lane + 1) * LANES] = values.astype(staged.dtype)
+        copies.append(pltpu.make_async_copy(staged.at[start:end], out.at[start:end], sem.at[number]))
+        copies[-1].start()
+    for copy in copies:
+        copy.wait()
+
+
+def local(sky, beam, wigner, m_list, *, ways, peers):
     slots, piece_rows, columns = sky.shape
     _, k_local, cycles, degrees = wigner.shape
     rows = k_local * cycles
@@ -256,12 +307,17 @@
         name="own_half",
     )(m_list, sky, wigner, beam)
 
-    blocks, _ = pl.pallas_call(
-        functools.partial(second_kernel, ways, tile),
-        out_shape=(pltpu.VMEM((cycles, width, columns), jnp.bfloat16), pltpu.VMEM(part.shape, part.dtype)),
+    outer = peers // INNER
+
+    def blocks(number):
+        return pltpu.VMEM((number, width, columns), jnp.bfloat16)
+
+    *sends, _ = pl.pallas_call(
+        functools.partial(second_kernel, ways, outer, tile),
+        out_shape=[blocks(outer)] * INNER + [pltpu.VMEM(part.shape, part.dtype)],
         in_specs=[whole(pltpu.VMEM)] * (ways + 2),
-        out_specs=(whole(pltpu.VMEM),) * 2,
-        input_output_aliases={1: 1},
+        out_specs=[whole(pltpu.VMEM)] * (INNER + 1),
+        input_output_aliases={1: INNER},
         scratch_shapes=[
             pltpu.VMEM((lane_tiles, cycles * (width + 1 - width % 2), LANES), jnp.float32),
         ],
@@ -271,8 +327,45 @@
         ),
         name="other_half",
     )(info, part, factors, *pieces)
-    received = lax.all_to_all(blocks, "blk", split_axis=0, concat_axis=0, tiled=True)
-    return received.reshape(1, -1, k_local, columns)
+
+    def send(array, number, step):
+        perm = []
+        for b in range(peers):
+            for core in range(ways):
+                over_outer = (step == 0) == bool(crossed(core, outer))
+                perm.append((b * ways + core, (b ^ (number * INNER if over_outer else number)) * ways + core))
+        return pltpu.with_memory_space_constraint(lax.ppermute(array, ("blk", "beamk"), perm), pltpu.VMEM)
+
+    first = list(sends)
+    for number in reversed(range(1, INNER)):
+        first[number] = send(first[number], number, 0)
+    second = list(
+        pl.pallas_call(
+            functools.partial(regroup_kernel, outer),
+            out_shape=[blocks(INNER)] * outer,
+            in_specs=[whole(pltpu.VMEM)] * INNER,
+            out_specs=[whole(pltpu.VMEM)] * outer,
+            compiler_params=params,
+            name="regroup",
+        )(*first)
+    )
+    for number in reversed(range(1, outer)):
+        second[number] = send(second[number], number, 1)
+    slot_count = slots * peers
+    out = pl.pallas_call(
+        functools.partial(place_kernel, outer),
+        out_shape=pltpu.HBM((k_local, slot_count, columns), jnp.bfloat16),
+        in_specs=[whole(pltpu.VMEM)] * outer,
+        out_specs=whole(pltpu.HBM),
+        scratch_shapes=[
+            pltpu.VMEM((lane_tiles, k_local * (slot_count + 1), LANES), jnp.float32),
+            pltpu.VMEM((k_local, slot_count, columns), jnp.bfloat16),
+            pltpu.SemaphoreType.DMA((4,)),
+        ],
+        compiler_params=params,
+        name="place",
+    )(*second)
+    return out.transpose(1, 0, 2)[None]
 
 
 def solution(mesh):
@@ -283,5 +376,5 @@
         P("blk"),
     )
     out_specs = P("blk", None, "beamk", None)
-    body = functools.partial(local, ways=mesh.shape["beamk"])
+    body = functools.partial(local, ways=mesh.shape["beamk"], peers=mesh.shape["blk"])
     return jax.shard_map(body, mesh=mesh, in_specs=in_specs, out_specs=out_specs, check_vma=False)

time: 30.6 us -> 29.6 us (0.967)
  blocking collectives: 21.4 us -> 0 us
  waiting for transfers between devices: 1.29 us -> 12.9 us
  starting transfers between devices: 0.45 us -> 9.37 us
  Pallas kernels: 6.19 us -> 7.17 us
  local copies, waits for them, and re-layouts: 0.94 us -> 0 us
    all_to_all x1 -> x0, blocking collectives: 21.4 us -> none  [local(): lax.all_to_all(blocks, 'blk', split_axis=0, concat_axis=0, tiled=True)]
    ppermute x0 -> x6, waiting for transfers between devices: none -> 11.6 us  [send(): lax.ppermute(array, ('blk', 'beamk'), perm)]
    ppermute x0 -> x6, starting transfers between devices: none -> 8.92 us  [send(): lax.ppermute(array, ('blk', 'beamk'), perm)]
    pallas_call x1 -> x3, Pallas kernels: 3.12 us -> 4.1 us  [the longest x1 3.13 us: local(): pl.pallas_call(functools.partial(second_kernel, ways, outer, tile), out_s...]
    reshape x2 -> x0, local copies, waits for them, and re-layouts: 0.94 us -> none  [local(): return received.reshape(1, -1, k_local, columns)]
  transfers between devices with their start and end apart: 1 -> 7, of which waited for: 1 -> 7; matrix products, arithmetic and copies ran while one was open for 0% -> 0% of each run, Pallas kernels for 10% -> 10%
where the time goes in v9:
time: 29.6 us; the launch traced here: 29.5 us
  waiting for transfers between devices  12.9 us (44%)
  starting transfers between devices  9.37 us (32%)
  Pallas kernels  7.17 us (24%)
    ppermute x6, waiting for transfers between devices, send(): lax.ppermute(array, ('blk', 'beamk'), perm)  11.6 us
    ppermute x6, starting transfers between devices, send(): lax.ppermute(array, ('blk', 'beamk'), perm)  8.92 us
    pallas_call x1, Pallas kernels, local(): pl.pallas_call(functools.partial(second_kernel, ways, outer, tile), out_s...  3.13 us
    pallas_call x1, Pallas kernels, local(): pl.pallas_call(functools.partial(first_kernel, ways, tile), out_shape=(pl...  3.07 us
    ppermute x1, waiting for transfers between devices, local(): lax.ppermute(sky, 'beamk', perm)  1.29 us
    pallas_call x1, Pallas kernels, local(): pl.pallas_call(functools.partial(place_kernel, outer), out_shape=pltpu.HB...  0.93 us
  transfers between devices with their start and end apart: 7, of which 7 were waited for; matrix products, arithmetic and copies ran while one was open for 0% of the time, Pallas kernels for 10%

profile of v9, /device:TPU:0, one launch (start us, length us, event | category | flops | bytes accessed | tf_op | source)
XLA Modules:
  0.0 29.5 jit_solution(9615211367560630030)
XLA Ops:
  0.0 0.5 %collective-permute-start = (bf16[2,1536,384]{2,1,0:T(8,128)(2,1)}, bf16[2,1536,384]{2,1,0:T(8,128)(2,1)S(1)}, u32[]{:S(2)}, u32[]{:S(2)}) collective-permute-start(bf16[2,1536,384]{2,1,0:T(8,128)(2,1)} %sky.1), channel_id=1, source_target_pairs={{0,1},{1,0},{2,3},{3,2},{4,5},{5,4},{6,7},{7,6},{8,9},{9,8},{10,11... | collective-permute-start | bytes 7077896 | tf_op jit(solution)/shard_map/ppermute | solution.py:279
  0.5 3.1 %own_half.1 = (f32[2,640,384]{2,1,0:T(8,128)S(1)}, bf16[1,2,640,1536]{3,2,1,0:T(8,128)(2,1)S(1)}, f32[8,128]{1,0:T(8,128)S(1)}) custom-call(s32[2]{0:T(128)} %m_list.1, bf16[2,1536,384]{2,1,0:T(8,128)(2,1)} %sky.1, bf16[2,20,16,3072]{3,2,1,0:T(8,128)(2,1)} %wigner.1, f32[20,2,3072]{2,1,0:T(2,128)} %beam.1), custom_call_target="tpu_custom_call" | custom-call | flops 1509949440 | bytes 8388608 | tf_op jit(solution)/shard_map/own_half/pallas_call | solution.py:282
  3.5 1.3 %collective-permute-done.refs_0_ = bf16[2,1536,384]{2,1,0:T(8,128)(2,1)S(1)} collective-permute-done((bf16[2,1536,384]{2,1,0:T(8,128)(2,1)}, bf16[2,1536,384]{2,1,0:T(8,128)(2,1)S(1)}, u32[]{:S(2)}, u32[]{:S(2)}) %collective-permute-start) | collective-permute-done | bytes 2359328 | tf_op jit(solution)/shard_map/ppermute | solution.py:279
  4.8 3.1 %other_half.1 = (bf16[4,40,384]{2,1,0:T(8,128)(2,1)S(1)}, bf16[4,40,384]{2,1,0:T(8,128)(2,1)S(1)}, bf16[4,40,384]{2,1,0:T(8,128)(2,1)S(1)}, bf16[4,40,384]{2,1,0:T(8,128)(2,1)S(1)}, f32[2,640,384]{2,1,0:T(8,128)S(1)}) custom-call(f32[8,128]{1,0:T(8,128)S(1)} %get-tuple-element.16.info, ...), custom_call_target="tpu_custom_call", output_to_operand_aliasing={{4}: (1, {})} | custom-call | flops 1509949440 | bytes 8388608 | tf_op jit(solution)/shard_map/other_half/pallas_call | solution.py:315
  8.0 2.9 %collective-permute-start.1 = (bf16[4,40,384]{2,1,0:T(8,128)(2,1)S(1)}, bf16[4,40,384]{2,1,0:T(8,128)(2,1)S(1)}, u32[]{:S(2)}, u32[]{:S(2)}) collective-permute-start(bf16[4,40,384]{2,1,0:T(8,128)(2,1)S(1)} %get-tuple-element.20), channel_id=1, source_target_pairs={{0,2},{1,9},{2,0},{3,11},{4,6},{5,13},{6,4},{7,15},{8,10},{9,1},{1... | collective-permute-start | bytes 368648 | tf_op jit(solution)/shard_map/ppermute | solution.py:337
  10.9 1.2 %collective-permute-start.2 = (bf16[4,40,384]{2,1,0:T(8,128)(2,1)S(1)}, bf16[4,40,384]{2,1,0:T(8,128)(2,1)S(1)}, u32[]{:S(2)}, u32[]{:S(2)}) collective-permute-start(bf16[4,40,384]{2,1,0:T(8,128)(2,1)S(1)} %get-tuple-element.21), channel_id=1, source_target_pairs={{0,4},{1,17},{2,6},{3,19},{4,0},{5,21},{6,2},{7,23},{8,12},{9,25},... | collective-permute-start | bytes 368648 | tf_op jit(solution)/shard_map/ppermute | solution.py:337
  12.1 0.4 %collective-permute-start.3 = (bf16[4,40,384]{2,1,0:T(8,128)(2,1)S(1)}, bf16[4,40,384]{2,1,0:T(8,128)(2,1)S(1)}, u32[]{:S(2)}, u32[]{:S(2)}) collective-permute-start(bf16[4,40,384]{2,1,0:T(8,128)(2,1)S(1)} %get-tuple-element.22), channel_id=1, source_target_pairs={{0,6},{1,25},{2,4},{3,27},{4,2},{5,29},{6,0},{7,31},{8,14},{9,17},... | collective-permute-start | bytes 368648 | tf_op jit(solution)/shard_map/ppermute | solution.py:337
  12.4 1.3 %collective-permute-done.1.refs_1_ = bf16[4,40,384]{2,1,0:T(8,128)(2,1)S(1)} collective-permute-done((bf16[4,40,384]{2,1,0:T(8,128)(2,1)S(1)}, bf16[4,40,384]{2,1,0:T(8,128)(2,1)S(1)}, u32[]{:S(2)}, u32[]{:S(2)}) %collective-permute-start.1) | collective-permute-done | bytes 122912 | tf_op jit(solution)/shard_map/ppermute | solution.py:337
  13.7 2.0 %collective-permute-done.2.refs_2_ = bf16[4,40,384]{2,1,0:T(8,128)(2,1)S(1)} collective-permute-done((bf16[4,40,384]{2,1,0:T(8,128)(2,1)S(1)}, bf16[4,40,384]{2,1,0:T(8,128)(2,1)S(1)}, u32[]{:S(2)}, u32[]{:S(2)}) %collective-permute-start.2) | collective-permute-done | bytes 122912 | tf_op jit(solution)/shard_map/ppermute | solution.py:337
  15.8 2.1 %collective-permute-done.3.refs_3_ = bf16[4,40,384]{2,1,0:T(8,128)(2,1)S(1)} collective-permute-done((bf16[4,40,384]{2,1,0:T(8,128)(2,1)S(1)}, bf16[4,40,384]{2,1,0:T(8,128)(2,1)S(1)}, u32[]{:S(2)}, u32[]{:S(2)}) %collective-permute-start.3) | collective-permute-done | bytes 122912 | tf_op jit(solution)/shard_map/ppermute | solution.py:337
  17.9 1.6 %collective-permute-start.4 = (bf16[4,40,384]{2,1,0:T(8,128)(2,1)S(1)}, bf16[4,40,384]{2,1,0:T(8,128)(2,1)S(1)}, u32[]{:S(2)}, u32[]{:S(2)}) collective-permute-start(bf16[4,40,384]{2,1,0:T(8,128)(2,1)S(1)} %get-tuple-element.24), channel_id=1, source_target_pairs={{0,8},{1,3},{2,10},{3,1},{4,12},{5,7},{6,14},{7,5},{8,0},{9,11},{1... | collective-permute-start | bytes 368648 | tf_op jit(solution)/shard_map/ppermute | solution.py:337
  19.5 2.2 %collective-permute-start.5 = (bf16[4,40,384]{2,1,0:T(8,128)(2,1)S(1)}, bf16[4,40,384]{2,1,0:T(8,128)(2,1)S(1)}, u32[]{:S(2)}, u32[]{:S(2)}) collective-permute-start(bf16[4,40,384]{2,1,0:T(8,128)(2,1)S(1)} %get-tuple-element.25), channel_id=1, source_target_pairs={{0,16},{1,5},{2,18},{3,7},{4,20},{5,1},{6,22},{7,3},{8,24},{9,13},... | collective-permute-start | bytes 368648 | tf_op jit(solution)/shard_map/ppermute | solution.py:337
  21.8 0.6 %collective-permute-start.6 = (bf16[4,40,384]{2,1,0:T(8,128)(2,1)S(1)}, bf16[4,40,384]{2,1,0:T(8,128)(2,1)S(1)}, u32[]{:S(2)}, u32[]{:S(2)}) collective-permute-start(bf16[4,40,384]{2,1,0:T(8,128)(2,1)S(1)} %get-tuple-element.26), channel_id=1, source_target_pairs={{0,24},{1,7},{2,26},{3,5},{4,28},{5,3},{6,30},{7,1},{8,16},{9,15},... | collective-permute-start | bytes 368648 | tf_op jit(solution)/shard_map/ppermute | solution.py:337
  22.3 0.5 %collective-permute-done.4.refs_1_ = bf16[4,40,384]{2,1,0:T(8,128)(2,1)S(1)} collective-permute-done((bf16[4,40,384]{2,1,0:T(8,128)(2,1)S(1)}, bf16[4,40,384]{2,1,0:T(8,128)(2,1)S(1)}, u32[]{:S(2)}, u32[]{:S(2)}) %collective-permute-start.4) | collective-permute-done | bytes 122912 | tf_op jit(solution)/shard_map/ppermute | solution.py:337
  22.8 3.8 %collective-permute-done.5.refs_2_ = bf16[4,40,384]{2,1,0:T(8,128)(2,1)S(1)} collective-permute-done((bf16[4,40,384]{2,1,0:T(8,128)(2,1)S(1)}, bf16[4,40,384]{2,1,0:T(8,128)(2,1)S(1)}, u32[]{:S(2)}, u32[]{:S(2)}) %collective-permute-start.5) | collective-permute-done | bytes 122912 | tf_op jit(solution)/shard_map/ppermute | solution.py:337
  26.6 1.9 %collective-permute-done.6.refs_3_ = bf16[4,40,384]{2,1,0:T(8,128)(2,1)S(1)} collective-permute-done((bf16[4,40,384]{2,1,0:T(8,128)(2,1)S(1)}, bf16[4,40,384]{2,1,0:T(8,128)(2,1)S(1)}, u32[]{:S(2)}, u32[]{:S(2)}) %collective-permute-start.6) | collective-permute-done | bytes 122912 | tf_op jit(solution)/shard_map/ppermute | solution.py:337
  28.6 0.9 %place.1 = bf16[20,32,384]{2,1,0:T(8,128)(2,1)} custom-call(bf16[4,40,384]{2,1,0:T(8,128)(2,1)S(1)} %get-tuple-element.23.refs_0_, bf16[4,40,384]{2,1,0:T(8,128)(2,1)S(1)} %collective-permute-done.4.refs_1_, bf16[4,40,384]{2,1,0:T(8,128)(2,1)S(1)} %collective-permute-done.5.refs_2_, bf16[4,40,384]{2,1,0:T(8,128)(2,1)S(1)} %collective-permute-done.6.refs_3_), custom_call_target="tpu_custom_call" | custom-call | tf_op jit(solution)/shard_map/place/pallas_call | solution.py:355
  (1 shorter events, 0.0 us)
Async XLA Ops:
  0.0 4.8 %collective-permute-start = (bf16[2,1536,384]{2,1,0:T(8,128)(2,1)}, bf16[2,1536,384]{2,1,0:T(8,128)(2,1)S(1)}, u32[]{:S(2)}, u32[]{:S(2)}) collective-permute-start(bf16[2,1536,384]{2,1,0:T(8,128)(2,1)} %sky.1), channel_id=1, source_target_pairs={{0,1},{1,0},{2,3},{3,2},{4,5},{5,4},{6,7},{7,6},{8,9},{9,8},{10,11... | collective-permute-start | bytes 7077896 | tf_op jit(solution)/shard_map/ppermute | solution.py:279
  8.0 5.8 %collective-permute-start.1 = (bf16[4,40,384]{2,1,0:T(8,128)(2,1)S(1)}, bf16[4,40,384]{2,1,0:T(8,128)(2,1)S(1)}, u32[]{:S(2)}, u32[]{:S(2)}) collective-permute-start(bf16[4,40,384]{2,1,0:T(8,128)(2,1)S(1)} %get-tuple-element.20), channel_id=1, source_target_pairs={{0,2},{1,9},{2,0},{3,11},{4,6},{5,13},{6,4},{7,15},{8,10},{9,1},{1... | collective-permute-start | bytes 368648 | tf_op jit(solution)/shard_map/ppermute | solution.py:337
  10.9 4.9 %collective-permute-start.2 = (bf16[4,40,384]{2,1,0:T(8,128)(2,1)S(1)}, bf16[4,40,384]{2,1,0:T(8,128)(2,1)S(1)}, u32[]{:S(2)}, u32[]{:S(2)}) collective-permute-start(bf16[4,40,384]{2,1,0:T(8,128)(2,1)S(1)} %get-tuple-element.21), channel_id=1, source_target_pairs={{0,4},{1,17},{2,6},{3,19},{4,0},{5,21},{6,2},{7,23},{8,12},{9,25},... | collective-permute-start | bytes 368648 | tf_op jit(solution)/shard_map/ppermute | solution.py:337
  12.1 5.8 %collective-permute-start.3 = (bf16[4,40,384]{2,1,0:T(8,128)(2,1)S(1)}, bf16[4,40,384]{2,1,0:T(8,128)(2,1)S(1)}, u32[]{:S(2)}, u32[]{:S(2)}) collective-permute-start(bf16[4,40,384]{2,1,0:T(8,128)(2,1)S(1)} %get-tuple-element.22), channel_id=1, source_target_pairs={{0,6},{1,25},{2,4},{3,27},{4,2},{5,29},{6,0},{7,31},{8,14},{9,17},... | collective-permute-start | bytes 368648 | tf_op jit(solution)/shard_map/ppermute | solution.py:337
  17.9 4.9 %collective-permute-start.4 = (bf16[4,40,384]{2,1,0:T(8,128)(2,1)S(1)}, bf16[4,40,384]{2,1,0:T(8,128)(2,1)S(1)}, u32[]{:S(2)}, u32[]{:S(2)}) collective-permute-start(bf16[4,40,384]{2,1,0:T(8,128)(2,1)S(1)} %get-tuple-element.24), channel_id=1, source_target_pairs={{0,8},{1,3},{2,10},{3,1},{4,12},{5,7},{6,14},{7,5},{8,0},{9,11},{1... | collective-permute-start | bytes 368648 | tf_op jit(solution)/shard_map/ppermute | solution.py:337
  19.5 7.1 %collective-permute-start.5 = (bf16[4,40,384]{2,1,0:T(8,128)(2,1)S(1)}, bf16[4,40,384]{2,1,0:T(8,128)(2,1)S(1)}, u32[]{:S(2)}, u32[]{:S(2)}) collective-permute-start(bf16[4,40,384]{2,1,0:T(8,128)(2,1)S(1)} %get-tuple-element.25), channel_id=1, source_target_pairs={{0,16},{1,5},{2,18},{3,7},{4,20},{5,1},{6,22},{7,3},{8,24},{9,13},... | collective-permute-start | bytes 368648 | tf_op jit(solution)/shard_map/ppermute | solution.py:337
  21.8 6.8 %collective-permute-start.6 = (bf16[4,40,384]{2,1,0:T(8,128)(2,1)S(1)}, bf16[4,40,384]{2,1,0:T(8,128)(2,1)S(1)}, u32[]{:S(2)}, u32[]{:S(2)}) collective-permute-start(bf16[4,40,384]{2,1,0:T(8,128)(2,1)S(1)} %get-tuple-element.26), channel_id=1, source_target_pairs={{0,24},{1,7},{2,26},{3,5},{4,28},{5,3},{6,30},{7,1},{8,16},{9,15},... | collective-permute-start | bytes 368648 | tf_op jit(solution)/shard_map/ppermute | solution.py:337

commit v10 on v9

--- a/solution.py
+++ b/solution.py
@@ -228,16 +228,21 @@
                 outs[first][second, :, lane * LANES : (lane + 1) * LANES] = block
 
 
+def far_first(arrays):
+    return [arrays[0], *reversed(arrays[1:])]
+
+
 def regroup_kernel(outer, *refs):
+    arrived, onward = far_first(refs[:INNER]), refs[INNER:]
     for second in range(outer):
         for first in range(INNER):
-            refs[INNER + second][first] = refs[first][second]
+            onward[second][first] = arrived[first][second]
 
 
 def place_kernel(outer, *refs):
-    out, turned, staged, sem = refs[outer:]
+    arrived, (out, turned, staged, sem) = far_first(refs[:outer]), refs[outer:]
     k_local, slot_count, columns = staged.shape
-    width = refs[0].shape[1]
+    width = arrived[0].shape[1]
     slots = width // k_local
     pitch = turned.shape[1] // k_local
     me = lax.axis_index("blk")
@@ -245,7 +250,7 @@
         span = slice(lane * LANES, (lane + 1) * LANES)
         for second in range(outer):
             for first in range(INNER):
-                block = refs[second][first, :, span].astype(jnp.float32)
+                block = arrived[second][first, :, span].astype(jnp.float32)
                 source = me ^ distance_of(first, second, outer)
                 for slot in range(slots):
                     turned[lane, pl.ds(slots * source + slot, k_local, stride=pitch), :] = block[slot * k_local : (slot + 1) * k_local]
@@ -337,7 +342,7 @@
         return pltpu.with_memory_space_constraint(lax.ppermute(array, ("blk", "beamk"), perm), pltpu.VMEM)
 
     first = list(sends)
-    for number in reversed(range(1, INNER)):
+    for number in range(1, INNER):
         first[number] = send(first[number], number, 0)
     second = list(
         pl.pallas_call(
@@ -347,9 +352,9 @@
             out_specs=[whole(pltpu.VMEM)] * outer,
             compiler_params=params,
             name="regroup",
-        )(*first)
+        )(*far_first(first))
     )
-    for number in reversed(range(1, outer)):
+    for number in range(1, outer):
         second[number] = send(second[number], number, 1)
     slot_count = slots * peers
     out = pl.pallas_call(
@@ -364,7 +369,7 @@
         ],
         compiler_params=params,
         name="place",
-    )(*second)
+    )(*far_first(second))
     return out.transpose(1, 0, 2)[None]
 
 

time: 29.6 us -> 28.1 us (0.949)
  waiting for transfers between devices: 12.9 us -> 11.3 us
    ppermute x6, waiting for transfers between devices: 11.6 us -> 9.96 us  [send(): lax.ppermute(array, ('blk', 'beamk'), perm)]
  transfers between devices with their start and end apart: 7 -> 7, of which waited for: 7 -> 6; matrix products, arithmetic and copies ran while one was open for 0% -> 0% of each run, Pallas kernels for 10% -> 11%
where the time goes in v10:
time: 28.1 us; the launch traced here: 27.8 us
  waiting for transfers between devices  11.3 us (40%)
  starting transfers between devices  9.33 us (33%)
  Pallas kernels  7.17 us (26%)
    ppermute x6, waiting for transfers between devices, send(): lax.ppermute(array, ('blk', 'beamk'), perm)  9.96 us
    ppermute x6, starting transfers between devices, send(): lax.ppermute(array, ('blk', 'beamk'), perm)  8.87 us
    pallas_call x1, Pallas kernels, local(): pl.pallas_call(functools.partial(second_kernel, ways, outer, tile), out_s...  3.13 us
    pallas_call x1, Pallas kernels, local(): pl.pallas_call(functools.partial(first_kernel, ways, tile), out_shape=(pl...  3.07 us
    ppermute x1, waiting for transfers between devices, local(): lax.ppermute(sky, 'beamk', perm)  1.29 us
    pallas_call x1, Pallas kernels, local(): pl.pallas_call(functools.partial(place_kernel, outer), out_shape=pltpu.HB...  0.93 us
  transfers between devices with their start and end apart: 7, of which 6 were waited for; matrix products, arithmetic and copies ran while one was open for 0% of the time, Pallas kernels for 11%

profile of v10, /device:TPU:0, one launch (start us, length us, event | category | flops | bytes accessed | tf_op | source)
XLA Modules:
  0.0 27.8 jit_solution(12745271896305005290)
XLA Ops:
  0.0 0.5 %collective-permute-start = (bf16[2,1536,384]{2,1,0:T(8,128)(2,1)}, bf16[2,1536,384]{2,1,0:T(8,128)(2,1)S(1)}, u32[]{:S(2)}, u32[]{:S(2)}) collective-permute-start(bf16[2,1536,384]{2,1,0:T(8,128)(2,1)} %sky.1), channel_id=1, source_target_pairs={{0,1},{1,0},{2,3},{3,2},{4,5},{5,4},{6,7},{7,6},{8,9},{9,8},{10,11... | collective-permute-start | bytes 7077896 | tf_op jit(solution)/shard_map/ppermute | solution.py:284
  0.5 3.1 %own_half.1 = (f32[2,640,384]{2,1,0:T(8,128)S(1)}, bf16[1,2,640,1536]{3,2,1,0:T(8,128)(2,1)S(1)}, f32[8,128]{1,0:T(8,128)S(1)}) custom-call(s32[2]{0:T(128)} %m_list.1, bf16[2,1536,384]{2,1,0:T(8,128)(2,1)} %sky.1, bf16[2,20,16,3072]{3,2,1,0:T(8,128)(2,1)} %wigner.1, f32[20,2,3072]{2,1,0:T(2,128)} %beam.1), custom_call_target="tpu_custom_call" | custom-call | flops 1509949440 | bytes 8388608 | tf_op jit(solution)/shard_map/own_half/pallas_call | solution.py:287
  3.5 1.3 %collective-permute-done.refs_0_ = bf16[2,1536,384]{2,1,0:T(8,128)(2,1)S(1)} collective-permute-done((bf16[2,1536,384]{2,1,0:T(8,128)(2,1)}, bf16[2,1536,384]{2,1,0:T(8,128)(2,1)S(1)}, u32[]{:S(2)}, u32[]{:S(2)}) %collective-permute-start) | collective-permute-done | bytes 2359328 | tf_op jit(solution)/shard_map/ppermute | solution.py:284
  4.8 3.1 %other_half.1 = (bf16[4,40,384]{2,1,0:T(8,128)(2,1)S(1)}, bf16[4,40,384]{2,1,0:T(8,128)(2,1)S(1)}, bf16[4,40,384]{2,1,0:T(8,128)(2,1)S(1)}, bf16[4,40,384]{2,1,0:T(8,128)(2,1)S(1)}, f32[2,640,384]{2,1,0:T(8,128)S(1)}) custom-call(f32[8,128]{1,0:T(8,128)S(1)} %get-tuple-element.16.info, ...), custom_call_target="tpu_custom_call", output_to_operand_aliasing={{4}: (1, {})} | custom-call | flops 1509949440 | bytes 8388608 | tf_op jit(solution)/shard_map/other_half/pallas_call | solution.py:320
  8.0 3.5 %collective-permute-start.1 = (bf16[4,40,384]{2,1,0:T(8,128)(2,1)S(1)}, bf16[4,40,384]{2,1,0:T(8,128)(2,1)S(1)}, u32[]{:S(2)}, u32[]{:S(2)}) collective-permute-start(bf16[4,40,384]{2,1,0:T(8,128)(2,1)S(1)} %get-tuple-element.20), channel_id=1, source_target_pairs={{0,6},{1,25},{2,4},{3,27},{4,2},{5,29},{6,0},{7,31},{8,14},{9,17},... | collective-permute-start | bytes 368648 | tf_op jit(solution)/shard_map/ppermute | solution.py:342
  11.5 0.8 %collective-permute-start.2 = (bf16[4,40,384]{2,1,0:T(8,128)(2,1)S(1)}, bf16[4,40,384]{2,1,0:T(8,128)(2,1)S(1)}, u32[]{:S(2)}, u32[]{:S(2)}) collective-permute-start(bf16[4,40,384]{2,1,0:T(8,128)(2,1)S(1)} %get-tuple-element.21), channel_id=1, source_target_pairs={{0,4},{1,17},{2,6},{3,19},{4,0},{5,21},{6,2},{7,23},{8,12},{9,25},... | collective-permute-start | bytes 368648 | tf_op jit(solution)/shard_map/ppermute | solution.py:342
  12.3 0.0 collective-permute-start.3
  12.4 2.0 %collective-permute-done.1.refs_1_ = bf16[4,40,384]{2,1,0:T(8,128)(2,1)S(1)} collective-permute-done((bf16[4,40,384]{2,1,0:T(8,128)(2,1)S(1)}, bf16[4,40,384]{2,1,0:T(8,128)(2,1)S(1)}, u32[]{:S(2)}, u32[]{:S(2)}) %collective-permute-start.1) | collective-permute-done | bytes 122912 | tf_op jit(solution)/shard_map/ppermute | solution.py:342
  14.4 2.0 %collective-permute-done.2.refs_2_ = bf16[4,40,384]{2,1,0:T(8,128)(2,1)S(1)} collective-permute-done((bf16[4,40,384]{2,1,0:T(8,128)(2,1)S(1)}, bf16[4,40,384]{2,1,0:T(8,128)(2,1)S(1)}, u32[]{:S(2)}, u32[]{:S(2)}) %collective-permute-start.2) | collective-permute-done | bytes 122912 | tf_op jit(solution)/shard_map/ppermute | solution.py:342
  16.4 0.8 %collective-permute-done.3.refs_3_ = bf16[4,40,384]{2,1,0:T(8,128)(2,1)S(1)} collective-permute-done((bf16[4,40,384]{2,1,0:T(8,128)(2,1)S(1)}, bf16[4,40,384]{2,1,0:T(8,128)(2,1)S(1)}, u32[]{:S(2)}, u32[]{:S(2)}) %collective-permute-start.3) | collective-permute-done | bytes 122912 | tf_op jit(solution)/shard_map/ppermute | solution.py:342
  17.3 3.0 %collective-permute-start.4 = (bf16[4,40,384]{2,1,0:T(8,128)(2,1)S(1)}, bf16[4,40,384]{2,1,0:T(8,128)(2,1)S(1)}, u32[]{:S(2)}, u32[]{:S(2)}) collective-permute-start(bf16[4,40,384]{2,1,0:T(8,128)(2,1)S(1)} %get-tuple-element.24), channel_id=1, source_target_pairs={{0,24},{1,7},{2,26},{3,5},{4,28},{5,3},{6,30},{7,1},{8,16},{9,15},... | collective-permute-start | bytes 368648 | tf_op jit(solution)/shard_map/ppermute | solution.py:342
  20.3 0.0 collective-permute-start.5
  20.3 1.5 %collective-permute-start.6 = (bf16[4,40,384]{2,1,0:T(8,128)(2,1)S(1)}, bf16[4,40,384]{2,1,0:T(8,128)(2,1)S(1)}, u32[]{:S(2)}, u32[]{:S(2)}) collective-permute-start(bf16[4,40,384]{2,1,0:T(8,128)(2,1)S(1)} %get-tuple-element.26), channel_id=1, source_target_pairs={{0,8},{1,3},{2,10},{3,1},{4,12},{5,7},{6,14},{7,5},{8,0},{9,11},{1... | collective-permute-start | bytes 368648 | tf_op jit(solution)/shard_map/ppermute | solution.py:342
  21.7 2.4 %collective-permute-done.4.refs_1_ = bf16[4,40,384]{2,1,0:T(8,128)(2,1)S(1)} collective-permute-done((bf16[4,40,384]{2,1,0:T(8,128)(2,1)S(1)}, bf16[4,40,384]{2,1,0:T(8,128)(2,1)S(1)}, u32[]{:S(2)}, u32[]{:S(2)}) %collective-permute-start.4) | collective-permute-done | bytes 122912 | tf_op jit(solution)/shard_map/ppermute | solution.py:342
  24.2 2.7 %collective-permute-done.5.refs_2_ = bf16[4,40,384]{2,1,0:T(8,128)(2,1)S(1)} collective-permute-done((bf16[4,40,384]{2,1,0:T(8,128)(2,1)S(1)}, bf16[4,40,384]{2,1,0:T(8,128)(2,1)S(1)}, u32[]{:S(2)}, u32[]{:S(2)}) %collective-permute-start.5) | collective-permute-done | bytes 122912 | tf_op jit(solution)/shard_map/ppermute | solution.py:342
  26.8 0.0 collective-permute-done.6.refs_3_
  26.8 0.9 %place.1 = bf16[20,32,384]{2,1,0:T(8,128)(2,1)} custom-call(bf16[4,40,384]{2,1,0:T(8,128)(2,1)S(1)} %get-tuple-element.23.refs_0_, bf16[4,40,384]{2,1,0:T(8,128)(2,1)S(1)} %collective-permute-done.4.refs_1_, bf16[4,40,384]{2,1,0:T(8,128)(2,1)S(1)} %collective-permute-done.5.refs_2_, bf16[4,40,384]{2,1,0:T(8,128)(2,1)S(1)} %collective-permute-done.6.refs_3_), custom_call_target="tpu_custom_call" | custom-call | tf_op jit(solution)/shard_map/place/pallas_call | solution.py:360
  (1 shorter events, 0.0 us)
Async XLA Ops:
  0.0 4.8 %collective-permute-start = (bf16[2,1536,384]{2,1,0:T(8,128)(2,1)}, bf16[2,1536,384]{2,1,0:T(8,128)(2,1)S(1)}, u32[]{:S(2)}, u32[]{:S(2)}) collective-permute-start(bf16[2,1536,384]{2,1,0:T(8,128)(2,1)} %sky.1), channel_id=1, source_target_pairs={{0,1},{1,0},{2,3},{3,2},{4,5},{5,4},{6,7},{7,6},{8,9},{9,8},{10,11... | collective-permute-start | bytes 7077896 | tf_op jit(solution)/shard_map/ppermute | solution.py:284
  8.0 6.4 %collective-permute-start.1 = (bf16[4,40,384]{2,1,0:T(8,128)(2,1)S(1)}, bf16[4,40,384]{2,1,0:T(8,128)(2,1)S(1)}, u32[]{:S(2)}, u32[]{:S(2)}) collective-permute-start(bf16[4,40,384]{2,1,0:T(8,128)(2,1)S(1)} %get-tuple-element.20), channel_id=1, source_target_pairs={{0,6},{1,25},{2,4},{3,27},{4,2},{5,29},{6,0},{7,31},{8,14},{9,17},... | collective-permute-start | bytes 368648 | tf_op jit(solution)/shard_map/ppermute | solution.py:342
  11.5 4.9 %collective-permute-start.2 = (bf16[4,40,384]{2,1,0:T(8,128)(2,1)S(1)}, bf16[4,40,384]{2,1,0:T(8,128)(2,1)S(1)}, u32[]{:S(2)}, u32[]{:S(2)}) collective-permute-start(bf16[4,40,384]{2,1,0:T(8,128)(2,1)S(1)} %get-tuple-element.21), channel_id=1, source_target_pairs={{0,4},{1,17},{2,6},{3,19},{4,0},{5,21},{6,2},{7,23},{8,12},{9,25},... | collective-permute-start | bytes 368648 | tf_op jit(solution)/shard_map/ppermute | solution.py:342
  12.3 4.9 %collective-permute-start.3 = (bf16[4,40,384]{2,1,0:T(8,128)(2,1)S(1)}, bf16[4,40,384]{2,1,0:T(8,128)(2,1)S(1)}, u32[]{:S(2)}, u32[]{:S(2)}) collective-permute-start(bf16[4,40,384]{2,1,0:T(8,128)(2,1)S(1)} %get-tuple-element.22), channel_id=1, source_target_pairs={{0,2},{1,9},{2,0},{3,11},{4,6},{5,13},{6,4},{7,15},{8,10},{9,1},{1... | collective-permute-start | bytes 368648 | tf_op jit(solution)/shard_map/ppermute | solution.py:342
  17.3 6.9 %collective-permute-start.4 = (bf16[4,40,384]{2,1,0:T(8,128)(2,1)S(1)}, bf16[4,40,384]{2,1,0:T(8,128)(2,1)S(1)}, u32[]{:S(2)}, u32[]{:S(2)}) collective-permute-start(bf16[4,40,384]{2,1,0:T(8,128)(2,1)S(1)} %get-tuple-element.24), channel_id=1, source_target_pairs={{0,24},{1,7},{2,26},{3,5},{4,28},{5,3},{6,30},{7,1},{8,16},{9,15},... | collective-permute-start | bytes 368648 | tf_op jit(solution)/shard_map/ppermute | solution.py:342
  20.3 6.6 %collective-permute-start.5 = (bf16[4,40,384]{2,1,0:T(8,128)(2,1)S(1)}, bf16[4,40,384]{2,1,0:T(8,128)(2,1)S(1)}, u32[]{:S(2)}, u32[]{:S(2)}) collective-permute-start(bf16[4,40,384]{2,1,0:T(8,128)(2,1)S(1)} %get-tuple-element.25), channel_id=1, source_target_pairs={{0,16},{1,5},{2,18},{3,7},{4,20},{5,1},{6,22},{7,3},{8,24},{9,13},... | collective-permute-start | bytes 368648 | tf_op jit(solution)/shard_map/ppermute | solution.py:342
  20.3 6.6 %collective-permute-start.6 = (bf16[4,40,384]{2,1,0:T(8,128)(2,1)S(1)}, bf16[4,40,384]{2,1,0:T(8,128)(2,1)S(1)}, u32[]{:S(2)}, u32[]{:S(2)}) collective-permute-start(bf16[4,40,384]{2,1,0:T(8,128)(2,1)S(1)} %get-tuple-element.26), channel_id=1, source_target_pairs={{0,8},{1,3},{2,10},{3,1},{4,12},{5,7},{6,14},{7,5},{8,0},{9,11},{1... | collective-permute-start | bytes 368648 | tf_op jit(solution)/shard_map/ppermute | solution.py:342

commit v11 on v10

--- a/solution.py
+++ b/solution.py
@@ -177,7 +177,7 @@
 
 
 def crossed(core, outer):
-    return (core % 2) * (outer == INNER)
+    return (1 - core % 2) * (outer == INNER)
 
 
 def distance_of(first, second, outer):

time: 28.1 us -> 31.5 us (1.12)
  starting transfers between devices: 9.33 us -> 12.6 us
    ppermute x6, starting transfers between devices: 8.87 us -> 12.2 us  [send(): lax.ppermute(array, ('blk', 'beamk'), perm)]
  transfers between devices with their start and end apart: 7 -> 7, of which waited for: 6 -> 5; matrix products, arithmetic and copies ran while one was open for 0% -> 0% of each run, Pallas kernels for 11% -> 10%
where the time goes in v11:
time: 31.5 us; the launch traced here: 31.1 us
  starting transfers between devices  12.6 us (40%)
  waiting for transfers between devices  11.3 us (36%)
  Pallas kernels  7.17 us (23%)
    ppermute x6, starting transfers between devices, send(): lax.ppermute(array, ('blk', 'beamk'), perm)  12.2 us
    ppermute x6, waiting for transfers between devices, send(): lax.ppermute(array, ('blk', 'beamk'), perm)  10 us
    pallas_call x1, Pallas kernels, local(): pl.pallas_call(functools.partial(second_kernel, ways, outer, tile), out_s...  3.13 us
    pallas_call x1, Pallas kernels, local(): pl.pallas_call(functools.partial(first_kernel, ways, tile), out_shape=(pl...  3.07 us
    ppermute x1, waiting for transfers between devices, local(): lax.ppermute(sky, 'beamk', perm)  1.29 us
    pallas_call x1, Pallas kernels, local(): pl.pallas_call(functools.partial(place_kernel, outer), out_shape=pltpu.HB...  0.93 us
  transfers between devices with their start and end apart: 7, of which 5 were waited for; matrix products, arithmetic and copies ran while one was open for 0% of the time, Pallas kernels for 10%

profile of v11, /device:TPU:0, one launch (start us, length us, event | category | flops | bytes accessed | tf_op | source)
XLA Modules:
  0.0 31.1 jit_solution(1350721737701290431)
XLA Ops:
  0.0 0.5 %collective-permute-start = (bf16[2,1536,384]{2,1,0:T(8,128)(2,1)}, bf16[2,1536,384]{2,1,0:T(8,128)(2,1)S(1)}, u32[]{:S(2)}, u32[]{:S(2)}) collective-permute-start(bf16[2,1536,384]{2,1,0:T(8,128)(2,1)} %sky.1), channel_id=1, source_target_pairs={{0,1},{1,0},{2,3},{3,2},{4,5},{5,4},{6,7},{7,6},{8,9},{9,8},{10,11... | collective-permute-start | bytes 7077896 | tf_op jit(solution)/shard_map/ppermute | solution.py:284
  0.5 3.1 %own_half.1 = (f32[2,640,384]{2,1,0:T(8,128)S(1)}, bf16[1,2,640,1536]{3,2,1,0:T(8,128)(2,1)S(1)}, f32[8,128]{1,0:T(8,128)S(1)}) custom-call(s32[2]{0:T(128)} %m_list.1, bf16[2,1536,384]{2,1,0:T(8,128)(2,1)} %sky.1, bf16[2,20,16,3072]{3,2,1,0:T(8,128)(2,1)} %wigner.1, f32[20,2,3072]{2,1,0:T(2,128)} %beam.1), custom_call_target="tpu_custom_call" | custom-call | flops 1509949440 | bytes 8388608 | tf_op jit(solution)/shard_map/own_half/pallas_call | solution.py:287
  3.5 1.3 %collective-permute-done.refs_0_ = bf16[2,1536,384]{2,1,0:T(8,128)(2,1)S(1)} collective-permute-done((bf16[2,1536,384]{2,1,0:T(8,128)(2,1)}, bf16[2,1536,384]{2,1,0:T(8,128)(2,1)S(1)}, u32[]{:S(2)}, u32[]{:S(2)}) %collective-permute-start) | collective-permute-done | bytes 2359328 | tf_op jit(solution)/shard_map/ppermute | solution.py:284
  4.8 3.1 %other_half.1 = (bf16[4,40,384]{2,1,0:T(8,128)(2,1)S(1)}, bf16[4,40,384]{2,1,0:T(8,128)(2,1)S(1)}, bf16[4,40,384]{2,1,0:T(8,128)(2,1)S(1)}, bf16[4,40,384]{2,1,0:T(8,128)(2,1)S(1)}, f32[2,640,384]{2,1,0:T(8,128)S(1)}) custom-call(f32[8,128]{1,0:T(8,128)S(1)} %get-tuple-element.16.info, ...), custom_call_target="tpu_custom_call", output_to_operand_aliasing={{4}: (1, {})} | custom-call | flops 1509949440 | bytes 8388608 | tf_op jit(solution)/shard_map/other_half/pallas_call | solution.py:320
  8.0 5.0 %collective-permute-start.1 = (bf16[4,40,384]{2,1,0:T(8,128)(2,1)S(1)}, bf16[4,40,384]{2,1,0:T(8,128)(2,1)S(1)}, u32[]{:S(2)}, u32[]{:S(2)}) collective-permute-start(bf16[4,40,384]{2,1,0:T(8,128)(2,1)S(1)} %get-tuple-element.20), channel_id=1, source_target_pairs={{0,24},{1,7},{2,26},{3,5},{4,28},{5,3},{6,30},{7,1},{8,16},{9,15},... | collective-permute-start | bytes 368648 | tf_op jit(solution)/shard_map/ppermute | solution.py:342
  13.0 0.0 collective-permute-start.2
  13.0 0.6 %collective-permute-start.3 = (bf16[4,40,384]{2,1,0:T(8,128)(2,1)S(1)}, bf16[4,40,384]{2,1,0:T(8,128)(2,1)S(1)}, u32[]{:S(2)}, u32[]{:S(2)}) collective-permute-start(bf16[4,40,384]{2,1,0:T(8,128)(2,1)S(1)} %get-tuple-element.22), channel_id=1, source_target_pairs={{0,8},{1,3},{2,10},{3,1},{4,12},{5,7},{6,14},{7,5},{8,0},{9,11},{1... | collective-permute-start | bytes 368648 | tf_op jit(solution)/shard_map/ppermute | solution.py:342
  13.6 2.3 %collective-permute-done.1.refs_1_ = bf16[4,40,384]{2,1,0:T(8,128)(2,1)S(1)} collective-permute-done((bf16[4,40,384]{2,1,0:T(8,128)(2,1)S(1)}, bf16[4,40,384]{2,1,0:T(8,128)(2,1)S(1)}, u32[]{:S(2)}, u32[]{:S(2)}) %collective-permute-start.1) | collective-permute-done | bytes 122912 | tf_op jit(solution)/shard_map/ppermute | solution.py:342
  15.9 3.5 %collective-permute-done.2.refs_2_ = bf16[4,40,384]{2,1,0:T(8,128)(2,1)S(1)} collective-permute-done((bf16[4,40,384]{2,1,0:T(8,128)(2,1)S(1)}, bf16[4,40,384]{2,1,0:T(8,128)(2,1)S(1)}, u32[]{:S(2)}, u32[]{:S(2)}) %collective-permute-start.2) | collective-permute-done | bytes 122912 | tf_op jit(solution)/shard_map/ppermute | solution.py:342
  19.4 0.0 collective-permute-done.3.refs_3_
  19.5 5.9 %collective-permute-start.4 = (bf16[4,40,384]{2,1,0:T(8,128)(2,1)S(1)}, bf16[4,40,384]{2,1,0:T(8,128)(2,1)S(1)}, u32[]{:S(2)}, u32[]{:S(2)}) collective-permute-start(bf16[4,40,384]{2,1,0:T(8,128)(2,1)S(1)} %get-tuple-element.24), channel_id=1, source_target_pairs={{0,6},{1,25},{2,4},{3,27},{4,2},{5,29},{6,0},{7,31},{8,14},{9,17},... | collective-permute-start | bytes 368648 | tf_op jit(solution)/shard_map/ppermute | solution.py:342
  25.3 0.0 collective-permute-start.5
  25.3 0.6 %collective-permute-start.6 = (bf16[4,40,384]{2,1,0:T(8,128)(2,1)S(1)}, bf16[4,40,384]{2,1,0:T(8,128)(2,1)S(1)}, u32[]{:S(2)}, u32[]{:S(2)}) collective-permute-start(bf16[4,40,384]{2,1,0:T(8,128)(2,1)S(1)} %get-tuple-element.26), channel_id=1, source_target_pairs={{0,2},{1,9},{2,0},{3,11},{4,6},{5,13},{6,4},{7,15},{8,10},{9,1},{1... | collective-permute-start | bytes 368648 | tf_op jit(solution)/shard_map/ppermute | solution.py:342
  26.0 2.2 %collective-permute-done.4.refs_1_ = bf16[4,40,384]{2,1,0:T(8,128)(2,1)S(1)} collective-permute-done((bf16[4,40,384]{2,1,0:T(8,128)(2,1)S(1)}, bf16[4,40,384]{2,1,0:T(8,128)(2,1)S(1)}, u32[]{:S(2)}, u32[]{:S(2)}) %collective-permute-start.4) | collective-permute-done | bytes 122912 | tf_op jit(solution)/shard_map/ppermute | solution.py:342
  28.2 2.0 %collective-permute-done.5.refs_2_ = bf16[4,40,384]{2,1,0:T(8,128)(2,1)S(1)} collective-permute-done((bf16[4,40,384]{2,1,0:T(8,128)(2,1)S(1)}, bf16[4,40,384]{2,1,0:T(8,128)(2,1)S(1)}, u32[]{:S(2)}, u32[]{:S(2)}) %collective-permute-start.5) | collective-permute-done | bytes 122912 | tf_op jit(solution)/shard_map/ppermute | solution.py:342
  30.2 0.0 collective-permute-done.6.refs_3_
  30.2 0.9 %place.1 = bf16[20,32,384]{2,1,0:T(8,128)(2,1)} custom-call(bf16[4,40,384]{2,1,0:T(8,128)(2,1)S(1)} %get-tuple-element.23.refs_0_, bf16[4,40,384]{2,1,0:T(8,128)(2,1)S(1)} %collective-permute-done.4.refs_1_, bf16[4,40,384]{2,1,0:T(8,128)(2,1)S(1)} %collective-permute-done.5.refs_2_, bf16[4,40,384]{2,1,0:T(8,128)(2,1)S(1)} %collective-permute-done.6.refs_3_), custom_call_target="tpu_custom_call" | custom-call | tf_op jit(solution)/shard_map/place/pallas_call | solution.py:360
  (1 shorter events, 0.0 us)
Async XLA Ops:
  0.0 4.8 %collective-permute-start = (bf16[2,1536,384]{2,1,0:T(8,128)(2,1)}, bf16[2,1536,384]{2,1,0:T(8,128)(2,1)S(1)}, u32[]{:S(2)}, u32[]{:S(2)}) collective-permute-start(bf16[2,1536,384]{2,1,0:T(8,128)(2,1)} %sky.1), channel_id=1, source_target_pairs={{0,1},{1,0},{2,3},{3,2},{4,5},{5,4},{6,7},{7,6},{8,9},{9,8},{10,11... | collective-permute-start | bytes 7077896 | tf_op jit(solution)/shard_map/ppermute | solution.py:284
  8.0 8.0 %collective-permute-start.1 = (bf16[4,40,384]{2,1,0:T(8,128)(2,1)S(1)}, bf16[4,40,384]{2,1,0:T(8,128)(2,1)S(1)}, u32[]{:S(2)}, u32[]{:S(2)}) collective-permute-start(bf16[4,40,384]{2,1,0:T(8,128)(2,1)S(1)} %get-tuple-element.20), channel_id=1, source_target_pairs={{0,24},{1,7},{2,26},{3,5},{4,28},{5,3},{6,30},{7,1},{8,16},{9,15},... | collective-permute-start | bytes 368648 | tf_op jit(solution)/shard_map/ppermute | solution.py:342
  13.0 6.4 %collective-permute-start.2 = (bf16[4,40,384]{2,1,0:T(8,128)(2,1)S(1)}, bf16[4,40,384]{2,1,0:T(8,128)(2,1)S(1)}, u32[]{:S(2)}, u32[]{:S(2)}) collective-permute-start(bf16[4,40,384]{2,1,0:T(8,128)(2,1)S(1)} %get-tuple-element.21), channel_id=1, source_target_pairs={{0,16},{1,5},{2,18},{3,7},{4,20},{5,1},{6,22},{7,3},{8,24},{9,13},... | collective-permute-start | bytes 368648 | tf_op jit(solution)/shard_map/ppermute | solution.py:342
  13.0 6.4 %collective-permute-start.3 = (bf16[4,40,384]{2,1,0:T(8,128)(2,1)S(1)}, bf16[4,40,384]{2,1,0:T(8,128)(2,1)S(1)}, u32[]{:S(2)}, u32[]{:S(2)}) collective-permute-start(bf16[4,40,384]{2,1,0:T(8,128)(2,1)S(1)} %get-tuple-element.22), channel_id=1, source_target_pairs={{0,8},{1,3},{2,10},{3,1},{4,12},{5,7},{6,14},{7,5},{8,0},{9,11},{1... | collective-permute-start | bytes 368648 | tf_op jit(solution)/shard_map/ppermute | solution.py:342
  19.5 8.7 %collective-permute-start.4 = (bf16[4,40,384]{2,1,0:T(8,128)(2,1)S(1)}, bf16[4,40,384]{2,1,0:T(8,128)(2,1)S(1)}, u32[]{:S(2)}, u32[]{:S(2)}) collective-permute-start(bf16[4,40,384]{2,1,0:T(8,128)(2,1)S(1)} %get-tuple-element.24), channel_id=1, source_target_pairs={{0,6},{1,25},{2,4},{3,27},{4,2},{5,29},{6,0},{7,31},{8,14},{9,17},... | collective-permute-start | bytes 368648 | tf_op jit(solution)/shard_map/ppermute | solution.py:342
  25.3 4.9 %collective-permute-start.5 = (bf16[4,40,384]{2,1,0:T(8,128)(2,1)S(1)}, bf16[4,40,384]{2,1,0:T(8,128)(2,1)S(1)}, u32[]{:S(2)}, u32[]{:S(2)}) collective-permute-start(bf16[4,40,384]{2,1,0:T(8,128)(2,1)S(1)} %get-tuple-element.25), channel_id=1, source_target_pairs={{0,4},{1,17},{2,6},{3,19},{4,0},{5,21},{6,2},{7,23},{8,12},{9,25},... | collective-permute-start | bytes 368648 | tf_op jit(solution)/shard_map/ppermute | solution.py:342
  25.3 4.9 %collective-permute-start.6 = (bf16[4,40,384]{2,1,0:T(8,128)(2,1)S(1)}, bf16[4,40,384]{2,1,0:T(8,128)(2,1)S(1)}, u32[]{:S(2)}, u32[]{:S(2)}) collective-permute-start(bf16[4,40,384]{2,1,0:T(8,128)(2,1)S(1)} %get-tuple-element.26), channel_id=1, source_target_pairs={{0,2},{1,9},{2,0},{3,11},{4,6},{5,13},{6,4},{7,15},{8,10},{9,1},{1... | collective-permute-start | bytes 368648 | tf_op jit(solution)/shard_map/ppermute | solution.py:342

commit v12 on v10

--- a/solution.py
+++ b/solution.py
@@ -8,6 +8,7 @@
 from jax.sharding import PartitionSpec as P
 
 KB = 40
+SLOTS = 2
 LANES = 128
 INNER = 4
 VMEM_LIMIT = 24 * 1024 * 1024
@@ -180,9 +181,21 @@
     return (core % 2) * (outer == INNER)
 
 
+def outer_distance(number, outer):
+    half = outer // 2
+    return [0, *range(half, outer), *range(1, half)][number]
+
+
+def inner_distance(number):
+    return [0, *reversed(range(1, INNER))][number]
+
+
 def distance_of(first, second, outer):
-    straight = second * INNER + first
-    return jnp.where(crossed(lax.axis_index("beamk"), outer) == 1, first * INNER + second, straight)
+    straight = outer_distance(second, outer) * INNER + inner_distance(first)
+    if outer != INNER:
+        return straight
+    other = outer_distance(first, outer) * INNER + inner_distance(second)
+    return jnp.where(crossed(lax.axis_index("beamk"), outer) == 1, other, straight)
 
 
 def second_kernel(ways, outer, tile, info, _, factors, *refs):
@@ -228,32 +241,36 @@
                 outs[first][second, :, lane * LANES : (lane + 1) * LANES] = block
 
 
-def far_first(arrays):
-    return [arrays[0], *reversed(arrays[1:])]
-
-
 def regroup_kernel(outer, *refs):
-    arrived, onward = far_first(refs[:INNER]), refs[INNER:]
+    arrived, onward = refs[:INNER], refs[INNER:]
     for second in range(outer):
         for first in range(INNER):
             onward[second][first] = arrived[first][second]
 
 
-def place_kernel(outer, *refs):
-    arrived, (out, turned, staged, sem) = far_first(refs[:outer]), refs[outer:]
-    k_local, slot_count, columns = staged.shape
+def place_kernel(outer, numbers, *refs):
+    arrived, refs = refs[: len(numbers)], refs[len(numbers) :]
     width = arrived[0].shape[1]
-    slots = width // k_local
+    final = numbers[-1] == outer - 1
+    if final:
+        _, out, turned, staged, sem = refs
+        k_local, slot_count, columns = staged.shape
+    else:
+        (turned,) = refs
+        slot_count = SLOTS * outer * INNER
+        k_local, columns = width // SLOTS, turned.shape[0] * LANES
     pitch = turned.shape[1] // k_local
     me = lax.axis_index("blk")
     for lane in range(columns // LANES):
         span = slice(lane * LANES, (lane + 1) * LANES)
-        for second in range(outer):
+        for array, second in zip(arrived, numbers):
             for first in range(INNER):
-                block = arrived[second][first, :, span].astype(jnp.float32)
+                block = array[first, :, span].astype(jnp.float32)
                 source = me ^ distance_of(first, second, outer)
-                for slot in range(slots):
-                    turned[lane, pl.ds(slots * source + slot, k_local, stride=pitch), :] = block[slot * k_local : (slot + 1) * k_local]
+                for slot in range(SLOTS):
+                    turned[lane, pl.ds(SLOTS * source + slot, k_local, stride=pitch), :] = block[slot * k_local : (slot + 1) * k_local]
+    if not final:
+        return
     copies = []
     step = -(-k_local // 4)
     for number, start in enumerate(range(0, k_local, step)):
@@ -338,7 +355,8 @@
         for b in range(peers):
             for core in range(ways):
                 over_outer = (step == 0) == bool(crossed(core, outer))
-                perm.append((b * ways + core, (b ^ (number * INNER if over_outer else number)) * ways + core))
+                distance = outer_distance(number, outer) * INNER if over_outer else inner_distance(number)
+                perm.append((b * ways + core, (b ^ distance) * ways + core))
         return pltpu.with_memory_space_constraint(lax.ppermute(array, ("blk", "beamk"), perm), pltpu.VMEM)
 
     first = list(sends)
@@ -352,24 +370,35 @@
             out_specs=[whole(pltpu.VMEM)] * outer,
             compiler_params=params,
             name="regroup",
-        )(*far_first(first))
+        )(*first)
     )
     for number in range(1, outer):
         second[number] = send(second[number], number, 1)
     slot_count = slots * peers
-    out = pl.pallas_call(
-        functools.partial(place_kernel, outer),
-        out_shape=pltpu.HBM((k_local, slot_count, columns), jnp.bfloat16),
-        in_specs=[whole(pltpu.VMEM)] * outer,
-        out_specs=whole(pltpu.HBM),
+    placed = pltpu.VMEM((lane_tiles, k_local * (slot_count + 1), LANES), jnp.float32)
+    result = pltpu.HBM((k_local, slot_count, columns), jnp.bfloat16)
+    early = outer // 2
+    turned = pl.pallas_call(
+        functools.partial(place_kernel, outer, range(early)),
+        out_shape=placed,
+        in_specs=[whole(pltpu.VMEM)] * early,
+        out_specs=whole(pltpu.VMEM),
+        compiler_params=params,
+        name="place_early",
+    )(*second[:early])
+    out, _ = pl.pallas_call(
+        functools.partial(place_kernel, outer, range(early, outer)),
+        out_shape=(result, placed),
+        in_specs=[whole(pltpu.VMEM)] * (outer - early + 1),
+        out_specs=(whole(pltpu.HBM), whole(pltpu.VMEM)),
+        input_output_aliases={outer - early: 1},
         scratch_shapes=[
-            pltpu.VMEM((lane_tiles, k_local * (slot_count + 1), LANES), jnp.float32),
             pltpu.VMEM((k_local, slot_count, columns), jnp.bfloat16),
             pltpu.SemaphoreType.DMA((4,)),
         ],
         compiler_params=params,
-        name="place",
-    )(*far_first(second))
+        name="place_late",
+    )(*second[early:], turned)
     return out.transpose(1, 0, 2)[None]
 
 

time: 28.1 us -> 28.3 us (level); the launches traced: 27.8 us -> 28.4 us
  waiting for transfers between devices: 11.3 us -> 12.3 us
  Pallas kernels: 7.17 us -> 6.84 us
    ppermute x6, waiting for transfers between devices: 9.96 us -> 11 us  [send(): lax.ppermute(array, ('blk', 'beamk'), perm)]
    pallas_call x1, Pallas kernels: 3.13 us -> 2.79 us  [local(): pl.pallas_call(functools.partial(second_kernel, ways, outer, tile), out_s...]
    pallas_call x1 -> x2, Pallas kernels: 0.93 us -> 0.94 us  [the longest x1 0.88 us: local(): pl.pallas_call(functools.partial(place_kernel, outer, range(early, outer)...]
  transfers between devices with their start and end apart: 7 -> 7, of which waited for: 6 -> 7; matrix products, arithmetic and copies ran while one was open for 0% -> 0% of each run, Pallas kernels for 11% -> 11%
where the time goes in v12:
time: 28.3 us; the launch traced here: 28.4 us
  waiting for transfers between devices  12.3 us (43%)
  starting transfers between devices  9.19 us (32%)
  Pallas kernels  6.84 us (24%)
    ppermute x6, waiting for transfers between devices, send(): lax.ppermute(array, ('blk', 'beamk'), perm)  11 us
    ppermute x6, starting transfers between devices, send(): lax.ppermute(array, ('blk', 'beamk'), perm)  8.74 us
    pallas_call x1, Pallas kernels, local(): pl.pallas_call(functools.partial(first_kernel, ways, tile), out_shape=(pl...  3.07 us
    pallas_call x1, Pallas kernels, local(): pl.pallas_call(functools.partial(second_kernel, ways, outer, tile), out_s...  2.79 us
    ppermute x1, waiting for transfers between devices, local(): lax.ppermute(sky, 'beamk', perm)  1.29 us
    pallas_call x1, Pallas kernels, local(): pl.pallas_call(functools.partial(place_kernel, outer, range(early, outer)...  0.88 us
  transfers between devices with their start and end apart: 7, of which 7 were waited for; matrix products, arithmetic and copies ran while one was open for 0% of the time, Pallas kernels for 11%

profile of v12, /device:TPU:0, one launch (start us, length us, event | category | flops | bytes accessed | tf_op | source)
XLA Modules:
  0.0 28.4 jit_solution(9943247878981065949)
XLA Ops:
  0.0 0.5 %collective-permute-start = (bf16[2,1536,384]{2,1,0:T(8,128)(2,1)}, bf16[2,1536,384]{2,1,0:T(8,128)(2,1)S(1)}, u32[]{:S(2)}, u32[]{:S(2)}) collective-permute-start(bf16[2,1536,384]{2,1,0:T(8,128)(2,1)} %sky.1), channel_id=1, source_target_pairs={{0,1},{1,0},{2,3},{3,2},{4,5},{5,4},{6,7},{7,6},{8,9},{9,8},{10,11... | collective-permute-start | bytes 7077896 | tf_op jit(solution)/shard_map/ppermute | solution.py:301
  0.5 3.1 %own_half.1 = (f32[2,640,384]{2,1,0:T(8,128)S(1)}, bf16[1,2,640,1536]{3,2,1,0:T(8,128)(2,1)S(1)}, f32[8,128]{1,0:T(8,128)S(1)}) custom-call(s32[2]{0:T(128)} %m_list.1, bf16[2,1536,384]{2,1,0:T(8,128)(2,1)} %sky.1, bf16[2,20,16,3072]{3,2,1,0:T(8,128)(2,1)} %wigner.1, f32[20,2,3072]{2,1,0:T(2,128)} %beam.1), custom_call_target="tpu_custom_call" | custom-call | flops 1509949440 | bytes 8388608 | tf_op jit(solution)/shard_map/own_half/pallas_call | solution.py:304
  3.5 1.3 %collective-permute-done.refs_0_ = bf16[2,1536,384]{2,1,0:T(8,128)(2,1)S(1)} collective-permute-done((bf16[2,1536,384]{2,1,0:T(8,128)(2,1)}, bf16[2,1536,384]{2,1,0:T(8,128)(2,1)S(1)}, u32[]{:S(2)}, u32[]{:S(2)}) %collective-permute-start) | collective-permute-done | bytes 2359328 | tf_op jit(solution)/shard_map/ppermute | solution.py:301
  4.8 2.8 %other_half.1 = (bf16[4,40,384]{2,1,0:T(8,128)(2,1)S(1)}, bf16[4,40,384]{2,1,0:T(8,128)(2,1)S(1)}, bf16[4,40,384]{2,1,0:T(8,128)(2,1)S(1)}, bf16[4,40,384]{2,1,0:T(8,128)(2,1)S(1)}, f32[2,640,384]{2,1,0:T(8,128)S(1)}) custom-call(f32[8,128]{1,0:T(8,128)S(1)} %get-tuple-element.17.info, ...), custom_call_target="tpu_custom_call", output_to_operand_aliasing={{4}: (1, {})} | custom-call | flops 1509949440 | bytes 8388608 | tf_op jit(solution)/shard_map/other_half/pallas_call | solution.py:337
  7.6 3.9 %collective-permute-start.1 = (bf16[4,40,384]{2,1,0:T(8,128)(2,1)S(1)}, bf16[4,40,384]{2,1,0:T(8,128)(2,1)S(1)}, u32[]{:S(2)}, u32[]{:S(2)}) collective-permute-start(bf16[4,40,384]{2,1,0:T(8,128)(2,1)S(1)} %get-tuple-element.21), channel_id=1, source_target_pairs={{0,6},{1,17},{2,4},{3,19},{4,2},{5,21},{6,0},{7,23},{8,14},{9,25},... | collective-permute-start | bytes 368648 | tf_op jit(solution)/shard_map/ppermute | solution.py:360
  11.5 0.8 %collective-permute-start.2 = (bf16[4,40,384]{2,1,0:T(8,128)(2,1)S(1)}, bf16[4,40,384]{2,1,0:T(8,128)(2,1)S(1)}, u32[]{:S(2)}, u32[]{:S(2)}) collective-permute-start(bf16[4,40,384]{2,1,0:T(8,128)(2,1)S(1)} %get-tuple-element.22), channel_id=1, source_target_pairs={{0,4},{1,25},{2,6},{3,27},{4,0},{5,29},{6,2},{7,31},{8,12},{9,17},... | collective-permute-start | bytes 368648 | tf_op jit(solution)/shard_map/ppermute | solution.py:360
  12.3 0.0 collective-permute-start.3
  12.4 2.0 %collective-permute-done.1.refs_1_ = bf16[4,40,384]{2,1,0:T(8,128)(2,1)S(1)} collective-permute-done((bf16[4,40,384]{2,1,0:T(8,128)(2,1)S(1)}, bf16[4,40,384]{2,1,0:T(8,128)(2,1)S(1)}, u32[]{:S(2)}, u32[]{:S(2)}) %collective-permute-start.1) | collective-permute-done | bytes 122912 | tf_op jit(solution)/shard_map/ppermute | solution.py:360
  14.4 2.0 %collective-permute-done.2.refs_2_ = bf16[4,40,384]{2,1,0:T(8,128)(2,1)S(1)} collective-permute-done((bf16[4,40,384]{2,1,0:T(8,128)(2,1)S(1)}, bf16[4,40,384]{2,1,0:T(8,128)(2,1)S(1)}, u32[]{:S(2)}, u32[]{:S(2)}) %collective-permute-start.2) | collective-permute-done | bytes 122912 | tf_op jit(solution)/shard_map/ppermute | solution.py:360
  16.4 0.8 %collective-permute-done.3.refs_3_ = bf16[4,40,384]{2,1,0:T(8,128)(2,1)S(1)} collective-permute-done((bf16[4,40,384]{2,1,0:T(8,128)(2,1)S(1)}, bf16[4,40,384]{2,1,0:T(8,128)(2,1)S(1)}, u32[]{:S(2)}, u32[]{:S(2)}) %collective-permute-start.3) | collective-permute-done | bytes 122912 | tf_op jit(solution)/shard_map/ppermute | solution.py:360
  17.3 2.7 %collective-permute-start.6 = (bf16[4,40,384]{2,1,0:T(8,128)(2,1)S(1)}, bf16[4,40,384]{2,1,0:T(8,128)(2,1)S(1)}, u32[]{:S(2)}, u32[]{:S(2)}) collective-permute-start(bf16[4,40,384]{2,1,0:T(8,128)(2,1)S(1)} %get-tuple-element.27), channel_id=1, source_target_pairs={{0,16},{1,7},{2,18},{3,5},{4,20},{5,3},{6,22},{7,1},{8,24},{9,15},... | collective-permute-start | bytes 368648 | tf_op jit(solution)/shard_map/ppermute | solution.py:360
  19.9 1.4 %collective-permute-start.4 = (bf16[4,40,384]{2,1,0:T(8,128)(2,1)S(1)}, bf16[4,40,384]{2,1,0:T(8,128)(2,1)S(1)}, u32[]{:S(2)}, u32[]{:S(2)}) collective-permute-start(bf16[4,40,384]{2,1,0:T(8,128)(2,1)S(1)} %get-tuple-element.24), channel_id=1, source_target_pairs={{0,24},{1,5},{2,26},{3,7},{4,28},{5,1},{6,30},{7,3},{8,16},{9,13},... | collective-permute-start | bytes 368648 | tf_op jit(solution)/shard_map/ppermute | solution.py:360
  21.3 0.0 collective-permute-start.5
  21.3 3.2 %collective-permute-done.6.refs_1_ = bf16[4,40,384]{2,1,0:T(8,128)(2,1)S(1)} collective-permute-done((bf16[4,40,384]{2,1,0:T(8,128)(2,1)S(1)}, bf16[4,40,384]{2,1,0:T(8,128)(2,1)S(1)}, u32[]{:S(2)}, u32[]{:S(2)}) %collective-permute-start.6) | collective-permute-done | bytes 122912 | tf_op jit(solution)/shard_map/ppermute | solution.py:360
  24.4 0.1 place_early.1.refs_2_
  24.5 2.3 %collective-permute-done.4.refs_0_ = bf16[4,40,384]{2,1,0:T(8,128)(2,1)S(1)} collective-permute-done((bf16[4,40,384]{2,1,0:T(8,128)(2,1)S(1)}, bf16[4,40,384]{2,1,0:T(8,128)(2,1)S(1)}, u32[]{:S(2)}, u32[]{:S(2)}) %collective-permute-start.4) | collective-permute-done | bytes 122912 | tf_op jit(solution)/shard_map/ppermute | solution.py:360
  26.8 0.7 %collective-permute-done.5.refs_1_ = bf16[4,40,384]{2,1,0:T(8,128)(2,1)S(1)} collective-permute-done((bf16[4,40,384]{2,1,0:T(8,128)(2,1)S(1)}, bf16[4,40,384]{2,1,0:T(8,128)(2,1)S(1)}, u32[]{:S(2)}, u32[]{:S(2)}) %collective-permute-start.5) | collective-permute-done | bytes 122912 | tf_op jit(solution)/shard_map/ppermute | solution.py:360
  27.5 0.9 %place_late.1 = (bf16[20,32,384]{2,1,0:T(8,128)(2,1)}, f32[3,660,128]{2,1,0:T(8,128)S(1)}) custom-call(bf16[4,40,384]{2,1,0:T(8,128)(2,1)S(1)} %collective-permute-done.4.refs_0_, bf16[4,40,384]{2,1,0:T(8,128)(2,1)S(1)} %collective-permute-done.5.refs_1_, f32[3,660,128]{2,1,0:T(8,128)S(1)} %place_early.1.refs_2_), custom_call_target="tpu_custom_call", output_to_operand_aliasing={{1}: (2, {})} | custom-call | tf_op jit(solution)/shard_map/place_late/pallas_call | solution.py:389
  (1 shorter events, 0.0 us)
Async XLA Ops:
  0.0 4.8 %collective-permute-start = (bf16[2,1536,384]{2,1,0:T(8,128)(2,1)}, bf16[2,1536,384]{2,1,0:T(8,128)(2,1)S(1)}, u32[]{:S(2)}, u32[]{:S(2)}) collective-permute-start(bf16[2,1536,384]{2,1,0:T(8,128)(2,1)} %sky.1), channel_id=1, source_target_pairs={{0,1},{1,0},{2,3},{3,2},{4,5},{5,4},{6,7},{7,6},{8,9},{9,8},{10,11... | collective-permute-start | bytes 7077896 | tf_op jit(solution)/shard_map/ppermute | solution.py:301
  7.6 6.7 %collective-permute-start.1 = (bf16[4,40,384]{2,1,0:T(8,128)(2,1)S(1)}, bf16[4,40,384]{2,1,0:T(8,128)(2,1)S(1)}, u32[]{:S(2)}, u32[]{:S(2)}) collective-permute-start(bf16[4,40,384]{2,1,0:T(8,128)(2,1)S(1)} %get-tuple-element.21), channel_id=1, source_target_pairs={{0,6},{1,17},{2,4},{3,19},{4,2},{5,21},{6,0},{7,23},{8,14},{9,25},... | collective-permute-start | bytes 368648 | tf_op jit(solution)/shard_map/ppermute | solution.py:360
  11.5 4.9 %collective-permute-start.2 = (bf16[4,40,384]{2,1,0:T(8,128)(2,1)S(1)}, bf16[4,40,384]{2,1,0:T(8,128)(2,1)S(1)}, u32[]{:S(2)}, u32[]{:S(2)}) collective-permute-start(bf16[4,40,384]{2,1,0:T(8,128)(2,1)S(1)} %get-tuple-element.22), channel_id=1, source_target_pairs={{0,4},{1,25},{2,6},{3,27},{4,0},{5,29},{6,2},{7,31},{8,12},{9,17},... | collective-permute-start | bytes 368648 | tf_op jit(solution)/shard_map/ppermute | solution.py:360
  12.3 4.9 %collective-permute-start.3 = (bf16[4,40,384]{2,1,0:T(8,128)(2,1)S(1)}, bf16[4,40,384]{2,1,0:T(8,128)(2,1)S(1)}, u32[]{:S(2)}, u32[]{:S(2)}) collective-permute-start(bf16[4,40,384]{2,1,0:T(8,128)(2,1)S(1)} %get-tuple-element.23), channel_id=1, source_target_pairs={{0,2},{1,9},{2,0},{3,11},{4,6},{5,13},{6,4},{7,15},{8,10},{9,1},{1... | collective-permute-start | bytes 368648 | tf_op jit(solution)/shard_map/ppermute | solution.py:360
  17.3 7.2 %collective-permute-start.6 = (bf16[4,40,384]{2,1,0:T(8,128)(2,1)S(1)}, bf16[4,40,384]{2,1,0:T(8,128)(2,1)S(1)}, u32[]{:S(2)}, u32[]{:S(2)}) collective-permute-start(bf16[4,40,384]{2,1,0:T(8,128)(2,1)S(1)} %get-tuple-element.27), channel_id=1, source_target_pairs={{0,16},{1,7},{2,18},{3,5},{4,20},{5,3},{6,22},{7,1},{8,24},{9,15},... | collective-permute-start | bytes 368648 | tf_op jit(solution)/shard_map/ppermute | solution.py:360
  19.9 6.8 %collective-permute-start.4 = (bf16[4,40,384]{2,1,0:T(8,128)(2,1)S(1)}, bf16[4,40,384]{2,1,0:T(8,128)(2,1)S(1)}, u32[]{:S(2)}, u32[]{:S(2)}) collective-permute-start(bf16[4,40,384]{2,1,0:T(8,128)(2,1)S(1)} %get-tuple-element.24), channel_id=1, source_target_pairs={{0,24},{1,5},{2,26},{3,7},{4,28},{5,1},{6,30},{7,3},{8,16},{9,13},... | collective-permute-start | bytes 368648 | tf_op jit(solution)/shard_map/ppermute | solution.py:360
  21.3 6.2 %collective-permute-start.5 = (bf16[4,40,384]{2,1,0:T(8,128)(2,1)S(1)}, bf16[4,40,384]{2,1,0:T(8,128)(2,1)S(1)}, u32[]{:S(2)}, u32[]{:S(2)}) collective-permute-start(bf16[4,40,384]{2,1,0:T(8,128)(2,1)S(1)} %get-tuple-element.25), channel_id=1, source_target_pairs={{0,8},{1,3},{2,10},{3,1},{4,12},{5,7},{6,14},{7,5},{8,0},{9,11},{1... | collective-permute-start | bytes 368648 | tf_op jit(solution)/shard_map/ppermute | solution.py:360

commit v13 on v12

--- a/solution.py
+++ b/solution.py
@@ -200,7 +200,7 @@
 
 def second_kernel(ways, outer, tile, info, _, factors, *refs):
     pieces, refs = refs[: ways - 1], refs[ways - 1 :]
-    outs, (acc, turned) = refs[:INNER], refs[INNER:]
+    outs, direct, (acc, turned) = refs[: INNER - 1], refs[INNER - 1 : outer + INNER - 1], refs[outer + INNER - 1 :]
     slots, rows, columns = acc.shape
     rows = rows // 2
     piece_rows = pieces[0].shape[1]
@@ -238,19 +238,25 @@
             start = (me ^ distance_of(first, second, outer)) * pitch
             for lane in range(columns // LANES):
                 block = turned[lane, pl.ds(start, width), :].astype(jnp.bfloat16)
-                outs[first][second, :, lane * LANES : (lane + 1) * LANES] = block
+                span = slice(lane * LANES, (lane + 1) * LANES)
+                if first:
+                    outs[first - 1][second, :, span] = block
+                else:
+                    direct[second][0, :, span] = block
 
 
 def regroup_kernel(outer, *refs):
-    arrived, onward = refs[:INNER], refs[INNER:]
+    arrived, direct, refs = refs[: INNER - 1], refs[INNER - 1 : INNER - 1 + outer], refs[INNER - 1 + outer :]
+    here, onward = refs[0], refs[1:]
     for second in range(outer):
-        for first in range(INNER):
-            onward[second][first] = arrived[first][second]
+        here[second] = direct[second][0]
+        for first in range(1, INNER):
+            onward[second][first - 1] = arrived[first - 1][second]
 
 
 def place_kernel(outer, numbers, *refs):
-    arrived, refs = refs[: len(numbers)], refs[len(numbers) :]
-    width = arrived[0].shape[1]
+    here, arrived, refs = refs[0], refs[1 : len(numbers) + 1], refs[len(numbers) + 1 :]
+    width = here.shape[1]
     final = numbers[-1] == outer - 1
     if final:
         _, out, turned, staged, sem = refs
@@ -265,7 +271,8 @@
         span = slice(lane * LANES, (lane + 1) * LANES)
         for array, second in zip(arrived, numbers):
             for first in range(INNER):
-                block = array[first, :, span].astype(jnp.float32)
+                block = array[first - 1, :, span] if first else here[second, :, span]
+                block = block.astype(jnp.float32)
                 source = me ^ distance_of(first, second, outer)
                 for slot in range(SLOTS):
                     turned[lane, pl.ds(SLOTS * source + slot, k_local, stride=pitch), :] = block[slot * k_local : (slot + 1) * k_local]
@@ -336,10 +343,10 @@
 
     *sends, _ = pl.pallas_call(
         functools.partial(second_kernel, ways, outer, tile),
-        out_shape=[blocks(outer)] * INNER + [pltpu.VMEM(part.shape, part.dtype)],
+        out_shape=[blocks(outer)] * (INNER - 1) + [blocks(1)] * outer + [pltpu.VMEM(part.shape, part.dtype)],
         in_specs=[whole(pltpu.VMEM)] * (ways + 2),
-        out_specs=[whole(pltpu.VMEM)] * (INNER + 1),
-        input_output_aliases={1: INNER},
+        out_specs=[whole(pltpu.VMEM)] * (outer + INNER),
+        input_output_aliases={1: outer + INNER - 1},
         scratch_shapes=[
             pltpu.VMEM((lane_tiles, cycles * (width + 1 - width % 2), LANES), jnp.float32),
         ],
@@ -359,19 +366,19 @@
                 perm.append((b * ways + core, (b ^ distance) * ways + core))
         return pltpu.with_memory_space_constraint(lax.ppermute(array, ("blk", "beamk"), perm), pltpu.VMEM)
 
-    first = list(sends)
+    first, direct = list(sends[: INNER - 1]), list(sends[INNER - 1 :])
     for number in range(1, INNER):
-        first[number] = send(first[number], number, 0)
-    second = list(
-        pl.pallas_call(
-            functools.partial(regroup_kernel, outer),
-            out_shape=[blocks(INNER)] * outer,
-            in_specs=[whole(pltpu.VMEM)] * INNER,
-            out_specs=[whole(pltpu.VMEM)] * outer,
-            compiler_params=params,
-            name="regroup",
-        )(*first)
-    )
+        first[number - 1] = send(first[number - 1], number, 0)
+    for number in range(1, outer):
+        direct[number] = send(direct[number], number, 1)
+    here, *second = pl.pallas_call(
+        functools.partial(regroup_kernel, outer),
+        out_shape=[blocks(outer)] + [blocks(INNER - 1)] * outer,
+        in_specs=[whole(pltpu.VMEM)] * (INNER - 1 + outer),
+        out_specs=[whole(pltpu.VMEM)] * (outer + 1),
+        compiler_params=params,
+        name="regroup",
+    )(*first, *direct)
     for number in range(1, outer):
         second[number] = send(second[number], number, 1)
     slot_count = slots * peers
@@ -381,24 +388,24 @@
     turned = pl.pallas_call(
         functools.partial(place_kernel, outer, range(early)),
         out_shape=placed,
-        in_specs=[whole(pltpu.VMEM)] * early,
+        in_specs=[whole(pltpu.VMEM)] * (early + 1),
         out_specs=whole(pltpu.VMEM),
         compiler_params=params,
         name="place_early",
-    )(*second[:early])
+    )(here, *second[:early])
     out, _ = pl.pallas_call(
         functools.partial(place_kernel, outer, range(early, outer)),
         out_shape=(result, placed),
-        in_specs=[whole(pltpu.VMEM)] * (outer - early + 1),
+        in_specs=[whole(pltpu.VMEM)] * (outer - early + 2),
         out_specs=(whole(pltpu.HBM), whole(pltpu.VMEM)),
-        input_output_aliases={outer - early: 1},
+        input_output_aliases={outer - early + 1: 1},
         scratch_shapes=[
             pltpu.VMEM((k_local, slot_count, columns), jnp.bfloat16),
             pltpu.SemaphoreType.DMA((4,)),
         ],
         compiler_params=params,
         name="place_late",
-    )(*second[early:], turned)
+    )(here, *second[early:], turned)
     return out.transpose(1, 0, 2)[None]
 
 

time: 28.3 us -> 31.8 us (1.12)
  starting transfers between devices: 9.19 us -> 16 us
  waiting for transfers between devices: 12.3 us -> 8.77 us
    ppermute x6 -> x9, starting transfers between devices: 8.74 us -> 15.5 us  [send(): lax.ppermute(array, ('blk', 'beamk'), perm)]
    ppermute x6 -> x9, waiting for transfers between devices: 11 us -> 7.97 us  [send(): lax.ppermute(array, ('blk', 'beamk'), perm)]
    pallas_call x1, Pallas kernels: 3.07 us -> 3.56 us  [local(): pl.pallas_call(functools.partial(first_kernel, ways, tile), out_shape=(pl...]
    ppermute x1, waiting for transfers between devices: 1.29 us -> 0.8 us  [local(): lax.ppermute(sky, 'beamk', perm)]
    pallas_call x1, Pallas kernels: 2.79 us -> 2.44 us  [local(): pl.pallas_call(functools.partial(second_kernel, ways, outer, tile), out_s...]
  transfers between devices with their start and end apart: 7 -> 10, of which waited for: 7 -> 7; matrix products, arithmetic and copies ran while one was open for 0% -> 0% of each run, Pallas kernels for 11% -> 11%
where the time goes in v13:
time: 31.8 us
  starting transfers between devices  16 us (50%)
  waiting for transfers between devices  8.77 us (28%)
  Pallas kernels  7 us (22%)
    ppermute x9, starting transfers between devices, send(): lax.ppermute(array, ('blk', 'beamk'), perm)  15.5 us
    ppermute x9, waiting for transfers between devices, send(): lax.ppermute(array, ('blk', 'beamk'), perm)  7.97 us
    pallas_call x1, Pallas kernels, local(): pl.pallas_call(functools.partial(first_kernel, ways, tile), out_shape=(pl...  3.56 us
    pallas_call x1, Pallas kernels, local(): pl.pallas_call(functools.partial(second_kernel, ways, outer, tile), out_s...  2.44 us
    pallas_call x1, Pallas kernels, local(): pl.pallas_call(functools.partial(place_kernel, outer, range(early, outer)...  0.88 us
    ppermute x1, waiting for transfers between devices, local(): lax.ppermute(sky, 'beamk', perm)  0.8 us
  transfers between devices with their start and end apart: 10, of which 7 were waited for; matrix products, arithmetic and copies ran while one was open for 0% of the time, Pallas kernels for 11%

profile of v13, /device:TPU:0, one launch (start us, length us, event | category | flops | bytes accessed | tf_op | source)
XLA Modules:
  0.0 31.8 jit_solution(8026189645016805351)
XLA Ops:
  0.0 0.5 %collective-permute-start = (bf16[2,1536,384]{2,1,0:T(8,128)(2,1)}, bf16[2,1536,384]{2,1,0:T(8,128)(2,1)S(1)}, u32[]{:S(2)}, u32[]{:S(2)}) collective-permute-start(bf16[2,1536,384]{2,1,0:T(8,128)(2,1)} %sky.1), channel_id=1, source_target_pairs={{0,1},{1,0},{2,3},{3,2},{4,5},{5,4},{6,7},{7,6},{8,9},{9,8},{10,11... | collective-permute-start | bytes 7077896 | tf_op jit(solution)/shard_map/ppermute | solution.py:308
  0.5 3.6 %own_half.1 = (f32[2,640,384]{2,1,0:T(8,128)S(1)}, bf16[1,2,640,1536]{3,2,1,0:T(8,128)(2,1)S(1)}, f32[8,128]{1,0:T(8,128)S(1)}) custom-call(s32[2]{0:T(128)} %m_list.1, bf16[2,1536,384]{2,1,0:T(8,128)(2,1)} %sky.1, bf16[2,20,16,3072]{3,2,1,0:T(8,128)(2,1)} %wigner.1, f32[20,2,3072]{2,1,0:T(2,128)} %beam.1), custom_call_target="tpu_custom_call" | custom-call | flops 1509949440 | bytes 8388608 | tf_op jit(solution)/shard_map/own_half/pallas_call | solution.py:311
  4.0 0.8 %collective-permute-done.refs_0_ = bf16[2,1536,384]{2,1,0:T(8,128)(2,1)S(1)} collective-permute-done((bf16[2,1536,384]{2,1,0:T(8,128)(2,1)}, bf16[2,1536,384]{2,1,0:T(8,128)(2,1)S(1)}, u32[]{:S(2)}, u32[]{:S(2)}) %collective-permute-start) | collective-permute-done | bytes 2359328 | tf_op jit(solution)/shard_map/ppermute | solution.py:308
  4.8 2.4 %other_half.1 = (bf16[4,40,384]{2,1,0:T(8,128)(2,1)S(1)}, bf16[4,40,384]{2,1,0:T(8,128)(2,1)S(1)}, bf16[4,40,384]{2,1,0:T(8,128)(2,1)S(1)}, bf16[1,40,384]{2,1,0...) custom-call(f32[8,128]{1,0:T(8,128)S(1)} %get-tuple-element.21.info,, ...), custom_call_target="tpu_custom_call", output_to_operand_aliasing={{7}: (1, {})} | custom-call | flops 1509949440 | bytes 8388608 | tf_op jit(solution)/shard_map/other_half/pallas_call | solution.py:344
  7.3 4.2 %collective-permute-start.1 = (bf16[4,40,384]{2,1,0:T(8,128)(2,1)S(1)}, bf16[4,40,384]{2,1,0:T(8,128)(2,1)S(1)}, u32[]{:S(2)}, u32[]{:S(2)}) collective-permute-start(bf16[4,40,384]{2,1,0:T(8,128)(2,1)S(1)} %get-tuple-element.24), channel_id=1, source_target_pairs={{0,6},{1,17},{2,4},{3,19},{4,2},{5,21},{6,0},{7,23},{8,14},{9,25},... | collective-permute-start | bytes 368648 | tf_op jit(solution)/shard_map/ppermute | solution.py:367
  11.5 0.2 collective-permute-start.2
  11.7 0.5 %collective-permute-start.3 = (bf16[4,40,384]{2,1,0:T(8,128)(2,1)S(1)}, bf16[4,40,384]{2,1,0:T(8,128)(2,1)S(1)}, u32[]{:S(2)}, u32[]{:S(2)}) collective-permute-start(bf16[4,40,384]{2,1,0:T(8,128)(2,1)S(1)} %get-tuple-element.26), channel_id=1, source_target_pairs={{0,2},{1,9},{2,0},{3,11},{4,6},{5,13},{6,4},{7,15},{8,10},{9,1},{1... | collective-permute-start | bytes 368648 | tf_op jit(solution)/shard_map/ppermute | solution.py:367
  12.1 3.0 %collective-permute-start.4 = (bf16[1,40,384]{2,1,0:T(8,128)(2,1)S(1)}, bf16[1,40,384]{2,1,0:T(8,128)(2,1)S(1)}, u32[]{:S(2)}, u32[]{:S(2)}) collective-permute-start(bf16[1,40,384]{2,1,0:T(8,128)(2,1)S(1)} %get-tuple-element.28), channel_id=1, source_target_pairs={{0,16},{1,7},{2,18},{3,5},{4,20},{5,3},{6,22},{7,1},{8,24},{9,15},... | collective-permute-start | bytes 92168 | tf_op jit(solution)/shard_map/ppermute | solution.py:367
  15.1 1.4 %collective-permute-start.5 = (bf16[1,40,384]{2,1,0:T(8,128)(2,1)S(1)}, bf16[1,40,384]{2,1,0:T(8,128)(2,1)S(1)}, u32[]{:S(2)}, u32[]{:S(2)}) collective-permute-start(bf16[1,40,384]{2,1,0:T(8,128)(2,1)S(1)} %get-tuple-element.29), channel_id=1, source_target_pairs={{0,24},{1,5},{2,26},{3,7},{4,28},{5,1},{6,30},{7,3},{8,16},{9,13},... | collective-permute-start | bytes 92168 | tf_op jit(solution)/shard_map/ppermute | solution.py:367
  16.5 0.7 %collective-permute-done.4.refs_4_ = bf16[1,40,384]{2,1,0:T(8,128)(2,1)S(1)} collective-permute-done((bf16[1,40,384]{2,1,0:T(8,128)(2,1)S(1)}, bf16[1,40,384]{2,1,0:T(8,128)(2,1)S(1)}, u32[]{:S(2)}, u32[]{:S(2)}) %collective-permute-start.4) | collective-permute-done | bytes 30752 | tf_op jit(solution)/shard_map/ppermute | solution.py:367
  17.2 1.7 %collective-permute-start.6 = (bf16[1,40,384]{2,1,0:T(8,128)(2,1)S(1)}, bf16[1,40,384]{2,1,0:T(8,128)(2,1)S(1)}, u32[]{:S(2)}, u32[]{:S(2)}) collective-permute-start(bf16[1,40,384]{2,1,0:T(8,128)(2,1)S(1)} %get-tuple-element.30), channel_id=1, source_target_pairs={{0,8},{1,3},{2,10},{3,1},{4,12},{5,7},{6,14},{7,5},{8,0},{9,11},{1... | collective-permute-start | bytes 92168 | tf_op jit(solution)/shard_map/ppermute | solution.py:367
  18.9 1.9 %collective-permute-done.5.refs_5_ = bf16[1,40,384]{2,1,0:T(8,128)(2,1)S(1)} collective-permute-done((bf16[1,40,384]{2,1,0:T(8,128)(2,1)S(1)}, bf16[1,40,384]{2,1,0:T(8,128)(2,1)S(1)}, u32[]{:S(2)}, u32[]{:S(2)}) %collective-permute-start.5) | collective-permute-done | bytes 30752 | tf_op jit(solution)/shard_map/ppermute | solution.py:367
  20.8 0.3 %collective-permute-done.6.refs_6_ = bf16[1,40,384]{2,1,0:T(8,128)(2,1)S(1)} collective-permute-done((bf16[1,40,384]{2,1,0:T(8,128)(2,1)S(1)}, bf16[1,40,384]{2,1,0:T(8,128)(2,1)S(1)}, u32[]{:S(2)}, u32[]{:S(2)}) %collective-permute-start.6) | collective-permute-done | bytes 30752 | tf_op jit(solution)/shard_map/ppermute | solution.py:367
  21.2 0.0 collective-permute-done.1.refs_0_
  21.2 0.0 collective-permute-done.2.refs_1_
  21.2 0.0 collective-permute-done.3.refs_2_
  21.2 2.7 %collective-permute-start.9 = (bf16[3,40,384]{2,1,0:T(8,128)(2,1)S(1)}, bf16[3,40,384]{2,1,0:T(8,128)(2,1)S(1)}, u32[]{:S(2)}, u32[]{:S(2)}) collective-permute-start(bf16[3,40,384]{2,1,0:T(8,128)(2,1)S(1)} %get-tuple-element.35), channel_id=1, source_target_pairs={{0,16},{1,7},{2,18},{3,5},{4,20},{5,3},{6,22},{7,1},{8,24},{9,15},... | collective-permute-start | bytes 276488 | tf_op jit(solution)/shard_map/ppermute | solution.py:367
  24.0 1.4 %collective-permute-start.7 = (bf16[3,40,384]{2,1,0:T(8,128)(2,1)S(1)}, bf16[3,40,384]{2,1,0:T(8,128)(2,1)S(1)}, u32[]{:S(2)}, u32[]{:S(2)}) collective-permute-start(bf16[3,40,384]{2,1,0:T(8,128)(2,1)S(1)} %get-tuple-element.32), channel_id=1, source_target_pairs={{0,24},{1,5},{2,26},{3,7},{4,28},{5,1},{6,30},{7,3},{8,16},{9,13},... | collective-permute-start | bytes 276488 | tf_op jit(solution)/shard_map/ppermute | solution.py:367
  25.4 0.5 %collective-permute-start.8 = (bf16[3,40,384]{2,1,0:T(8,128)(2,1)S(1)}, bf16[3,40,384]{2,1,0:T(8,128)(2,1)S(1)}, u32[]{:S(2)}, u32[]{:S(2)}) collective-permute-start(bf16[3,40,384]{2,1,0:T(8,128)(2,1)S(1)} %get-tuple-element.33), channel_id=1, source_target_pairs={{0,8},{1,3},{2,10},{3,1},{4,12},{5,7},{6,14},{7,5},{8,0},{9,11},{1... | collective-permute-start | bytes 276488 | tf_op jit(solution)/shard_map/ppermute | solution.py:367
  25.9 0.9 %collective-permute-done.9.refs_2_ = bf16[3,40,384]{2,1,0:T(8,128)(2,1)S(1)} collective-permute-done((bf16[3,40,384]{2,1,0:T(8,128)(2,1)S(1)}, bf16[3,40,384]{2,1,0:T(8,128)(2,1)S(1)}, u32[]{:S(2)}, u32[]{:S(2)}) %collective-permute-start.9) | collective-permute-done | bytes 92192 | tf_op jit(solution)/shard_map/ppermute | solution.py:367
  26.7 0.1 place_early.1.refs_3_
  26.8 3.7 %collective-permute-done.7.refs_1_ = bf16[3,40,384]{2,1,0:T(8,128)(2,1)S(1)} collective-permute-done((bf16[3,40,384]{2,1,0:T(8,128)(2,1)S(1)}, bf16[3,40,384]{2,1,0:T(8,128)(2,1)S(1)}, u32[]{:S(2)}, u32[]{:S(2)}) %collective-permute-start.7) | collective-permute-done | bytes 92192 | tf_op jit(solution)/shard_map/ppermute | solution.py:367
  30.5 0.5 %collective-permute-done.8.refs_2_ = bf16[3,40,384]{2,1,0:T(8,128)(2,1)S(1)} collective-permute-done((bf16[3,40,384]{2,1,0:T(8,128)(2,1)S(1)}, bf16[3,40,384]{2,1,0:T(8,128)(2,1)S(1)}, u32[]{:S(2)}, u32[]{:S(2)}) %collective-permute-start.8) | collective-permute-done | bytes 92192 | tf_op jit(solution)/shard_map/ppermute | solution.py:367
  30.9 0.9 %place_late.1 = (bf16[20,32,384]{2,1,0:T(8,128)(2,1)}, f32[3,660,128]{2,1,0:T(8,128)S(1)}) custom-call(bf16[4,40,384]{2,1,0:T(8,128)(2,1)S(1)} %get-tuple-element.31.refs_0_, bf16[3,40,384]{2,1,0:T(8,128)(2,1)S(1)} %collective-permute-done.7.refs_1_, bf16[3,40,384]{2,1,0:T(8,128)(2,1)S(1)} %collective-permute-done.8.refs_2_, ...), custom_call_target="tpu_custom_call", output_to_operand_aliasing={{1}: (3, {})} | custom-call | tf_op jit(solution)/shard_map/place_late/pallas_call | solution.py:396
  (1 shorter events, 0.0 us)
Async XLA Ops:
  0.0 4.8 %collective-permute-start = (bf16[2,1536,384]{2,1,0:T(8,128)(2,1)}, bf16[2,1536,384]{2,1,0:T(8,128)(2,1)S(1)}, u32[]{:S(2)}, u32[]{:S(2)}) collective-permute-start(bf16[2,1536,384]{2,1,0:T(8,128)(2,1)} %sky.1), channel_id=1, source_target_pairs={{0,1},{1,0},{2,3},{3,2},{4,5},{5,4},{6,7},{7,6},{8,9},{9,8},{10,11... | collective-permute-start | bytes 7077896 | tf_op jit(solution)/shard_map/ppermute | solution.py:308
  7.3 13.9 %collective-permute-start.1 = (bf16[4,40,384]{2,1,0:T(8,128)(2,1)S(1)}, bf16[4,40,384]{2,1,0:T(8,128)(2,1)S(1)}, u32[]{:S(2)}, u32[]{:S(2)}) collective-permute-start(bf16[4,40,384]{2,1,0:T(8,128)(2,1)S(1)} %get-tuple-element.24), channel_id=1, source_target_pairs={{0,6},{1,17},{2,4},{3,19},{4,2},{5,21},{6,0},{7,23},{8,14},{9,25},... | collective-permute-start | bytes 368648 | tf_op jit(solution)/shard_map/ppermute | solution.py:367
  11.5 9.7 %collective-permute-start.2 = (bf16[4,40,384]{2,1,0:T(8,128)(2,1)S(1)}, bf16[4,40,384]{2,1,0:T(8,128)(2,1)S(1)}, u32[]{:S(2)}, u32[]{:S(2)}) collective-permute-start(bf16[4,40,384]{2,1,0:T(8,128)(2,1)S(1)} %get-tuple-element.25), channel_id=1, source_target_pairs={{0,4},{1,25},{2,6},{3,27},{4,0},{5,29},{6,2},{7,31},{8,12},{9,17},... | collective-permute-start | bytes 368648 | tf_op jit(solution)/shard_map/ppermute | solution.py:367
  11.7 9.5 %collective-permute-start.3 = (bf16[4,40,384]{2,1,0:T(8,128)(2,1)S(1)}, bf16[4,40,384]{2,1,0:T(8,128)(2,1)S(1)}, u32[]{:S(2)}, u32[]{:S(2)}) collective-permute-start(bf16[4,40,384]{2,1,0:T(8,128)(2,1)S(1)} %get-tuple-element.26), channel_id=1, source_target_pairs={{0,2},{1,9},{2,0},{3,11},{4,6},{5,13},{6,4},{7,15},{8,10},{9,1},{1... | collective-permute-start | bytes 368648 | tf_op jit(solution)/shard_map/ppermute | solution.py:367
  12.1 5.1 %collective-permute-start.4 = (bf16[1,40,384]{2,1,0:T(8,128)(2,1)S(1)}, bf16[1,40,384]{2,1,0:T(8,128)(2,1)S(1)}, u32[]{:S(2)}, u32[]{:S(2)}) collective-permute-start(bf16[1,40,384]{2,1,0:T(8,128)(2,1)S(1)} %get-tuple-element.28), channel_id=1, source_target_pairs={{0,16},{1,7},{2,18},{3,5},{4,20},{5,3},{6,22},{7,1},{8,24},{9,15},... | collective-permute-start | bytes 92168 | tf_op jit(solution)/shard_map/ppermute | solution.py:367
  15.1 5.7 %collective-permute-start.5 = (bf16[1,40,384]{2,1,0:T(8,128)(2,1)S(1)}, bf16[1,40,384]{2,1,0:T(8,128)(2,1)S(1)}, u32[]{:S(2)}, u32[]{:S(2)}) collective-permute-start(bf16[1,40,384]{2,1,0:T(8,128)(2,1)S(1)} %get-tuple-element.29), channel_id=1, source_target_pairs={{0,24},{1,5},{2,26},{3,7},{4,28},{5,1},{6,30},{7,3},{8,16},{9,13},... | collective-permute-start | bytes 92168 | tf_op jit(solution)/shard_map/ppermute | solution.py:367
  17.2 3.9 %collective-permute-start.6 = (bf16[1,40,384]{2,1,0:T(8,128)(2,1)S(1)}, bf16[1,40,384]{2,1,0:T(8,128)(2,1)S(1)}, u32[]{:S(2)}, u32[]{:S(2)}) collective-permute-start(bf16[1,40,384]{2,1,0:T(8,128)(2,1)S(1)} %get-tuple-element.30), channel_id=1, source_target_pairs={{0,8},{1,3},{2,10},{3,1},{4,12},{5,7},{6,14},{7,5},{8,0},{9,11},{1... | collective-permute-start | bytes 92168 | tf_op jit(solution)/shard_map/ppermute | solution.py:367
  21.2 5.5 %collective-permute-start.9 = (bf16[3,40,384]{2,1,0:T(8,128)(2,1)S(1)}, bf16[3,40,384]{2,1,0:T(8,128)(2,1)S(1)}, u32[]{:S(2)}, u32[]{:S(2)}) collective-permute-start(bf16[3,40,384]{2,1,0:T(8,128)(2,1)S(1)} %get-tuple-element.35), channel_id=1, source_target_pairs={{0,16},{1,7},{2,18},{3,5},{4,20},{5,3},{6,22},{7,1},{8,24},{9,15},... | collective-permute-start | bytes 276488 | tf_op jit(solution)/shard_map/ppermute | solution.py:367
  24.0 6.5 %collective-permute-start.7 = (bf16[3,40,384]{2,1,0:T(8,128)(2,1)S(1)}, bf16[3,40,384]{2,1,0:T(8,128)(2,1)S(1)}, u32[]{:S(2)}, u32[]{:S(2)}) collective-permute-start(bf16[3,40,384]{2,1,0:T(8,128)(2,1)S(1)} %get-tuple-element.32), channel_id=1, source_target_pairs={{0,24},{1,5},{2,26},{3,7},{4,28},{5,1},{6,30},{7,3},{8,16},{9,13},... | collective-permute-start | bytes 276488 | tf_op jit(solution)/shard_map/ppermute | solution.py:367
  25.4 5.5 %collective-permute-start.8 = (bf16[3,40,384]{2,1,0:T(8,128)(2,1)S(1)}, bf16[3,40,384]{2,1,0:T(8,128)(2,1)S(1)}, u32[]{:S(2)}, u32[]{:S(2)}) collective-permute-start(bf16[3,40,384]{2,1,0:T(8,128)(2,1)S(1)} %get-tuple-element.33), channel_id=1, source_target_pairs={{0,8},{1,3},{2,10},{3,1},{4,12},{5,7},{6,14},{7,5},{8,0},{9,11},{1... | collective-permute-start | bytes 276488 | tf_op jit(solution)/shard_map/ppermute | solution.py:367

commit v14 on v9

--- a/solution.py
+++ b/solution.py
@@ -8,6 +8,7 @@
 from jax.sharding import PartitionSpec as P
 
 KB = 40
+SLOTS = 2
 LANES = 128
 INNER = 4
 VMEM_LIMIT = 24 * 1024 * 1024
@@ -180,19 +181,21 @@
     return (core % 2) * (outer == INNER)
 
 
-def distance_of(first, second, outer):
+def device_of(first, second, outer):
     straight = second * INNER + first
+    if outer != INNER:
+        return straight
     return jnp.where(crossed(lax.axis_index("beamk"), outer) == 1, first * INNER + second, straight)
 
 
 def second_kernel(ways, outer, tile, info, _, factors, *refs):
     pieces, refs = refs[: ways - 1], refs[ways - 1 :]
-    outs, (acc, turned) = refs[:INNER], refs[INNER:]
+    out, acc, turned = refs
     slots, rows, columns = acc.shape
     rows = rows // 2
     piece_rows = pieces[0].shape[1]
     tiles = piece_rows // tile
-    width = outs[0].shape[1]
+    width = out.shape[2]
     cycles = outer * INNER
     k_local = width // slots
     pitch = turned.shape[1] // cycles
@@ -219,36 +222,32 @@
             for lane in range(columns // LANES):
                 turned[lane, pl.ds(slot * k_local + k, cycles, stride=pitch), :] = total[:, lane * LANES : (lane + 1) * LANES]
 
-    me = lax.axis_index("blk")
     for first in range(INNER):
         for second in range(outer):
-            start = (me ^ distance_of(first, second, outer)) * pitch
+            start = device_of(first, second, outer) * pitch
             for lane in range(columns // LANES):
                 block = turned[lane, pl.ds(start, width), :].astype(jnp.bfloat16)
-                outs[first][second, :, lane * LANES : (lane + 1) * LANES] = block
-
-
-def regroup_kernel(outer, *refs):
-    for second in range(outer):
-        for first in range(INNER):
-            refs[INNER + second][first] = refs[first][second]
-
-
-def place_kernel(outer, *refs):
-    out, turned, staged, sem = refs[outer:]
-    k_local, slot_count, columns = staged.shape
-    width = refs[0].shape[1]
-    slots = width // k_local
+                out[first, second, :, lane * LANES : (lane + 1) * LANES] = block
+
+
+def regroup_kernel(arrived, onward):
+    for first in range(arrived.shape[0]):
+        for second in range(arrived.shape[1]):
+            onward[second, first] = arrived[first, second]
+
+
+def place_kernel(arrived, out, turned, staged, sem):
+    outer, _, width, columns = arrived.shape
+    k_local, slot_count, _ = staged.shape
     pitch = turned.shape[1] // k_local
-    me = lax.axis_index("blk")
     for lane in range(columns // LANES):
         span = slice(lane * LANES, (lane + 1) * LANES)
         for second in range(outer):
             for first in range(INNER):
-                block = refs[second][first, :, span].astype(jnp.float32)
-                source = me ^ distance_of(first, second, outer)
-                for slot in range(slots):
-                    turned[lane, pl.ds(slots * source + slot, k_local, stride=pitch), :] = block[slot * k_local : (slot + 1) * k_local]
+                block = arrived[second, first, :, span].astype(jnp.float32)
+                source = device_of(first, second, outer)
+                for slot in range(SLOTS):
+                    turned[lane, pl.ds(SLOTS * source + slot, k_local, stride=pitch), :] = block[slot * k_local : (slot + 1) * k_local]
     copies = []
     step = -(-k_local // 4)
     for number, start in enumerate(range(0, k_local, step)):
@@ -309,15 +308,15 @@
 
     outer = peers // INNER
 
-    def blocks(number):
-        return pltpu.VMEM((number, width, columns), jnp.bfloat16)
-
-    *sends, _ = pl.pallas_call(
+    def blocks(*numbers):
+        return pltpu.VMEM((*numbers, width, columns), jnp.bfloat16)
+
+    blocks_out, _ = pl.pallas_call(
         functools.partial(second_kernel, ways, outer, tile),
-        out_shape=[blocks(outer)] * INNER + [pltpu.VMEM(part.shape, part.dtype)],
+        out_shape=(blocks(INNER, outer), pltpu.VMEM(part.shape, part.dtype)),
         in_specs=[whole(pltpu.VMEM)] * (ways + 2),
-        out_specs=[whole(pltpu.VMEM)] * (INNER + 1),
-        input_output_aliases={1: INNER},
+        out_specs=(whole(pltpu.VMEM),) * 2,
+        input_output_aliases={1: 1},
         scratch_shapes=[
             pltpu.VMEM((lane_tiles, cycles * (width + 1 - width % 2), LANES), jnp.float32),
         ],
@@ -328,34 +327,32 @@
         name="other_half",
     )(info, part, factors, *pieces)
 
-    def send(array, number, step):
-        perm = []
-        for b in range(peers):
-            for core in range(ways):
-                over_outer = (step == 0) == bool(crossed(core, outer))
-                perm.append((b * ways + core, (b ^ (number * INNER if over_outer else number)) * ways + core))
-        return pltpu.with_memory_space_constraint(lax.ppermute(array, ("blk", "beamk"), perm), pltpu.VMEM)
-
-    first = list(sends)
-    for number in reversed(range(1, INNER)):
-        first[number] = send(first[number], number, 0)
-    second = list(
-        pl.pallas_call(
-            functools.partial(regroup_kernel, outer),
-            out_shape=[blocks(INNER)] * outer,
-            in_specs=[whole(pltpu.VMEM)] * INNER,
-            out_specs=[whole(pltpu.VMEM)] * outer,
-            compiler_params=params,
-            name="regroup",
-        )(*first)
-    )
-    for number in reversed(range(1, outer)):
-        second[number] = send(second[number], number, 1)
+    def exchange(array, step):
+        groups = []
+        for core in range(ways):
+            if (step == 0) == bool(crossed(core, outer)):
+                places = [[o * INNER + i for o in range(outer)] for i in range(INNER)]
+            else:
+                places = [[o * INNER + i for i in range(INNER)] for o in range(outer)]
+            groups += [[b * ways + core for b in group] for group in places]
+        array = lax.all_to_all(array, ("blk", "beamk"), 0, 0, axis_index_groups=groups, tiled=True)
+        return pltpu.with_memory_space_constraint(array, pltpu.VMEM)
+
+    first = exchange(blocks_out, 0)
+    second = pl.pallas_call(
+        regroup_kernel,
+        out_shape=blocks(outer, INNER),
+        in_specs=[whole(pltpu.VMEM)],
+        out_specs=whole(pltpu.VMEM),
+        compiler_params=params,
+        name="regroup",
+    )(first)
+    second = exchange(second, 1)
     slot_count = slots * peers
     out = pl.pallas_call(
-        functools.partial(place_kernel, outer),
+        place_kernel,
         out_shape=pltpu.HBM((k_local, slot_count, columns), jnp.bfloat16),
-        in_specs=[whole(pltpu.VMEM)] * outer,
+        in_specs=[whole(pltpu.VMEM)],
         out_specs=whole(pltpu.HBM),
         scratch_shapes=[
             pltpu.VMEM((lane_tiles, k_local * (slot_count + 1), LANES), jnp.float32),
@@ -364,7 +361,7 @@
         ],
         compiler_params=params,
         name="place",
-    )(*second)
+    )(second)
     return out.transpose(1, 0, 2)[None]
 
 

time: 29.6 us -> 35.4 us (1.20)
  blocking collectives: 0 us -> 26.5 us
  waiting for transfers between devices: 12.9 us -> 1.29 us
  starting transfers between devices: 9.37 us -> 0.45 us
    all_to_all x0 -> x2, blocking collectives: none -> 26.5 us  [exchange(): lax.all_to_all(array, ('blk', 'beamk'), 0, 0, axis_index_groups=groups, t...]
    ppermute x6 -> x0, waiting for transfers between devices: 11.6 us -> none  [send(): lax.ppermute(array, ('blk', 'beamk'), perm)]
    ppermute x6 -> x0, starting transfers between devices: 8.92 us -> none  [send(): lax.ppermute(array, ('blk', 'beamk'), perm)]
  transfers between devices with their start and end apart: 7 -> 1, of which waited for: 7 -> 1; matrix products, arithmetic and copies ran while one was open for 0% -> 0% of each run, Pallas kernels for 10% -> 9%
where the time goes in v14:
time: 35.4 us; the launch traced here: 35.5 us
  blocking collectives  26.5 us (75%)
  Pallas kernels  7.18 us (20%)
  waiting for transfers between devices  1.29 us (4%)
  starting transfers between devices  0.45 us (1%)
    all_to_all x2, blocking collectives, exchange(): lax.all_to_all(array, ('blk', 'beamk'), 0, 0, axis_index_groups=groups, t...  26.5 us
    pallas_call x1, Pallas kernels, local(): pl.pallas_call(functools.partial(second_kernel, ways, outer, tile), out_s...  3.13 us
    pallas_call x1, Pallas kernels, local(): pl.pallas_call(functools.partial(first_kernel, ways, tile), out_shape=(pl...  3.07 us
    ppermute x1, waiting for transfers between devices, local(): lax.ppermute(sky, 'beamk', perm)  1.29 us
    pallas_call x1, Pallas kernels, local(): pl.pallas_call(place_kernel, out_shape=pltpu.HBM((k_local, slot_count, co...  0.93 us
  transfers between devices with their start and end apart: 1, of which 1 were waited for; matrix products, arithmetic and copies ran while one was open for 0% of the time, Pallas kernels for 9%

profile of v14, /device:TPU:0, one launch (start us, length us, event | category | flops | bytes accessed | tf_op | source)
XLA Modules:
  0.0 35.5 jit_solution(18306237380305135005)
XLA Ops:
  0.0 0.5 %collective-permute-start = (bf16[2,1536,384]{2,1,0:T(8,128)(2,1)}, bf16[2,1536,384]{2,1,0:T(8,128)(2,1)S(1)}, u32[]{:S(2)}, u32[]{:S(2)}) collective-permute-start(bf16[2,1536,384]{2,1,0:T(8,128)(2,1)} %sky.1), channel_id=1, source_target_pairs={{0,1},{1,0},{2,3},{3,2},{4,5},{5,4},{6,7},{7,6},{8,9},{9,8},{10,11... | collective-permute-start | bytes 7077896 | tf_op jit(solution)/shard_map/ppermute | solution.py:278
  0.5 3.1 %own_half.1 = (f32[2,640,384]{2,1,0:T(8,128)S(1)}, bf16[1,2,640,1536]{3,2,1,0:T(8,128)(2,1)S(1)}, f32[8,128]{1,0:T(8,128)S(1)}) custom-call(s32[2]{0:T(128)} %m_list.1, bf16[2,1536,384]{2,1,0:T(8,128)(2,1)} %sky.1, bf16[2,20,16,3072]{3,2,1,0:T(8,128)(2,1)} %wigner.1, f32[20,2,3072]{2,1,0:T(2,128)} %beam.1), custom_call_target="tpu_custom_call" | custom-call | flops 1509949440 | bytes 8388608 | tf_op jit(solution)/shard_map/own_half/pallas_call | solution.py:281
  3.5 1.3 %collective-permute-done.refs_0_ = bf16[2,1536,384]{2,1,0:T(8,128)(2,1)S(1)} collective-permute-done((bf16[2,1536,384]{2,1,0:T(8,128)(2,1)}, bf16[2,1536,384]{2,1,0:T(8,128)(2,1)S(1)}, u32[]{:S(2)}, u32[]{:S(2)}) %collective-permute-start) | collective-permute-done | bytes 2359328 | tf_op jit(solution)/shard_map/ppermute | solution.py:278
  4.8 3.1 %other_half.1 = (bf16[4,4,40,384]{3,2,1,0:T(8,128)(2,1)S(1)}, f32[2,640,384]{2,1,0:T(8,128)S(1)}) custom-call(f32[8,128]{1,0:T(8,128)S(1)} %get-tuple-element.9.info, f32[2,640,384]{2,1,0:T(8,128)S(1)} %get-tuple-element.10._, bf16[1,2,640,1536]{3,2,1,0:T(8,128)(2,1)S(1)} %get-tuple-element.11.factors, ...), custom_call_target="tpu_custom_call", output_to_operand_aliasing={{1}: (1, {})} | custom-call | flops 1509949440 | bytes 8388608 | tf_op jit(solution)/shard_map/other_half/pallas_call | solution.py:314
  8.0 11.9 %all_to_all.10.arrived = bf16[4,4,40,384]{3,2,1,0:T(8,128)(2,1)S(1)} all-to-all(bf16[4,4,40,384]{3,2,1,0:T(8,128)(2,1)S(1)} %get-tuple-element.12), channel_id=1, replica_groups={{0,2,4,6},{8,10,12,14},{16,18,20,22},{24,26,28,30},{1,9,17,25},{3,11,19..., dimensions={0} | all-to-all | bytes 983040 | tf_op jit(solution)/shard_map/all_to_all | solution.py:338
  19.9 14.6 %all_to_all.11.arrived = bf16[4,4,40,384]{3,2,1,0:T(8,128)(2,1)S(1)} all-to-all(bf16[4,4,40,384]{3,2,1,0:T(8,128)(2,1)S(1)} %regroup.1), channel_id=1, replica_groups={{0,8,16,24},{2,10,18,26},{4,12,20,28},{6,14,22,30},{1,3,5,7},{9,11,13,1..., dimensions={0} | all-to-all | bytes 983040 | tf_op jit(solution)/shard_map/all_to_all | solution.py:338
  34.5 0.9 %place.1 = bf16[20,32,384]{2,1,0:T(8,128)(2,1)} custom-call(bf16[4,4,40,384]{3,2,1,0:T(8,128)(2,1)S(1)} %all_to_all.11.arrived), custom_call_target="tpu_custom_call" | custom-call | tf_op jit(solution)/shard_map/place/pallas_call | solution.py:352
  (1 shorter events, 0.0 us)
Async XLA Ops:
  0.0 4.8 %collective-permute-start = (bf16[2,1536,384]{2,1,0:T(8,128)(2,1)}, bf16[2,1536,384]{2,1,0:T(8,128)(2,1)S(1)}, u32[]{:S(2)}, u32[]{:S(2)}) collective-permute-start(bf16[2,1536,384]{2,1,0:T(8,128)(2,1)} %sky.1), channel_id=1, source_target_pairs={{0,1},{1,0},{2,3},{3,2},{4,5},{5,4},{6,7},{7,6},{8,9},{9,8},{10,11... | collective-permute-start | bytes 7077896 | tf_op jit(solution)/shard_map/ppermute | solution.py:278

commit v15 on v10

--- a/solution.py
+++ b/solution.py
@@ -197,28 +197,34 @@
     k_local = width // slots
     pitch = turned.shape[1] // cycles
 
-    @pl.loop(0, slots)
-    def _(slot):
-        m_value = jnp.max(info[pl.ds(slot, 1), :]).astype(jnp.int32)
-        for distance in range(1, ways):
-            missing = first_tile(m_value, owner_of(distance, ways), piece_rows, tile)
-            for skipped in range(tiles):
-
-                @pl.when(missing == skipped)
-                def _():
-                    span = slice(skipped * tile, piece_rows)
-                    acc[slot] += jnp.dot(
-                        factors[distance - 1, slot, :, span],
-                        pieces[distance - 1][slot, span],
-                        preferred_element_type=jnp.float32,
-                    )
-
+    m_values = [jnp.max(info[slot : slot + 1, :]).astype(jnp.int32) for slot in range(slots)]
+
+    def finish(slot):
         for k in range(k_local):
             span = slice(k * cycles, (k + 1) * cycles)
             total = acc[slot, span] + turn_by_i(acc[slot, rows + k * cycles : rows + (k + 1) * cycles])
             for lane in range(columns // LANES):
                 turned[lane, pl.ds(slot * k_local + k, cycles, stride=pitch), :] = total[:, lane * LANES : (lane + 1) * LANES]
 
+    for slot in range(slots):
+        for distance in range(1, ways):
+            beside = slot > 0 and distance == ways - 1
+            missing = first_tile(m_values[slot], owner_of(distance, ways), piece_rows, tile)
+            for skipped in range(tiles + (1 if beside else 0)):
+
+                @pl.when(missing == skipped)
+                def _():
+                    span = slice(skipped * tile, piece_rows)
+                    if skipped < tiles:
+                        acc[slot] += jnp.dot(
+                            factors[distance - 1, slot, :, span],
+                            pieces[distance - 1][slot, span],
+                            preferred_element_type=jnp.float32,
+                        )
+                    if beside:
+                        finish(slot - 1)
+
+    finish(slots - 1)
     me = lax.axis_index("blk")
     for first in range(INNER):
         for second in range(outer):

time: 28.1 us -> 27.9 us (level)
  starting transfers between devices: 9.33 us -> 10.2 us
  Pallas kernels: 7.17 us -> 6.66 us
  waiting for transfers between devices: 11.3 us -> 10.9 us
    pallas_call x1, Pallas kernels: 3.13 us -> 2.12 us  [local(): pl.pallas_call(functools.partial(second_kernel, ways, outer, tile), out_s...]
    ppermute x6, starting transfers between devices: 8.87 us -> 9.75 us  [send(): lax.ppermute(array, ('blk', 'beamk'), perm)]
    ppermute x1, waiting for transfers between devices: 1.29 us -> 0.8 us  [local(): lax.ppermute(sky, 'beamk', perm)]
    pallas_call x1, Pallas kernels: 3.07 us -> 3.56 us  [local(): pl.pallas_call(functools.partial(first_kernel, ways, tile), out_shape=(pl...]
  transfers between devices with their start and end apart: 7 -> 7, of which waited for: 6 -> 6; matrix products, arithmetic and copies ran while one was open for 0% -> 0% of each run, Pallas kernels for 11% -> 13%
where the time goes in v15:
time: 27.9 us; the launch traced here: 27.8 us
  waiting for transfers between devices  10.9 us (39%)
  starting transfers between devices  10.2 us (37%)
  Pallas kernels  6.66 us (24%)
    ppermute x6, waiting for transfers between devices, send(): lax.ppermute(array, ('blk', 'beamk'), perm)  10.1 us
    ppermute x6, starting transfers between devices, send(): lax.ppermute(array, ('blk', 'beamk'), perm)  9.75 us
    pallas_call x1, Pallas kernels, local(): pl.pallas_call(functools.partial(first_kernel, ways, tile), out_shape=(pl...  3.56 us
    pallas_call x1, Pallas kernels, local(): pl.pallas_call(functools.partial(second_kernel, ways, outer, tile), out_s...  2.12 us
    pallas_call x1, Pallas kernels, local(): pl.pallas_call(functools.partial(place_kernel, outer), out_shape=pltpu.HB...  0.93 us
    ppermute x1, waiting for transfers between devices, local(): lax.ppermute(sky, 'beamk', perm)  0.8 us
  transfers between devices with their start and end apart: 7, of which 6 were waited for; matrix products, arithmetic and copies ran while one was open for 0% of the time, Pallas kernels for 13%

profile of v15, /device:TPU:0, one launch (start us, length us, event | category | flops | bytes accessed | tf_op | source)
XLA Modules:
  0.0 27.8 jit_solution(3331742997946640807)
XLA Ops:
  0.0 0.5 %collective-permute-start = (bf16[2,1536,384]{2,1,0:T(8,128)(2,1)}, bf16[2,1536,384]{2,1,0:T(8,128)(2,1)S(1)}, u32[]{:S(2)}, u32[]{:S(2)}) collective-permute-start(bf16[2,1536,384]{2,1,0:T(8,128)(2,1)} %sky.1), channel_id=1, source_target_pairs={{0,1},{1,0},{2,3},{3,2},{4,5},{5,4},{6,7},{7,6},{8,9},{9,8},{10,11... | collective-permute-start | bytes 7077896 | tf_op jit(solution)/shard_map/ppermute | solution.py:290
  0.5 3.6 %own_half.1 = (f32[2,640,384]{2,1,0:T(8,128)S(1)}, bf16[1,2,640,1536]{3,2,1,0:T(8,128)(2,1)S(1)}, f32[8,128]{1,0:T(8,128)S(1)}) custom-call(s32[2]{0:T(128)} %m_list.1, bf16[2,1536,384]{2,1,0:T(8,128)(2,1)} %sky.1, bf16[2,20,16,3072]{3,2,1,0:T(8,128)(2,1)} %wigner.1, f32[20,2,3072]{2,1,0:T(2,128)} %beam.1), custom_call_target="tpu_custom_call" | custom-call | flops 1509949440 | bytes 8388608 | tf_op jit(solution)/shard_map/own_half/pallas_call | solution.py:293
  4.0 0.8 %collective-permute-done.refs_0_ = bf16[2,1536,384]{2,1,0:T(8,128)(2,1)S(1)} collective-permute-done((bf16[2,1536,384]{2,1,0:T(8,128)(2,1)}, bf16[2,1536,384]{2,1,0:T(8,128)(2,1)S(1)}, u32[]{:S(2)}, u32[]{:S(2)}) %collective-permute-start) | collective-permute-done | bytes 2359328 | tf_op jit(solution)/shard_map/ppermute | solution.py:290
  4.8 2.1 %other_half.1 = (bf16[4,40,384]{2,1,0:T(8,128)(2,1)S(1)}, bf16[4,40,384]{2,1,0:T(8,128)(2,1)S(1)}, bf16[4,40,384]{2,1,0:T(8,128)(2,1)S(1)}, bf16[4,40,384]{2,1,0:T(8,128)(2,1)S(1)}, f32[2,640,384]{2,1,0:T(8,128)S(1)}) custom-call(f32[8,128]{1,0:T(8,128)S(1)} %get-tuple-element.16.info, ...), custom_call_target="tpu_custom_call", output_to_operand_aliasing={{4}: (1, {})} | custom-call | flops 1509949440 | bytes 8388608 | tf_op jit(solution)/shard_map/other_half/pallas_call | solution.py:326
  7.0 3.9 %collective-permute-start.1 = (bf16[4,40,384]{2,1,0:T(8,128)(2,1)S(1)}, bf16[4,40,384]{2,1,0:T(8,128)(2,1)S(1)}, u32[]{:S(2)}, u32[]{:S(2)}) collective-permute-start(bf16[4,40,384]{2,1,0:T(8,128)(2,1)S(1)} %get-tuple-element.20), channel_id=1, source_target_pairs={{0,6},{1,25},{2,4},{3,27},{4,2},{5,29},{6,0},{7,31},{8,14},{9,17},... | collective-permute-start | bytes 368648 | tf_op jit(solution)/shard_map/ppermute | solution.py:348
  10.8 0.5 %collective-permute-start.2 = (bf16[4,40,384]{2,1,0:T(8,128)(2,1)S(1)}, bf16[4,40,384]{2,1,0:T(8,128)(2,1)S(1)}, u32[]{:S(2)}, u32[]{:S(2)}) collective-permute-start(bf16[4,40,384]{2,1,0:T(8,128)(2,1)S(1)} %get-tuple-element.21), channel_id=1, source_target_pairs={{0,4},{1,17},{2,6},{3,19},{4,0},{5,21},{6,2},{7,23},{8,12},{9,25},... | collective-permute-start | bytes 368648 | tf_op jit(solution)/shard_map/ppermute | solution.py:348
  11.3 0.4 %collective-permute-start.3 = (bf16[4,40,384]{2,1,0:T(8,128)(2,1)S(1)}, bf16[4,40,384]{2,1,0:T(8,128)(2,1)S(1)}, u32[]{:S(2)}, u32[]{:S(2)}) collective-permute-start(bf16[4,40,384]{2,1,0:T(8,128)(2,1)S(1)} %get-tuple-element.22), channel_id=1, source_target_pairs={{0,2},{1,9},{2,0},{3,11},{4,6},{5,13},{6,4},{7,15},{8,10},{9,1},{1... | collective-permute-start | bytes 368648 | tf_op jit(solution)/shard_map/ppermute | solution.py:348
  11.7 2.0 %collective-permute-done.1.refs_1_ = bf16[4,40,384]{2,1,0:T(8,128)(2,1)S(1)} collective-permute-done((bf16[4,40,384]{2,1,0:T(8,128)(2,1)S(1)}, bf16[4,40,384]{2,1,0:T(8,128)(2,1)S(1)}, u32[]{:S(2)}, u32[]{:S(2)}) %collective-permute-start.1) | collective-permute-done | bytes 122912 | tf_op jit(solution)/shard_map/ppermute | solution.py:348
  13.7 2.0 %collective-permute-done.2.refs_2_ = bf16[4,40,384]{2,1,0:T(8,128)(2,1)S(1)} collective-permute-done((bf16[4,40,384]{2,1,0:T(8,128)(2,1)S(1)}, bf16[4,40,384]{2,1,0:T(8,128)(2,1)S(1)}, u32[]{:S(2)}, u32[]{:S(2)}) %collective-permute-start.2) | collective-permute-done | bytes 122912 | tf_op jit(solution)/shard_map/ppermute | solution.py:348
  15.7 0.5 %collective-permute-done.3.refs_3_ = bf16[4,40,384]{2,1,0:T(8,128)(2,1)S(1)} collective-permute-done((bf16[4,40,384]{2,1,0:T(8,128)(2,1)S(1)}, bf16[4,40,384]{2,1,0:T(8,128)(2,1)S(1)}, u32[]{:S(2)}, u32[]{:S(2)}) %collective-permute-start.3) | collective-permute-done | bytes 122912 | tf_op jit(solution)/shard_map/ppermute | solution.py:348
  16.3 4.4 %collective-permute-start.4 = (bf16[4,40,384]{2,1,0:T(8,128)(2,1)S(1)}, bf16[4,40,384]{2,1,0:T(8,128)(2,1)S(1)}, u32[]{:S(2)}, u32[]{:S(2)}) collective-permute-start(bf16[4,40,384]{2,1,0:T(8,128)(2,1)S(1)} %get-tuple-element.24), channel_id=1, source_target_pairs={{0,24},{1,7},{2,26},{3,5},{4,28},{5,3},{6,30},{7,1},{8,16},{9,15},... | collective-permute-start | bytes 368648 | tf_op jit(solution)/shard_map/ppermute | solution.py:348
  20.6 0.0 collective-permute-start.5
  20.6 0.6 %collective-permute-start.6 = (bf16[4,40,384]{2,1,0:T(8,128)(2,1)S(1)}, bf16[4,40,384]{2,1,0:T(8,128)(2,1)S(1)}, u32[]{:S(2)}, u32[]{:S(2)}) collective-permute-start(bf16[4,40,384]{2,1,0:T(8,128)(2,1)S(1)} %get-tuple-element.26), channel_id=1, source_target_pairs={{0,8},{1,3},{2,10},{3,1},{4,12},{5,7},{6,14},{7,5},{8,0},{9,11},{1... | collective-permute-start | bytes 368648 | tf_op jit(solution)/shard_map/ppermute | solution.py:348
  21.3 2.3 %collective-permute-done.4.refs_1_ = bf16[4,40,384]{2,1,0:T(8,128)(2,1)S(1)} collective-permute-done((bf16[4,40,384]{2,1,0:T(8,128)(2,1)S(1)}, bf16[4,40,384]{2,1,0:T(8,128)(2,1)S(1)}, u32[]{:S(2)}, u32[]{:S(2)}) %collective-permute-start.4) | collective-permute-done | bytes 122912 | tf_op jit(solution)/shard_map/ppermute | solution.py:348
  23.6 3.2 %collective-permute-done.5.refs_2_ = bf16[4,40,384]{2,1,0:T(8,128)(2,1)S(1)} collective-permute-done((bf16[4,40,384]{2,1,0:T(8,128)(2,1)S(1)}, bf16[4,40,384]{2,1,0:T(8,128)(2,1)S(1)}, u32[]{:S(2)}, u32[]{:S(2)}) %collective-permute-start.5) | collective-permute-done | bytes 122912 | tf_op jit(solution)/shard_map/ppermute | solution.py:348
  26.8 0.0 collective-permute-done.6.refs_3_
  26.8 0.9 %place.1 = bf16[20,32,384]{2,1,0:T(8,128)(2,1)} custom-call(bf16[4,40,384]{2,1,0:T(8,128)(2,1)S(1)} %get-tuple-element.23.refs_0_, bf16[4,40,384]{2,1,0:T(8,128)(2,1)S(1)} %collective-permute-done.4.refs_1_, bf16[4,40,384]{2,1,0:T(8,128)(2,1)S(1)} %collective-permute-done.5.refs_2_, bf16[4,40,384]{2,1,0:T(8,128)(2,1)S(1)} %collective-permute-done.6.refs_3_), custom_call_target="tpu_custom_call" | custom-call | tf_op jit(solution)/shard_map/place/pallas_call | solution.py:366
  (1 shorter events, 0.0 us)
Async XLA Ops:
  0.0 4.8 %collective-permute-start = (bf16[2,1536,384]{2,1,0:T(8,128)(2,1)}, bf16[2,1536,384]{2,1,0:T(8,128)(2,1)S(1)}, u32[]{:S(2)}, u32[]{:S(2)}) collective-permute-start(bf16[2,1536,384]{2,1,0:T(8,128)(2,1)} %sky.1), channel_id=1, source_target_pairs={{0,1},{1,0},{2,3},{3,2},{4,5},{5,4},{6,7},{7,6},{8,9},{9,8},{10,11... | collective-permute-start | bytes 7077896 | tf_op jit(solution)/shard_map/ppermute | solution.py:290
  7.0 6.7 %collective-permute-start.1 = (bf16[4,40,384]{2,1,0:T(8,128)(2,1)S(1)}, bf16[4,40,384]{2,1,0:T(8,128)(2,1)S(1)}, u32[]{:S(2)}, u32[]{:S(2)}) collective-permute-start(bf16[4,40,384]{2,1,0:T(8,128)(2,1)S(1)} %get-tuple-element.20), channel_id=1, source_target_pairs={{0,6},{1,25},{2,4},{3,27},{4,2},{5,29},{6,0},{7,31},{8,14},{9,17},... | collective-permute-start | bytes 368648 | tf_op jit(solution)/shard_map/ppermute | solution.py:348
  10.8 4.9 %collective-permute-start.2 = (bf16[4,40,384]{2,1,0:T(8,128)(2,1)S(1)}, bf16[4,40,384]{2,1,0:T(8,128)(2,1)S(1)}, u32[]{:S(2)}, u32[]{:S(2)}) collective-permute-start(bf16[4,40,384]{2,1,0:T(8,128)(2,1)S(1)} %get-tuple-element.21), channel_id=1, source_target_pairs={{0,4},{1,17},{2,6},{3,19},{4,0},{5,21},{6,2},{7,23},{8,12},{9,25},... | collective-permute-start | bytes 368648 | tf_op jit(solution)/shard_map/ppermute | solution.py:348
  11.3 4.9 %collective-permute-start.3 = (bf16[4,40,384]{2,1,0:T(8,128)(2,1)S(1)}, bf16[4,40,384]{2,1,0:T(8,128)(2,1)S(1)}, u32[]{:S(2)}, u32[]{:S(2)}) collective-permute-start(bf16[4,40,384]{2,1,0:T(8,128)(2,1)S(1)} %get-tuple-element.22), channel_id=1, source_target_pairs={{0,2},{1,9},{2,0},{3,11},{4,6},{5,13},{6,4},{7,15},{8,10},{9,1},{1... | collective-permute-start | bytes 368648 | tf_op jit(solution)/shard_map/ppermute | solution.py:348
  16.3 7.3 %collective-permute-start.4 = (bf16[4,40,384]{2,1,0:T(8,128)(2,1)S(1)}, bf16[4,40,384]{2,1,0:T(8,128)(2,1)S(1)}, u32[]{:S(2)}, u32[]{:S(2)}) collective-permute-start(bf16[4,40,384]{2,1,0:T(8,128)(2,1)S(1)} %get-tuple-element.24), channel_id=1, source_target_pairs={{0,24},{1,7},{2,26},{3,5},{4,28},{5,3},{6,30},{7,1},{8,16},{9,15},... | collective-permute-start | bytes 368648 | tf_op jit(solution)/shard_map/ppermute | solution.py:348
  20.6 6.2 %collective-permute-start.5 = (bf16[4,40,384]{2,1,0:T(8,128)(2,1)S(1)}, bf16[4,40,384]{2,1,0:T(8,128)(2,1)S(1)}, u32[]{:S(2)}, u32[]{:S(2)}) collective-permute-start(bf16[4,40,384]{2,1,0:T(8,128)(2,1)S(1)} %get-tuple-element.25), channel_id=1, source_target_pairs={{0,16},{1,5},{2,18},{3,7},{4,20},{5,1},{6,22},{7,3},{8,24},{9,13},... | collective-permute-start | bytes 368648 | tf_op jit(solution)/shard_map/ppermute | solution.py:348
  20.6 6.2 %collective-permute-start.6 = (bf16[4,40,384]{2,1,0:T(8,128)(2,1)S(1)}, bf16[4,40,384]{2,1,0:T(8,128)(2,1)S(1)}, u32[]{:S(2)}, u32[]{:S(2)}) collective-permute-start(bf16[4,40,384]{2,1,0:T(8,128)(2,1)S(1)} %get-tuple-element.26), channel_id=1, source_target_pairs={{0,8},{1,3},{2,10},{3,1},{4,12},{5,7},{6,14},{7,5},{8,0},{9,11},{1... | collective-permute-start | bytes 368648 | tf_op jit(solution)/shard_map/ppermute | solution.py:348

commit v16 on v15

--- a/solution.py
+++ b/solution.py
@@ -180,9 +180,20 @@
     return (core % 2) * (outer == INNER)
 
 
+def outer_distance(number, outer):
+    return (outer - number) % outer
+
+
+def inner_distance(number):
+    return (0, 1, 3, 2)[number]
+
+
 def distance_of(first, second, outer):
-    straight = second * INNER + first
-    return jnp.where(crossed(lax.axis_index("beamk"), outer) == 1, first * INNER + second, straight)
+    straight = outer_distance(second, outer) * INNER + inner_distance(first)
+    if outer != INNER:
+        return straight
+    other = outer_distance(first, outer) * INNER + inner_distance(second)
+    return jnp.where(crossed(lax.axis_index("beamk"), outer) == 1, other, straight)
 
 
 def second_kernel(ways, outer, tile, info, _, factors, *refs):
@@ -234,24 +245,22 @@
                 outs[first][second, :, lane * LANES : (lane + 1) * LANES] = block
 
 
-def far_first(arrays):
-    return [arrays[0], *reversed(arrays[1:])]
-
-
 def regroup_kernel(outer, *refs):
-    arrived, onward = far_first(refs[:INNER]), refs[INNER:]
+    arrived, onward = refs[:INNER], refs[INNER:]
     for second in range(outer):
         for first in range(INNER):
             onward[second][first] = arrived[first][second]
 
 
 def place_kernel(outer, *refs):
-    arrived, (out, turned, staged, sem) = far_first(refs[:outer]), refs[outer:]
-    k_local, slot_count, columns = staged.shape
+    arrived, (out, turned, staged, sem) = refs[:outer], refs[outer:]
+    lane_tiles, k_local, slot_count, _ = staged.shape
+    columns = lane_tiles * LANES
     width = arrived[0].shape[1]
     slots = width // k_local
     pitch = turned.shape[1] // k_local
     me = lax.axis_index("blk")
+    copies = []
     for lane in range(columns // LANES):
         span = slice(lane * LANES, (lane + 1) * LANES)
         for second in range(outer):
@@ -260,15 +269,9 @@
                 source = me ^ distance_of(first, second, outer)
                 for slot in range(slots):
                     turned[lane, pl.ds(slots * source + slot, k_local, stride=pitch), :] = block[slot * k_local : (slot + 1) * k_local]
-    copies = []
-    step = -(-k_local // 4)
-    for number, start in enumerate(range(0, k_local, step)):
-        end = min(start + step, k_local)
-        for k in range(start, end):
-            for lane in range(columns // LANES):
-                values = turned[lane, k * pitch : k * pitch + slot_count]
-                staged[k, :, lane * LANES : (lane + 1) * LANES] = values.astype(staged.dtype)
-        copies.append(pltpu.make_async_copy(staged.at[start:end], out.at[start:end], sem.at[number]))
+        for k in range(k_local):
+            staged[lane, k] = turned[lane, k * pitch : k * pitch + slot_count].astype(staged.dtype)
+        copies.append(pltpu.make_async_copy(staged.at[lane], out.at[:, :, span], sem.at[lane]))
         copies[-1].start()
     for copy in copies:
         copy.wait()
@@ -344,7 +347,8 @@
         for b in range(peers):
             for core in range(ways):
                 over_outer = (step == 0) == bool(crossed(core, outer))
-                perm.append((b * ways + core, (b ^ (number * INNER if over_outer else number)) * ways + core))
+                distance = outer_distance(number, outer) * INNER if over_outer else inner_distance(number)
+                perm.append((b * ways + core, (b ^ distance) * ways + core))
         return pltpu.with_memory_space_constraint(lax.ppermute(array, ("blk", "beamk"), perm), pltpu.VMEM)
 
     first = list(sends)
@@ -358,7 +362,7 @@
             out_specs=[whole(pltpu.VMEM)] * outer,
             compiler_params=params,
             name="regroup",
-        )(*far_first(first))
+        )(*first)
     )
     for number in range(1, outer):
         second[number] = send(second[number], number, 1)
@@ -370,12 +374,12 @@
         out_specs=whole(pltpu.HBM),
         scratch_shapes=[
             pltpu.VMEM((lane_tiles, k_local * (slot_count + 1), LANES), jnp.float32),
-            pltpu.VMEM((k_local, slot_count, columns), jnp.bfloat16),
-            pltpu.SemaphoreType.DMA((4,)),
+            pltpu.VMEM((lane_tiles, k_local, slot_count, LANES), jnp.bfloat16),
+            pltpu.SemaphoreType.DMA((lane_tiles,)),
         ],
         compiler_params=params,
         name="place",
-    )(*far_first(second))
+    )(*second)
     return out.transpose(1, 0, 2)[None]
 
 

time: 27.9 us -> 28.5 us (1.022)
  waiting for transfers between devices: 10.9 us -> 12.7 us
  starting transfers between devices: 10.2 us -> 8.69 us
    ppermute x6, starting transfers between devices: 9.75 us -> 8.23 us  [send(): lax.ppermute(array, ('blk', 'beamk'), perm)]
    ppermute x6, waiting for transfers between devices: 10.1 us -> 11.4 us  [send(): lax.ppermute(array, ('blk', 'beamk'), perm)]
    pallas_call x1, Pallas kernels: 2.12 us -> 2.81 us  [local(): pl.pallas_call(functools.partial(second_kernel, ways, outer, tile), out_s...]
    pallas_call x1, Pallas kernels: 3.56 us -> 3.07 us  [local(): pl.pallas_call(functools.partial(first_kernel, ways, tile), out_shape=(pl...]
    ppermute x1, waiting for transfers between devices: 0.8 us -> 1.29 us  [local(): lax.ppermute(sky, 'beamk', perm)]
  transfers between devices with their start and end apart: 7 -> 7, of which waited for: 6 -> 6; matrix products, arithmetic and copies ran while one was open for 0% -> 0% of each run, Pallas kernels for 13% -> 11%
where the time goes in v16:
time: 28.5 us; the launch traced here: 28.2 us
  waiting for transfers between devices  12.7 us (45%)
  starting transfers between devices  8.69 us (30%)
  Pallas kernels  6.8 us (24%)
    ppermute x6, waiting for transfers between devices, send(): lax.ppermute(array, ('blk', 'beamk'), perm)  11.4 us
    ppermute x6, starting transfers between devices, send(): lax.ppermute(array, ('blk', 'beamk'), perm)  8.23 us
    pallas_call x1, Pallas kernels, local(): pl.pallas_call(functools.partial(first_kernel, ways, tile), out_shape=(pl...  3.07 us
    pallas_call x1, Pallas kernels, local(): pl.pallas_call(functools.partial(second_kernel, ways, outer, tile), out_s...  2.81 us
    ppermute x1, waiting for transfers between devices, local(): lax.ppermute(sky, 'beamk', perm)  1.29 us
    pallas_call x1, Pallas kernels, local(): pl.pallas_call(functools.partial(place_kernel, outer), out_shape=pltpu.HB...  0.88 us
  transfers between devices with their start and end apart: 7, of which 6 were waited for; matrix products, arithmetic and copies ran while one was open for 0% of the time, Pallas kernels for 11%

profile of v16, /device:TPU:0, one launch (start us, length us, event | category | flops | bytes accessed | tf_op | source)
XLA Modules:
  0.0 28.2 jit_solution(17314459453378501407)
XLA Ops:
  0.0 0.5 %collective-permute-start = (bf16[2,1536,384]{2,1,0:T(8,128)(2,1)}, bf16[2,1536,384]{2,1,0:T(8,128)(2,1)S(1)}, u32[]{:S(2)}, u32[]{:S(2)}) collective-permute-start(bf16[2,1536,384]{2,1,0:T(8,128)(2,1)} %sky.1), channel_id=1, source_target_pairs={{0,1},{1,0},{2,3},{3,2},{4,5},{5,4},{6,7},{7,6},{8,9},{9,8},{10,11... | collective-permute-start | bytes 7077896 | tf_op jit(solution)/shard_map/ppermute | solution.py:293
  0.5 3.1 %own_half.1 = (f32[2,640,384]{2,1,0:T(8,128)S(1)}, bf16[1,2,640,1536]{3,2,1,0:T(8,128)(2,1)S(1)}, f32[8,128]{1,0:T(8,128)S(1)}) custom-call(s32[2]{0:T(128)} %m_list.1, bf16[2,1536,384]{2,1,0:T(8,128)(2,1)} %sky.1, bf16[2,20,16,3072]{3,2,1,0:T(8,128)(2,1)} %wigner.1, f32[20,2,3072]{2,1,0:T(2,128)} %beam.1), custom_call_target="tpu_custom_call" | custom-call | flops 1509949440 | bytes 8388608 | tf_op jit(solution)/shard_map/own_half/pallas_call | solution.py:296
  3.5 1.3 %collective-permute-done.refs_0_ = bf16[2,1536,384]{2,1,0:T(8,128)(2,1)S(1)} collective-permute-done((bf16[2,1536,384]{2,1,0:T(8,128)(2,1)}, bf16[2,1536,384]{2,1,0:T(8,128)(2,1)S(1)}, u32[]{:S(2)}, u32[]{:S(2)}) %collective-permute-start) | collective-permute-done | bytes 2359328 | tf_op jit(solution)/shard_map/ppermute | solution.py:293
  4.8 2.8 %other_half.1 = (bf16[4,40,384]{2,1,0:T(8,128)(2,1)S(1)}, bf16[4,40,384]{2,1,0:T(8,128)(2,1)S(1)}, bf16[4,40,384]{2,1,0:T(8,128)(2,1)S(1)}, bf16[4,40,384]{2,1,0:T(8,128)(2,1)S(1)}, f32[2,640,384]{2,1,0:T(8,128)S(1)}) custom-call(f32[8,128]{1,0:T(8,128)S(1)} %get-tuple-element.16.info, ...), custom_call_target="tpu_custom_call", output_to_operand_aliasing={{4}: (1, {})} | custom-call | flops 1509949440 | bytes 8388608 | tf_op jit(solution)/shard_map/other_half/pallas_call | solution.py:329
  7.6 2.2 %collective-permute-start.1 = (bf16[4,40,384]{2,1,0:T(8,128)(2,1)S(1)}, bf16[4,40,384]{2,1,0:T(8,128)(2,1)S(1)}, u32[]{:S(2)}, u32[]{:S(2)}) collective-permute-start(bf16[4,40,384]{2,1,0:T(8,128)(2,1)S(1)} %get-tuple-element.20), channel_id=1, source_target_pairs={{0,2},{1,25},{2,0},{3,27},{4,6},{5,29},{6,4},{7,31},{8,10},{9,17},... | collective-permute-start | bytes 368648 | tf_op jit(solution)/shard_map/ppermute | solution.py:352
  9.9 1.5 %collective-permute-start.2 = (bf16[4,40,384]{2,1,0:T(8,128)(2,1)S(1)}, bf16[4,40,384]{2,1,0:T(8,128)(2,1)S(1)}, u32[]{:S(2)}, u32[]{:S(2)}) collective-permute-start(bf16[4,40,384]{2,1,0:T(8,128)(2,1)S(1)} %get-tuple-element.21), channel_id=1, source_target_pairs={{0,6},{1,17},{2,4},{3,19},{4,2},{5,21},{6,0},{7,23},{8,14},{9,25},... | collective-permute-start | bytes 368648 | tf_op jit(solution)/shard_map/ppermute | solution.py:352
  11.4 0.1 collective-permute-start.3
  11.4 1.3 %collective-permute-done.1.refs_1_ = bf16[4,40,384]{2,1,0:T(8,128)(2,1)S(1)} collective-permute-done((bf16[4,40,384]{2,1,0:T(8,128)(2,1)S(1)}, bf16[4,40,384]{2,1,0:T(8,128)(2,1)S(1)}, u32[]{:S(2)}, u32[]{:S(2)}) %collective-permute-start.1) | collective-permute-done | bytes 122912 | tf_op jit(solution)/shard_map/ppermute | solution.py:352
  12.7 3.0 %collective-permute-done.2.refs_2_ = bf16[4,40,384]{2,1,0:T(8,128)(2,1)S(1)} collective-permute-done((bf16[4,40,384]{2,1,0:T(8,128)(2,1)S(1)}, bf16[4,40,384]{2,1,0:T(8,128)(2,1)S(1)}, u32[]{:S(2)}, u32[]{:S(2)}) %collective-permute-start.2) | collective-permute-done | bytes 122912 | tf_op jit(solution)/shard_map/ppermute | solution.py:352
  15.7 1.2 %collective-permute-done.3.refs_3_ = bf16[4,40,384]{2,1,0:T(8,128)(2,1)S(1)} collective-permute-done((bf16[4,40,384]{2,1,0:T(8,128)(2,1)S(1)}, bf16[4,40,384]{2,1,0:T(8,128)(2,1)S(1)}, u32[]{:S(2)}, u32[]{:S(2)}) %collective-permute-start.3) | collective-permute-done | bytes 122912 | tf_op jit(solution)/shard_map/ppermute | solution.py:352
  17.0 3.7 %collective-permute-start.4 = (bf16[4,40,384]{2,1,0:T(8,128)(2,1)S(1)}, bf16[4,40,384]{2,1,0:T(8,128)(2,1)S(1)}, u32[]{:S(2)}, u32[]{:S(2)}) collective-permute-start(bf16[4,40,384]{2,1,0:T(8,128)(2,1)S(1)} %get-tuple-element.24), channel_id=1, source_target_pairs={{0,24},{1,3},{2,26},{3,1},{4,28},{5,7},{6,30},{7,5},{8,16},{9,11},... | collective-permute-start | bytes 368648 | tf_op jit(solution)/shard_map/ppermute | solution.py:352
  20.7 0.0 collective-permute-start.5
  20.7 0.8 %collective-permute-start.6 = (bf16[4,40,384]{2,1,0:T(8,128)(2,1)S(1)}, bf16[4,40,384]{2,1,0:T(8,128)(2,1)S(1)}, u32[]{:S(2)}, u32[]{:S(2)}) collective-permute-start(bf16[4,40,384]{2,1,0:T(8,128)(2,1)S(1)} %get-tuple-element.26), channel_id=1, source_target_pairs={{0,8},{1,5},{2,10},{3,7},{4,12},{5,1},{6,14},{7,3},{8,0},{9,13},{1... | collective-permute-start | bytes 368648 | tf_op jit(solution)/shard_map/ppermute | solution.py:352
  21.5 2.4 %collective-permute-done.4.refs_1_ = bf16[4,40,384]{2,1,0:T(8,128)(2,1)S(1)} collective-permute-done((bf16[4,40,384]{2,1,0:T(8,128)(2,1)S(1)}, bf16[4,40,384]{2,1,0:T(8,128)(2,1)S(1)}, u32[]{:S(2)}, u32[]{:S(2)}) %collective-permute-start.4) | collective-permute-done | bytes 122912 | tf_op jit(solution)/shard_map/ppermute | solution.py:352
  23.9 3.5 %collective-permute-done.5.refs_2_ = bf16[4,40,384]{2,1,0:T(8,128)(2,1)S(1)} collective-permute-done((bf16[4,40,384]{2,1,0:T(8,128)(2,1)S(1)}, bf16[4,40,384]{2,1,0:T(8,128)(2,1)S(1)}, u32[]{:S(2)}, u32[]{:S(2)}) %collective-permute-start.5) | collective-permute-done | bytes 122912 | tf_op jit(solution)/shard_map/ppermute | solution.py:352
  27.3 0.0 collective-permute-done.6.refs_3_
  27.3 0.9 %place.1 = bf16[20,32,384]{2,1,0:T(8,128)(2,1)} custom-call(bf16[4,40,384]{2,1,0:T(8,128)(2,1)S(1)} %get-tuple-element.23.refs_0_, bf16[4,40,384]{2,1,0:T(8,128)(2,1)S(1)} %collective-permute-done.4.refs_1_, bf16[4,40,384]{2,1,0:T(8,128)(2,1)S(1)} %collective-permute-done.5.refs_2_, bf16[4,40,384]{2,1,0:T(8,128)(2,1)S(1)} %collective-permute-done.6.refs_3_), custom_call_target="tpu_custom_call" | custom-call | tf_op jit(solution)/shard_map/place/pallas_call | solution.py:370
  (1 shorter events, 0.0 us)
Async XLA Ops:
  0.0 4.8 %collective-permute-start = (bf16[2,1536,384]{2,1,0:T(8,128)(2,1)}, bf16[2,1536,384]{2,1,0:T(8,128)(2,1)S(1)}, u32[]{:S(2)}, u32[]{:S(2)}) collective-permute-start(bf16[2,1536,384]{2,1,0:T(8,128)(2,1)} %sky.1), channel_id=1, source_target_pairs={{0,1},{1,0},{2,3},{3,2},{4,5},{5,4},{6,7},{7,6},{8,9},{9,8},{10,11... | collective-permute-start | bytes 7077896 | tf_op jit(solution)/shard_map/ppermute | solution.py:293
  7.6 5.1 %collective-permute-start.1 = (bf16[4,40,384]{2,1,0:T(8,128)(2,1)S(1)}, bf16[4,40,384]{2,1,0:T(8,128)(2,1)S(1)}, u32[]{:S(2)}, u32[]{:S(2)}) collective-permute-start(bf16[4,40,384]{2,1,0:T(8,128)(2,1)S(1)} %get-tuple-element.20), channel_id=1, source_target_pairs={{0,2},{1,25},{2,0},{3,27},{4,6},{5,29},{6,4},{7,31},{8,10},{9,17},... | collective-permute-start | bytes 368648 | tf_op jit(solution)/shard_map/ppermute | solution.py:352
  9.9 5.9 %collective-permute-start.2 = (bf16[4,40,384]{2,1,0:T(8,128)(2,1)S(1)}, bf16[4,40,384]{2,1,0:T(8,128)(2,1)S(1)}, u32[]{:S(2)}, u32[]{:S(2)}) collective-permute-start(bf16[4,40,384]{2,1,0:T(8,128)(2,1)S(1)} %get-tuple-element.21), channel_id=1, source_target_pairs={{0,6},{1,17},{2,4},{3,19},{4,2},{5,21},{6,0},{7,23},{8,14},{9,25},... | collective-permute-start | bytes 368648 | tf_op jit(solution)/shard_map/ppermute | solution.py:352
  11.4 5.6 %collective-permute-start.3 = (bf16[4,40,384]{2,1,0:T(8,128)(2,1)S(1)}, bf16[4,40,384]{2,1,0:T(8,128)(2,1)S(1)}, u32[]{:S(2)}, u32[]{:S(2)}) collective-permute-start(bf16[4,40,384]{2,1,0:T(8,128)(2,1)S(1)} %get-tuple-element.22), channel_id=1, source_target_pairs={{0,4},{1,9},{2,6},{3,11},{4,0},{5,13},{6,2},{7,15},{8,12},{9,1},{1... | collective-permute-start | bytes 368648 | tf_op jit(solution)/shard_map/ppermute | solution.py:352
  17.0 6.9 %collective-permute-start.4 = (bf16[4,40,384]{2,1,0:T(8,128)(2,1)S(1)}, bf16[4,40,384]{2,1,0:T(8,128)(2,1)S(1)}, u32[]{:S(2)}, u32[]{:S(2)}) collective-permute-start(bf16[4,40,384]{2,1,0:T(8,128)(2,1)S(1)} %get-tuple-element.24), channel_id=1, source_target_pairs={{0,24},{1,3},{2,26},{3,1},{4,28},{5,7},{6,30},{7,5},{8,16},{9,11},... | collective-permute-start | bytes 368648 | tf_op jit(solution)/shard_map/ppermute | solution.py:352
  20.7 6.6 %collective-permute-start.5 = (bf16[4,40,384]{2,1,0:T(8,128)(2,1)S(1)}, bf16[4,40,384]{2,1,0:T(8,128)(2,1)S(1)}, u32[]{:S(2)}, u32[]{:S(2)}) collective-permute-start(bf16[4,40,384]{2,1,0:T(8,128)(2,1)S(1)} %get-tuple-element.25), channel_id=1, source_target_pairs={{0,16},{1,7},{2,18},{3,5},{4,20},{5,3},{6,22},{7,1},{8,24},{9,15},... | collective-permute-start | bytes 368648 | tf_op jit(solution)/shard_map/ppermute | solution.py:352
  20.7 6.6 %collective-permute-start.6 = (bf16[4,40,384]{2,1,0:T(8,128)(2,1)S(1)}, bf16[4,40,384]{2,1,0:T(8,128)(2,1)S(1)}, u32[]{:S(2)}, u32[]{:S(2)}) collective-permute-start(bf16[4,40,384]{2,1,0:T(8,128)(2,1)S(1)} %get-tuple-element.26), channel_id=1, source_target_pairs={{0,8},{1,5},{2,10},{3,7},{4,12},{5,1},{6,14},{7,3},{8,0},{9,13},{1... | collective-permute-start | bytes 368648 | tf_op jit(solution)/shard_map/ppermute | solution.py:352

commit v17 on v15

--- a/solution.py
+++ b/solution.py
@@ -15,6 +15,14 @@
 
 def tile_of(rows):
     return max(t for t in range(LANES, min(rows, 512) + 1, LANES) if rows % t == 0)
+
+
+def pitch_of(rows):
+    return rows + 1 - rows % 2
+
+
+def turning(lane_tiles, groups, rows):
+    return pltpu.VMEM((lane_tiles, -(-groups // 8) * 8 * pitch_of(rows) + 8, LANES), jnp.float32)
 
 
 def whole(memory):
@@ -195,7 +203,7 @@
     width = outs[0].shape[1]
     cycles = outer * INNER
     k_local = width // slots
-    pitch = turned.shape[1] // cycles
+    pitch = pitch_of(width)
 
     m_values = [jnp.max(info[slot : slot + 1, :]).astype(jnp.int32) for slot in range(slots)]
 
@@ -250,7 +258,7 @@
     k_local, slot_count, columns = staged.shape
     width = arrived[0].shape[1]
     slots = width // k_local
-    pitch = turned.shape[1] // k_local
+    pitch = pitch_of(slot_count)
     me = lax.axis_index("blk")
     for lane in range(columns // LANES):
         span = slice(lane * LANES, (lane + 1) * LANES)
@@ -330,7 +338,7 @@
         out_specs=[whole(pltpu.VMEM)] * (INNER + 1),
         input_output_aliases={1: INNER},
         scratch_shapes=[
-            pltpu.VMEM((lane_tiles, cycles * (width + 1 - width % 2), LANES), jnp.float32),
+            turning(lane_tiles, cycles, width),
         ],
         compiler_params=params,
         cost_estimate=pl.CostEstimate(
@@ -369,7 +377,7 @@
         in_specs=[whole(pltpu.VMEM)] * outer,
         out_specs=whole(pltpu.HBM),
         scratch_shapes=[
-            pltpu.VMEM((lane_tiles, k_local * (slot_count + 1), LANES), jnp.float32),
+            turning(lane_tiles, k_local, slot_count),
             pltpu.VMEM((k_local, slot_count, columns), jnp.bfloat16),
             pltpu.SemaphoreType.DMA((4,)),
         ],

time: 27.9 us -> 27.5 us (0.986)
  starting transfers between devices: 10.2 us -> 9.12 us
  waiting for transfers between devices: 10.9 us -> 11.3 us
    ppermute x6, starting transfers between devices: 9.75 us -> 8.67 us  [send(): lax.ppermute(array, ('blk', 'beamk'), perm)]
    pallas_call x1, Pallas kernels: 2.12 us -> 2.81 us  [local(): pl.pallas_call(functools.partial(second_kernel, ways, outer, tile), out_s...]
    pallas_call x1, Pallas kernels: 3.56 us -> 3.07 us  [local(): pl.pallas_call(functools.partial(first_kernel, ways, tile), out_shape=(pl...]
    ppermute x1, waiting for transfers between devices: 0.8 us -> 1.29 us  [local(): lax.ppermute(sky, 'beamk', perm)]
  transfers between devices with their start and end apart: 7 -> 7, of which waited for: 6 -> 6; matrix products, arithmetic and copies ran while one was open for 0% -> 0% of each run, Pallas kernels for 13% -> 11%
where the time goes in v17:
time: 27.5 us; the launch traced here: 27.3 us
  waiting for transfers between devices  11.3 us (41%)
  starting transfers between devices  9.12 us (33%)
  Pallas kernels  6.85 us (25%)
    ppermute x6, waiting for transfers between devices, send(): lax.ppermute(array, ('blk', 'beamk'), perm)  10 us
    ppermute x6, starting transfers between devices, send(): lax.ppermute(array, ('blk', 'beamk'), perm)  8.67 us
    pallas_call x1, Pallas kernels, local(): pl.pallas_call(functools.partial(first_kernel, ways, tile), out_shape=(pl...  3.07 us
    pallas_call x1, Pallas kernels, local(): pl.pallas_call(functools.partial(second_kernel, ways, outer, tile), out_s...  2.81 us
    ppermute x1, waiting for transfers between devices, local(): lax.ppermute(sky, 'beamk', perm)  1.29 us
    pallas_call x1, Pallas kernels, local(): pl.pallas_call(functools.partial(place_kernel, outer), out_shape=pltpu.HB...  0.93 us
  transfers between devices with their start and end apart: 7, of which 6 were waited for; matrix products, arithmetic and copies ran while one was open for 0% of the time, Pallas kernels for 11%

profile of v17, /device:TPU:0, one launch (start us, length us, event | category | flops | bytes accessed | tf_op | source)
XLA Modules:
  0.0 27.3 jit_solution(3653351433764502938)
XLA Ops:
  0.0 0.5 %collective-permute-start = (bf16[2,1536,384]{2,1,0:T(8,128)(2,1)}, bf16[2,1536,384]{2,1,0:T(8,128)(2,1)S(1)}, u32[]{:S(2)}, u32[]{:S(2)}) collective-permute-start(bf16[2,1536,384]{2,1,0:T(8,128)(2,1)} %sky.1), channel_id=1, source_target_pairs={{0,1},{1,0},{2,3},{3,2},{4,5},{5,4},{6,7},{7,6},{8,9},{9,8},{10,11... | collective-permute-start | bytes 7077896 | tf_op jit(solution)/shard_map/ppermute | solution.py:298
  0.5 3.1 %own_half.1 = (f32[2,640,384]{2,1,0:T(8,128)S(1)}, bf16[1,2,640,1536]{3,2,1,0:T(8,128)(2,1)S(1)}, f32[8,128]{1,0:T(8,128)S(1)}) custom-call(s32[2]{0:T(128)} %m_list.1, bf16[2,1536,384]{2,1,0:T(8,128)(2,1)} %sky.1, bf16[2,20,16,3072]{3,2,1,0:T(8,128)(2,1)} %wigner.1, f32[20,2,3072]{2,1,0:T(2,128)} %beam.1), custom_call_target="tpu_custom_call" | custom-call | flops 1509949440 | bytes 8388608 | tf_op jit(solution)/shard_map/own_half/pallas_call | solution.py:301
  3.5 1.3 %collective-permute-done.refs_0_ = bf16[2,1536,384]{2,1,0:T(8,128)(2,1)S(1)} collective-permute-done((bf16[2,1536,384]{2,1,0:T(8,128)(2,1)}, bf16[2,1536,384]{2,1,0:T(8,128)(2,1)S(1)}, u32[]{:S(2)}, u32[]{:S(2)}) %collective-permute-start) | collective-permute-done | bytes 2359328 | tf_op jit(solution)/shard_map/ppermute | solution.py:298
  4.8 2.8 %other_half.1 = (bf16[4,40,384]{2,1,0:T(8,128)(2,1)S(1)}, bf16[4,40,384]{2,1,0:T(8,128)(2,1)S(1)}, bf16[4,40,384]{2,1,0:T(8,128)(2,1)S(1)}, bf16[4,40,384]{2,1,0:T(8,128)(2,1)S(1)}, f32[2,640,384]{2,1,0:T(8,128)S(1)}) custom-call(f32[8,128]{1,0:T(8,128)S(1)} %get-tuple-element.16.info, ...), custom_call_target="tpu_custom_call", output_to_operand_aliasing={{4}: (1, {})} | custom-call | flops 1509949440 | bytes 8388608 | tf_op jit(solution)/shard_map/other_half/pallas_call | solution.py:334
  7.6 3.5 %collective-permute-start.1 = (bf16[4,40,384]{2,1,0:T(8,128)(2,1)S(1)}, bf16[4,40,384]{2,1,0:T(8,128)(2,1)S(1)}, u32[]{:S(2)}, u32[]{:S(2)}) collective-permute-start(bf16[4,40,384]{2,1,0:T(8,128)(2,1)S(1)} %get-tuple-element.20), channel_id=1, source_target_pairs={{0,6},{1,25},{2,4},{3,27},{4,2},{5,29},{6,0},{7,31},{8,14},{9,17},... | collective-permute-start | bytes 368648 | tf_op jit(solution)/shard_map/ppermute | solution.py:356
  11.2 0.2 collective-permute-start.2
  11.3 0.5 %collective-permute-start.3 = (bf16[4,40,384]{2,1,0:T(8,128)(2,1)S(1)}, bf16[4,40,384]{2,1,0:T(8,128)(2,1)S(1)}, u32[]{:S(2)}, u32[]{:S(2)}) collective-permute-start(bf16[4,40,384]{2,1,0:T(8,128)(2,1)S(1)} %get-tuple-element.22), channel_id=1, source_target_pairs={{0,2},{1,9},{2,0},{3,11},{4,6},{5,13},{6,4},{7,15},{8,10},{9,1},{1... | collective-permute-start | bytes 368648 | tf_op jit(solution)/shard_map/ppermute | solution.py:356
  11.8 2.2 %collective-permute-done.1.refs_1_ = bf16[4,40,384]{2,1,0:T(8,128)(2,1)S(1)} collective-permute-done((bf16[4,40,384]{2,1,0:T(8,128)(2,1)S(1)}, bf16[4,40,384]{2,1,0:T(8,128)(2,1)S(1)}, u32[]{:S(2)}, u32[]{:S(2)}) %collective-permute-start.1) | collective-permute-done | bytes 122912 | tf_op jit(solution)/shard_map/ppermute | solution.py:356
  14.0 2.0 %collective-permute-done.2.refs_2_ = bf16[4,40,384]{2,1,0:T(8,128)(2,1)S(1)} collective-permute-done((bf16[4,40,384]{2,1,0:T(8,128)(2,1)S(1)}, bf16[4,40,384]{2,1,0:T(8,128)(2,1)S(1)}, u32[]{:S(2)}, u32[]{:S(2)}) %collective-permute-start.2) | collective-permute-done | bytes 122912 | tf_op jit(solution)/shard_map/ppermute | solution.py:356
  16.1 0.2 collective-permute-done.3.refs_3_
  16.3 3.8 %collective-permute-start.4 = (bf16[4,40,384]{2,1,0:T(8,128)(2,1)S(1)}, bf16[4,40,384]{2,1,0:T(8,128)(2,1)S(1)}, u32[]{:S(2)}, u32[]{:S(2)}) collective-permute-start(bf16[4,40,384]{2,1,0:T(8,128)(2,1)S(1)} %get-tuple-element.24), channel_id=1, source_target_pairs={{0,24},{1,7},{2,26},{3,5},{4,28},{5,3},{6,30},{7,1},{8,16},{9,15},... | collective-permute-start | bytes 368648 | tf_op jit(solution)/shard_map/ppermute | solution.py:356
  20.1 0.0 collective-permute-start.5
  20.1 0.6 %collective-permute-start.6 = (bf16[4,40,384]{2,1,0:T(8,128)(2,1)S(1)}, bf16[4,40,384]{2,1,0:T(8,128)(2,1)S(1)}, u32[]{:S(2)}, u32[]{:S(2)}) collective-permute-start(bf16[4,40,384]{2,1,0:T(8,128)(2,1)S(1)} %get-tuple-element.26), channel_id=1, source_target_pairs={{0,8},{1,3},{2,10},{3,1},{4,12},{5,7},{6,14},{7,5},{8,0},{9,11},{1... | collective-permute-start | bytes 368648 | tf_op jit(solution)/shard_map/ppermute | solution.py:356
  20.8 2.4 %collective-permute-done.4.refs_1_ = bf16[4,40,384]{2,1,0:T(8,128)(2,1)S(1)} collective-permute-done((bf16[4,40,384]{2,1,0:T(8,128)(2,1)S(1)}, bf16[4,40,384]{2,1,0:T(8,128)(2,1)S(1)}, u32[]{:S(2)}, u32[]{:S(2)}) %collective-permute-start.4) | collective-permute-done | bytes 122912 | tf_op jit(solution)/shard_map/ppermute | solution.py:356
  23.1 3.2 %collective-permute-done.5.refs_2_ = bf16[4,40,384]{2,1,0:T(8,128)(2,1)S(1)} collective-permute-done((bf16[4,40,384]{2,1,0:T(8,128)(2,1)S(1)}, bf16[4,40,384]{2,1,0:T(8,128)(2,1)S(1)}, u32[]{:S(2)}, u32[]{:S(2)}) %collective-permute-start.5) | collective-permute-done | bytes 122912 | tf_op jit(solution)/shard_map/ppermute | solution.py:356
  26.4 0.0 collective-permute-done.6.refs_3_
  26.4 0.9 %place.1 = bf16[20,32,384]{2,1,0:T(8,128)(2,1)} custom-call(bf16[4,40,384]{2,1,0:T(8,128)(2,1)S(1)} %get-tuple-element.23.refs_0_, bf16[4,40,384]{2,1,0:T(8,128)(2,1)S(1)} %collective-permute-done.4.refs_1_, bf16[4,40,384]{2,1,0:T(8,128)(2,1)S(1)} %collective-permute-done.5.refs_2_, bf16[4,40,384]{2,1,0:T(8,128)(2,1)S(1)} %collective-permute-done.6.refs_3_), custom_call_target="tpu_custom_call" | custom-call | tf_op jit(solution)/shard_map/place/pallas_call | solution.py:374
  (1 shorter events, 0.0 us)
Async XLA Ops:
  0.0 4.8 %collective-permute-start = (bf16[2,1536,384]{2,1,0:T(8,128)(2,1)}, bf16[2,1536,384]{2,1,0:T(8,128)(2,1)S(1)}, u32[]{:S(2)}, u32[]{:S(2)}) collective-permute-start(bf16[2,1536,384]{2,1,0:T(8,128)(2,1)} %sky.1), channel_id=1, source_target_pairs={{0,1},{1,0},{2,3},{3,2},{4,5},{5,4},{6,7},{7,6},{8,9},{9,8},{10,11... | collective-permute-start | bytes 7077896 | tf_op jit(solution)/shard_map/ppermute | solution.py:298
  7.6 6.4 %collective-permute-start.1 = (bf16[4,40,384]{2,1,0:T(8,128)(2,1)S(1)}, bf16[4,40,384]{2,1,0:T(8,128)(2,1)S(1)}, u32[]{:S(2)}, u32[]{:S(2)}) collective-permute-start(bf16[4,40,384]{2,1,0:T(8,128)(2,1)S(1)} %get-tuple-element.20), channel_id=1, source_target_pairs={{0,6},{1,25},{2,4},{3,27},{4,2},{5,29},{6,0},{7,31},{8,14},{9,17},... | collective-permute-start | bytes 368648 | tf_op jit(solution)/shard_map/ppermute | solution.py:356
  11.2 4.9 %collective-permute-start.2 = (bf16[4,40,384]{2,1,0:T(8,128)(2,1)S(1)}, bf16[4,40,384]{2,1,0:T(8,128)(2,1)S(1)}, u32[]{:S(2)}, u32[]{:S(2)}) collective-permute-start(bf16[4,40,384]{2,1,0:T(8,128)(2,1)S(1)} %get-tuple-element.21), channel_id=1, source_target_pairs={{0,4},{1,17},{2,6},{3,19},{4,0},{5,21},{6,2},{7,23},{8,12},{9,25},... | collective-permute-start | bytes 368648 | tf_op jit(solution)/shard_map/ppermute | solution.py:356
  11.3 4.9 %collective-permute-start.3 = (bf16[4,40,384]{2,1,0:T(8,128)(2,1)S(1)}, bf16[4,40,384]{2,1,0:T(8,128)(2,1)S(1)}, u32[]{:S(2)}, u32[]{:S(2)}) collective-permute-start(bf16[4,40,384]{2,1,0:T(8,128)(2,1)S(1)} %get-tuple-element.22), channel_id=1, source_target_pairs={{0,2},{1,9},{2,0},{3,11},{4,6},{5,13},{6,4},{7,15},{8,10},{9,1},{1... | collective-permute-start | bytes 368648 | tf_op jit(solution)/shard_map/ppermute | solution.py:356
  16.3 6.8 %collective-permute-start.4 = (bf16[4,40,384]{2,1,0:T(8,128)(2,1)S(1)}, bf16[4,40,384]{2,1,0:T(8,128)(2,1)S(1)}, u32[]{:S(2)}, u32[]{:S(2)}) collective-permute-start(bf16[4,40,384]{2,1,0:T(8,128)(2,1)S(1)} %get-tuple-element.24), channel_id=1, source_target_pairs={{0,24},{1,7},{2,26},{3,5},{4,28},{5,3},{6,30},{7,1},{8,16},{9,15},... | collective-permute-start | bytes 368648 | tf_op jit(solution)/shard_map/ppermute | solution.py:356
  20.1 6.2 %collective-permute-start.5 = (bf16[4,40,384]{2,1,0:T(8,128)(2,1)S(1)}, bf16[4,40,384]{2,1,0:T(8,128)(2,1)S(1)}, u32[]{:S(2)}, u32[]{:S(2)}) collective-permute-start(bf16[4,40,384]{2,1,0:T(8,128)(2,1)S(1)} %get-tuple-element.25), channel_id=1, source_target_pairs={{0,16},{1,5},{2,18},{3,7},{4,20},{5,1},{6,22},{7,3},{8,24},{9,13},... | collective-permute-start | bytes 368648 | tf_op jit(solution)/shard_map/ppermute | solution.py:356
  20.1 6.2 %collective-permute-start.6 = (bf16[4,40,384]{2,1,0:T(8,128)(2,1)S(1)}, bf16[4,40,384]{2,1,0:T(8,128)(2,1)S(1)}, u32[]{:S(2)}, u32[]{:S(2)}) collective-permute-start(bf16[4,40,384]{2,1,0:T(8,128)(2,1)S(1)} %get-tuple-element.26), channel_id=1, source_target_pairs={{0,8},{1,3},{2,10},{3,1},{4,12},{5,7},{6,14},{7,5},{8,0},{9,11},{1... | collective-permute-start | bytes 368648 | tf_op jit(solution)/shard_map/ppermute | solution.py:356

commit v18 on v17

--- a/solution.py
+++ b/solution.py
@@ -251,20 +251,27 @@
     for second in range(outer):
         for first in range(INNER):
             onward[second][first] = arrived[first][second]
+            if second == 1:
+                onward[outer][first] = arrived[first][second]
 
 
 def place_kernel(outer, *refs):
-    arrived, (out, turned, staged, sem) = far_first(refs[:outer]), refs[outer:]
+    here, low, *others, high = refs[: outer + 1]
+    out, turned, staged, sem = refs[outer + 1 :]
+    arrived = far_first([here, *others, high])
     k_local, slot_count, columns = staged.shape
     width = arrived[0].shape[1]
     slots = width // k_local
     pitch = pitch_of(slot_count)
     me = lax.axis_index("blk")
+    in_low = jnp.logical_or(crossed(lax.axis_index("beamk"), outer) == 1, me < outer // 2 * INNER)
     for lane in range(columns // LANES):
         span = slice(lane * LANES, (lane + 1) * LANES)
         for second in range(outer):
             for first in range(INNER):
                 block = arrived[second][first, :, span].astype(jnp.float32)
+                if second == 1:
+                    block = jnp.where(in_low, low[first, :, span].astype(jnp.float32), block)
                 source = me ^ distance_of(first, second, outer)
                 for slot in range(slots):
                     turned[lane, pl.ds(slots * source + slot, k_local, stride=pitch), :] = block[slot * k_local : (slot + 1) * k_local]
@@ -347,12 +354,13 @@
         name="other_half",
     )(info, part, factors, *pieces)
 
-    def send(array, number, step):
+    def send(array, number, step, low=None):
         perm = []
         for b in range(peers):
             for core in range(ways):
                 over_outer = (step == 0) == bool(crossed(core, outer))
-                perm.append((b * ways + core, (b ^ (number * INNER if over_outer else number)) * ways + core))
+                if low is None or low == (not over_outer or b < outer // 2 * INNER):
+                    perm.append((b * ways + core, (b ^ (number * INNER if over_outer else number)) * ways + core))
         return pltpu.with_memory_space_constraint(lax.ppermute(array, ("blk", "beamk"), perm), pltpu.VMEM)
 
     first = list(sends)
@@ -361,20 +369,23 @@
     second = list(
         pl.pallas_call(
             functools.partial(regroup_kernel, outer),
-            out_shape=[blocks(INNER)] * outer,
+            out_shape=[blocks(INNER)] * (outer + 1),
             in_specs=[whole(pltpu.VMEM)] * INNER,
-            out_specs=[whole(pltpu.VMEM)] * outer,
+            out_specs=[whole(pltpu.VMEM)] * (outer + 1),
             compiler_params=params,
             name="regroup",
         )(*far_first(first))
     )
-    for number in range(1, outer):
+    low = send(second.pop(), 1, 1, True)
+    second[1] = send(second[1], 1, 1, False)
+    for number in range(2, outer):
         second[number] = send(second[number], number, 1)
+    here, *others = far_first(second)
     slot_count = slots * peers
     out = pl.pallas_call(
         functools.partial(place_kernel, outer),
         out_shape=pltpu.HBM((k_local, slot_count, columns), jnp.bfloat16),
-        in_specs=[whole(pltpu.VMEM)] * outer,
+        in_specs=[whole(pltpu.VMEM)] * (outer + 1),
         out_specs=whole(pltpu.HBM),
         scratch_shapes=[
             turning(lane_tiles, k_local, slot_count),
@@ -383,7 +394,7 @@
         ],
         compiler_params=params,
         name="place",
-    )(*far_first(second))
+    )(here, low, *others)
     return out.transpose(1, 0, 2)[None]
 
 

time: 27.5 us -> 30.7 us (1.12)
  starting transfers between devices: 9.12 us -> 11.8 us
  waiting for transfers between devices: 11.3 us -> 12.2 us
    ppermute x6 -> x7, starting transfers between devices: 8.67 us -> 11.3 us  [send(): lax.ppermute(array, ('blk', 'beamk'), perm)]
    ppermute x6 -> x7, waiting for transfers between devices: 10 us -> 11.4 us  [send(): lax.ppermute(array, ('blk', 'beamk'), perm)]
    pallas_call x1, Pallas kernels: 2.81 us -> 2.12 us  [local(): pl.pallas_call(functools.partial(second_kernel, ways, outer, tile), out_s...]
    pallas_call x1, Pallas kernels: 3.07 us -> 3.56 us  [local(): pl.pallas_call(functools.partial(first_kernel, ways, tile), out_shape=(pl...]
    ppermute x1, waiting for transfers between devices: 1.29 us -> 0.8 us  [local(): lax.ppermute(sky, 'beamk', perm)]
  transfers between devices with their start and end apart: 7 -> 8, of which waited for: 6 -> 7; matrix products, arithmetic and copies ran while one was open for 0% -> 0% of each run, Pallas kernels for 11% -> 12%
where the time goes in v18:
time: 30.7 us
  waiting for transfers between devices  12.2 us (40%)
  starting transfers between devices  11.8 us (38%)
  Pallas kernels  6.68 us (22%)
    ppermute x7, waiting for transfers between devices, send(): lax.ppermute(array, ('blk', 'beamk'), perm)  11.4 us
    ppermute x7, starting transfers between devices, send(): lax.ppermute(array, ('blk', 'beamk'), perm)  11.3 us
    pallas_call x1, Pallas kernels, local(): pl.pallas_call(functools.partial(first_kernel, ways, tile), out_shape=(pl...  3.56 us
    pallas_call x1, Pallas kernels, local(): pl.pallas_call(functools.partial(second_kernel, ways, outer, tile), out_s...  2.12 us
    pallas_call x1, Pallas kernels, local(): pl.pallas_call(functools.partial(place_kernel, outer), out_shape=pltpu.HB...  0.94 us
    ppermute x1, waiting for transfers between devices, local(): lax.ppermute(sky, 'beamk', perm)  0.8 us
  transfers between devices with their start and end apart: 8, of which 7 were waited for; matrix products, arithmetic and copies ran while one was open for 0% of the time, Pallas kernels for 12%

profile of v18, /device:TPU:0, one launch (start us, length us, event | category | flops | bytes accessed | tf_op | source)
XLA Modules:
  0.0 30.7 jit_solution(618925849419575488)
XLA Ops:
  0.0 0.5 %collective-permute-start = (bf16[2,1536,384]{2,1,0:T(8,128)(2,1)}, bf16[2,1536,384]{2,1,0:T(8,128)(2,1)S(1)}, u32[]{:S(2)}, u32[]{:S(2)}) collective-permute-start(bf16[2,1536,384]{2,1,0:T(8,128)(2,1)} %sky.1), channel_id=1, source_target_pairs={{0,1},{1,0},{2,3},{3,2},{4,5},{5,4},{6,7},{7,6},{8,9},{9,8},{10,11... | collective-permute-start | bytes 7077896 | tf_op jit(solution)/shard_map/ppermute | solution.py:305
  0.5 3.6 %own_half.1 = (f32[2,640,384]{2,1,0:T(8,128)S(1)}, bf16[1,2,640,1536]{3,2,1,0:T(8,128)(2,1)S(1)}, f32[8,128]{1,0:T(8,128)S(1)}) custom-call(s32[2]{0:T(128)} %m_list.1, bf16[2,1536,384]{2,1,0:T(8,128)(2,1)} %sky.1, bf16[2,20,16,3072]{3,2,1,0:T(8,128)(2,1)} %wigner.1, f32[20,2,3072]{2,1,0:T(2,128)} %beam.1), custom_call_target="tpu_custom_call" | custom-call | flops 1509949440 | bytes 8388608 | tf_op jit(solution)/shard_map/own_half/pallas_call | solution.py:308
  4.0 0.8 %collective-permute-done.refs_0_ = bf16[2,1536,384]{2,1,0:T(8,128)(2,1)S(1)} collective-permute-done((bf16[2,1536,384]{2,1,0:T(8,128)(2,1)}, bf16[2,1536,384]{2,1,0:T(8,128)(2,1)S(1)}, u32[]{:S(2)}, u32[]{:S(2)}) %collective-permute-start) | collective-permute-done | bytes 2359328 | tf_op jit(solution)/shard_map/ppermute | solution.py:305
  4.8 2.1 %other_half.1 = (bf16[4,40,384]{2,1,0:T(8,128)(2,1)S(1)}, bf16[4,40,384]{2,1,0:T(8,128)(2,1)S(1)}, bf16[4,40,384]{2,1,0:T(8,128)(2,1)S(1)}, bf16[4,40,384]{2,1,0:T(8,128)(2,1)S(1)}, f32[2,640,384]{2,1,0:T(8,128)S(1)}) custom-call(f32[8,128]{1,0:T(8,128)S(1)} %get-tuple-element.17.info, ...), custom_call_target="tpu_custom_call", output_to_operand_aliasing={{4}: (1, {})} | custom-call | flops 1509949440 | bytes 8388608 | tf_op jit(solution)/shard_map/other_half/pallas_call | solution.py:341
  7.0 4.6 %collective-permute-start.1 = (bf16[4,40,384]{2,1,0:T(8,128)(2,1)S(1)}, bf16[4,40,384]{2,1,0:T(8,128)(2,1)S(1)}, u32[]{:S(2)}, u32[]{:S(2)}) collective-permute-start(bf16[4,40,384]{2,1,0:T(8,128)(2,1)S(1)} %get-tuple-element.21), channel_id=1, source_target_pairs={{0,6},{1,25},{2,4},{3,27},{4,2},{5,29},{6,0},{7,31},{8,14},{9,17},... | collective-permute-start | bytes 368648 | tf_op jit(solution)/shard_map/ppermute | solution.py:364
  11.5 0.5 %collective-permute-start.2 = (bf16[4,40,384]{2,1,0:T(8,128)(2,1)S(1)}, bf16[4,40,384]{2,1,0:T(8,128)(2,1)S(1)}, u32[]{:S(2)}, u32[]{:S(2)}) collective-permute-start(bf16[4,40,384]{2,1,0:T(8,128)(2,1)S(1)} %get-tuple-element.22), channel_id=1, source_target_pairs={{0,4},{1,17},{2,6},{3,19},{4,0},{5,21},{6,2},{7,23},{8,12},{9,25},... | collective-permute-start | bytes 368648 | tf_op jit(solution)/shard_map/ppermute | solution.py:364
  12.0 0.1 collective-permute-start.3
  12.2 2.2 %collective-permute-done.1.refs_1_ = bf16[4,40,384]{2,1,0:T(8,128)(2,1)S(1)} collective-permute-done((bf16[4,40,384]{2,1,0:T(8,128)(2,1)S(1)}, bf16[4,40,384]{2,1,0:T(8,128)(2,1)S(1)}, u32[]{:S(2)}, u32[]{:S(2)}) %collective-permute-start.1) | collective-permute-done | bytes 122912 | tf_op jit(solution)/shard_map/ppermute | solution.py:364
  14.4 2.0 %collective-permute-done.2.refs_2_ = bf16[4,40,384]{2,1,0:T(8,128)(2,1)S(1)} collective-permute-done((bf16[4,40,384]{2,1,0:T(8,128)(2,1)S(1)}, bf16[4,40,384]{2,1,0:T(8,128)(2,1)S(1)}, u32[]{:S(2)}, u32[]{:S(2)}) %collective-permute-start.2) | collective-permute-done | bytes 122912 | tf_op jit(solution)/shard_map/ppermute | solution.py:364
  16.4 0.5 %collective-permute-done.3.refs_3_ = bf16[4,40,384]{2,1,0:T(8,128)(2,1)S(1)} collective-permute-done((bf16[4,40,384]{2,1,0:T(8,128)(2,1)S(1)}, bf16[4,40,384]{2,1,0:T(8,128)(2,1)S(1)}, u32[]{:S(2)}, u32[]{:S(2)}) %collective-permute-start.3) | collective-permute-done | bytes 122912 | tf_op jit(solution)/shard_map/ppermute | solution.py:364
  16.9 0.1 regroup.1
  17.0 3.5 %collective-permute-start.4 = (bf16[4,40,384]{2,1,0:T(8,128)(2,1)S(1)}, bf16[4,40,384]{2,1,0:T(8,128)(2,1)S(1)}, u32[]{:S(2)}, u32[]{:S(2)}) collective-permute-start(bf16[4,40,384]{2,1,0:T(8,128)(2,1)S(1)} %get-tuple-element.25), channel_id=1, source_target_pairs={{0,8},{1,3},{2,10},{3,1},{4,12},{5,7},{6,14},{7,5},{8,0},{9,11},{1... | collective-permute-start | bytes 368648 | tf_op jit(solution)/shard_map/ppermute | solution.py:364
  20.5 0.8 %collective-permute-start.5 = (bf16[4,40,384]{2,1,0:T(8,128)(2,1)S(1)}, bf16[4,40,384]{2,1,0:T(8,128)(2,1)S(1)}, u32[]{:S(2)}, u32[]{:S(2)}) collective-permute-start(bf16[4,40,384]{2,1,0:T(8,128)(2,1)S(1)} %get-tuple-element.26), channel_id=1, source_target_pairs={{0,24},{1,7},{2,26},{3,5},{4,28},{5,3},{6,30},{7,1},{8,16},{9,15},... | collective-permute-start | bytes 368648 | tf_op jit(solution)/shard_map/ppermute | solution.py:364
  21.3 1.1 %collective-permute-start.6 = (bf16[4,40,384]{2,1,0:T(8,128)(2,1)S(1)}, bf16[4,40,384]{2,1,0:T(8,128)(2,1)S(1)}, u32[]{:S(2)}, u32[]{:S(2)}) collective-permute-start(bf16[4,40,384]{2,1,0:T(8,128)(2,1)S(1)} %get-tuple-element.27), channel_id=1, source_target_pairs={{0,16},{1,5},{2,18},{3,7},{4,20},{5,1},{6,22},{7,3},{8,24},{9,13},... | collective-permute-start | bytes 368648 | tf_op jit(solution)/shard_map/ppermute | solution.py:364
  22.4 0.7 %collective-permute-start.7 = (bf16[4,40,384]{2,1,0:T(8,128)(2,1)S(1)}, bf16[4,40,384]{2,1,0:T(8,128)(2,1)S(1)}, u32[]{:S(2)}, u32[]{:S(2)}) collective-permute-start(bf16[4,40,384]{2,1,0:T(8,128)(2,1)S(1)} %get-tuple-element.28), channel_id=1, source_target_pairs={{16,24},{18,26},{20,28},{22,30},{24,16},{26,18},{28,20},{30,22}} | collective-permute-start | bytes 368648 | tf_op jit(solution)/shard_map/ppermute | solution.py:364
  23.1 0.6 %collective-permute-done.4.refs_1_ = bf16[4,40,384]{2,1,0:T(8,128)(2,1)S(1)} collective-permute-done((bf16[4,40,384]{2,1,0:T(8,128)(2,1)S(1)}, bf16[4,40,384]{2,1,0:T(8,128)(2,1)S(1)}, u32[]{:S(2)}, u32[]{:S(2)}) %collective-permute-start.4) | collective-permute-done | bytes 122912 | tf_op jit(solution)/shard_map/ppermute | solution.py:364
  23.7 3.6 %collective-permute-done.5.refs_2_ = bf16[4,40,384]{2,1,0:T(8,128)(2,1)S(1)} collective-permute-done((bf16[4,40,384]{2,1,0:T(8,128)(2,1)S(1)}, bf16[4,40,384]{2,1,0:T(8,128)(2,1)S(1)}, u32[]{:S(2)}, u32[]{:S(2)}) %collective-permute-start.5) | collective-permute-done | bytes 122912 | tf_op jit(solution)/shard_map/ppermute | solution.py:364
  27.3 2.4 %collective-permute-done.6.refs_3_ = bf16[4,40,384]{2,1,0:T(8,128)(2,1)S(1)} collective-permute-done((bf16[4,40,384]{2,1,0:T(8,128)(2,1)S(1)}, bf16[4,40,384]{2,1,0:T(8,128)(2,1)S(1)}, u32[]{:S(2)}, u32[]{:S(2)}) %collective-permute-start.6) | collective-permute-done | bytes 122912 | tf_op jit(solution)/shard_map/ppermute | solution.py:364
  29.7 0.0 collective-permute-done.7.refs_4_
  29.7 0.9 %place.1 = bf16[20,32,384]{2,1,0:T(8,128)(2,1)} custom-call(bf16[4,40,384]{2,1,0:T(8,128)(2,1)S(1)} %get-tuple-element.24.refs_0_, bf16[4,40,384]{2,1,0:T(8,128)(2,1)S(1)} %collective-permute-done.4.refs_1_, bf16[4,40,384]{2,1,0:T(8,128)(2,1)S(1)} %collective-permute-done.5.refs_2_, bf16[4,40,384]{2,1,0:T(8,128)(2,1)S(1)} %collective-permute-done.6.refs_3_, ...), custom_call_target="tpu_custom_call" | custom-call | tf_op jit(solution)/shard_map/place/pallas_call | solution.py:385
Async XLA Ops:
  0.0 4.8 %collective-permute-start = (bf16[2,1536,384]{2,1,0:T(8,128)(2,1)}, bf16[2,1536,384]{2,1,0:T(8,128)(2,1)S(1)}, u32[]{:S(2)}, u32[]{:S(2)}) collective-permute-start(bf16[2,1536,384]{2,1,0:T(8,128)(2,1)} %sky.1), channel_id=1, source_target_pairs={{0,1},{1,0},{2,3},{3,2},{4,5},{5,4},{6,7},{7,6},{8,9},{9,8},{10,11... | collective-permute-start | bytes 7077896 | tf_op jit(solution)/shard_map/ppermute | solution.py:305
  7.0 7.4 %collective-permute-start.1 = (bf16[4,40,384]{2,1,0:T(8,128)(2,1)S(1)}, bf16[4,40,384]{2,1,0:T(8,128)(2,1)S(1)}, u32[]{:S(2)}, u32[]{:S(2)}) collective-permute-start(bf16[4,40,384]{2,1,0:T(8,128)(2,1)S(1)} %get-tuple-element.21), channel_id=1, source_target_pairs={{0,6},{1,25},{2,4},{3,27},{4,2},{5,29},{6,0},{7,31},{8,14},{9,17},... | collective-permute-start | bytes 368648 | tf_op jit(solution)/shard_map/ppermute | solution.py:364
  11.5 4.9 %collective-permute-start.2 = (bf16[4,40,384]{2,1,0:T(8,128)(2,1)S(1)}, bf16[4,40,384]{2,1,0:T(8,128)(2,1)S(1)}, u32[]{:S(2)}, u32[]{:S(2)}) collective-permute-start(bf16[4,40,384]{2,1,0:T(8,128)(2,1)S(1)} %get-tuple-element.22), channel_id=1, source_target_pairs={{0,4},{1,17},{2,6},{3,19},{4,0},{5,21},{6,2},{7,23},{8,12},{9,25},... | collective-permute-start | bytes 368648 | tf_op jit(solution)/shard_map/ppermute | solution.py:364
  12.0 4.9 %collective-permute-start.3 = (bf16[4,40,384]{2,1,0:T(8,128)(2,1)S(1)}, bf16[4,40,384]{2,1,0:T(8,128)(2,1)S(1)}, u32[]{:S(2)}, u32[]{:S(2)}) collective-permute-start(bf16[4,40,384]{2,1,0:T(8,128)(2,1)S(1)} %get-tuple-element.23), channel_id=1, source_target_pairs={{0,2},{1,9},{2,0},{3,11},{4,6},{5,13},{6,4},{7,15},{8,10},{9,1},{1... | collective-permute-start | bytes 368648 | tf_op jit(solution)/shard_map/ppermute | solution.py:364
  17.0 6.8 %collective-permute-start.4 = (bf16[4,40,384]{2,1,0:T(8,128)(2,1)S(1)}, bf16[4,40,384]{2,1,0:T(8,128)(2,1)S(1)}, u32[]{:S(2)}, u32[]{:S(2)}) collective-permute-start(bf16[4,40,384]{2,1,0:T(8,128)(2,1)S(1)} %get-tuple-element.25), channel_id=1, source_target_pairs={{0,8},{1,3},{2,10},{3,1},{4,12},{5,7},{6,14},{7,5},{8,0},{9,11},{1... | collective-permute-start | bytes 368648 | tf_op jit(solution)/shard_map/ppermute | solution.py:364
  20.5 6.8 %collective-permute-start.5 = (bf16[4,40,384]{2,1,0:T(8,128)(2,1)S(1)}, bf16[4,40,384]{2,1,0:T(8,128)(2,1)S(1)}, u32[]{:S(2)}, u32[]{:S(2)}) collective-permute-start(bf16[4,40,384]{2,1,0:T(8,128)(2,1)S(1)} %get-tuple-element.26), channel_id=1, source_target_pairs={{0,24},{1,7},{2,26},{3,5},{4,28},{5,3},{6,30},{7,1},{8,16},{9,15},... | collective-permute-start | bytes 368648 | tf_op jit(solution)/shard_map/ppermute | solution.py:364
  21.3 8.4 %collective-permute-start.6 = (bf16[4,40,384]{2,1,0:T(8,128)(2,1)S(1)}, bf16[4,40,384]{2,1,0:T(8,128)(2,1)S(1)}, u32[]{:S(2)}, u32[]{:S(2)}) collective-permute-start(bf16[4,40,384]{2,1,0:T(8,128)(2,1)S(1)} %get-tuple-element.27), channel_id=1, source_target_pairs={{0,16},{1,5},{2,18},{3,7},{4,20},{5,1},{6,22},{7,3},{8,24},{9,13},... | collective-permute-start | bytes 368648 | tf_op jit(solution)/shard_map/ppermute | solution.py:364
  22.4 7.3 %collective-permute-start.7 = (bf16[4,40,384]{2,1,0:T(8,128)(2,1)S(1)}, bf16[4,40,384]{2,1,0:T(8,128)(2,1)S(1)}, u32[]{:S(2)}, u32[]{:S(2)}) collective-permute-start(bf16[4,40,384]{2,1,0:T(8,128)(2,1)S(1)} %get-tuple-element.28), channel_id=1, source_target_pairs={{16,24},{18,26},{20,28},{22,30},{24,16},{26,18},{28,20},{30,22}} | collective-permute-start | bytes 368648 | tf_op jit(solution)/shard_map/ppermute | solution.py:364

commit v19 on v17

--- a/solution.py
+++ b/solution.py
@@ -246,6 +246,11 @@
     return [arrays[0], *reversed(arrays[1:])]
 
 
+def middle_first(arrays):
+    half = len(arrays) // 2
+    return [arrays[0], arrays[half], *arrays[2:half], arrays[1], *arrays[half + 1 :]]
+
+
 def regroup_kernel(outer, *refs):
     arrived, onward = far_first(refs[:INNER]), refs[INNER:]
     for second in range(outer):
@@ -254,7 +259,7 @@
 
 
 def place_kernel(outer, *refs):
-    arrived, (out, turned, staged, sem) = far_first(refs[:outer]), refs[outer:]
+    arrived, (out, turned, staged, sem) = middle_first(refs[:outer]), refs[outer:]
     k_local, slot_count, columns = staged.shape
     width = arrived[0].shape[1]
     slots = width // k_local
@@ -383,7 +388,7 @@
         ],
         compiler_params=params,
         name="place",
-    )(*far_first(second))
+    )(*middle_first(second))
     return out.transpose(1, 0, 2)[None]
 
 

time: 27.5 us -> 28.5 us (1.036)
  waiting for transfers between devices: 11.3 us -> 12.1 us
    ppermute x6, waiting for transfers between devices: 10 us -> 10.8 us  [send(): lax.ppermute(array, ('blk', 'beamk'), perm)]
  transfers between devices with their start and end apart: 7 -> 7, of which waited for: 6 -> 7; matrix products, arithmetic and copies ran while one was open for 0% -> 0% of each run, Pallas kernels for 11% -> 11%
where the time goes in v19:
time: 28.5 us; the launch traced here: 28.3 us
  waiting for transfers between devices  12.1 us (42%)
  starting transfers between devices  9.32 us (33%)
  Pallas kernels  6.85 us (24%)
    ppermute x6, waiting for transfers between devices, send(): lax.ppermute(array, ('blk', 'beamk'), perm)  10.8 us
    ppermute x6, starting transfers between devices, send(): lax.ppermute(array, ('blk', 'beamk'), perm)  8.87 us
    pallas_call x1, Pallas kernels, local(): pl.pallas_call(functools.partial(first_kernel, ways, tile), out_shape=(pl...  3.07 us
    pallas_call x1, Pallas kernels, local(): pl.pallas_call(functools.partial(second_kernel, ways, outer, tile), out_s...  2.81 us
    ppermute x1, waiting for transfers between devices, local(): lax.ppermute(sky, 'beamk', perm)  1.29 us
    pallas_call x1, Pallas kernels, local(): pl.pallas_call(functools.partial(place_kernel, outer), out_shape=pltpu.HB...  0.93 us
  transfers between devices with their start and end apart: 7, of which 7 were waited for; matrix products, arithmetic and copies ran while one was open for 0% of the time, Pallas kernels for 11%

profile of v19, /device:TPU:0, one launch (start us, length us, event | category | flops | bytes accessed | tf_op | source)
XLA Modules:
  0.0 28.3 jit_solution(3955016158156933866)
XLA Ops:
  0.0 0.5 %collective-permute-start = (bf16[2,1536,384]{2,1,0:T(8,128)(2,1)}, bf16[2,1536,384]{2,1,0:T(8,128)(2,1)S(1)}, u32[]{:S(2)}, u32[]{:S(2)}) collective-permute-start(bf16[2,1536,384]{2,1,0:T(8,128)(2,1)} %sky.1), channel_id=1, source_target_pairs={{0,1},{1,0},{2,3},{3,2},{4,5},{5,4},{6,7},{7,6},{8,9},{9,8},{10,11... | collective-permute-start | bytes 7077896 | tf_op jit(solution)/shard_map/ppermute | solution.py:303
  0.5 3.1 %own_half.1 = (f32[2,640,384]{2,1,0:T(8,128)S(1)}, bf16[1,2,640,1536]{3,2,1,0:T(8,128)(2,1)S(1)}, f32[8,128]{1,0:T(8,128)S(1)}) custom-call(s32[2]{0:T(128)} %m_list.1, bf16[2,1536,384]{2,1,0:T(8,128)(2,1)} %sky.1, bf16[2,20,16,3072]{3,2,1,0:T(8,128)(2,1)} %wigner.1, f32[20,2,3072]{2,1,0:T(2,128)} %beam.1), custom_call_target="tpu_custom_call" | custom-call | flops 1509949440 | bytes 8388608 | tf_op jit(solution)/shard_map/own_half/pallas_call | solution.py:306
  3.5 1.3 %collective-permute-done.refs_0_ = bf16[2,1536,384]{2,1,0:T(8,128)(2,1)S(1)} collective-permute-done((bf16[2,1536,384]{2,1,0:T(8,128)(2,1)}, bf16[2,1536,384]{2,1,0:T(8,128)(2,1)S(1)}, u32[]{:S(2)}, u32[]{:S(2)}) %collective-permute-start) | collective-permute-done | bytes 2359328 | tf_op jit(solution)/shard_map/ppermute | solution.py:303
  4.8 2.8 %other_half.1 = (bf16[4,40,384]{2,1,0:T(8,128)(2,1)S(1)}, bf16[4,40,384]{2,1,0:T(8,128)(2,1)S(1)}, bf16[4,40,384]{2,1,0:T(8,128)(2,1)S(1)}, bf16[4,40,384]{2,1,0:T(8,128)(2,1)S(1)}, f32[2,640,384]{2,1,0:T(8,128)S(1)}) custom-call(f32[8,128]{1,0:T(8,128)S(1)} %get-tuple-element.16.info, ...), custom_call_target="tpu_custom_call", output_to_operand_aliasing={{4}: (1, {})} | custom-call | flops 1509949440 | bytes 8388608 | tf_op jit(solution)/shard_map/other_half/pallas_call | solution.py:339
  7.6 3.5 %collective-permute-start.1 = (bf16[4,40,384]{2,1,0:T(8,128)(2,1)S(1)}, bf16[4,40,384]{2,1,0:T(8,128)(2,1)S(1)}, u32[]{:S(2)}, u32[]{:S(2)}) collective-permute-start(bf16[4,40,384]{2,1,0:T(8,128)(2,1)S(1)} %get-tuple-element.20), channel_id=1, source_target_pairs={{0,6},{1,25},{2,4},{3,27},{4,2},{5,29},{6,0},{7,31},{8,14},{9,17},... | collective-permute-start | bytes 368648 | tf_op jit(solution)/shard_map/ppermute | solution.py:361
  11.2 0.8 %collective-permute-start.2 = (bf16[4,40,384]{2,1,0:T(8,128)(2,1)S(1)}, bf16[4,40,384]{2,1,0:T(8,128)(2,1)S(1)}, u32[]{:S(2)}, u32[]{:S(2)}) collective-permute-start(bf16[4,40,384]{2,1,0:T(8,128)(2,1)S(1)} %get-tuple-element.21), channel_id=1, source_target_pairs={{0,4},{1,17},{2,6},{3,19},{4,0},{5,21},{6,2},{7,23},{8,12},{9,25},... | collective-permute-start | bytes 368648 | tf_op jit(solution)/shard_map/ppermute | solution.py:361
  12.0 0.0 collective-permute-start.3
  12.1 2.0 %collective-permute-done.1.refs_1_ = bf16[4,40,384]{2,1,0:T(8,128)(2,1)S(1)} collective-permute-done((bf16[4,40,384]{2,1,0:T(8,128)(2,1)S(1)}, bf16[4,40,384]{2,1,0:T(8,128)(2,1)S(1)}, u32[]{:S(2)}, u32[]{:S(2)}) %collective-permute-start.1) | collective-permute-done | bytes 122912 | tf_op jit(solution)/shard_map/ppermute | solution.py:361
  14.0 2.0 %collective-permute-done.2.refs_2_ = bf16[4,40,384]{2,1,0:T(8,128)(2,1)S(1)} collective-permute-done((bf16[4,40,384]{2,1,0:T(8,128)(2,1)S(1)}, bf16[4,40,384]{2,1,0:T(8,128)(2,1)S(1)}, u32[]{:S(2)}, u32[]{:S(2)}) %collective-permute-start.2) | collective-permute-done | bytes 122912 | tf_op jit(solution)/shard_map/ppermute | solution.py:361
  16.1 0.8 %collective-permute-done.3.refs_3_ = bf16[4,40,384]{2,1,0:T(8,128)(2,1)S(1)} collective-permute-done((bf16[4,40,384]{2,1,0:T(8,128)(2,1)S(1)}, bf16[4,40,384]{2,1,0:T(8,128)(2,1)S(1)}, u32[]{:S(2)}, u32[]{:S(2)}) %collective-permute-start.3) | collective-permute-done | bytes 122912 | tf_op jit(solution)/shard_map/ppermute | solution.py:361
  17.0 2.7 %collective-permute-start.4 = (bf16[4,40,384]{2,1,0:T(8,128)(2,1)S(1)}, bf16[4,40,384]{2,1,0:T(8,128)(2,1)S(1)}, u32[]{:S(2)}, u32[]{:S(2)}) collective-permute-start(bf16[4,40,384]{2,1,0:T(8,128)(2,1)S(1)} %get-tuple-element.24), channel_id=1, source_target_pairs={{0,16},{1,5},{2,18},{3,7},{4,20},{5,1},{6,22},{7,3},{8,24},{9,13},... | collective-permute-start | bytes 368648 | tf_op jit(solution)/shard_map/ppermute | solution.py:361
  19.6 1.1 %collective-permute-start.5 = (bf16[4,40,384]{2,1,0:T(8,128)(2,1)S(1)}, bf16[4,40,384]{2,1,0:T(8,128)(2,1)S(1)}, u32[]{:S(2)}, u32[]{:S(2)}) collective-permute-start(bf16[4,40,384]{2,1,0:T(8,128)(2,1)S(1)} %get-tuple-element.25), channel_id=1, source_target_pairs={{0,8},{1,3},{2,10},{3,1},{4,12},{5,7},{6,14},{7,5},{8,0},{9,11},{1... | collective-permute-start | bytes 368648 | tf_op jit(solution)/shard_map/ppermute | solution.py:361
  20.7 0.7 %collective-permute-start.6 = (bf16[4,40,384]{2,1,0:T(8,128)(2,1)S(1)}, bf16[4,40,384]{2,1,0:T(8,128)(2,1)S(1)}, u32[]{:S(2)}, u32[]{:S(2)}) collective-permute-start(bf16[4,40,384]{2,1,0:T(8,128)(2,1)S(1)} %get-tuple-element.26), channel_id=1, source_target_pairs={{0,24},{1,7},{2,26},{3,5},{4,28},{5,3},{6,30},{7,1},{8,16},{9,15},... | collective-permute-start | bytes 368648 | tf_op jit(solution)/shard_map/ppermute | solution.py:361
  21.4 2.8 %collective-permute-done.4.refs_1_ = bf16[4,40,384]{2,1,0:T(8,128)(2,1)S(1)} collective-permute-done((bf16[4,40,384]{2,1,0:T(8,128)(2,1)S(1)}, bf16[4,40,384]{2,1,0:T(8,128)(2,1)S(1)}, u32[]{:S(2)}, u32[]{:S(2)}) %collective-permute-start.4) | collective-permute-done | bytes 122912 | tf_op jit(solution)/shard_map/ppermute | solution.py:361
  24.2 1.2 %collective-permute-done.5.refs_2_ = bf16[4,40,384]{2,1,0:T(8,128)(2,1)S(1)} collective-permute-done((bf16[4,40,384]{2,1,0:T(8,128)(2,1)S(1)}, bf16[4,40,384]{2,1,0:T(8,128)(2,1)S(1)}, u32[]{:S(2)}, u32[]{:S(2)}) %collective-permute-start.5) | collective-permute-done | bytes 122912 | tf_op jit(solution)/shard_map/ppermute | solution.py:361
  25.4 2.0 %collective-permute-done.6.refs_3_ = bf16[4,40,384]{2,1,0:T(8,128)(2,1)S(1)} collective-permute-done((bf16[4,40,384]{2,1,0:T(8,128)(2,1)S(1)}, bf16[4,40,384]{2,1,0:T(8,128)(2,1)S(1)}, u32[]{:S(2)}, u32[]{:S(2)}) %collective-permute-start.6) | collective-permute-done | bytes 122912 | tf_op jit(solution)/shard_map/ppermute | solution.py:361
  27.4 0.9 %place.1 = bf16[20,32,384]{2,1,0:T(8,128)(2,1)} custom-call(bf16[4,40,384]{2,1,0:T(8,128)(2,1)S(1)} %get-tuple-element.23.refs_0_, bf16[4,40,384]{2,1,0:T(8,128)(2,1)S(1)} %collective-permute-done.4.refs_1_, bf16[4,40,384]{2,1,0:T(8,128)(2,1)S(1)} %collective-permute-done.5.refs_2_, bf16[4,40,384]{2,1,0:T(8,128)(2,1)S(1)} %collective-permute-done.6.refs_3_), custom_call_target="tpu_custom_call" | custom-call | tf_op jit(solution)/shard_map/place/pallas_call | solution.py:379
  (1 shorter events, 0.0 us)
Async XLA Ops:
  0.0 4.8 %collective-permute-start = (bf16[2,1536,384]{2,1,0:T(8,128)(2,1)}, bf16[2,1536,384]{2,1,0:T(8,128)(2,1)S(1)}, u32[]{:S(2)}, u32[]{:S(2)}) collective-permute-start(bf16[2,1536,384]{2,1,0:T(8,128)(2,1)} %sky.1), channel_id=1, source_target_pairs={{0,1},{1,0},{2,3},{3,2},{4,5},{5,4},{6,7},{7,6},{8,9},{9,8},{10,11... | collective-permute-start | bytes 7077896 | tf_op jit(solution)/shard_map/ppermute | solution.py:303
  7.6 6.4 %collective-permute-start.1 = (bf16[4,40,384]{2,1,0:T(8,128)(2,1)S(1)}, bf16[4,40,384]{2,1,0:T(8,128)(2,1)S(1)}, u32[]{:S(2)}, u32[]{:S(2)}) collective-permute-start(bf16[4,40,384]{2,1,0:T(8,128)(2,1)S(1)} %get-tuple-element.20), channel_id=1, source_target_pairs={{0,6},{1,25},{2,4},{3,27},{4,2},{5,29},{6,0},{7,31},{8,14},{9,17},... | collective-permute-start | bytes 368648 | tf_op jit(solution)/shard_map/ppermute | solution.py:361
  11.2 4.9 %collective-permute-start.2 = (bf16[4,40,384]{2,1,0:T(8,128)(2,1)S(1)}, bf16[4,40,384]{2,1,0:T(8,128)(2,1)S(1)}, u32[]{:S(2)}, u32[]{:S(2)}) collective-permute-start(bf16[4,40,384]{2,1,0:T(8,128)(2,1)S(1)} %get-tuple-element.21), channel_id=1, source_target_pairs={{0,4},{1,17},{2,6},{3,19},{4,0},{5,21},{6,2},{7,23},{8,12},{9,25},... | collective-permute-start | bytes 368648 | tf_op jit(solution)/shard_map/ppermute | solution.py:361
  12.0 4.9 %collective-permute-start.3 = (bf16[4,40,384]{2,1,0:T(8,128)(2,1)S(1)}, bf16[4,40,384]{2,1,0:T(8,128)(2,1)S(1)}, u32[]{:S(2)}, u32[]{:S(2)}) collective-permute-start(bf16[4,40,384]{2,1,0:T(8,128)(2,1)S(1)} %get-tuple-element.22), channel_id=1, source_target_pairs={{0,2},{1,9},{2,0},{3,11},{4,6},{5,13},{6,4},{7,15},{8,10},{9,1},{1... | collective-permute-start | bytes 368648 | tf_op jit(solution)/shard_map/ppermute | solution.py:361
  17.0 7.3 %collective-permute-start.4 = (bf16[4,40,384]{2,1,0:T(8,128)(2,1)S(1)}, bf16[4,40,384]{2,1,0:T(8,128)(2,1)S(1)}, u32[]{:S(2)}, u32[]{:S(2)}) collective-permute-start(bf16[4,40,384]{2,1,0:T(8,128)(2,1)S(1)} %get-tuple-element.24), channel_id=1, source_target_pairs={{0,16},{1,5},{2,18},{3,7},{4,20},{5,1},{6,22},{7,3},{8,24},{9,13},... | collective-permute-start | bytes 368648 | tf_op jit(solution)/shard_map/ppermute | solution.py:361
  19.6 5.8 %collective-permute-start.5 = (bf16[4,40,384]{2,1,0:T(8,128)(2,1)S(1)}, bf16[4,40,384]{2,1,0:T(8,128)(2,1)S(1)}, u32[]{:S(2)}, u32[]{:S(2)}) collective-permute-start(bf16[4,40,384]{2,1,0:T(8,128)(2,1)S(1)} %get-tuple-element.25), channel_id=1, source_target_pairs={{0,8},{1,3},{2,10},{3,1},{4,12},{5,7},{6,14},{7,5},{8,0},{9,11},{1... | collective-permute-start | bytes 368648 | tf_op jit(solution)/shard_map/ppermute | solution.py:361
  20.7 6.7 %collective-permute-start.6 = (bf16[4,40,384]{2,1,0:T(8,128)(2,1)S(1)}, bf16[4,40,384]{2,1,0:T(8,128)(2,1)S(1)}, u32[]{:S(2)}, u32[]{:S(2)}) collective-permute-start(bf16[4,40,384]{2,1,0:T(8,128)(2,1)S(1)} %get-tuple-element.26), channel_id=1, source_target_pairs={{0,24},{1,7},{2,26},{3,5},{4,28},{5,3},{6,30},{7,1},{8,16},{9,15},... | collective-permute-start | bytes 368648 | tf_op jit(solution)/shard_map/ppermute | solution.py:361

commit v20 on v17

--- a/solution.py
+++ b/solution.py
@@ -260,6 +260,7 @@
     slots = width // k_local
     pitch = pitch_of(slot_count)
     me = lax.axis_index("blk")
+    origin = me // (outer * INNER)
     for lane in range(columns // LANES):
         span = slice(lane * LANES, (lane + 1) * LANES)
         for second in range(outer):
@@ -274,7 +275,7 @@
         end = min(start + step, k_local)
         for k in range(start, end):
             for lane in range(columns // LANES):
-                values = turned[lane, k * pitch : k * pitch + slot_count]
+                values = turned[lane, pl.ds(origin + k * pitch, slot_count)]
                 staged[k, :, lane * LANES : (lane + 1) * LANES] = values.astype(staged.dtype)
         copies.append(pltpu.make_async_copy(staged.at[start:end], out.at[start:end], sem.at[number]))
         copies[-1].start()

time: 27.5 us -> 27.6 us (level)
  starting transfers between devices: 9.12 us -> 9.98 us
  waiting for transfers between devices: 11.3 us -> 10.8 us
    ppermute x6, starting transfers between devices: 8.67 us -> 9.53 us  [send(): lax.ppermute(array, ('blk', 'beamk'), perm)]
    pallas_call x1, Pallas kernels: 2.81 us -> 2.12 us  [local(): pl.pallas_call(functools.partial(second_kernel, ways, outer, tile), out_s...]
    pallas_call x1, Pallas kernels: 3.07 us -> 3.56 us  [local(): pl.pallas_call(functools.partial(first_kernel, ways, tile), out_shape=(pl...]
    ppermute x1, waiting for transfers between devices: 1.29 us -> 0.8 us  [local(): lax.ppermute(sky, 'beamk', perm)]
  transfers between devices with their start and end apart: 7 -> 7, of which waited for: 6 -> 6; matrix products, arithmetic and copies ran while one was open for 0% -> 0% of each run, Pallas kernels for 11% -> 13%
where the time goes in v20:
time: 27.6 us; the launch traced here: 27.5 us
  waiting for transfers between devices  10.8 us (39%)
  starting transfers between devices  9.98 us (36%)
  Pallas kernels  6.66 us (24%)
    ppermute x6, waiting for transfers between devices, send(): lax.ppermute(array, ('blk', 'beamk'), perm)  9.99 us
    ppermute x6, starting transfers between devices, send(): lax.ppermute(array, ('blk', 'beamk'), perm)  9.53 us
    pallas_call x1, Pallas kernels, local(): pl.pallas_call(functools.partial(first_kernel, ways, tile), out_shape=(pl...  3.56 us
    pallas_call x1, Pallas kernels, local(): pl.pallas_call(functools.partial(second_kernel, ways, outer, tile), out_s...  2.12 us
    pallas_call x1, Pallas kernels, local(): pl.pallas_call(functools.partial(place_kernel, outer), out_shape=pltpu.HB...  0.93 us
    ppermute x1, waiting for transfers between devices, local(): lax.ppermute(sky, 'beamk', perm)  0.8 us
  transfers between devices with their start and end apart: 7, of which 6 were waited for; matrix products, arithmetic and copies ran while one was open for 0% of the time, Pallas kernels for 13%

profile of v20, /device:TPU:0, one launch (start us, length us, event | category | flops | bytes accessed | tf_op | source)
XLA Modules:
  0.0 27.5 jit_solution(2582249664947223137)
XLA Ops:
  0.0 0.5 %collective-permute-start = (bf16[2,1536,384]{2,1,0:T(8,128)(2,1)}, bf16[2,1536,384]{2,1,0:T(8,128)(2,1)S(1)}, u32[]{:S(2)}, u32[]{:S(2)}) collective-permute-start(bf16[2,1536,384]{2,1,0:T(8,128)(2,1)} %sky.1), channel_id=1, source_target_pairs={{0,1},{1,0},{2,3},{3,2},{4,5},{5,4},{6,7},{7,6},{8,9},{9,8},{10,11... | collective-permute-start | bytes 7077896 | tf_op jit(solution)/shard_map/ppermute | solution.py:299
  0.5 3.6 %own_half.1 = (f32[2,640,384]{2,1,0:T(8,128)S(1)}, bf16[1,2,640,1536]{3,2,1,0:T(8,128)(2,1)S(1)}, f32[8,128]{1,0:T(8,128)S(1)}) custom-call(s32[2]{0:T(128)} %m_list.1, bf16[2,1536,384]{2,1,0:T(8,128)(2,1)} %sky.1, bf16[2,20,16,3072]{3,2,1,0:T(8,128)(2,1)} %wigner.1, f32[20,2,3072]{2,1,0:T(2,128)} %beam.1), custom_call_target="tpu_custom_call" | custom-call | flops 1509949440 | bytes 8388608 | tf_op jit(solution)/shard_map/own_half/pallas_call | solution.py:302
  4.0 0.8 %collective-permute-done.refs_0_ = bf16[2,1536,384]{2,1,0:T(8,128)(2,1)S(1)} collective-permute-done((bf16[2,1536,384]{2,1,0:T(8,128)(2,1)}, bf16[2,1536,384]{2,1,0:T(8,128)(2,1)S(1)}, u32[]{:S(2)}, u32[]{:S(2)}) %collective-permute-start) | collective-permute-done | bytes 2359328 | tf_op jit(solution)/shard_map/ppermute | solution.py:299
  4.8 2.1 %other_half.1 = (bf16[4,40,384]{2,1,0:T(8,128)(2,1)S(1)}, bf16[4,40,384]{2,1,0:T(8,128)(2,1)S(1)}, bf16[4,40,384]{2,1,0:T(8,128)(2,1)S(1)}, bf16[4,40,384]{2,1,0:T(8,128)(2,1)S(1)}, f32[2,640,384]{2,1,0:T(8,128)S(1)}) custom-call(f32[8,128]{1,0:T(8,128)S(1)} %get-tuple-element.16.info, ...), custom_call_target="tpu_custom_call", output_to_operand_aliasing={{4}: (1, {})} | custom-call | flops 1509949440 | bytes 8388608 | tf_op jit(solution)/shard_map/other_half/pallas_call | solution.py:335
  7.0 3.9 %collective-permute-start.1 = (bf16[4,40,384]{2,1,0:T(8,128)(2,1)S(1)}, bf16[4,40,384]{2,1,0:T(8,128)(2,1)S(1)}, u32[]{:S(2)}, u32[]{:S(2)}) collective-permute-start(bf16[4,40,384]{2,1,0:T(8,128)(2,1)S(1)} %get-tuple-element.20), channel_id=1, source_target_pairs={{0,6},{1,25},{2,4},{3,27},{4,2},{5,29},{6,0},{7,31},{8,14},{9,17},... | collective-permute-start | bytes 368648 | tf_op jit(solution)/shard_map/ppermute | solution.py:357
  10.8 1.2 %collective-permute-start.2 = (bf16[4,40,384]{2,1,0:T(8,128)(2,1)S(1)}, bf16[4,40,384]{2,1,0:T(8,128)(2,1)S(1)}, u32[]{:S(2)}, u32[]{:S(2)}) collective-permute-start(bf16[4,40,384]{2,1,0:T(8,128)(2,1)S(1)} %get-tuple-element.21), channel_id=1, source_target_pairs={{0,4},{1,17},{2,6},{3,19},{4,0},{5,21},{6,2},{7,23},{8,12},{9,25},... | collective-permute-start | bytes 368648 | tf_op jit(solution)/shard_map/ppermute | solution.py:357
  12.0 0.0 collective-permute-start.3
  12.0 1.7 %collective-permute-done.1.refs_1_ = bf16[4,40,384]{2,1,0:T(8,128)(2,1)S(1)} collective-permute-done((bf16[4,40,384]{2,1,0:T(8,128)(2,1)S(1)}, bf16[4,40,384]{2,1,0:T(8,128)(2,1)S(1)}, u32[]{:S(2)}, u32[]{:S(2)}) %collective-permute-start.1) | collective-permute-done | bytes 122912 | tf_op jit(solution)/shard_map/ppermute | solution.py:357
  13.7 2.0 %collective-permute-done.2.refs_2_ = bf16[4,40,384]{2,1,0:T(8,128)(2,1)S(1)} collective-permute-done((bf16[4,40,384]{2,1,0:T(8,128)(2,1)S(1)}, bf16[4,40,384]{2,1,0:T(8,128)(2,1)S(1)}, u32[]{:S(2)}, u32[]{:S(2)}) %collective-permute-start.2) | collective-permute-done | bytes 122912 | tf_op jit(solution)/shard_map/ppermute | solution.py:357
  15.7 1.2 %collective-permute-done.3.refs_3_ = bf16[4,40,384]{2,1,0:T(8,128)(2,1)S(1)} collective-permute-done((bf16[4,40,384]{2,1,0:T(8,128)(2,1)S(1)}, bf16[4,40,384]{2,1,0:T(8,128)(2,1)S(1)}, u32[]{:S(2)}, u32[]{:S(2)}) %collective-permute-start.3) | collective-permute-done | bytes 122912 | tf_op jit(solution)/shard_map/ppermute | solution.py:357
  17.0 3.3 %collective-permute-start.4 = (bf16[4,40,384]{2,1,0:T(8,128)(2,1)S(1)}, bf16[4,40,384]{2,1,0:T(8,128)(2,1)S(1)}, u32[]{:S(2)}, u32[]{:S(2)}) collective-permute-start(bf16[4,40,384]{2,1,0:T(8,128)(2,1)S(1)} %get-tuple-element.24), channel_id=1, source_target_pairs={{0,24},{1,7},{2,26},{3,5},{4,28},{5,3},{6,30},{7,1},{8,16},{9,15},... | collective-permute-start | bytes 368648 | tf_op jit(solution)/shard_map/ppermute | solution.py:357
  20.3 0.0 collective-permute-start.5
  20.3 1.1 %collective-permute-start.6 = (bf16[4,40,384]{2,1,0:T(8,128)(2,1)S(1)}, bf16[4,40,384]{2,1,0:T(8,128)(2,1)S(1)}, u32[]{:S(2)}, u32[]{:S(2)}) collective-permute-start(bf16[4,40,384]{2,1,0:T(8,128)(2,1)S(1)} %get-tuple-element.26), channel_id=1, source_target_pairs={{0,8},{1,3},{2,10},{3,1},{4,12},{5,7},{6,14},{7,5},{8,0},{9,11},{1... | collective-permute-start | bytes 368648 | tf_op jit(solution)/shard_map/ppermute | solution.py:357
  21.4 2.4 %collective-permute-done.4.refs_1_ = bf16[4,40,384]{2,1,0:T(8,128)(2,1)S(1)} collective-permute-done((bf16[4,40,384]{2,1,0:T(8,128)(2,1)S(1)}, bf16[4,40,384]{2,1,0:T(8,128)(2,1)S(1)}, u32[]{:S(2)}, u32[]{:S(2)}) %collective-permute-start.4) | collective-permute-done | bytes 122912 | tf_op jit(solution)/shard_map/ppermute | solution.py:357
  23.8 2.7 %collective-permute-done.5.refs_2_ = bf16[4,40,384]{2,1,0:T(8,128)(2,1)S(1)} collective-permute-done((bf16[4,40,384]{2,1,0:T(8,128)(2,1)S(1)}, bf16[4,40,384]{2,1,0:T(8,128)(2,1)S(1)}, u32[]{:S(2)}, u32[]{:S(2)}) %collective-permute-start.5) | collective-permute-done | bytes 122912 | tf_op jit(solution)/shard_map/ppermute | solution.py:357
  26.5 0.0 collective-permute-done.6.refs_3_
  26.5 0.9 %place.1 = bf16[20,32,384]{2,1,0:T(8,128)(2,1)} custom-call(bf16[4,40,384]{2,1,0:T(8,128)(2,1)S(1)} %get-tuple-element.23.refs_0_, bf16[4,40,384]{2,1,0:T(8,128)(2,1)S(1)} %collective-permute-done.4.refs_1_, bf16[4,40,384]{2,1,0:T(8,128)(2,1)S(1)} %collective-permute-done.5.refs_2_, bf16[4,40,384]{2,1,0:T(8,128)(2,1)S(1)} %collective-permute-done.6.refs_3_), custom_call_target="tpu_custom_call" | custom-call | tf_op jit(solution)/shard_map/place/pallas_call | solution.py:375
  (1 shorter events, 0.0 us)
Async XLA Ops:
  0.0 4.8 %collective-permute-start = (bf16[2,1536,384]{2,1,0:T(8,128)(2,1)}, bf16[2,1536,384]{2,1,0:T(8,128)(2,1)S(1)}, u32[]{:S(2)}, u32[]{:S(2)}) collective-permute-start(bf16[2,1536,384]{2,1,0:T(8,128)(2,1)} %sky.1), channel_id=1, source_target_pairs={{0,1},{1,0},{2,3},{3,2},{4,5},{5,4},{6,7},{7,6},{8,9},{9,8},{10,11... | collective-permute-start | bytes 7077896 | tf_op jit(solution)/shard_map/ppermute | solution.py:299
  7.0 6.7 %collective-permute-start.1 = (bf16[4,40,384]{2,1,0:T(8,128)(2,1)S(1)}, bf16[4,40,384]{2,1,0:T(8,128)(2,1)S(1)}, u32[]{:S(2)}, u32[]{:S(2)}) collective-permute-start(bf16[4,40,384]{2,1,0:T(8,128)(2,1)S(1)} %get-tuple-element.20), channel_id=1, source_target_pairs={{0,6},{1,25},{2,4},{3,27},{4,2},{5,29},{6,0},{7,31},{8,14},{9,17},... | collective-permute-start | bytes 368648 | tf_op jit(solution)/shard_map/ppermute | solution.py:357
  10.8 4.9 %collective-permute-start.2 = (bf16[4,40,384]{2,1,0:T(8,128)(2,1)S(1)}, bf16[4,40,384]{2,1,0:T(8,128)(2,1)S(1)}, u32[]{:S(2)}, u32[]{:S(2)}) collective-permute-start(bf16[4,40,384]{2,1,0:T(8,128)(2,1)S(1)} %get-tuple-element.21), channel_id=1, source_target_pairs={{0,4},{1,17},{2,6},{3,19},{4,0},{5,21},{6,2},{7,23},{8,12},{9,25},... | collective-permute-start | bytes 368648 | tf_op jit(solution)/shard_map/ppermute | solution.py:357
  12.0 4.9 %collective-permute-start.3 = (bf16[4,40,384]{2,1,0:T(8,128)(2,1)S(1)}, bf16[4,40,384]{2,1,0:T(8,128)(2,1)S(1)}, u32[]{:S(2)}, u32[]{:S(2)}) collective-permute-start(bf16[4,40,384]{2,1,0:T(8,128)(2,1)S(1)} %get-tuple-element.22), channel_id=1, source_target_pairs={{0,2},{1,9},{2,0},{3,11},{4,6},{5,13},{6,4},{7,15},{8,10},{9,1},{1... | collective-permute-start | bytes 368648 | tf_op jit(solution)/shard_map/ppermute | solution.py:357
  17.0 6.8 %collective-permute-start.4 = (bf16[4,40,384]{2,1,0:T(8,128)(2,1)S(1)}, bf16[4,40,384]{2,1,0:T(8,128)(2,1)S(1)}, u32[]{:S(2)}, u32[]{:S(2)}) collective-permute-start(bf16[4,40,384]{2,1,0:T(8,128)(2,1)S(1)} %get-tuple-element.24), channel_id=1, source_target_pairs={{0,24},{1,7},{2,26},{3,5},{4,28},{5,3},{6,30},{7,1},{8,16},{9,15},... | collective-permute-start | bytes 368648 | tf_op jit(solution)/shard_map/ppermute | solution.py:357
  20.3 6.2 %collective-permute-start.5 = (bf16[4,40,384]{2,1,0:T(8,128)(2,1)S(1)}, bf16[4,40,384]{2,1,0:T(8,128)(2,1)S(1)}, u32[]{:S(2)}, u32[]{:S(2)}) collective-permute-start(bf16[4,40,384]{2,1,0:T(8,128)(2,1)S(1)} %get-tuple-element.25), channel_id=1, source_target_pairs={{0,16},{1,5},{2,18},{3,7},{4,20},{5,1},{6,22},{7,3},{8,24},{9,13},... | collective-permute-start | bytes 368648 | tf_op jit(solution)/shard_map/ppermute | solution.py:357
  20.3 6.2 %collective-permute-start.6 = (bf16[4,40,384]{2,1,0:T(8,128)(2,1)S(1)}, bf16[4,40,384]{2,1,0:T(8,128)(2,1)S(1)}, u32[]{:S(2)}, u32[]{:S(2)}) collective-permute-start(bf16[4,40,384]{2,1,0:T(8,128)(2,1)S(1)} %get-tuple-element.26), channel_id=1, source_target_pairs={{0,8},{1,3},{2,10},{3,1},{4,12},{5,7},{6,14},{7,5},{8,0},{9,11},{1... | collective-permute-start | bytes 368648 | tf_op jit(solution)/shard_map/ppermute | solution.py:357

commit v21 on v17

--- a/solution.py
+++ b/solution.py
@@ -188,9 +188,21 @@
     return (core % 2) * (outer == INNER)
 
 
-def distance_of(first, second, outer):
-    straight = second * INNER + first
-    return jnp.where(crossed(lax.axis_index("beamk"), outer) == 1, first * INNER + second, straight)
+def inner_distance(number):
+    return (0, 3, 2, 1)[number]
+
+
+def device_at(first, second, outer, sign):
+    me = lax.axis_index("blk")
+
+    def at(shift, distance):
+        group = lax.rem(me // INNER + (sign * shift + outer), outer)
+        return group * INNER + (me % INNER ^ distance)
+
+    straight = at(second, inner_distance(first))
+    if outer != INNER:
+        return straight
+    return jnp.where(crossed(lax.axis_index("beamk"), outer) == 1, at(first, inner_distance(second)), straight)
 
 
 def second_kernel(ways, outer, tile, info, _, factors, *refs):
@@ -233,39 +245,33 @@
                         finish(slot - 1)
 
     finish(slots - 1)
-    me = lax.axis_index("blk")
     for first in range(INNER):
         for second in range(outer):
-            start = (me ^ distance_of(first, second, outer)) * pitch
+            start = device_at(first, second, outer, 1) * pitch
             for lane in range(columns // LANES):
                 block = turned[lane, pl.ds(start, width), :].astype(jnp.bfloat16)
                 outs[first][second, :, lane * LANES : (lane + 1) * LANES] = block
 
 
-def far_first(arrays):
-    return [arrays[0], *reversed(arrays[1:])]
-
-
 def regroup_kernel(outer, *refs):
-    arrived, onward = far_first(refs[:INNER]), refs[INNER:]
+    arrived, onward = refs[:INNER], refs[INNER:]
     for second in range(outer):
         for first in range(INNER):
             onward[second][first] = arrived[first][second]
 
 
 def place_kernel(outer, *refs):
-    arrived, (out, turned, staged, sem) = far_first(refs[:outer]), refs[outer:]
+    arrived, (out, turned, staged, sem) = refs[:outer], refs[outer:]
     k_local, slot_count, columns = staged.shape
     width = arrived[0].shape[1]
     slots = width // k_local
     pitch = pitch_of(slot_count)
-    me = lax.axis_index("blk")
     for lane in range(columns // LANES):
         span = slice(lane * LANES, (lane + 1) * LANES)
         for second in range(outer):
             for first in range(INNER):
                 block = arrived[second][first, :, span].astype(jnp.float32)
-                source = me ^ distance_of(first, second, outer)
+                source = device_at(first, second, outer, -1)
                 for slot in range(slots):
                     turned[lane, pl.ds(slots * source + slot, k_local, stride=pitch), :] = block[slot * k_local : (slot + 1) * k_local]
     copies = []
@@ -352,7 +358,8 @@
         for b in range(peers):
             for core in range(ways):
                 over_outer = (step == 0) == bool(crossed(core, outer))
-                perm.append((b * ways + core, (b ^ (number * INNER if over_outer else number)) * ways + core))
+                there = (b + number * INNER) % peers if over_outer else b ^ inner_distance(number)
+                perm.append((b * ways + core, there * ways + core))
         return pltpu.with_memory_space_constraint(lax.ppermute(array, ("blk", "beamk"), perm), pltpu.VMEM)
 
     first = list(sends)
@@ -366,7 +373,7 @@
             out_specs=[whole(pltpu.VMEM)] * outer,
             compiler_params=params,
             name="regroup",
-        )(*far_first(first))
+        )(*first)
     )
     for number in range(1, outer):
         second[number] = send(second[number], number, 1)
@@ -383,7 +390,7 @@
         ],
         compiler_params=params,
         name="place",
-    )(*far_first(second))
+    )(*second)
     return out.transpose(1, 0, 2)[None]
 
 

time: 27.5 us -> 28.1 us (1.022); the launches traced: 27.3 us -> 28.2 us
  starting transfers between devices: 9.12 us -> 10.5 us
  Pallas kernels: 6.85 us -> 6.52 us
    ppermute x6, starting transfers between devices: 8.67 us -> 10.1 us  [send(): lax.ppermute(array, ('blk', 'beamk'), perm)]
    pallas_call x1, Pallas kernels: 2.81 us -> 2.46 us  [local(): pl.pallas_call(functools.partial(second_kernel, ways, outer, tile), out_s...]
  transfers between devices with their start and end apart: 7 -> 7, of which waited for: 6 -> 7; matrix products, arithmetic and copies ran while one was open for 0% -> 0% of each run, Pallas kernels for 11% -> 11%
where the time goes in v21:
time: 28.1 us; the launch traced here: 28.2 us
  waiting for transfers between devices  11.1 us (40%)
  starting transfers between devices  10.5 us (37%)
  Pallas kernels  6.52 us (23%)
    ppermute x6, starting transfers between devices, send(): lax.ppermute(array, ('blk', 'beamk'), perm)  10.1 us
    ppermute x6, waiting for transfers between devices, send(): lax.ppermute(array, ('blk', 'beamk'), perm)  9.83 us
    pallas_call x1, Pallas kernels, local(): pl.pallas_call(functools.partial(first_kernel, ways, tile), out_shape=(pl...  3.07 us
    pallas_call x1, Pallas kernels, local(): pl.pallas_call(functools.partial(second_kernel, ways, outer, tile), out_s...  2.46 us
    ppermute x1, waiting for transfers between devices, local(): lax.ppermute(sky, 'beamk', perm)  1.29 us
    pallas_call x1, Pallas kernels, local(): pl.pallas_call(functools.partial(place_kernel, outer), out_shape=pltpu.HB...  0.94 us
  transfers between devices with their start and end apart: 7, of which 7 were waited for; matrix products, arithmetic and copies ran while one was open for 0% of the time, Pallas kernels for 11%

profile of v21, /device:TPU:0, one launch (start us, length us, event | category | flops | bytes accessed | tf_op | source)
XLA Modules:
  0.0 28.2 jit_solution(12519430986699694387)
XLA Ops:
  0.0 0.5 %collective-permute-start = (bf16[2,1536,384]{2,1,0:T(8,128)(2,1)}, bf16[2,1536,384]{2,1,0:T(8,128)(2,1)S(1)}, u32[]{:S(2)}, u32[]{:S(2)}) collective-permute-start(bf16[2,1536,384]{2,1,0:T(8,128)(2,1)} %sky.1), channel_id=1, source_target_pairs={{0,1},{1,0},{2,3},{3,2},{4,5},{5,4},{6,7},{7,6},{8,9},{9,8},{10,11... | collective-permute-start | bytes 7077896 | tf_op jit(solution)/shard_map/ppermute | solution.py:304
  0.5 3.1 %own_half.1 = (f32[2,640,384]{2,1,0:T(8,128)S(1)}, bf16[1,2,640,1536]{3,2,1,0:T(8,128)(2,1)S(1)}, f32[8,128]{1,0:T(8,128)S(1)}) custom-call(s32[2]{0:T(128)} %m_list.1, bf16[2,1536,384]{2,1,0:T(8,128)(2,1)} %sky.1, bf16[2,20,16,3072]{3,2,1,0:T(8,128)(2,1)} %wigner.1, f32[20,2,3072]{2,1,0:T(2,128)} %beam.1), custom_call_target="tpu_custom_call" | custom-call | flops 1509949440 | bytes 8388608 | tf_op jit(solution)/shard_map/own_half/pallas_call | solution.py:307
  3.5 1.3 %collective-permute-done.refs_0_ = bf16[2,1536,384]{2,1,0:T(8,128)(2,1)S(1)} collective-permute-done((bf16[2,1536,384]{2,1,0:T(8,128)(2,1)}, bf16[2,1536,384]{2,1,0:T(8,128)(2,1)S(1)}, u32[]{:S(2)}, u32[]{:S(2)}) %collective-permute-start) | collective-permute-done | bytes 2359328 | tf_op jit(solution)/shard_map/ppermute | solution.py:304
  4.8 2.5 %other_half.1 = (bf16[4,40,384]{2,1,0:T(8,128)(2,1)S(1)}, bf16[4,40,384]{2,1,0:T(8,128)(2,1)S(1)}, bf16[4,40,384]{2,1,0:T(8,128)(2,1)S(1)}, bf16[4,40,384]{2,1,0:T(8,128)(2,1)S(1)}, f32[2,640,384]{2,1,0:T(8,128)S(1)}) custom-call(f32[8,128]{1,0:T(8,128)S(1)} %get-tuple-element.16.info, ...), custom_call_target="tpu_custom_call", output_to_operand_aliasing={{4}: (1, {})} | custom-call | flops 1509949440 | bytes 8388608 | tf_op jit(solution)/shard_map/other_half/pallas_call | solution.py:340
  7.3 4.2 %collective-permute-start.1 = (bf16[4,40,384]{2,1,0:T(8,128)(2,1)S(1)}, bf16[4,40,384]{2,1,0:T(8,128)(2,1)S(1)}, u32[]{:S(2)}, u32[]{:S(2)}) collective-permute-start(bf16[4,40,384]{2,1,0:T(8,128)(2,1)S(1)} %get-tuple-element.20), channel_id=1, source_target_pairs={{0,6},{1,9},{2,4},{3,11},{4,2},{5,13},{6,0},{7,15},{8,14},{9,17},{... | collective-permute-start | bytes 368648 | tf_op jit(solution)/shard_map/ppermute | solution.py:363
  11.5 0.5 %collective-permute-start.2 = (bf16[4,40,384]{2,1,0:T(8,128)(2,1)S(1)}, bf16[4,40,384]{2,1,0:T(8,128)(2,1)S(1)}, u32[]{:S(2)}, u32[]{:S(2)}) collective-permute-start(bf16[4,40,384]{2,1,0:T(8,128)(2,1)S(1)} %get-tuple-element.21), channel_id=1, source_target_pairs={{0,4},{1,17},{2,6},{3,19},{4,0},{5,21},{6,2},{7,23},{8,12},{9,25},... | collective-permute-start | bytes 368648 | tf_op jit(solution)/shard_map/ppermute | solution.py:363
  12.0 0.1 collective-permute-start.3
  12.1 2.2 %collective-permute-done.1.refs_1_ = bf16[4,40,384]{2,1,0:T(8,128)(2,1)S(1)} collective-permute-done((bf16[4,40,384]{2,1,0:T(8,128)(2,1)S(1)}, bf16[4,40,384]{2,1,0:T(8,128)(2,1)S(1)}, u32[]{:S(2)}, u32[]{:S(2)}) %collective-permute-start.1) | collective-permute-done | bytes 122912 | tf_op jit(solution)/shard_map/ppermute | solution.py:363
  14.4 2.0 %collective-permute-done.2.refs_2_ = bf16[4,40,384]{2,1,0:T(8,128)(2,1)S(1)} collective-permute-done((bf16[4,40,384]{2,1,0:T(8,128)(2,1)S(1)}, bf16[4,40,384]{2,1,0:T(8,128)(2,1)S(1)}, u32[]{:S(2)}, u32[]{:S(2)}) %collective-permute-start.2) | collective-permute-done | bytes 122912 | tf_op jit(solution)/shard_map/ppermute | solution.py:363
  16.4 0.5 %collective-permute-done.3.refs_3_ = bf16[4,40,384]{2,1,0:T(8,128)(2,1)S(1)} collective-permute-done((bf16[4,40,384]{2,1,0:T(8,128)(2,1)S(1)}, bf16[4,40,384]{2,1,0:T(8,128)(2,1)S(1)}, u32[]{:S(2)}, u32[]{:S(2)}) %collective-permute-start.3) | collective-permute-done | bytes 122912 | tf_op jit(solution)/shard_map/ppermute | solution.py:363
  16.9 1.6 %collective-permute-start.4 = (bf16[4,40,384]{2,1,0:T(8,128)(2,1)S(1)}, bf16[4,40,384]{2,1,0:T(8,128)(2,1)S(1)}, u32[]{:S(2)}, u32[]{:S(2)}) collective-permute-start(bf16[4,40,384]{2,1,0:T(8,128)(2,1)S(1)} %get-tuple-element.24), channel_id=1, source_target_pairs={{0,8},{1,7},{2,10},{3,5},{4,12},{5,3},{6,14},{7,1},{8,16},{9,15},{... | collective-permute-start | bytes 368648 | tf_op jit(solution)/shard_map/ppermute | solution.py:363
  18.6 2.6 %collective-permute-start.5 = (bf16[4,40,384]{2,1,0:T(8,128)(2,1)S(1)}, bf16[4,40,384]{2,1,0:T(8,128)(2,1)S(1)}, u32[]{:S(2)}, u32[]{:S(2)}) collective-permute-start(bf16[4,40,384]{2,1,0:T(8,128)(2,1)S(1)} %get-tuple-element.25), channel_id=1, source_target_pairs={{0,16},{1,5},{2,18},{3,7},{4,20},{5,1},{6,22},{7,3},{8,24},{9,13},... | collective-permute-start | bytes 368648 | tf_op jit(solution)/shard_map/ppermute | solution.py:363
  21.2 1.0 %collective-permute-start.6 = (bf16[4,40,384]{2,1,0:T(8,128)(2,1)S(1)}, bf16[4,40,384]{2,1,0:T(8,128)(2,1)S(1)}, u32[]{:S(2)}, u32[]{:S(2)}) collective-permute-start(bf16[4,40,384]{2,1,0:T(8,128)(2,1)S(1)} %get-tuple-element.26), channel_id=1, source_target_pairs={{0,24},{1,3},{2,26},{3,1},{4,28},{5,7},{6,30},{7,5},{8,0},{9,11},{... | collective-permute-start | bytes 368648 | tf_op jit(solution)/shard_map/ppermute | solution.py:363
  22.2 1.6 %collective-permute-done.4.refs_1_ = bf16[4,40,384]{2,1,0:T(8,128)(2,1)S(1)} collective-permute-done((bf16[4,40,384]{2,1,0:T(8,128)(2,1)S(1)}, bf16[4,40,384]{2,1,0:T(8,128)(2,1)S(1)}, u32[]{:S(2)}, u32[]{:S(2)}) %collective-permute-start.4) | collective-permute-done | bytes 122912 | tf_op jit(solution)/shard_map/ppermute | solution.py:363
  23.7 2.7 %collective-permute-done.5.refs_2_ = bf16[4,40,384]{2,1,0:T(8,128)(2,1)S(1)} collective-permute-done((bf16[4,40,384]{2,1,0:T(8,128)(2,1)S(1)}, bf16[4,40,384]{2,1,0:T(8,128)(2,1)S(1)}, u32[]{:S(2)}, u32[]{:S(2)}) %collective-permute-start.5) | collective-permute-done | bytes 122912 | tf_op jit(solution)/shard_map/ppermute | solution.py:363
  26.4 0.8 %collective-permute-done.6.refs_3_ = bf16[4,40,384]{2,1,0:T(8,128)(2,1)S(1)} collective-permute-done((bf16[4,40,384]{2,1,0:T(8,128)(2,1)S(1)}, bf16[4,40,384]{2,1,0:T(8,128)(2,1)S(1)}, u32[]{:S(2)}, u32[]{:S(2)}) %collective-permute-start.6) | collective-permute-done | bytes 122912 | tf_op jit(solution)/shard_map/ppermute | solution.py:363
  27.3 0.9 %place.1 = bf16[20,32,384]{2,1,0:T(8,128)(2,1)} custom-call(bf16[4,40,384]{2,1,0:T(8,128)(2,1)S(1)} %get-tuple-element.23.refs_0_, bf16[4,40,384]{2,1,0:T(8,128)(2,1)S(1)} %collective-permute-done.4.refs_1_, bf16[4,40,384]{2,1,0:T(8,128)(2,1)S(1)} %collective-permute-done.5.refs_2_, bf16[4,40,384]{2,1,0:T(8,128)(2,1)S(1)} %collective-permute-done.6.refs_3_), custom_call_target="tpu_custom_call" | custom-call | tf_op jit(solution)/shard_map/place/pallas_call | solution.py:381
  (1 shorter events, 0.0 us)
Async XLA Ops:
  0.0 4.8 %collective-permute-start = (bf16[2,1536,384]{2,1,0:T(8,128)(2,1)}, bf16[2,1536,384]{2,1,0:T(8,128)(2,1)S(1)}, u32[]{:S(2)}, u32[]{:S(2)}) collective-permute-start(bf16[2,1536,384]{2,1,0:T(8,128)(2,1)} %sky.1), channel_id=1, source_target_pairs={{0,1},{1,0},{2,3},{3,2},{4,5},{5,4},{6,7},{7,6},{8,9},{9,8},{10,11... | collective-permute-start | bytes 7077896 | tf_op jit(solution)/shard_map/ppermute | solution.py:304
  7.3 7.1 %collective-permute-start.1 = (bf16[4,40,384]{2,1,0:T(8,128)(2,1)S(1)}, bf16[4,40,384]{2,1,0:T(8,128)(2,1)S(1)}, u32[]{:S(2)}, u32[]{:S(2)}) collective-permute-start(bf16[4,40,384]{2,1,0:T(8,128)(2,1)S(1)} %get-tuple-element.20), channel_id=1, source_target_pairs={{0,6},{1,9},{2,4},{3,11},{4,2},{5,13},{6,0},{7,15},{8,14},{9,17},{... | collective-permute-start | bytes 368648 | tf_op jit(solution)/shard_map/ppermute | solution.py:363
  11.5 4.9 %collective-permute-start.2 = (bf16[4,40,384]{2,1,0:T(8,128)(2,1)S(1)}, bf16[4,40,384]{2,1,0:T(8,128)(2,1)S(1)}, u32[]{:S(2)}, u32[]{:S(2)}) collective-permute-start(bf16[4,40,384]{2,1,0:T(8,128)(2,1)S(1)} %get-tuple-element.21), channel_id=1, source_target_pairs={{0,4},{1,17},{2,6},{3,19},{4,0},{5,21},{6,2},{7,23},{8,12},{9,25},... | collective-permute-start | bytes 368648 | tf_op jit(solution)/shard_map/ppermute | solution.py:363
  12.0 4.9 %collective-permute-start.3 = (bf16[4,40,384]{2,1,0:T(8,128)(2,1)S(1)}, bf16[4,40,384]{2,1,0:T(8,128)(2,1)S(1)}, u32[]{:S(2)}, u32[]{:S(2)}) collective-permute-start(bf16[4,40,384]{2,1,0:T(8,128)(2,1)S(1)} %get-tuple-element.22), channel_id=1, source_target_pairs={{0,2},{1,25},{2,0},{3,27},{4,6},{5,29},{6,4},{7,31},{8,10},{9,1},{... | collective-permute-start | bytes 368648 | tf_op jit(solution)/shard_map/ppermute | solution.py:363
  16.9 6.8 %collective-permute-start.4 = (bf16[4,40,384]{2,1,0:T(8,128)(2,1)S(1)}, bf16[4,40,384]{2,1,0:T(8,128)(2,1)S(1)}, u32[]{:S(2)}, u32[]{:S(2)}) collective-permute-start(bf16[4,40,384]{2,1,0:T(8,128)(2,1)S(1)} %get-tuple-element.24), channel_id=1, source_target_pairs={{0,8},{1,7},{2,10},{3,5},{4,12},{5,3},{6,14},{7,1},{8,16},{9,15},{... | collective-permute-start | bytes 368648 | tf_op jit(solution)/shard_map/ppermute | solution.py:363
  18.6 7.8 %collective-permute-start.5 = (bf16[4,40,384]{2,1,0:T(8,128)(2,1)S(1)}, bf16[4,40,384]{2,1,0:T(8,128)(2,1)S(1)}, u32[]{:S(2)}, u32[]{:S(2)}) collective-permute-start(bf16[4,40,384]{2,1,0:T(8,128)(2,1)S(1)} %get-tuple-element.25), channel_id=1, source_target_pairs={{0,16},{1,5},{2,18},{3,7},{4,20},{5,1},{6,22},{7,3},{8,24},{9,13},... | collective-permute-start | bytes 368648 | tf_op jit(solution)/shard_map/ppermute | solution.py:363
  21.2 6.1 %collective-permute-start.6 = (bf16[4,40,384]{2,1,0:T(8,128)(2,1)S(1)}, bf16[4,40,384]{2,1,0:T(8,128)(2,1)S(1)}, u32[]{:S(2)}, u32[]{:S(2)}) collective-permute-start(bf16[4,40,384]{2,1,0:T(8,128)(2,1)S(1)} %get-tuple-element.26), channel_id=1, source_target_pairs={{0,24},{1,3},{2,26},{3,1},{4,28},{5,7},{6,30},{7,5},{8,0},{9,11},{... | collective-permute-start | bytes 368648 | tf_op jit(solution)/shard_map/ppermute | solution.py:363

commit v22 on v21

--- a/solution.py
+++ b/solution.py
@@ -188,21 +188,25 @@
     return (core % 2) * (outer == INNER)
 
 
-def inner_distance(number):
-    return (0, 3, 2, 1)[number]
+def inner_shift(number):
+    return (0, 2, 1, 3)[number]
+
+
+def ring(place):
+    return place ^ (place >> 1)
 
 
 def device_at(first, second, outer, sign):
     me = lax.axis_index("blk")
 
-    def at(shift, distance):
+    def at(shift, inner):
         group = lax.rem(me // INNER + (sign * shift + outer), outer)
-        return group * INNER + (me % INNER ^ distance)
-
-    straight = at(second, inner_distance(first))
+        return group * INNER + ring(lax.rem(ring(lax.rem(me, INNER)) + (sign * inner + INNER), INNER))
+
+    straight = at(second, inner_shift(first))
     if outer != INNER:
         return straight
-    return jnp.where(crossed(lax.axis_index("beamk"), outer) == 1, at(first, inner_distance(second)), straight)
+    return jnp.where(crossed(lax.axis_index("beamk"), outer) == 1, at(first, inner_shift(second)), straight)
 
 
 def second_kernel(ways, outer, tile, info, _, factors, *refs):
@@ -358,7 +362,7 @@
         for b in range(peers):
             for core in range(ways):
                 over_outer = (step == 0) == bool(crossed(core, outer))
-                there = (b + number * INNER) % peers if over_outer else b ^ inner_distance(number)
+                there = (b + number * INNER) % peers if over_outer else b // INNER * INNER + ring((ring(b % INNER) + inner_shift(number)) % INNER)
                 perm.append((b * ways + core, there * ways + core))
         return pltpu.with_memory_space_constraint(lax.ppermute(array, ("blk", "beamk"), perm), pltpu.VMEM)
 

time: 28.1 us -> 27.7 us (0.986); the launches traced: 28.2 us -> 27.4 us
  waiting for transfers between devices: 11.1 us -> 8.62 us
  starting transfers between devices: 10.5 us -> 11.9 us
  Pallas kernels: 6.52 us -> 6.87 us
    ppermute x6, waiting for transfers between devices: 9.83 us -> 7.32 us  [send(): lax.ppermute(array, ('blk', 'beamk'), perm)]
    ppermute x6, starting transfers between devices: 10.1 us -> 11.5 us  [send(): lax.ppermute(array, ('blk', 'beamk'), perm)]
    pallas_call x1, Pallas kernels: 2.46 us -> 2.8 us  [local(): pl.pallas_call(functools.partial(second_kernel, ways, outer, tile), out_s...]
where the time goes in v22:
time: 27.7 us; the launch traced here: 27.4 us
  starting transfers between devices  11.9 us (43%)
  waiting for transfers between devices  8.62 us (31%)
  Pallas kernels  6.87 us (25%)
    ppermute x6, starting transfers between devices, send(): lax.ppermute(array, ('blk', 'beamk'), perm)  11.5 us
    ppermute x6, waiting for transfers between devices, send(): lax.ppermute(array, ('blk', 'beamk'), perm)  7.32 us
    pallas_call x1, Pallas kernels, local(): pl.pallas_call(functools.partial(first_kernel, ways, tile), out_shape=(pl...  3.07 us
    pallas_call x1, Pallas kernels, local(): pl.pallas_call(functools.partial(second_kernel, ways, outer, tile), out_s...  2.8 us
    ppermute x1, waiting for transfers between devices, local(): lax.ppermute(sky, 'beamk', perm)  1.29 us
    pallas_call x1, Pallas kernels, local(): pl.pallas_call(functools.partial(place_kernel, outer), out_shape=pltpu.HB...  0.95 us
  transfers between devices with their start and end apart: 7, of which 7 were waited for; matrix products, arithmetic and copies ran while one was open for 0% of the time, Pallas kernels for 11%

profile of v22, /device:TPU:0, one launch (start us, length us, event | category | flops | bytes accessed | tf_op | source)
XLA Modules:
  0.0 27.4 jit_solution(10107512892689043222)
XLA Ops:
  0.0 0.5 %collective-permute-start = (bf16[2,1536,384]{2,1,0:T(8,128)(2,1)}, bf16[2,1536,384]{2,1,0:T(8,128)(2,1)S(1)}, u32[]{:S(2)}, u32[]{:S(2)}) collective-permute-start(bf16[2,1536,384]{2,1,0:T(8,128)(2,1)} %sky.1), channel_id=1, source_target_pairs={{0,1},{1,0},{2,3},{3,2},{4,5},{5,4},{6,7},{7,6},{8,9},{9,8},{10,11... | collective-permute-start | bytes 7077896 | tf_op jit(solution)/shard_map/ppermute | solution.py:308
  0.5 3.1 %own_half.1 = (f32[2,640,384]{2,1,0:T(8,128)S(1)}, bf16[1,2,640,1536]{3,2,1,0:T(8,128)(2,1)S(1)}, f32[8,128]{1,0:T(8,128)S(1)}) custom-call(s32[2]{0:T(128)} %m_list.1, bf16[2,1536,384]{2,1,0:T(8,128)(2,1)} %sky.1, bf16[2,20,16,3072]{3,2,1,0:T(8,128)(2,1)} %wigner.1, f32[20,2,3072]{2,1,0:T(2,128)} %beam.1), custom_call_target="tpu_custom_call" | custom-call | flops 1509949440 | bytes 8388608 | tf_op jit(solution)/shard_map/own_half/pallas_call | solution.py:311
  3.5 1.3 %collective-permute-done.refs_0_ = bf16[2,1536,384]{2,1,0:T(8,128)(2,1)S(1)} collective-permute-done((bf16[2,1536,384]{2,1,0:T(8,128)(2,1)}, bf16[2,1536,384]{2,1,0:T(8,128)(2,1)S(1)}, u32[]{:S(2)}, u32[]{:S(2)}) %collective-permute-start) | collective-permute-done | bytes 2359328 | tf_op jit(solution)/shard_map/ppermute | solution.py:308
  4.8 2.8 %other_half.1 = (bf16[4,40,384]{2,1,0:T(8,128)(2,1)S(1)}, bf16[4,40,384]{2,1,0:T(8,128)(2,1)S(1)}, bf16[4,40,384]{2,1,0:T(8,128)(2,1)S(1)}, bf16[4,40,384]{2,1,0:T(8,128)(2,1)S(1)}, f32[2,640,384]{2,1,0:T(8,128)S(1)}) custom-call(f32[8,128]{1,0:T(8,128)S(1)} %get-tuple-element.16.info, ...), custom_call_target="tpu_custom_call", output_to_operand_aliasing={{4}: (1, {})} | custom-call | flops 1509949440 | bytes 8388608 | tf_op jit(solution)/shard_map/other_half/pallas_call | solution.py:344
  7.6 3.9 %collective-permute-start.1 = (bf16[4,40,384]{2,1,0:T(8,128)(2,1)S(1)}, bf16[4,40,384]{2,1,0:T(8,128)(2,1)S(1)}, u32[]{:S(2)}, u32[]{:S(2)}) collective-permute-start(bf16[4,40,384]{2,1,0:T(8,128)(2,1)S(1)} %get-tuple-element.20), channel_id=1, source_target_pairs={{0,6},{1,9},{2,4},{3,11},{4,2},{5,13},{6,0},{7,15},{8,14},{9,17},{... | collective-permute-start | bytes 368648 | tf_op jit(solution)/shard_map/ppermute | solution.py:367
  11.5 0.2 collective-permute-start.2
  11.7 1.8 %collective-permute-start.3 = (bf16[4,40,384]{2,1,0:T(8,128)(2,1)S(1)}, bf16[4,40,384]{2,1,0:T(8,128)(2,1)S(1)}, u32[]{:S(2)}, u32[]{:S(2)}) collective-permute-start(bf16[4,40,384]{2,1,0:T(8,128)(2,1)S(1)} %get-tuple-element.22), channel_id=1, source_target_pairs={{0,4},{1,25},{2,0},{3,27},{4,6},{5,29},{6,2},{7,31},{8,12},{9,1},{... | collective-permute-start | bytes 368648 | tf_op jit(solution)/shard_map/ppermute | solution.py:367
  13.5 0.8 %collective-permute-done.1.refs_1_ = bf16[4,40,384]{2,1,0:T(8,128)(2,1)S(1)} collective-permute-done((bf16[4,40,384]{2,1,0:T(8,128)(2,1)S(1)}, bf16[4,40,384]{2,1,0:T(8,128)(2,1)S(1)}, u32[]{:S(2)}, u32[]{:S(2)}) %collective-permute-start.1) | collective-permute-done | bytes 122912 | tf_op jit(solution)/shard_map/ppermute | solution.py:367
  14.4 2.0 %collective-permute-done.2.refs_2_ = bf16[4,40,384]{2,1,0:T(8,128)(2,1)S(1)} collective-permute-done((bf16[4,40,384]{2,1,0:T(8,128)(2,1)S(1)}, bf16[4,40,384]{2,1,0:T(8,128)(2,1)S(1)}, u32[]{:S(2)}, u32[]{:S(2)}) %collective-permute-start.2) | collective-permute-done | bytes 122912 | tf_op jit(solution)/shard_map/ppermute | solution.py:367
  16.4 0.2 collective-permute-done.3.refs_3_
  16.6 2.0 %collective-permute-start.4 = (bf16[4,40,384]{2,1,0:T(8,128)(2,1)S(1)}, bf16[4,40,384]{2,1,0:T(8,128)(2,1)S(1)}, u32[]{:S(2)}, u32[]{:S(2)}) collective-permute-start(bf16[4,40,384]{2,1,0:T(8,128)(2,1)S(1)} %get-tuple-element.24), channel_id=1, source_target_pairs={{0,8},{1,7},{2,10},{3,5},{4,12},{5,3},{6,14},{7,1},{8,16},{9,15},{... | collective-permute-start | bytes 368648 | tf_op jit(solution)/shard_map/ppermute | solution.py:367
  18.6 2.1 %collective-permute-start.5 = (bf16[4,40,384]{2,1,0:T(8,128)(2,1)S(1)}, bf16[4,40,384]{2,1,0:T(8,128)(2,1)S(1)}, u32[]{:S(2)}, u32[]{:S(2)}) collective-permute-start(bf16[4,40,384]{2,1,0:T(8,128)(2,1)S(1)} %get-tuple-element.25), channel_id=1, source_target_pairs={{0,16},{1,3},{2,18},{3,7},{4,20},{5,1},{6,22},{7,5},{8,24},{9,11},... | collective-permute-start | bytes 368648 | tf_op jit(solution)/shard_map/ppermute | solution.py:367
  20.7 1.5 %collective-permute-start.6 = (bf16[4,40,384]{2,1,0:T(8,128)(2,1)S(1)}, bf16[4,40,384]{2,1,0:T(8,128)(2,1)S(1)}, u32[]{:S(2)}, u32[]{:S(2)}) collective-permute-start(bf16[4,40,384]{2,1,0:T(8,128)(2,1)S(1)} %get-tuple-element.26), channel_id=1, source_target_pairs={{0,24},{1,5},{2,26},{3,1},{4,28},{5,7},{6,30},{7,3},{8,0},{9,13},{... | collective-permute-start | bytes 368648 | tf_op jit(solution)/shard_map/ppermute | solution.py:367
  22.2 1.2 %collective-permute-done.4.refs_1_ = bf16[4,40,384]{2,1,0:T(8,128)(2,1)S(1)} collective-permute-done((bf16[4,40,384]{2,1,0:T(8,128)(2,1)S(1)}, bf16[4,40,384]{2,1,0:T(8,128)(2,1)S(1)}, u32[]{:S(2)}, u32[]{:S(2)}) %collective-permute-start.4) | collective-permute-done | bytes 122912 | tf_op jit(solution)/shard_map/ppermute | solution.py:367
  23.4 2.7 %collective-permute-done.5.refs_2_ = bf16[4,40,384]{2,1,0:T(8,128)(2,1)S(1)} collective-permute-done((bf16[4,40,384]{2,1,0:T(8,128)(2,1)S(1)}, bf16[4,40,384]{2,1,0:T(8,128)(2,1)S(1)}, u32[]{:S(2)}, u32[]{:S(2)}) %collective-permute-start.5) | collective-permute-done | bytes 122912 | tf_op jit(solution)/shard_map/ppermute | solution.py:367
  26.1 0.4 %collective-permute-done.6.refs_3_ = bf16[4,40,384]{2,1,0:T(8,128)(2,1)S(1)} collective-permute-done((bf16[4,40,384]{2,1,0:T(8,128)(2,1)S(1)}, bf16[4,40,384]{2,1,0:T(8,128)(2,1)S(1)}, u32[]{:S(2)}, u32[]{:S(2)}) %collective-permute-start.6) | collective-permute-done | bytes 122912 | tf_op jit(solution)/shard_map/ppermute | solution.py:367
  26.5 0.9 %place.1 = bf16[20,32,384]{2,1,0:T(8,128)(2,1)} custom-call(bf16[4,40,384]{2,1,0:T(8,128)(2,1)S(1)} %get-tuple-element.23.refs_0_, bf16[4,40,384]{2,1,0:T(8,128)(2,1)S(1)} %collective-permute-done.4.refs_1_, bf16[4,40,384]{2,1,0:T(8,128)(2,1)S(1)} %collective-permute-done.5.refs_2_, bf16[4,40,384]{2,1,0:T(8,128)(2,1)S(1)} %collective-permute-done.6.refs_3_), custom_call_target="tpu_custom_call" | custom-call | tf_op jit(solution)/shard_map/place/pallas_call | solution.py:385
  (1 shorter events, 0.0 us)
Async XLA Ops:
  0.0 4.8 %collective-permute-start = (bf16[2,1536,384]{2,1,0:T(8,128)(2,1)}, bf16[2,1536,384]{2,1,0:T(8,128)(2,1)S(1)}, u32[]{:S(2)}, u32[]{:S(2)}) collective-permute-start(bf16[2,1536,384]{2,1,0:T(8,128)(2,1)} %sky.1), channel_id=1, source_target_pairs={{0,1},{1,0},{2,3},{3,2},{4,5},{5,4},{6,7},{7,6},{8,9},{9,8},{10,11... | collective-permute-start | bytes 7077896 | tf_op jit(solution)/shard_map/ppermute | solution.py:308
  7.6 6.7 %collective-permute-start.1 = (bf16[4,40,384]{2,1,0:T(8,128)(2,1)S(1)}, bf16[4,40,384]{2,1,0:T(8,128)(2,1)S(1)}, u32[]{:S(2)}, u32[]{:S(2)}) collective-permute-start(bf16[4,40,384]{2,1,0:T(8,128)(2,1)S(1)} %get-tuple-element.20), channel_id=1, source_target_pairs={{0,6},{1,9},{2,4},{3,11},{4,2},{5,13},{6,0},{7,15},{8,14},{9,17},{... | collective-permute-start | bytes 368648 | tf_op jit(solution)/shard_map/ppermute | solution.py:367
  11.5 4.9 %collective-permute-start.2 = (bf16[4,40,384]{2,1,0:T(8,128)(2,1)S(1)}, bf16[4,40,384]{2,1,0:T(8,128)(2,1)S(1)}, u32[]{:S(2)}, u32[]{:S(2)}) collective-permute-start(bf16[4,40,384]{2,1,0:T(8,128)(2,1)S(1)} %get-tuple-element.21), channel_id=1, source_target_pairs={{0,2},{1,17},{2,6},{3,19},{4,0},{5,21},{6,4},{7,23},{8,10},{9,25},... | collective-permute-start | bytes 368648 | tf_op jit(solution)/shard_map/ppermute | solution.py:367
  11.7 4.9 %collective-permute-start.3 = (bf16[4,40,384]{2,1,0:T(8,128)(2,1)S(1)}, bf16[4,40,384]{2,1,0:T(8,128)(2,1)S(1)}, u32[]{:S(2)}, u32[]{:S(2)}) collective-permute-start(bf16[4,40,384]{2,1,0:T(8,128)(2,1)S(1)} %get-tuple-element.22), channel_id=1, source_target_pairs={{0,4},{1,25},{2,0},{3,27},{4,6},{5,29},{6,2},{7,31},{8,12},{9,1},{... | collective-permute-start | bytes 368648 | tf_op jit(solution)/shard_map/ppermute | solution.py:367
  16.6 6.8 %collective-permute-start.4 = (bf16[4,40,384]{2,1,0:T(8,128)(2,1)S(1)}, bf16[4,40,384]{2,1,0:T(8,128)(2,1)S(1)}, u32[]{:S(2)}, u32[]{:S(2)}) collective-permute-start(bf16[4,40,384]{2,1,0:T(8,128)(2,1)S(1)} %get-tuple-element.24), channel_id=1, source_target_pairs={{0,8},{1,7},{2,10},{3,5},{4,12},{5,3},{6,14},{7,1},{8,16},{9,15},{... | collective-permute-start | bytes 368648 | tf_op jit(solution)/shard_map/ppermute | solution.py:367
  18.6 7.5 %collective-permute-start.5 = (bf16[4,40,384]{2,1,0:T(8,128)(2,1)S(1)}, bf16[4,40,384]{2,1,0:T(8,128)(2,1)S(1)}, u32[]{:S(2)}, u32[]{:S(2)}) collective-permute-start(bf16[4,40,384]{2,1,0:T(8,128)(2,1)S(1)} %get-tuple-element.25), channel_id=1, source_target_pairs={{0,16},{1,3},{2,18},{3,7},{4,20},{5,1},{6,22},{7,5},{8,24},{9,11},... | collective-permute-start | bytes 368648 | tf_op jit(solution)/shard_map/ppermute | solution.py:367
  20.7 5.8 %collective-permute-start.6 = (bf16[4,40,384]{2,1,0:T(8,128)(2,1)S(1)}, bf16[4,40,384]{2,1,0:T(8,128)(2,1)S(1)}, u32[]{:S(2)}, u32[]{:S(2)}) collective-permute-start(bf16[4,40,384]{2,1,0:T(8,128)(2,1)S(1)} %get-tuple-element.26), channel_id=1, source_target_pairs={{0,24},{1,5},{2,26},{3,1},{4,28},{5,7},{6,30},{7,3},{8,0},{9,13},{... | collective-permute-start | bytes 368648 | tf_op jit(solution)/shard_map/ppermute | solution.py:367
